TPU v7x, 32 devices: a whole 2x2x4 slice. The times are simulated.
32 devices in a mesh: ens: 2 (over x), tile: 16 (over z, y, core).
Axes of the slice: x: 2, y: 2, z: 4, core: 2. Of those that a mesh axis runs over, the one named last changes fastest.
Arguments:
- fields: bfloat16 [2, 16, 48, 48, 128], P('ens', 'tile'), may hold values from -6 to 6
- weight_first: bfloat16 [3, 3, 128, 128], replicated, may hold values from -0.1875 to 0.1875
- weight_second: bfloat16 [3, 3, 128, 128], replicated, may hold values from -0.1875 to 0.1875
- neighbours: int32 [16, 4], replicated, may hold values from 0 to 15, as said below
- cotangent: bfloat16 [2, 16, 48, 48, 128], P('ens', 'tile'), may hold values from -6 to 6
Outputs:
- out_field: bfloat16 [2, 16, 48, 48, 128], P('ens', 'tile')
- grad_fields: bfloat16 [2, 16, 48, 48, 128], P('ens', 'tile')
- grad_first: float32 [3, 3, 128, 128], replicated
- grad_second: float32 [3, 3, 128, 128], replicated
Inputs may be any that keep to these rules, and one draw needn't show every extreme that they name: The tiles form a grid of 4 rows of 4: the tile at index p has the four neighbours p - 4, p + 1, p + 4 and p - 1 modulo 16, one beside each side, listed clockwise from a starting side that varies from tile to tile; the relation is mutual.
All inputs are finite; a program needn't handle non-finite values.
Results may differ from a plain program's by a relative error of at most 0.0061.
Values may be sent and summed in bfloat16 or wider, within the bound.
No kernel may reach another device: no remote copies, remote signals or barrier semaphores. Data moves between devices by JAX's collectives and lax.ppermute only.
A program may use at most 64 MiB of HBM per device.

v0:
```python
import jax
import jax.numpy as jnp
from jax import lax
from jax.sharding import PartitionSpec as P

root_half = 0.7071067811865476
inv_root_tau = 0.3989422804014327


def from_behind(block, axis, distance):
    devices = range(lax.axis_size(axis))
    route = [((i - distance) % len(devices), i) for i in devices]
    return lax.ppermute(block, axis, route)


def gelu_value(pre):
    return 0.5 * pre * (1.0 + lax.erf(pre * root_half))


def gelu_slope(pre):
    return 0.5 * (1.0 + lax.erf(pre * root_half)) + pre * jnp.exp(-0.5 * pre * pre) * inv_root_tau


def strips(block):
    top_row = block[..., 0, :, :]
    right_col = block[..., :, -1, :]
    bottom_row = block[..., -1, ::-1, :]
    left_col = block[..., ::-1, 0, :]
    return jnp.stack([top_row, right_col, bottom_row, left_col], axis=-3)


def assemble(block, halo_strips):
    top_row = halo_strips[..., 0, :, :]
    right_col = halo_strips[..., 1, :, :]
    bottom_row = halo_strips[..., 2, ::-1, :]
    left_col = halo_strips[..., 3, ::-1, :]
    corner_nw = 0.5 * (top_row[..., 0, :] + left_col[..., 0, :])
    corner_ne = 0.5 * (top_row[..., -1, :] + right_col[..., 0, :])
    corner_sw = 0.5 * (left_col[..., -1, :] + bottom_row[..., 0, :])
    corner_se = 0.5 * (bottom_row[..., -1, :] + right_col[..., -1, :])
    first_row = jnp.concatenate(
        [corner_nw[..., None, :], top_row, corner_ne[..., None, :]], axis=-2
    )
    last_row = jnp.concatenate(
        [corner_sw[..., None, :], bottom_row, corner_se[..., None, :]], axis=-2
    )
    middle = jnp.concatenate(
        [left_col[..., :, None, :], block, right_col[..., :, None, :]], axis=-2
    )
    return jnp.concatenate([first_row[..., None, :, :], middle, last_row[..., None, :, :]], axis=-3)


def convolve(padded, weight):
    extent = padded.shape[-2] - 2
    accumulated = 0.0
    for a in range(3):
        for b in range(3):
            window = padded[..., a : a + extent, b : b + extent, :].reshape(-1, padded.shape[-1])
            accumulated = accumulated + jnp.dot(
                window, weight[a, b], preferred_element_type=jnp.float32
            )
    return accumulated.reshape(padded.shape[:-3] + (extent, extent, weight.shape[-1]))


def weight_grad(padded, delta):
    extent = delta.shape[-2]
    flat_delta = delta.reshape(-1, delta.shape[-1])
    tap_rows = []
    for a in range(3):
        tap_cols = []
        for b in range(3):
            window = padded[..., a : a + extent, b : b + extent, :].reshape(-1, padded.shape[-1])
            tap_cols.append(jnp.dot(window.T, flat_delta, preferred_element_type=jnp.float32))
        tap_rows.append(jnp.stack(tap_cols))
    return jnp.stack(tap_rows)


def convolve_back(delta, weight):
    flat_delta = delta.reshape(-1, delta.shape[-1])
    accumulated = 0.0
    for a in range(3):
        for b in range(3):
            term = jnp.dot(flat_delta, weight[a, b].T, preferred_element_type=jnp.float32)
            term = term.reshape(delta.shape[:-1] + (weight.shape[-2],))
            widths = [(0, 0)] * (delta.ndim - 3) + [(a, 2 - a), (b, 2 - b), (0, 0)]
            accumulated = accumulated + jnp.pad(term, widths)
    return accumulated


def pull_strips(own_strips, neighbours, returning):
    tile_index = lax.axis_index("tile")
    tile_count = lax.axis_size("tile")
    row_length = max(4, tile_count // 8)
    offsets = [1, -1, row_length, -row_length]
    own_links = lax.dynamic_slice(neighbours, (tile_index, 0), (1, 4))[0]
    relative = (own_links - tile_index) % tile_count
    strip_width = own_strips.shape[1] * own_strips.shape[2]
    flattened = own_strips.reshape(4, strip_width)
    received = []
    for offset in offsets:
        if returning:
            bundle = from_behind(flattened, "tile", -offset)
        else:
            bundle = from_behind(flattened, "tile", -offset)
        sender = (tile_index + offset) % tile_count
        sender_links = lax.dynamic_slice(neighbours, (sender, 0), (1, 4))
        choose_side = (sender_links == tile_index).astype(jnp.bfloat16)
        incoming = jnp.dot(choose_side, bundle, preferred_element_type=jnp.float32).astype(
            jnp.bfloat16
        )
        received.append(incoming)
    stacked = jnp.concatenate(received, axis=0)
    targets = jnp.array([offset % tile_count for offset in offsets], jnp.int32)
    direction_hit = (relative[:, None] == targets[None, :]).astype(jnp.bfloat16)
    halo_strips = jnp.dot(direction_hit, stacked, preferred_element_type=jnp.float32).astype(
        jnp.bfloat16
    )
    return halo_strips.reshape(own_strips.shape)[:, ::-1, :]


def forward_layer(block, weight, neighbours):
    halo_strips = pull_strips(strips(block), neighbours, False)
    padded = assemble(block.astype(jnp.float32), halo_strips.astype(jnp.float32)).astype(
        jnp.bfloat16
    )
    return (padded, halo_strips, convolve(padded, weight))


def backward_layer(block, halo_strips, delta, weight, neighbours):
    grad_padded = convolve_back(delta, weight)
    unused, adjoint = jax.vjp(assemble, block.astype(jnp.float32), halo_strips.astype(jnp.float32))
    grad_block, grad_halo = adjoint(grad_padded)
    returned = pull_strips(grad_halo.astype(jnp.bfloat16), neighbours, True)
    unused_two, strip_adjoint = jax.vjp(strips, block.astype(jnp.float32))
    (rim_term,) = strip_adjoint(returned.astype(jnp.float32))
    return grad_block + rim_term


def local(fields, weight_first, weight_second, neighbours, cotangent):
    block = fields[0, 0]
    padded_one, halo_one, first_pre = forward_layer(block, weight_first, neighbours)
    hidden = gelu_value(first_pre).astype(jnp.bfloat16)
    padded_two, halo_two, second_pre = forward_layer(hidden, weight_second, neighbours)
    out_field = gelu_value(second_pre).astype(jnp.bfloat16)
    delta_second = (cotangent[0, 0].astype(jnp.float32) * gelu_slope(second_pre)).astype(
        jnp.bfloat16
    )
    grad_second = weight_grad(padded_two, delta_second)
    grad_hidden = backward_layer(hidden, halo_two, delta_second, weight_second, neighbours)
    delta_first = (grad_hidden * gelu_slope(first_pre)).astype(jnp.bfloat16)
    grad_first = weight_grad(padded_one, delta_first)
    grad_block = backward_layer(block, halo_one, delta_first, weight_first, neighbours)
    grad_first, grad_second = lax.psum((grad_first, grad_second), ("ens", "tile"))
    return (
        out_field[None, None],
        grad_block.astype(jnp.bfloat16)[None, None],
        grad_first,
        grad_second,
    )


def solution(mesh):
    placed = (P("ens", "tile", None, None, None), P(), P(), P(), P("ens", "tile", None, None, None))
    return jax.shard_map(
        local,
        mesh=mesh,
        in_specs=placed,
        out_specs=(
            P("ens", "tile", None, None, None),
            P("ens", "tile", None, None, None),
            P(),
            P(),
        ),
        check_vma=False,
    )
```

profile of v0, /device:TPU:0, one launch (start us, length us, event | category | flops | bytes accessed | tf_op | source)
XLA Modules:
  0.0 226.0 jit_solution(4503843929109409163)
XLA Ops:
  7.2 0.8 slice_bitcast_fusion.12
  8.0 1.0 slice_bitcast_fusion.9
  9.2 3.1 %collective-permute-start.3 = (bf16[4,6144]{1,0:T(4,128)(2,1)S(1)}, bf16[4,6144]{1,0:T(4,128)(2,1)S(1)}, u32[]{:S(2)}, u32[]{:S(2)}) collective-permute-start(bf16[4,6144]{1,0:T(4,128)(2,1)S(1)} %pad_maximum_fusion.8), channel_id=1, source_target_pairs={{12,0},{13,1},{14,2},{15,3},{0,4},{1,5},{2,6},{3,7},{4,8},{5,9},{6... | collective-permute-start | bytes 147464 | tf_op jit(solution)/shard_map/ppermute | solution.py:13
  12.3 2.1 collective-permute-start.2
  14.4 4.4 %collective-permute-start = (bf16[4,6144]{1,0:T(4,128)(2,1)S(1)}, bf16[4,6144]{1,0:T(4,128)(2,1)S(1)}, u32[]{:S(2)}, u32[]{:S(2)}) collective-permute-start(bf16[4,6144]{1,0:T(4,128)(2,1)S(1)} %pad_maximum_fusion.8), channel_id=1, source_target_pairs={{1,0},{2,1},{3,2},{4,3},{5,4},{6,5},{7,6},{8,7},{9,8},{10,9},{11,1... | collective-permute-start | bytes 147464 | tf_op jit(solution)/shard_map/ppermute | solution.py:13
  18.9 0.9 subtract_reduce_fusion
  19.8 1.1 fusion.158
  22.3 0.5 pad_maximum_fusion.4
  22.9 0.4 pad_maximum_fusion
  23.7 0.6 copy-done.1
  24.5 0.6 copy-done.8
  28.6 3.8 %collective-permute-start.6 = (bf16[4,6144]{1,0:T(4,128)(2,1)S(1)}, bf16[4,6144]{1,0:T(4,128)(2,1)S(1)}, u32[]{:S(2)}, u32[]{:S(2)}) collective-permute-start(bf16[4,6144]{1,0:T(4,128)(2,1)S(1)} %pad_maximum_fusion.9), channel_id=1, source_target_pairs={{4,0},{5,1},{6,2},{7,3},{8,4},{9,5},{10,6},{11,7},{12,8},{13,9},{1... | collective-permute-start | bytes 147464 | tf_op jit(solution)/shard_map/ppermute | solution.py:13
  32.4 4.4 %collective-permute-start.4 = (bf16[4,6144]{1,0:T(4,128)(2,1)S(1)}, bf16[4,6144]{1,0:T(4,128)(2,1)S(1)}, u32[]{:S(2)}, u32[]{:S(2)}) collective-permute-start(bf16[4,6144]{1,0:T(4,128)(2,1)S(1)} %pad_maximum_fusion.9), channel_id=1, source_target_pairs={{1,0},{2,1},{3,2},{4,3},{5,4},{6,5},{7,6},{8,7},{9,8},{10,9},{11,1... | collective-permute-start | bytes 147464 | tf_op jit(solution)/shard_map/ppermute | solution.py:13
  37.1 1.4 collective-permute-done.5
  39.5 0.6 fusion.244
  40.2 0.7 rev.69
  41.0 0.5 pad_maximum_fusion.2
  41.5 0.4 pad_maximum_fusion.1
  42.6 0.6 copy-done.9
  45.7 0.8 copy-done.11
  46.4 1.7 fusion.5
  48.1 0.5 fusion.17
  49.7 0.4 convolution_bitcast_fusion
  50.1 0.4 convolution_bitcast_fusion.1
  50.5 0.4 convolution_bitcast_fusion.2
  54.8 0.9 pad_add_fusion.1
  55.8 1.1 copy-done.3
  57.0 3.8 %collective-permute-start.10 = (bf16[4,6144]{1,0:T(4,128)(2,1)S(1)}, bf16[4,6144]{1,0:T(4,128)(2,1)S(1)}, u32[]{:S(2)}, u32[]{:S(2)}) collective-permute-start(bf16[4,6144]{1,0:T(4,128)(2,1)S(1)} %bitcast.589), channel_id=1, source_target_pairs={{4,0},{5,1},{6,2},{7,3},{8,4},{9,5},{10,6},{11,7},{12,8},{13,9},{1... | collective-permute-start | bytes 147464 | tf_op jit(solution)/shard_map/ppermute | solution.py:13
  60.8 4.4 %collective-permute-start.8 = (bf16[4,6144]{1,0:T(4,128)(2,1)S(1)}, bf16[4,6144]{1,0:T(4,128)(2,1)S(1)}, u32[]{:S(2)}, u32[]{:S(2)}) collective-permute-start(bf16[4,6144]{1,0:T(4,128)(2,1)S(1)} %bitcast.591), channel_id=1, source_target_pairs={{1,0},{2,1},{3,2},{4,3},{5,4},{6,5},{7,6},{8,7},{9,8},{10,9},{11,1... | collective-permute-start | bytes 147464 | tf_op jit(solution)/shard_map/ppermute | solution.py:13
  65.4 0.9 pad_maximum_fusion.7
  66.6 0.5 collective-permute-done.9
  68.0 2.1 fusion.11
  70.5 0.7 copy-done.5
  71.6 0.4 convolution_bitcast_fusion.9
  72.0 0.4 convolution_bitcast_fusion.10
  72.3 0.4 convolution_bitcast_fusion.11
  73.1 0.4 convolution_bitcast_fusion.15
  73.5 0.4 convolution_bitcast_fusion.16
  73.9 0.4 convolution_bitcast_fusion.17
  77.1 0.9 pad_add_fusion
  78.2 3.8 %collective-permute-start.14 = (bf16[4,6144]{1,0:T(4,128)(2,1)S(1)}, bf16[4,6144]{1,0:T(4,128)(2,1)S(1)}, u32[]{:S(2)}, u32[]{:S(2)}) collective-permute-start(bf16[4,6144]{1,0:T(4,128)(2,1)S(1)} %bitcast.585), channel_id=1, source_target_pairs={{4,0},{5,1},{6,2},{7,3},{8,4},{9,5},{10,6},{11,7},{12,8},{13,9},{1... | collective-permute-start | bytes 147464 | tf_op jit(solution)/shard_map/ppermute | solution.py:13
  82.0 4.4 %collective-permute-start.12 = (bf16[4,6144]{1,0:T(4,128)(2,1)S(1)}, bf16[4,6144]{1,0:T(4,128)(2,1)S(1)}, u32[]{:S(2)}, u32[]{:S(2)}) collective-permute-start(bf16[4,6144]{1,0:T(4,128)(2,1)S(1)} %bitcast.587), channel_id=1, source_target_pairs={{1,0},{2,1},{3,2},{4,3},{5,4},{6,5},{7,6},{8,7},{9,8},{10,9},{11,1... | collective-permute-start | bytes 147464 | tf_op jit(solution)/shard_map/ppermute | solution.py:13
  86.5 0.9 pad_maximum_fusion.6
  87.7 0.5 collective-permute-done.13
  89.2 1.4 fusion.21
  90.5 125.8 %all-reduce.49.cloned.1.call-done = (f32[3,3,128,128]{3,2,1,0:T(8,128)}, f32[3,3,128,128]{3,2,1,0:T(8,128)}) async-done(((f32[3,3,128,128]{3,2,1,0:T(8,128)}, f32[3,3,128,128]{3,2,1,0:T(8,128)}), (f32[3,3,128,128]{3,2,1,0:T(8,128)}, f32[3,3,128,128]{3,2,1,0:T(8,128)})) %all-reduce.49.cloned.1.call-update) | async-done | bytes 1179664 | tf_op jit(solution)/shard_map/psum | solution.py:153
  216.3 2.0 copy.87
  218.3 0.8 copy.88
  (239 shorter events, 21.4 us)
Async XLA Ops:
  7.2 14.5 %copy-start.22 = (s32[4]{0:T(128)S(1)}, s32[4]{0:T(128)}, u32[]{:S(2)}) copy-start(s32[4]{0:T(128)} %constant.95.clone) | copy-start | bytes 52
  7.2 15.1 %copy-start = (bf16[1,1,48,48,128]{4,3,2,1,0:T(8,128)(2,1)S(1)}, bf16[1,1,48,48,128]{4,3,2,1,0:T(8,128)(2,1)}, u32[]{:S(2)}) copy-start(bf16[1,1,48,48,128]{4,3,2,1,0:T(8,128)(2,1)} %param.9) | copy-start | bytes 1769476
  7.2 209.1 %all-reduce.49.cloned.1.call-start = ((), (), s32[]{:S(2)}) async-start(), calls=%async_computation | async-start | bytes 2359296 | tf_op jit(solution)/shard_map/psum | solution.py:153
  9.2 11.7 %collective-permute-start.3 = (bf16[4,6144]{1,0:T(4,128)(2,1)S(1)}, bf16[4,6144]{1,0:T(4,128)(2,1)S(1)}, u32[]{:S(2)}, u32[]{:S(2)}) collective-permute-start(bf16[4,6144]{1,0:T(4,128)(2,1)S(1)} %pad_maximum_fusion.8), channel_id=1, source_target_pairs={{12,0},{13,1},{14,2},{15,3},{0,4},{1,5},{2,6},{3,7},{4,8},{5,9},{6... | collective-permute-start | bytes 147464 | tf_op jit(solution)/shard_map/ppermute | solution.py:13
  12.3 8.7 %collective-permute-start.2 = (bf16[4,6144]{1,0:T(4,128)(2,1)S(1)}, bf16[4,6144]{1,0:T(4,128)(2,1)S(1)}, u32[]{:S(2)}, u32[]{:S(2)}) collective-permute-start(bf16[4,6144]{1,0:T(4,128)(2,1)S(1)} %pad_maximum_fusion.8), channel_id=1, source_target_pairs={{4,0},{5,1},{6,2},{7,3},{8,4},{9,5},{10,6},{11,7},{12,8},{13,9},{1... | collective-permute-start | bytes 147464 | tf_op jit(solution)/shard_map/ppermute | solution.py:13
  14.4 6.8 %collective-permute-start.1 = (bf16[4,6144]{1,0:T(4,128)(2,1)S(1)}, bf16[4,6144]{1,0:T(4,128)(2,1)S(1)}, u32[]{:S(2)}, u32[]{:S(2)}) collective-permute-start(bf16[4,6144]{1,0:T(4,128)(2,1)S(1)} %pad_maximum_fusion.8), channel_id=1, source_target_pairs={{15,0},{0,1},{1,2},{2,3},{3,4},{4,5},{5,6},{6,7},{7,8},{8,9},{9,10... | collective-permute-start | bytes 147464 | tf_op jit(solution)/shard_map/ppermute | solution.py:13
  14.4 7.1 %collective-permute-start = (bf16[4,6144]{1,0:T(4,128)(2,1)S(1)}, bf16[4,6144]{1,0:T(4,128)(2,1)S(1)}, u32[]{:S(2)}, u32[]{:S(2)}) collective-permute-start(bf16[4,6144]{1,0:T(4,128)(2,1)S(1)} %pad_maximum_fusion.8), channel_id=1, source_target_pairs={{1,0},{2,1},{3,2},{4,3},{5,4},{6,5},{7,6},{8,7},{9,8},{10,9},{11,1... | collective-permute-start | bytes 147464 | tf_op jit(solution)/shard_map/ppermute | solution.py:13
  19.7 19.3 %copy-start.20 = (s32[4]{0:T(128)}, s32[4]{0:T(128)S(1)}, u32[]{:S(2)}) copy-start(s32[4]{0:T(128)S(1)} %and_select_fusion) | copy-start | bytes 52
  20.9 16.0 %copy-start.18 = (pred[4]{0:T(512)(128)(4,1)}, pred[4]{0:T(512)(128)(4,1)S(1)}, u32[]{:S(2)}) copy-start(pred[4]{0:T(512)(128)(4,1)S(1)} %get-tuple-element.10) | copy-start | bytes 16
  20.9 16.1 %copy-start.16 = (pred[4]{0:T(512)(128)(4,1)}, pred[4]{0:T(512)(128)(4,1)S(1)}, u32[]{:S(2)}) copy-start(pred[4]{0:T(512)(128)(4,1)S(1)} %get-tuple-element.11) | copy-start | bytes 16
  20.9 17.7 %copy-start.14 = (pred[4]{0:T(512)(128)(4,1)}, pred[4]{0:T(512)(128)(4,1)S(1)}, u32[]{:S(2)}) copy-start(pred[4]{0:T(512)(128)(4,1)S(1)} %get-tuple-element.9) | copy-start | bytes 16
  20.9 18.0 %copy-start.12 = (pred[4]{0:T(512)(128)(4,1)}, pred[4]{0:T(512)(128)(4,1)S(1)}, u32[]{:S(2)}) copy-start(pred[4]{0:T(512)(128)(4,1)S(1)} %get-tuple-element.8) | copy-start | bytes 16
  22.8 3.2 %copy-start.4 = (bf16[48,48,128]{2,1,0:T(8,128)(2,1)}, bf16[48,48,128]{2,1,0:T(8,128)(2,1)S(1)}, u32[]{:S(2)}) copy-start(bf16[48,48,128]{2,1,0:T(8,128)(2,1)S(1)} %get-tuple-element.55) | copy-start | bytes 1769476
  22.9 3.9 %copy-start.6 = (bf16[48,48,128]{2,1,0:T(8,128)(2,1)}, bf16[48,48,128]{2,1,0:T(8,128)(2,1)S(1)}, u32[]{:S(2)}) copy-start(bf16[48,48,128]{2,1,0:T(8,128)(2,1)S(1)} %get-tuple-element.54) | copy-start | bytes 1769476
  23.3 0.9 copy-start.1
  24.2 1.0 copy-start.8
  28.5 8.3 %collective-permute-start.7 = (bf16[4,6144]{1,0:T(4,128)(2,1)S(1)}, bf16[4,6144]{1,0:T(4,128)(2,1)S(1)}, u32[]{:S(2)}, u32[]{:S(2)}) collective-permute-start(bf16[4,6144]{1,0:T(4,128)(2,1)S(1)} %pad_maximum_fusion.9), channel_id=1, source_target_pairs={{12,0},{13,1},{14,2},{15,3},{0,4},{1,5},{2,6},{3,7},{4,8},{5,9},{6... | collective-permute-start | bytes 147464 | tf_op jit(solution)/shard_map/ppermute | solution.py:13
  28.6 8.4 %collective-permute-start.6 = (bf16[4,6144]{1,0:T(4,128)(2,1)S(1)}, bf16[4,6144]{1,0:T(4,128)(2,1)S(1)}, u32[]{:S(2)}, u32[]{:S(2)}) collective-permute-start(bf16[4,6144]{1,0:T(4,128)(2,1)S(1)} %pad_maximum_fusion.9), channel_id=1, source_target_pairs={{4,0},{5,1},{6,2},{7,3},{8,4},{9,5},{10,6},{11,7},{12,8},{13,9},{1... | collective-permute-start | bytes 147464 | tf_op jit(solution)/shard_map/ppermute | solution.py:13
  32.4 6.2 %collective-permute-start.5 = (bf16[4,6144]{1,0:T(4,128)(2,1)S(1)}, bf16[4,6144]{1,0:T(4,128)(2,1)S(1)}, u32[]{:S(2)}, u32[]{:S(2)}) collective-permute-start(bf16[4,6144]{1,0:T(4,128)(2,1)S(1)} %pad_maximum_fusion.9), channel_id=1, source_target_pairs={{15,0},{0,1},{1,2},{2,3},{3,4},{4,5},{5,6},{6,7},{7,8},{8,9},{9,10... | collective-permute-start | bytes 147464 | tf_op jit(solution)/shard_map/ppermute | solution.py:13
  32.4 6.5 %collective-permute-start.4 = (bf16[4,6144]{1,0:T(4,128)(2,1)S(1)}, bf16[4,6144]{1,0:T(4,128)(2,1)S(1)}, u32[]{:S(2)}, u32[]{:S(2)}) collective-permute-start(bf16[4,6144]{1,0:T(4,128)(2,1)S(1)} %pad_maximum_fusion.9), channel_id=1, source_target_pairs={{1,0},{2,1},{3,2},{4,3},{5,4},{6,5},{7,6},{8,7},{9,8},{10,9},{11,1... | collective-permute-start | bytes 147464 | tf_op jit(solution)/shard_map/ppermute | solution.py:13
  42.3 1.0 copy-start.9
  45.4 1.1 copy-start.11
  55.7 1.1 copy-start.3
  56.9 9.3 %copy-start.19 = (pred[4]{0:T(512)(128)(4,1)S(1)}, pred[4]{0:T(512)(128)(4,1)}, u32[]{:S(2)}) copy-start(pred[4]{0:T(512)(128)(4,1)} %copy-done.18) | copy-start | bytes 16
  56.9 9.5 %copy-start.17 = (pred[4]{0:T(512)(128)(4,1)S(1)}, pred[4]{0:T(512)(128)(4,1)}, u32[]{:S(2)}) copy-start(pred[4]{0:T(512)(128)(4,1)} %copy-done.16) | copy-start | bytes 16
  56.9 10.1 %copy-start.15 = (pred[4]{0:T(512)(128)(4,1)S(1)}, pred[4]{0:T(512)(128)(4,1)}, u32[]{:S(2)}) copy-start(pred[4]{0:T(512)(128)(4,1)} %copy-done.14) | copy-start | bytes 16
  57.0 9.3 %collective-permute-start.11 = (bf16[4,6144]{1,0:T(4,128)(2,1)S(1)}, bf16[4,6144]{1,0:T(4,128)(2,1)S(1)}, u32[]{:S(2)}, u32[]{:S(2)}) collective-permute-start(bf16[4,6144]{1,0:T(4,128)(2,1)S(1)} %bitcast.588), channel_id=1, source_target_pairs={{12,0},{13,1},{14,2},{15,3},{0,4},{1,5},{2,6},{3,7},{4,8},{5,9},{6... | collective-permute-start | bytes 147464 | tf_op jit(solution)/shard_map/ppermute | solution.py:13
  57.0 9.4 %collective-permute-start.10 = (bf16[4,6144]{1,0:T(4,128)(2,1)S(1)}, bf16[4,6144]{1,0:T(4,128)(2,1)S(1)}, u32[]{:S(2)}, u32[]{:S(2)}) collective-permute-start(bf16[4,6144]{1,0:T(4,128)(2,1)S(1)} %bitcast.589), channel_id=1, source_target_pairs={{4,0},{5,1},{6,2},{7,3},{8,4},{9,5},{10,6},{11,7},{12,8},{13,9},{1... | collective-permute-start | bytes 147464 | tf_op jit(solution)/shard_map/ppermute | solution.py:13
  60.8 6.2 %collective-permute-start.9 = (bf16[4,6144]{1,0:T(4,128)(2,1)S(1)}, bf16[4,6144]{1,0:T(4,128)(2,1)S(1)}, u32[]{:S(2)}, u32[]{:S(2)}) collective-permute-start(bf16[4,6144]{1,0:T(4,128)(2,1)S(1)} %bitcast.590), channel_id=1, source_target_pairs={{15,0},{0,1},{1,2},{2,3},{3,4},{4,5},{5,6},{6,7},{7,8},{8,9},{9,10... | collective-permute-start | bytes 147464 | tf_op jit(solution)/shard_map/ppermute | solution.py:13
  60.8 6.5 %collective-permute-start.8 = (bf16[4,6144]{1,0:T(4,128)(2,1)S(1)}, bf16[4,6144]{1,0:T(4,128)(2,1)S(1)}, u32[]{:S(2)}, u32[]{:S(2)}) collective-permute-start(bf16[4,6144]{1,0:T(4,128)(2,1)S(1)} %bitcast.591), channel_id=1, source_target_pairs={{1,0},{2,1},{3,2},{4,3},{5,4},{6,5},{7,6},{8,7},{9,8},{10,9},{11,1... | collective-permute-start | bytes 147464 | tf_op jit(solution)/shard_map/ppermute | solution.py:13
  65.3 2.0 copy-start.13
  65.3 2.2 copy-start.21
  65.3 2.2 copy-start.23
  68.0 2.2 copy-start.7
  70.2 1.1 copy-start.5
  70.2 1.4 copy-start.2
  78.2 9.3 %collective-permute-start.15 = (bf16[4,6144]{1,0:T(4,128)(2,1)S(1)}, bf16[4,6144]{1,0:T(4,128)(2,1)S(1)}, u32[]{:S(2)}, u32[]{:S(2)}) collective-permute-start(bf16[4,6144]{1,0:T(4,128)(2,1)S(1)} %bitcast.584), channel_id=1, source_target_pairs={{12,0},{13,1},{14,2},{15,3},{0,4},{1,5},{2,6},{3,7},{4,8},{5,9},{6... | collective-permute-start | bytes 147464 | tf_op jit(solution)/shard_map/ppermute | solution.py:13
  78.2 9.4 %collective-permute-start.14 = (bf16[4,6144]{1,0:T(4,128)(2,1)S(1)}, bf16[4,6144]{1,0:T(4,128)(2,1)S(1)}, u32[]{:S(2)}, u32[]{:S(2)}) collective-permute-start(bf16[4,6144]{1,0:T(4,128)(2,1)S(1)} %bitcast.585), channel_id=1, source_target_pairs={{4,0},{5,1},{6,2},{7,3},{8,4},{9,5},{10,6},{11,7},{12,8},{13,9},{1... | collective-permute-start | bytes 147464 | tf_op jit(solution)/shard_map/ppermute | solution.py:13
  82.0 6.2 %collective-permute-start.13 = (bf16[4,6144]{1,0:T(4,128)(2,1)S(1)}, bf16[4,6144]{1,0:T(4,128)(2,1)S(1)}, u32[]{:S(2)}, u32[]{:S(2)}) collective-permute-start(bf16[4,6144]{1,0:T(4,128)(2,1)S(1)} %bitcast.586), channel_id=1, source_target_pairs={{15,0},{0,1},{1,2},{2,3},{3,4},{4,5},{5,6},{6,7},{7,8},{8,9},{9,10... | collective-permute-start | bytes 147464 | tf_op jit(solution)/shard_map/ppermute | solution.py:13
  82.0 6.5 %collective-permute-start.12 = (bf16[4,6144]{1,0:T(4,128)(2,1)S(1)}, bf16[4,6144]{1,0:T(4,128)(2,1)S(1)}, u32[]{:S(2)}, u32[]{:S(2)}) collective-permute-start(bf16[4,6144]{1,0:T(4,128)(2,1)S(1)} %bitcast.587), channel_id=1, source_target_pairs={{1,0},{2,1},{3,2},{4,3},{5,4},{6,5},{7,6},{8,7},{9,8},{10,9},{11,1... | collective-permute-start | bytes 147464 | tf_op jit(solution)/shard_map/ppermute | solution.py:13
  216.3 2.0 copy-start.10
Sparse Core Ops, SparseCore 0:
  87.5 128.7 all-reduce.48
where the time goes:
time: 226 us
  waiting for transfers between devices  128 us (57%)
  starting transfers between devices  34.6 us (15%)
  matrix products  22.4 us (10%)
  between operations  15.4 us (7%)
  local copies, waits for them, and re-layouts  13 us (6%)
  other arithmetic  12.3 us (5%)
    psum x1, waiting for transfers between devices, local(): lax.psum((grad_first, grad_second), ('ens', 'tile'))  126 us
    ppermute x16, starting transfers between devices, from_behind(): return lax.ppermute(block, axis, route)  34.5 us
    unnamed x60, local copies, waits for them, and re-layouts  8.17 us
    dot_general x18, matrix products, convolve(): jnp.dot(window, weight[a, b], preferred_element_type=jnp.float32)  6.73 us
    dot_general x18, matrix products, weight_grad(): jnp.dot(window.T, flat_delta, preferred_element_type=jnp.float32)  6.62 us
    dot_general x18, matrix products, convolve_back(): jnp.dot(flat_delta, weight[a, b].T, preferred_element_type=jnp.float32)  5.69 us
  transfers between devices with their start and end apart: 17, of which 4 were waited for; matrix products, arithmetic and copies ran while one was open for 3% of the time, Pallas kernels for 0%

commit v1 on v0

--- a/solution.py
+++ b/solution.py
@@ -136,6 +136,55 @@
     return grad_block + rim_term
 
 
+def flip_swap(block, mask_ens, mask_tile):
+    ens, tile = lax.axis_size("ens"), lax.axis_size("tile")
+    route = [
+        (e * tile + t, (e ^ mask_ens) * tile + (t ^ mask_tile))
+        for e in range(ens)
+        for t in range(tile)
+    ]
+    return lax.ppermute(block, ("ens", "tile"), route)
+
+
+def pick(parts, index):
+    return lax.dynamic_index_in_dim(parts, index, 0, keepdims=False)
+
+
+def all_sum(block):
+    tile = lax.axis_index("tile")
+    core = tile & 1
+    rows, lanes = block.shape
+    halves = block.reshape(2, rows // 2, lanes)
+    given = flip_swap(pick(halves, 1 - core).astype(jnp.bfloat16), 0, 1)
+    part = pick(halves, core) + given.astype(jnp.float32)
+    seat = lax.axis_index("ens") * 2 + (tile >> 1 & 1)
+    quarters = part.reshape(4, rows // 8, lanes)
+    sent = quarters.astype(jnp.bfloat16)
+    part = pick(quarters, seat)
+    for k in (1, 2, 3):
+        part = part + flip_swap(pick(sent, seat ^ k), k >> 1, (k & 1) << 1).astype(jnp.float32)
+    bit = 4
+    while bit < lax.axis_size("tile"):
+        own = part.astype(jnp.bfloat16)
+        part = lax.reduce_precision(part, 8, 7)
+        if bit * 2 < lax.axis_size("tile"):
+            one, two, three = (flip_swap(own, 0, bit * k).astype(jnp.float32) for k in (1, 2, 3))
+            part = (part + one) + (two + three)
+            bit *= 4
+        else:
+            part = part + flip_swap(own, 0, bit).astype(jnp.float32)
+            bit *= 2
+    part = part.astype(jnp.bfloat16)
+    whole = jnp.zeros((4,) + part.shape, part.dtype)
+    whole = lax.dynamic_update_index_in_dim(whole, part, seat, 0)
+    for k in (1, 2, 3):
+        got = flip_swap(part, k >> 1, (k & 1) << 1)
+        whole = lax.dynamic_update_index_in_dim(whole, got, seat ^ k, 0)
+    half = whole.reshape(rows // 2, lanes)
+    other = flip_swap(half, 0, 1)
+    return jnp.concatenate([jnp.where(core == 0, half, other), jnp.where(core == 0, other, half)])
+
+
 def local(fields, weight_first, weight_second, neighbours, cotangent):
     block = fields[0, 0]
     padded_one, halo_one, first_pre = forward_layer(block, weight_first, neighbours)
@@ -150,7 +199,10 @@
     delta_first = (grad_hidden * gelu_slope(first_pre)).astype(jnp.bfloat16)
     grad_first = weight_grad(padded_one, delta_first)
     grad_block = backward_layer(block, halo_one, delta_first, weight_first, neighbours)
-    grad_first, grad_second = lax.psum((grad_first, grad_second), ("ens", "tile"))
+    shape = grad_first.shape
+    both = jnp.stack([grad_first, grad_second]).reshape(-1, shape[-1])
+    both = all_sum(both).astype(jnp.float32).reshape((2,) + shape)
+    grad_first, grad_second = both[0], both[1]
     return (
         out_field[None, None],
         grad_block.astype(jnp.bfloat16)[None, None],

time: 226 us -> 112 us (0.50)
  waiting for transfers between devices: 128 us -> 27.4 us
  between operations: 15.4 us -> 2.26 us
  local copies, waits for them, and re-layouts: 13 us -> 10.5 us
  matrix products: 22.4 us -> 24.8 us
    psum x1 -> x0, waiting for transfers between devices: 126 us -> none  [local(): lax.psum((grad_first, grad_second), ('ens', 'tile'))]
    ppermute x0 -> x11, waiting for transfers between devices: none -> 13.1 us  [flip_swap(): return lax.ppermute(block, ('ens', 'tile'), route)]
    ppermute x16, starting transfers between devices: 34.5 us -> 22.4 us  [from_behind(): return lax.ppermute(block, axis, route)]
    ppermute x0 -> x11, starting transfers between devices: none -> 11.9 us  [flip_swap(): return lax.ppermute(block, ('ens', 'tile'), route)]
    ppermute x16, waiting for transfers between devices: 2.46 us -> 14.3 us  [from_behind(): return lax.ppermute(block, axis, route)]
    dot_general x18, matrix products: 6.62 us -> 9.12 us  [weight_grad(): jnp.dot(window.T, flat_delta, preferred_element_type=jnp.float32)]
    unnamed x60 -> x78, local copies, waits for them, and re-layouts: 8.17 us -> 5.75 us
  transfers between devices with their start and end apart: 17 -> 27, of which waited for: 4 -> 12; matrix products, arithmetic and copies ran while one was open for 3% -> 6% of each run, Pallas kernels for 0% -> 0%
where the time goes in v1:
time: 112 us; the launch traced here: 111 us
  starting transfers between devices  34.3 us (31%)
  waiting for transfers between devices  27.4 us (24%)
  matrix products  24.8 us (22%)
  other arithmetic  12.2 us (11%)
  local copies, waits for them, and re-layouts  10.5 us (9%)
  between operations  2.26 us (2%)
    ppermute x16, starting transfers between devices, from_behind(): return lax.ppermute(block, axis, route)  22.4 us
    ppermute x16, waiting for transfers between devices, from_behind(): return lax.ppermute(block, axis, route)  14.3 us
    ppermute x11, waiting for transfers between devices, flip_swap(): return lax.ppermute(block, ('ens', 'tile'), route)  13.1 us
    ppermute x11, starting transfers between devices, flip_swap(): return lax.ppermute(block, ('ens', 'tile'), route)  11.9 us
    dot_general x18, matrix products, weight_grad(): jnp.dot(window.T, flat_delta, preferred_element_type=jnp.float32)  9.12 us
    dot_general x18, matrix products, convolve(): jnp.dot(window, weight[a, b], preferred_element_type=jnp.float32)  6.72 us
    unnamed x78, local copies, waits for them, and re-layouts  5.75 us
    dot_general x18, matrix products, convolve_back(): jnp.dot(flat_delta, weight[a, b].T, preferred_element_type=jnp.float32)  5.64 us
  transfers between devices with their start and end apart: 27, of which 12 were waited for; matrix products, arithmetic and copies ran while one was open for 6% of the time, Pallas kernels for 0%

profile of v1, /device:TPU:0, one launch (start us, length us, event | category | flops | bytes accessed | tf_op | source)
XLA Modules:
  0.0 111.4 jit_solution(7690328353727947435)
XLA Ops:
  0.7 0.8 slice_bitcast_fusion.12
  1.5 1.0 slice_bitcast_fusion.9
  2.7 5.5 %collective-permute-start = (bf16[4,6144]{1,0:T(4,128)(2,1)S(1)}, bf16[4,6144]{1,0:T(4,128)(2,1)S(1)}, u32[]{:S(2)}, u32[]{:S(2)}) collective-permute-start(bf16[4,6144]{1,0:T(4,128)(2,1)S(1)} %pad_maximum_fusion.8), channel_id=1, source_target_pairs={{1,0},{2,1},{3,2},{4,3},{5,4},{6,5},{7,6},{8,7},{9,8},{10,9},{11,1... | collective-permute-start | bytes 147464 | tf_op jit(solution)/shard_map/ppermute | solution.py:13
  8.6 1.6 %collective-permute-start.3 = (bf16[4,6144]{1,0:T(4,128)(2,1)S(1)}, bf16[4,6144]{1,0:T(4,128)(2,1)S(1)}, u32[]{:S(2)}, u32[]{:S(2)}) collective-permute-start(bf16[4,6144]{1,0:T(4,128)(2,1)S(1)} %pad_maximum_fusion.8), channel_id=1, source_target_pairs={{12,0},{13,1},{14,2},{15,3},{0,4},{1,5},{2,6},{3,7},{4,8},{5,9},{6... | collective-permute-start | bytes 147464 | tf_op jit(solution)/shard_map/ppermute | solution.py:13
  10.2 0.9 fusion.167
  11.1 1.1 fusion.175
  12.4 2.0 %collective-permute-done.1 = bf16[4,6144]{1,0:T(4,128)(2,1)S(1)} collective-permute-done((bf16[4,6144]{1,0:T(4,128)(2,1)S(1)}, bf16[4,6144]{1,0:T(4,128)(2,1)S(1)}, u32[]{:S(2)}, u32[]{:S(2)}) %collective-permute-start.1) | collective-permute-done | bytes 49184 | tf_op jit(solution)/shard_map/ppermute | solution.py:13
  17.0 0.5 copy-done.1
  17.8 0.7 copy-done.9
  21.8 3.8 %collective-permute-start.4 = (bf16[4,6144]{1,0:T(4,128)(2,1)S(1)}, bf16[4,6144]{1,0:T(4,128)(2,1)S(1)}, u32[]{:S(2)}, u32[]{:S(2)}) collective-permute-start(bf16[4,6144]{1,0:T(4,128)(2,1)S(1)} %pad_maximum_fusion.9), channel_id=1, source_target_pairs={{1,0},{2,1},{3,2},{4,3},{5,4},{6,5},{7,6},{8,7},{9,8},{10,9},{11,1... | collective-permute-start | bytes 147464 | tf_op jit(solution)/shard_map/ppermute | solution.py:13
  25.6 2.0 %collective-permute-start.7 = (bf16[4,6144]{1,0:T(4,128)(2,1)S(1)}, bf16[4,6144]{1,0:T(4,128)(2,1)S(1)}, u32[]{:S(2)}, u32[]{:S(2)}) collective-permute-start(bf16[4,6144]{1,0:T(4,128)(2,1)S(1)} %pad_maximum_fusion.9), channel_id=1, source_target_pairs={{12,0},{13,1},{14,2},{15,3},{0,4},{1,5},{2,6},{3,7},{4,8},{5,9},{6... | collective-permute-start | bytes 147464 | tf_op jit(solution)/shard_map/ppermute | solution.py:13
  27.7 4.4 %collective-permute-done.5 = bf16[4,6144]{1,0:T(4,128)(2,1)S(1)} collective-permute-done((bf16[4,6144]{1,0:T(4,128)(2,1)S(1)}, bf16[4,6144]{1,0:T(4,128)(2,1)S(1)}, u32[]{:S(2)}, u32[]{:S(2)}) %collective-permute-start.5) | collective-permute-done | bytes 49184 | tf_op jit(solution)/shard_map/ppermute | solution.py:13
  35.0 0.6 copy-done.10
  38.1 0.8 copy-done.11
  38.8 1.7 %fusion.5 = (bf16[2304,128]{1,0:T(8,128)(2,1)S(1)}, bf16[2304,128]{1,0:T(8,128)(2,1)}, f32[2304,128]{1,0:T(8,128)S(1)}) fusion(bf16[1,1,48,48,128]{4,3,2,1,0:T(8,128)(2,1)S(1)} %copy-done.11, f32[2304,128]{1,0:T(8,128)S(1)} %convolution_add_fusion.1, bf16[2304,128]{1,0:T(8,128)(2,1)S(1)} %bitcast.603, bf16[3,3,128,128]{3,2,1,0:T(8,128)(2,1)S(1)} %copy-done.10), kind=kOutput, calls=%fused_computation.34 | convolution fusion | flops 79921152 | bytes 4751360 | tf_op jit(solution)/shard_map/dot_general | solution.py:59
  40.5 0.5 fusion.17
  42.1 1.0 convolution_bitcast_fusion.3
  43.1 1.0 convolution_bitcast_fusion.5
  44.1 1.0 convolution_bitcast_fusion.4
  49.1 0.9 pad_add_fusion.1
  50.1 1.1 copy-done.3
  51.3 2.5 %collective-permute-start.8 = (bf16[4,6144]{1,0:T(4,128)(2,1)S(1)}, bf16[4,6144]{1,0:T(4,128)(2,1)S(1)}, u32[]{:S(2)}, u32[]{:S(2)}) collective-permute-start(bf16[4,6144]{1,0:T(4,128)(2,1)S(1)} %bitcast.637), channel_id=1, source_target_pairs={{1,0},{2,1},{3,2},{4,3},{5,4},{6,5},{7,6},{8,7},{9,8},{10,9},{11,1... | collective-permute-start | bytes 147464 | tf_op jit(solution)/shard_map/ppermute | solution.py:13
  53.8 2.0 %collective-permute-start.11 = (bf16[4,6144]{1,0:T(4,128)(2,1)S(1)}, bf16[4,6144]{1,0:T(4,128)(2,1)S(1)}, u32[]{:S(2)}, u32[]{:S(2)}) collective-permute-start(bf16[4,6144]{1,0:T(4,128)(2,1)S(1)} %bitcast.640), channel_id=1, source_target_pairs={{12,0},{13,1},{14,2},{15,3},{0,4},{1,5},{2,6},{3,7},{4,8},{5,9},{6... | collective-permute-start | bytes 147464 | tf_op jit(solution)/shard_map/ppermute | solution.py:13
  56.1 4.2 %collective-permute-done.9 = bf16[4,6144]{1,0:T(4,128)(2,1)S(1)} collective-permute-done((bf16[4,6144]{1,0:T(4,128)(2,1)S(1)}, bf16[4,6144]{1,0:T(4,128)(2,1)S(1)}, u32[]{:S(2)}, u32[]{:S(2)}) %collective-permute-start.9) | collective-permute-done | bytes 49184 | tf_op jit(solution)/shard_map/ppermute | solution.py:13
  61.5 2.1 %fusion.11 = bf16[48,48,128]{2,1,0:T(8,128)(2,1)S(1)} fusion(f32[48,48,128]{2,1,0:T(8,128)S(1)} %bitcast.573, f32[50,50,128]{2,1,0:T(8,128)} %copy-done.3, f32[48,48,128]{2,0,1:T(8,128)S(1)} %pad_add_fusion.3, f32[1,48,128]{2,1,0:T(8,128)S(1)} %get-tuple-element.81), kind=kLoop, calls=%fused_computation.40 | loop fusion | flops 3538944 | bytes 4153344 | tf_op jit(solution)/shard_map/convert_element_type | solution.py:199
  64.8 0.7 copy-done.8
  65.5 1.0 convolution_bitcast_fusion.12
  71.2 0.9 pad_add_fusion
  72.2 2.5 %collective-permute-start.12 = (bf16[4,6144]{1,0:T(4,128)(2,1)S(1)}, bf16[4,6144]{1,0:T(4,128)(2,1)S(1)}, u32[]{:S(2)}, u32[]{:S(2)}) collective-permute-start(bf16[4,6144]{1,0:T(4,128)(2,1)S(1)} %bitcast.633), channel_id=1, source_target_pairs={{1,0},{2,1},{3,2},{4,3},{5,4},{6,5},{7,6},{8,7},{9,8},{10,9},{11,1... | collective-permute-start | bytes 147464 | tf_op jit(solution)/shard_map/ppermute | solution.py:13
  74.7 2.0 %collective-permute-start.15 = (bf16[4,6144]{1,0:T(4,128)(2,1)S(1)}, bf16[4,6144]{1,0:T(4,128)(2,1)S(1)}, u32[]{:S(2)}, u32[]{:S(2)}) collective-permute-start(bf16[4,6144]{1,0:T(4,128)(2,1)S(1)} %bitcast.636), channel_id=1, source_target_pairs={{12,0},{13,1},{14,2},{15,3},{0,4},{1,5},{2,6},{3,7},{4,8},{5,9},{6... | collective-permute-start | bytes 147464 | tf_op jit(solution)/shard_map/ppermute | solution.py:13
  77.6 3.7 %collective-permute-done.13 = bf16[4,6144]{1,0:T(4,128)(2,1)S(1)} collective-permute-done((bf16[4,6144]{1,0:T(4,128)(2,1)S(1)}, bf16[4,6144]{1,0:T(4,128)(2,1)S(1)}, u32[]{:S(2)}, u32[]{:S(2)}) %collective-permute-start.13) | collective-permute-done | bytes 49184 | tf_op jit(solution)/shard_map/ppermute | solution.py:13
  83.0 1.5 %collective-permute-start.18 = (bf16[288,128]{1,0:T(8,128)(2,1)S(1)}, bf16[288,128]{1,0:T(8,128)(2,1)S(1)}, u32[]{:S(2)}, u32[]{:S(2)}) collective-permute-start(bf16[288,128]{1,0:T(8,128)(2,1)S(1)} %get-tuple-element.66), channel_id=1, source_target_pairs={{0,16},{1,17},{2,18},{3,19},{4,20},{5,21},{6,22},{7,23},{8,24},{9,... | collective-permute-start | bytes 221192 | tf_op jit(solution)/shard_map/ppermute | solution.py:146
  84.4 1.6 %collective-permute-start.19 = (bf16[288,128]{1,0:T(8,128)(2,1)S(1)}, bf16[288,128]{1,0:T(8,128)(2,1)S(1)}, u32[]{:S(2)}, u32[]{:S(2)}) collective-permute-start(bf16[288,128]{1,0:T(8,128)(2,1)S(1)} %get-tuple-element.65), channel_id=1, source_target_pairs={{0,18},{1,19},{2,16},{3,17},{4,22},{5,23},{6,20},{7,21},{8,26},{9,... | collective-permute-start | bytes 221192 | tf_op jit(solution)/shard_map/ppermute | solution.py:146
  86.1 1.5 %collective-permute-done.17 = bf16[288,128]{1,0:T(8,128)(2,1)S(1)} collective-permute-done((bf16[288,128]{1,0:T(8,128)(2,1)S(1)}, bf16[288,128]{1,0:T(8,128)(2,1)S(1)}, u32[]{:S(2)}, u32[]{:S(2)}) %collective-permute-start.17) | collective-permute-done | bytes 73760 | tf_op jit(solution)/shard_map/ppermute | solution.py:146
  87.6 2.3 %collective-permute-done.19 = bf16[288,128]{1,0:T(8,128)(2,1)S(1)} collective-permute-done((bf16[288,128]{1,0:T(8,128)(2,1)S(1)}, bf16[288,128]{1,0:T(8,128)(2,1)S(1)}, u32[]{:S(2)}, u32[]{:S(2)}) %collective-permute-start.19) | collective-permute-done | bytes 73760 | tf_op jit(solution)/shard_map/ppermute | solution.py:146
  90.0 2.6 %collective-permute-start.21 = (bf16[288,128]{1,0:T(8,128)(2,1)S(1)}, bf16[288,128]{1,0:T(8,128)(2,1)S(1)}, u32[]{:S(2)}, u32[]{:S(2)}) collective-permute-start(bf16[288,128]{1,0:T(8,128)(2,1)S(1)} %fusion.208), channel_id=1, source_target_pairs={{0,8},{1,9},{2,10},{3,11},{4,12},{5,13},{6,14},{7,15},{8,0},{9,1},... | collective-permute-start | bytes 221192 | tf_op jit(solution)/shard_map/ppermute | solution.py:146
  92.6 1.8 %collective-permute-start.22 = (bf16[288,128]{1,0:T(8,128)(2,1)S(1)}, bf16[288,128]{1,0:T(8,128)(2,1)S(1)}, u32[]{:S(2)}, u32[]{:S(2)}) collective-permute-start(bf16[288,128]{1,0:T(8,128)(2,1)S(1)} %fusion.208), channel_id=1, source_target_pairs={{0,12},{1,13},{2,14},{3,15},{4,8},{5,9},{6,10},{7,11},{8,4},{9,5},... | collective-permute-start | bytes 221192 | tf_op jit(solution)/shard_map/ppermute | solution.py:146
  94.4 1.5 %collective-permute-done.20 = bf16[288,128]{1,0:T(8,128)(2,1)S(1)} collective-permute-done((bf16[288,128]{1,0:T(8,128)(2,1)S(1)}, bf16[288,128]{1,0:T(8,128)(2,1)S(1)}, u32[]{:S(2)}, u32[]{:S(2)}) %collective-permute-start.20) | collective-permute-done | bytes 73760 | tf_op jit(solution)/shard_map/ppermute | solution.py:146
  95.9 3.3 %collective-permute-done.21 = bf16[288,128]{1,0:T(8,128)(2,1)S(1)} collective-permute-done((bf16[288,128]{1,0:T(8,128)(2,1)S(1)}, bf16[288,128]{1,0:T(8,128)(2,1)S(1)}, u32[]{:S(2)}, u32[]{:S(2)}) %collective-permute-start.21) | collective-permute-done | bytes 73760 | tf_op jit(solution)/shard_map/ppermute | solution.py:146
  99.3 1.0 bitcast_dynamic-update-slice_fusion.3
  100.3 1.6 %collective-permute-start.23 = (bf16[288,128]{1,0:T(8,128)(2,1)S(1)}, bf16[288,128]{1,0:T(8,128)(2,1)S(1)}, u32[]{:S(2)}, u32[]{:S(2)}) collective-permute-start(bf16[288,128]{1,0:T(8,128)(2,1)S(1)} %get-tuple-element.13), channel_id=1, source_target_pairs={{0,2},{1,3},{2,0},{3,1},{4,6},{5,7},{6,4},{7,5},{8,10},{9,11},{10,... | collective-permute-start | bytes 221192 | tf_op jit(solution)/shard_map/ppermute | solution.py:146
  102.0 1.3 %collective-permute-start.24 = (bf16[288,128]{1,0:T(8,128)(2,1)S(1)}, bf16[288,128]{1,0:T(8,128)(2,1)S(1)}, u32[]{:S(2)}, u32[]{:S(2)}) collective-permute-start(bf16[288,128]{1,0:T(8,128)(2,1)S(1)} %get-tuple-element.13), channel_id=1, source_target_pairs={{0,16},{1,17},{2,18},{3,19},{4,20},{5,21},{6,22},{7,23},{8,24},{9,... | collective-permute-start | bytes 221192 | tf_op jit(solution)/shard_map/ppermute | solution.py:146
  103.2 0.9 collective-permute-start.25
  104.2 1.4 %collective-permute-done.23 = bf16[288,128]{1,0:T(8,128)(2,1)S(1)} collective-permute-done((bf16[288,128]{1,0:T(8,128)(2,1)S(1)}, bf16[288,128]{1,0:T(8,128)(2,1)S(1)}, u32[]{:S(2)}, u32[]{:S(2)}) %collective-permute-start.23) | collective-permute-done | bytes 73760 | tf_op jit(solution)/shard_map/ppermute | solution.py:146
  105.5 0.9 collective-permute-done.24
  106.4 2.1 %collective-permute-done.25 = bf16[288,128]{1,0:T(8,128)(2,1)S(1)} collective-permute-done((bf16[288,128]{1,0:T(8,128)(2,1)S(1)}, bf16[288,128]{1,0:T(8,128)(2,1)S(1)}, u32[]{:S(2)}, u32[]{:S(2)}) %collective-permute-start.25) | collective-permute-done | bytes 73760 | tf_op jit(solution)/shard_map/ppermute | solution.py:146
  108.6 1.4 %fusion.21 = bf16[1,1,48,48,128]{4,3,2,1,0:T(8,128)(2,1)} fusion(f32[1,48,128]{2,1,0:T(8,128)S(1)} %get-tuple-element.80, f32[48,48,128]{2,0,1:T(8,128)S(1)} %pad_add_fusion.2, f32[50,50,128]{2,1,0:T(8,128)S(1)} %pad_add_fusion), kind=kLoop, calls=%fused_computation.82 | loop fusion | flops 884736 | bytes 2973696 | tf_op jit(solution)/shard_map/broadcast_in_dim | solution.py:208
  110.3 1.1 fusion.253
  (289 shorter events, 27.2 us)
Async XLA Ops:
  0.6 14.4 %copy-start.31 = (s32[4]{0:T(128)S(1)}, s32[4]{0:T(128)}, u32[]{:S(2)}) copy-start(s32[4]{0:T(128)} %constant.135.clone) | copy-start | bytes 52
  0.6 15.0 %copy-start = (bf16[1,1,48,48,128]{4,3,2,1,0:T(8,128)(2,1)S(1)}, bf16[1,1,48,48,128]{4,3,2,1,0:T(8,128)(2,1)}, u32[]{:S(2)}) copy-start(bf16[1,1,48,48,128]{4,3,2,1,0:T(8,128)(2,1)} %param.9) | copy-start | bytes 1769476
  2.7 9.6 %collective-permute-start = (bf16[4,6144]{1,0:T(4,128)(2,1)S(1)}, bf16[4,6144]{1,0:T(4,128)(2,1)S(1)}, u32[]{:S(2)}, u32[]{:S(2)}) collective-permute-start(bf16[4,6144]{1,0:T(4,128)(2,1)S(1)} %pad_maximum_fusion.8), channel_id=1, source_target_pairs={{1,0},{2,1},{3,2},{4,3},{5,4},{6,5},{7,6},{8,7},{9,8},{10,9},{11,1... | collective-permute-start | bytes 147464 | tf_op jit(solution)/shard_map/ppermute | solution.py:13
  8.2 6.2 %collective-permute-start.1 = (bf16[4,6144]{1,0:T(4,128)(2,1)S(1)}, bf16[4,6144]{1,0:T(4,128)(2,1)S(1)}, u32[]{:S(2)}, u32[]{:S(2)}) collective-permute-start(bf16[4,6144]{1,0:T(4,128)(2,1)S(1)} %pad_maximum_fusion.8), channel_id=1, source_target_pairs={{15,0},{0,1},{1,2},{2,3},{3,4},{4,5},{5,6},{6,7},{7,8},{8,9},{9,10... | collective-permute-start | bytes 147464 | tf_op jit(solution)/shard_map/ppermute | solution.py:13
  8.2 6.4 %collective-permute-start.2 = (bf16[4,6144]{1,0:T(4,128)(2,1)S(1)}, bf16[4,6144]{1,0:T(4,128)(2,1)S(1)}, u32[]{:S(2)}, u32[]{:S(2)}) collective-permute-start(bf16[4,6144]{1,0:T(4,128)(2,1)S(1)} %pad_maximum_fusion.8), channel_id=1, source_target_pairs={{4,0},{5,1},{6,2},{7,3},{8,4},{9,5},{10,6},{11,7},{12,8},{13,9},{1... | collective-permute-start | bytes 147464 | tf_op jit(solution)/shard_map/ppermute | solution.py:13
  8.6 6.2 %collective-permute-start.3 = (bf16[4,6144]{1,0:T(4,128)(2,1)S(1)}, bf16[4,6144]{1,0:T(4,128)(2,1)S(1)}, u32[]{:S(2)}, u32[]{:S(2)}) collective-permute-start(bf16[4,6144]{1,0:T(4,128)(2,1)S(1)} %pad_maximum_fusion.8), channel_id=1, source_target_pairs={{12,0},{13,1},{14,2},{15,3},{0,4},{1,5},{2,6},{3,7},{4,8},{5,9},{6... | collective-permute-start | bytes 147464 | tf_op jit(solution)/shard_map/ppermute | solution.py:13
  11.1 21.7 %copy-start.28 = (s32[4]{0:T(128)}, s32[4]{0:T(128)S(1)}, u32[]{:S(2)}) copy-start(s32[4]{0:T(128)S(1)} %and_select_fusion) | copy-start | bytes 52
  12.2 15.4 %copy-start.25 = (pred[4]{0:T(512)(128)(4,1)}, pred[4]{0:T(512)(128)(4,1)S(1)}, u32[]{:S(2)}) copy-start(pred[4]{0:T(512)(128)(4,1)S(1)} %get-tuple-element.8) | copy-start | bytes 16
  12.2 19.9 %copy-start.22 = (pred[4]{0:T(512)(128)(4,1)}, pred[4]{0:T(512)(128)(4,1)S(1)}, u32[]{:S(2)}) copy-start(pred[4]{0:T(512)(128)(4,1)S(1)} %get-tuple-element.9) | copy-start | bytes 16
  12.2 20.1 %copy-start.19 = (pred[4]{0:T(512)(128)(4,1)}, pred[4]{0:T(512)(128)(4,1)S(1)}, u32[]{:S(2)}) copy-start(pred[4]{0:T(512)(128)(4,1)S(1)} %get-tuple-element.11) | copy-start | bytes 16
  12.2 20.3 %copy-start.16 = (pred[4]{0:T(512)(128)(4,1)}, pred[4]{0:T(512)(128)(4,1)S(1)}, u32[]{:S(2)}) copy-start(pred[4]{0:T(512)(128)(4,1)S(1)} %get-tuple-element.10) | copy-start | bytes 16
  21.8 5.8 %collective-permute-start.4 = (bf16[4,6144]{1,0:T(4,128)(2,1)S(1)}, bf16[4,6144]{1,0:T(4,128)(2,1)S(1)}, u32[]{:S(2)}, u32[]{:S(2)}) collective-permute-start(bf16[4,6144]{1,0:T(4,128)(2,1)S(1)} %pad_maximum_fusion.9), channel_id=1, source_target_pairs={{1,0},{2,1},{3,2},{4,3},{5,4},{6,5},{7,6},{8,7},{9,8},{10,9},{11,1... | collective-permute-start | bytes 147464 | tf_op jit(solution)/shard_map/ppermute | solution.py:13
  25.6 6.6 %collective-permute-start.5 = (bf16[4,6144]{1,0:T(4,128)(2,1)S(1)}, bf16[4,6144]{1,0:T(4,128)(2,1)S(1)}, u32[]{:S(2)}, u32[]{:S(2)}) collective-permute-start(bf16[4,6144]{1,0:T(4,128)(2,1)S(1)} %pad_maximum_fusion.9), channel_id=1, source_target_pairs={{15,0},{0,1},{1,2},{2,3},{3,4},{4,5},{5,6},{6,7},{7,8},{8,9},{9,10... | collective-permute-start | bytes 147464 | tf_op jit(solution)/shard_map/ppermute | solution.py:13
  25.6 6.7 %collective-permute-start.6 = (bf16[4,6144]{1,0:T(4,128)(2,1)S(1)}, bf16[4,6144]{1,0:T(4,128)(2,1)S(1)}, u32[]{:S(2)}, u32[]{:S(2)}) collective-permute-start(bf16[4,6144]{1,0:T(4,128)(2,1)S(1)} %pad_maximum_fusion.9), channel_id=1, source_target_pairs={{4,0},{5,1},{6,2},{7,3},{8,4},{9,5},{10,6},{11,7},{12,8},{13,9},{1... | collective-permute-start | bytes 147464 | tf_op jit(solution)/shard_map/ppermute | solution.py:13
  25.6 7.0 %collective-permute-start.7 = (bf16[4,6144]{1,0:T(4,128)(2,1)S(1)}, bf16[4,6144]{1,0:T(4,128)(2,1)S(1)}, u32[]{:S(2)}, u32[]{:S(2)}) collective-permute-start(bf16[4,6144]{1,0:T(4,128)(2,1)S(1)} %pad_maximum_fusion.9), channel_id=1, source_target_pairs={{12,0},{13,1},{14,2},{15,3},{0,4},{1,5},{2,6},{3,7},{4,8},{5,9},{6... | collective-permute-start | bytes 147464 | tf_op jit(solution)/shard_map/ppermute | solution.py:13
  49.1 6.7 %copy-start.12 = (f32[1,128,128]{2,1,0:T(8,128)S(1)}, f32[1,128,128]{2,1,0:T(8,128)}, u32[]{:S(2)}) copy-start(f32[1,128,128]{2,1,0:T(8,128)} %convolution_bitcast_fusion.3) | copy-start | bytes 196612
  49.1 6.7 %copy-start.13 = (f32[1,128,128]{2,1,0:T(8,128)S(1)}, f32[1,128,128]{2,1,0:T(8,128)}, u32[]{:S(2)}) copy-start(f32[1,128,128]{2,1,0:T(8,128)} %convolution_bitcast_fusion.5) | copy-start | bytes 196612
  49.1 6.7 %copy-start.14 = (f32[1,128,128]{2,1,0:T(8,128)S(1)}, f32[1,128,128]{2,1,0:T(8,128)}, u32[]{:S(2)}) copy-start(f32[1,128,128]{2,1,0:T(8,128)} %convolution_bitcast_fusion.4) | copy-start | bytes 196612
  51.2 4.7 %copy-start.26 = (pred[4]{0:T(512)(128)(4,1)S(1)}, pred[4]{0:T(512)(128)(4,1)}, u32[]{:S(2)}) copy-start(pred[4]{0:T(512)(128)(4,1)} %copy-done.25) | copy-start | bytes 16
  51.3 9.1 %copy-start.23 = (pred[4]{0:T(512)(128)(4,1)S(1)}, pred[4]{0:T(512)(128)(4,1)}, u32[]{:S(2)}) copy-start(pred[4]{0:T(512)(128)(4,1)} %copy-done.22) | copy-start | bytes 16
  51.3 9.3 %copy-start.20 = (pred[4]{0:T(512)(128)(4,1)S(1)}, pred[4]{0:T(512)(128)(4,1)}, u32[]{:S(2)}) copy-start(pred[4]{0:T(512)(128)(4,1)} %copy-done.19) | copy-start | bytes 16
  51.3 4.7 %collective-permute-start.8 = (bf16[4,6144]{1,0:T(4,128)(2,1)S(1)}, bf16[4,6144]{1,0:T(4,128)(2,1)S(1)}, u32[]{:S(2)}, u32[]{:S(2)}) collective-permute-start(bf16[4,6144]{1,0:T(4,128)(2,1)S(1)} %bitcast.637), channel_id=1, source_target_pairs={{1,0},{2,1},{3,2},{4,3},{5,4},{6,5},{7,6},{8,7},{9,8},{10,9},{11,1... | collective-permute-start | bytes 147464 | tf_op jit(solution)/shard_map/ppermute | solution.py:13
  53.8 6.6 %collective-permute-start.9 = (bf16[4,6144]{1,0:T(4,128)(2,1)S(1)}, bf16[4,6144]{1,0:T(4,128)(2,1)S(1)}, u32[]{:S(2)}, u32[]{:S(2)}) collective-permute-start(bf16[4,6144]{1,0:T(4,128)(2,1)S(1)} %bitcast.638), channel_id=1, source_target_pairs={{15,0},{0,1},{1,2},{2,3},{3,4},{4,5},{5,6},{6,7},{7,8},{8,9},{9,10... | collective-permute-start | bytes 147464 | tf_op jit(solution)/shard_map/ppermute | solution.py:13
  53.8 6.7 %collective-permute-start.10 = (bf16[4,6144]{1,0:T(4,128)(2,1)S(1)}, bf16[4,6144]{1,0:T(4,128)(2,1)S(1)}, u32[]{:S(2)}, u32[]{:S(2)}) collective-permute-start(bf16[4,6144]{1,0:T(4,128)(2,1)S(1)} %bitcast.639), channel_id=1, source_target_pairs={{4,0},{5,1},{6,2},{7,3},{8,4},{9,5},{10,6},{11,7},{12,8},{13,9},{1... | collective-permute-start | bytes 147464 | tf_op jit(solution)/shard_map/ppermute | solution.py:13
  53.8 7.0 %collective-permute-start.11 = (bf16[4,6144]{1,0:T(4,128)(2,1)S(1)}, bf16[4,6144]{1,0:T(4,128)(2,1)S(1)}, u32[]{:S(2)}, u32[]{:S(2)}) collective-permute-start(bf16[4,6144]{1,0:T(4,128)(2,1)S(1)} %bitcast.640), channel_id=1, source_target_pairs={{12,0},{13,1},{14,2},{15,3},{0,4},{1,5},{2,6},{3,7},{4,8},{5,9},{6... | collective-permute-start | bytes 147464 | tf_op jit(solution)/shard_map/ppermute | solution.py:13
  55.8 5.0 %copy-start.17 = (pred[4]{0:T(512)(128)(4,1)S(1)}, pred[4]{0:T(512)(128)(4,1)}, u32[]{:S(2)}) copy-start(pred[4]{0:T(512)(128)(4,1)} %copy-done.16) | copy-start | bytes 16
  55.9 5.1 %copy-start.29 = (s32[4]{0:T(128)S(1)}, s32[4]{0:T(128)}, u32[]{:S(2)}) copy-start(s32[4]{0:T(128)} %copy-done.28) | copy-start | bytes 52
  55.9 5.1 %copy-start.32 = (s32[4]{0:T(128)S(1)}, s32[4]{0:T(128)}, u32[]{:S(2)}) copy-start(s32[4]{0:T(128)} %constant.135.clone) | copy-start | bytes 52
  71.2 5.6 %copy-start.15 = (f32[1,128,128]{2,1,0:T(8,128)S(1)}, f32[1,128,128]{2,1,0:T(8,128)}, u32[]{:S(2)}) copy-start(f32[1,128,128]{2,1,0:T(8,128)} %convolution_bitcast_fusion.12) | copy-start | bytes 196612
  72.2 4.9 %collective-permute-start.12 = (bf16[4,6144]{1,0:T(4,128)(2,1)S(1)}, bf16[4,6144]{1,0:T(4,128)(2,1)S(1)}, u32[]{:S(2)}, u32[]{:S(2)}) collective-permute-start(bf16[4,6144]{1,0:T(4,128)(2,1)S(1)} %bitcast.633), channel_id=1, source_target_pairs={{1,0},{2,1},{3,2},{4,3},{5,4},{6,5},{7,6},{8,7},{9,8},{10,9},{11,1... | collective-permute-start | bytes 147464 | tf_op jit(solution)/shard_map/ppermute | solution.py:13
  74.7 6.6 %collective-permute-start.13 = (bf16[4,6144]{1,0:T(4,128)(2,1)S(1)}, bf16[4,6144]{1,0:T(4,128)(2,1)S(1)}, u32[]{:S(2)}, u32[]{:S(2)}) collective-permute-start(bf16[4,6144]{1,0:T(4,128)(2,1)S(1)} %bitcast.634), channel_id=1, source_target_pairs={{15,0},{0,1},{1,2},{2,3},{3,4},{4,5},{5,6},{6,7},{7,8},{8,9},{9,10... | collective-permute-start | bytes 147464 | tf_op jit(solution)/shard_map/ppermute | solution.py:13
  74.7 6.7 %collective-permute-start.14 = (bf16[4,6144]{1,0:T(4,128)(2,1)S(1)}, bf16[4,6144]{1,0:T(4,128)(2,1)S(1)}, u32[]{:S(2)}, u32[]{:S(2)}) collective-permute-start(bf16[4,6144]{1,0:T(4,128)(2,1)S(1)} %bitcast.635), channel_id=1, source_target_pairs={{4,0},{5,1},{6,2},{7,3},{8,4},{9,5},{10,6},{11,7},{12,8},{13,9},{1... | collective-permute-start | bytes 147464 | tf_op jit(solution)/shard_map/ppermute | solution.py:13
  74.7 7.0 %collective-permute-start.15 = (bf16[4,6144]{1,0:T(4,128)(2,1)S(1)}, bf16[4,6144]{1,0:T(4,128)(2,1)S(1)}, u32[]{:S(2)}, u32[]{:S(2)}) collective-permute-start(bf16[4,6144]{1,0:T(4,128)(2,1)S(1)} %bitcast.636), channel_id=1, source_target_pairs={{12,0},{13,1},{14,2},{15,3},{0,4},{1,5},{2,6},{3,7},{4,8},{5,9},{6... | collective-permute-start | bytes 147464 | tf_op jit(solution)/shard_map/ppermute | solution.py:13
  76.9 4.9 %copy-start.18 = (pred[4]{0:T(512)(128)(4,1)S(1)}, pred[4]{0:T(512)(128)(4,1)}, u32[]{:S(2)}) copy-start(pred[4]{0:T(512)(128)(4,1)} %copy-done.16) | copy-start | bytes 16
  76.9 5.0 %copy-start.30 = (s32[4]{0:T(128)S(1)}, s32[4]{0:T(128)}, u32[]{:S(2)}) copy-start(s32[4]{0:T(128)} %copy-done.28) | copy-start | bytes 52
  76.9 5.0 %copy-start.33 = (s32[4]{0:T(128)S(1)}, s32[4]{0:T(128)}, u32[]{:S(2)}) copy-start(s32[4]{0:T(128)} %constant.135.clone) | copy-start | bytes 52
  77.1 5.2 %collective-permute-start.16 = (bf16[1152,128]{1,0:T(8,128)(2,1)S(1)}, bf16[1152,128]{1,0:T(8,128)(2,1)S(1)}, u32[]{:S(2)}, u32[]{:S(2)}) collective-permute-start(bf16[1152,128]{1,0:T(8,128)(2,1)S(1)} %fusion.27), channel_id=1, source_target_pairs={{0,1},{1,0},{2,3},{3,2},{4,5},{5,4},{6,7},{7,6},{8,9},{9,8},{10,11... | collective-permute-start | bytes 884744 | tf_op jit(solution)/shard_map/ppermute | solution.py:146
  82.4 7.5 %copy-start.4 = (f32[1152,128]{1,0:T(8,128)}, f32[1152,128]{1,0:T(8,128)S(1)}, u32[]{:S(2)}) copy-start(f32[1152,128]{1,0:T(8,128)S(1)} %fusion.26) | copy-start | bytes 1769476
  82.5 5.1 %collective-permute-start.17 = (bf16[288,128]{1,0:T(8,128)(2,1)S(1)}, bf16[288,128]{1,0:T(8,128)(2,1)S(1)}, u32[]{:S(2)}, u32[]{:S(2)}) collective-permute-start(bf16[288,128]{1,0:T(8,128)(2,1)S(1)} %get-tuple-element.64), channel_id=1, source_target_pairs={{0,2},{1,3},{2,0},{3,1},{4,6},{5,7},{6,4},{7,5},{8,10},{9,11},{10,... | collective-permute-start | bytes 221192 | tf_op jit(solution)/shard_map/ppermute | solution.py:146
  83.0 4.6 %collective-permute-start.18 = (bf16[288,128]{1,0:T(8,128)(2,1)S(1)}, bf16[288,128]{1,0:T(8,128)(2,1)S(1)}, u32[]{:S(2)}, u32[]{:S(2)}) collective-permute-start(bf16[288,128]{1,0:T(8,128)(2,1)S(1)} %get-tuple-element.66), channel_id=1, source_target_pairs={{0,16},{1,17},{2,18},{3,19},{4,20},{5,21},{6,22},{7,23},{8,24},{9,... | collective-permute-start | bytes 221192 | tf_op jit(solution)/shard_map/ppermute | solution.py:146
  84.4 5.5 %collective-permute-start.19 = (bf16[288,128]{1,0:T(8,128)(2,1)S(1)}, bf16[288,128]{1,0:T(8,128)(2,1)S(1)}, u32[]{:S(2)}, u32[]{:S(2)}) collective-permute-start(bf16[288,128]{1,0:T(8,128)(2,1)S(1)} %get-tuple-element.65), channel_id=1, source_target_pairs={{0,18},{1,19},{2,16},{3,17},{4,22},{5,23},{6,20},{7,21},{8,26},{9,... | collective-permute-start | bytes 221192 | tf_op jit(solution)/shard_map/ppermute | solution.py:146
  89.9 6.0 %collective-permute-start.20 = (bf16[288,128]{1,0:T(8,128)(2,1)S(1)}, bf16[288,128]{1,0:T(8,128)(2,1)S(1)}, u32[]{:S(2)}, u32[]{:S(2)}) collective-permute-start(bf16[288,128]{1,0:T(8,128)(2,1)S(1)} %fusion.208), channel_id=1, source_target_pairs={{0,4},{1,5},{2,6},{3,7},{4,0},{5,1},{6,2},{7,3},{8,12},{9,13},{10,... | collective-permute-start | bytes 221192 | tf_op jit(solution)/shard_map/ppermute | solution.py:146
  90.0 9.2 %collective-permute-start.21 = (bf16[288,128]{1,0:T(8,128)(2,1)S(1)}, bf16[288,128]{1,0:T(8,128)(2,1)S(1)}, u32[]{:S(2)}, u32[]{:S(2)}) collective-permute-start(bf16[288,128]{1,0:T(8,128)(2,1)S(1)} %fusion.208), channel_id=1, source_target_pairs={{0,8},{1,9},{2,10},{3,11},{4,12},{5,13},{6,14},{7,15},{8,0},{9,1},... | collective-permute-start | bytes 221192 | tf_op jit(solution)/shard_map/ppermute | solution.py:146
  92.6 6.6 %collective-permute-start.22 = (bf16[288,128]{1,0:T(8,128)(2,1)S(1)}, bf16[288,128]{1,0:T(8,128)(2,1)S(1)}, u32[]{:S(2)}, u32[]{:S(2)}) collective-permute-start(bf16[288,128]{1,0:T(8,128)(2,1)S(1)} %fusion.208), channel_id=1, source_target_pairs={{0,12},{1,13},{2,14},{3,15},{4,8},{5,9},{6,10},{7,11},{8,4},{9,5},... | collective-permute-start | bytes 221192 | tf_op jit(solution)/shard_map/ppermute | solution.py:146
  100.3 5.2 %collective-permute-start.23 = (bf16[288,128]{1,0:T(8,128)(2,1)S(1)}, bf16[288,128]{1,0:T(8,128)(2,1)S(1)}, u32[]{:S(2)}, u32[]{:S(2)}) collective-permute-start(bf16[288,128]{1,0:T(8,128)(2,1)S(1)} %get-tuple-element.13), channel_id=1, source_target_pairs={{0,2},{1,3},{2,0},{3,1},{4,6},{5,7},{6,4},{7,5},{8,10},{9,11},{10,... | collective-permute-start | bytes 221192 | tf_op jit(solution)/shard_map/ppermute | solution.py:146
  102.0 4.4 %collective-permute-start.24 = (bf16[288,128]{1,0:T(8,128)(2,1)S(1)}, bf16[288,128]{1,0:T(8,128)(2,1)S(1)}, u32[]{:S(2)}, u32[]{:S(2)}) collective-permute-start(bf16[288,128]{1,0:T(8,128)(2,1)S(1)} %get-tuple-element.13), channel_id=1, source_target_pairs={{0,16},{1,17},{2,18},{3,19},{4,20},{5,21},{6,22},{7,23},{8,24},{9,... | collective-permute-start | bytes 221192 | tf_op jit(solution)/shard_map/ppermute | solution.py:146
  103.2 5.3 %collective-permute-start.25 = (bf16[288,128]{1,0:T(8,128)(2,1)S(1)}, bf16[288,128]{1,0:T(8,128)(2,1)S(1)}, u32[]{:S(2)}, u32[]{:S(2)}) collective-permute-start(bf16[288,128]{1,0:T(8,128)(2,1)S(1)} %get-tuple-element.13), channel_id=1, source_target_pairs={{0,18},{1,19},{2,16},{3,17},{4,22},{5,23},{6,20},{7,21},{8,26},{9,... | collective-permute-start | bytes 221192 | tf_op jit(solution)/shard_map/ppermute | solution.py:146
  108.5 1.6 %collective-permute-start.26 = (bf16[1152,128]{1,0:T(8,128)(2,1)S(1)}, bf16[1152,128]{1,0:T(8,128)(2,1)S(1)}, u32[]{:S(2)}, u32[]{:S(2)}) collective-permute-start(bf16[1152,128]{1,0:T(8,128)(2,1)S(1)} %bitcast.602), channel_id=1, source_target_pairs={{0,1},{1,0},{2,3},{3,2},{4,5},{5,4},{6,7},{7,6},{8,9},{9,8},{10,11... | collective-permute-start | bytes 884744 | tf_op jit(solution)/shard_map/ppermute | solution.py:146
  (13 other events, 27.1 us)

commit v2 on v1

v2 whole, which is shorter than its diff:
```python
import functools

import jax
import jax.numpy as jnp
from jax import lax
from jax.experimental import pallas as pl
from jax.experimental.pallas import tpu as pltpu
from jax.sharding import PartitionSpec as P

root_half = 0.7071067811865476
inv_root_tau = 0.3989422804014327
bf16, f32 = jnp.bfloat16, jnp.float32
NT = (((1,), (1,)), ((), ()))
TN = (((0,), (0,)), ((), ()))


def gelu_both(pre):
    bell = 0.5 * (1.0 + lax.erf(pre * root_half))
    return pre * bell, bell + pre * jnp.exp(-0.5 * pre * pre) * inv_root_tau


def partners(index, count, cols):
    odd, row_odd = index & 1, (index // cols) & 1
    return [
        (index + cols * (2 * row_odd - 1) + count) % count,
        (index + cols * (1 - 2 * row_odd) + count) % count,
        (index - 1 + 2 * odd + count) % count,
        (index + 1 - 2 * odd + count) % count,
    ]


def links(table, cols):
    count = lax.axis_size("tile")
    me = lax.axis_index("tile")
    found = []
    for other in partners(me, count, cols):
        side, back = jnp.int32(0), jnp.int32(0)
        for s in range(1, 4):
            side = jnp.where(table[me, s] == other, s, side)
            back = jnp.where(table[other, s] == me, s, back)
        found.append((side, (side >= 2) == (back >= 2)))
    return found


def send_strips(table, cols, strips, outs):
    size = strips.shape[1]
    at_row = lax.broadcasted_iota(jnp.int32, (size, size), 0)
    at_col = lax.broadcasted_iota(jnp.int32, (size, size), 1)
    for (side, turn), out in zip(links(table, cols), outs):
        order = (at_col == jnp.where(turn, size - 1 - at_row, at_row)).astype(f32).astype(bf16)
        out[...] = jnp.dot(order, strips[side].astype(bf16), preferred_element_type=f32).astype(
            bf16
        )


def take_strips(table, cols, received, strips):
    for (side, _), block in zip(links(table, cols), received):
        strips[side] = block[...].astype(f32)


def swap_all(blocks, cols):
    count = lax.axis_size("tile")
    ways = [partners(p, count, cols) for p in range(count)]
    return [
        lax.ppermute(block, "tile", [(p, ways[p][k]) for p in range(count)])
        for k, block in enumerate(blocks)
    ]


def fill_columns(shifted, pairs):
    count, size, lanes = pairs.shape
    c = lanes // 2
    at = lax.broadcasted_iota(jnp.int32, (size, c), 0)
    first, last = at == 0, at == size - 1
    shifted[0:size, 0 : 3 * c] = jnp.zeros((size, 3 * c), bf16)
    shifted[count * size :, 3 * c :] = jnp.zeros((size, 3 * c), bf16)
    for i in range(count):
        for parity, row, lane in ((1, (i + 1) * size, 0), (0, i * size, 3 * c)):
            value = pairs[i, :, parity * c : (parity + 1) * c].astype(f32)
            before = jnp.where(first, 0.0, pltpu.roll(value, 1, 0))
            after = jnp.where(last, 0.0, pltpu.roll(value, size - 1, 0))
            shifted[row : row + size, lane : lane + c] = before.astype(bf16)
            shifted[row : row + size, lane + c : lane + 2 * c] = value.astype(bf16)
            shifted[row : row + size, lane + 2 * c : lane + 3 * c] = after.astype(bf16)


def blocks_of_pairs(tap, lower, upper, c):
    for b in range(3):
        for half, parity, target, a in (
            (lower, 0, 0, 0),
            (lower, 0, 1, None),
            (lower, 1, 0, 1),
            (lower, 1, 1, 0),
            (upper, 0, 0, 2),
            (upper, 0, 1, 1),
            (upper, 1, 0, None),
            (upper, 1, 1, 2),
        ):
            yield half, (parity * 3 + b) * c, target * c, tap(a, b) if a is not None else None


def bulk_conv(shifted, weight, lower, upper, out, backward):
    c = weight.shape[-1]
    count, size, lanes = out.shape
    if backward:
        tap = lambda a, b: weight[(2 - a) * 3 + 2 - b]
    else:
        tap = lambda a, b: weight[a * 3 + b]
    for half, depth, target, block in blocks_of_pairs(tap, lower, upper, c):
        if block is None:
            block = jnp.zeros((c, c), bf16)
        if backward:
            half[target : target + c, depth : depth + c] = block
        else:
            half[depth : depth + c, target : target + c] = block
    rows = count * size
    dims = NT if backward else (((1,), (0,)), ((), ()))
    total = lax.dot_general(
        shifted[0:rows, :], lower[...], dims, preferred_element_type=f32
    ) + lax.dot_general(shifted[size : size + rows, :], upper[...], dims, preferred_element_type=f32)
    out[...] = total.reshape(count, size, lanes)


def bulk_weight_grad(shifted, delta, out):
    count, size, lanes = delta.shape
    c = lanes // 2
    rows = count * size
    flat = delta[...].reshape(rows, lanes)
    low = lax.dot_general(shifted[0:rows, :], flat, TN, preferred_element_type=f32)
    high = lax.dot_general(shifted[size : size + rows, :], flat, TN, preferred_element_type=f32)
    for b in range(3):
        here, there = b * c, (3 + b) * c
        out[b] = low[here : here + c, 0:c] + low[there : there + c, c:]
        out[3 + b] = low[there : there + c, 0:c] + high[here : here + c, c:]
        out[6 + b] = high[here : here + c, 0:c] + high[there : there + c, c:]


def load_edges(left, right, top, bottom):
    return left[...], right[...], top[0], bottom[0]


def to_pairs(strip, room):
    room[...] = strip
    half = strip.shape[0] // 2
    return jnp.concatenate(
        [room[pl.ds(0, half, stride=2), :], room[pl.ds(1, half, stride=2), :]], axis=1
    )


def add_strips(edges, strips, rooms):
    left, right, top, bottom = edges
    t, r, b, l = strips
    c = t.shape[1]
    half, depth, size = left.shape[0], left.shape[1], t.shape[0]
    at = lax.broadcasted_iota(jnp.int32, left.shape, 1)
    left_room, right_room, top_room, bottom_room, strip_a, strip_b = rooms
    left_room[...] = left + jnp.where(at == 0, to_pairs(l, strip_a)[:, None, :], 0.0)
    right_room[...] = right + jnp.where(at == depth - 1, to_pairs(r, strip_b)[:, None, :], 0.0)
    left_room[0, :, 0:c] += t[0:depth]
    left_room[half - 1, :, c:] += b[0:depth]
    right_room[0, :, 0:c] += t[size - depth :]
    right_room[half - 1, :, c:] += b[size - depth :]
    top_room[...] = top + t
    bottom_room[...] = bottom + b
    top_room[0:depth] = left_room[0, :, 0:c]
    top_room[size - depth :] = right_room[0, :, 0:c]
    bottom_room[0:depth] = left_room[half - 1, :, c:]
    bottom_room[size - depth :] = right_room[half - 1, :, c:]
    return left_room[...], right_room[...], top_room[...], bottom_room[...]


def edge_strips(edges, strips):
    left, right, top, bottom = edges
    c = top.shape[1]
    half = left.shape[0]
    strips[0] = top
    strips[2] = bottom
    for side, column in ((1, right[:, -1, :]), (3, left[:, 0, :])):
        strips[side, pl.ds(0, half, stride=2), :] = column[:, 0:c]
        strips[side, pl.ds(1, half, stride=2), :] = column[:, c:]


def lay_edges(pairs, left, right, top, bottom):
    depth = left.shape[1]
    size = pairs.shape[1]
    c = top.shape[-1]
    pairs[:, 0:depth, :] = left[...]
    pairs[:, size - depth :, :] = right[...]
    pairs[0, :, 0:c] = top[...]
    pairs[pairs.shape[0] - 1, :, c:] = bottom[...]


def halo_windows(strips, rooms):
    size = strips.shape[1]
    top, right, bottom, left = (strips[s] for s in range(4))
    zero = jnp.zeros_like(top[0:1])
    ends = [
        (0.5 * (top[0:1] + left[0:1]), 0.5 * (top[size - 1 :] + right[0:1])),
        (zero, zero),
        (0.5 * (left[size - 1 :] + bottom[0:1]), 0.5 * (bottom[size - 1 :] + right[size - 1 :])),
        (zero, zero),
    ]
    windows = []
    for s, (strip, (before, after)) in enumerate(zip((top, right, bottom, left), ends)):
        rooms[s, 7:8, :] = before
        rooms[s, 8 : 8 + size, :] = strip
        rooms[s, 8 + size : 9 + size, :] = after
        windows.append(
            jnp.concatenate([rooms[s, 7 + k : 7 + k + size, :] for k in range(3)], axis=1).astype(
                bf16
            )
        )
    return windows


side_taps = ((0, 1, 2), (2, 5, 8), (6, 7, 8), (0, 3, 6))


def halo_terms(windows, weight):
    return [
        jnp.dot(
            window,
            jnp.concatenate([weight[tap] for tap in taps], axis=0),
            preferred_element_type=f32,
        )
        for window, taps in zip(windows, side_taps)
    ]


def halo_weight_grad(windows, strips, out):
    c = out.shape[-1]
    for s, (window, taps) in enumerate(zip(windows, side_taps)):
        term = lax.dot_general(window, strips[s].astype(bf16), TN, preferred_element_type=f32)
        for k, tap in enumerate(taps):
            out[tap] += term[k * c : (k + 1) * c]


def halo_grads(strips, weight, rooms, grads):
    size, c = strips.shape[1:]
    long = size + 8
    for s, taps in enumerate(side_taps):
        rooms[s, 0:8, :] = jnp.zeros((8, c), f32)
        rooms[s, 8 : 8 + size, :] = strips[s]
        rooms[s, 8 + size :, :] = jnp.zeros((8, c), f32)
        copies = jnp.concatenate([rooms[s, 8 - k : 8 - k + long, :] for k in range(3)], axis=1)
        rims = jnp.concatenate([weight[tap] for tap in taps], axis=1)
        rim = lax.dot_general(copies.astype(bf16), rims, NT, preferred_element_type=f32)
        rooms[s, 0:long, :] = rim
        at = lax.broadcasted_iota(jnp.int32, (size, c), 0)
        corner = jnp.where(at == 0, rooms[s, 0:1, :], 0.0) + jnp.where(
            at == size - 1, rooms[s, size + 1 : size + 2, :], 0.0
        )
        grads[s] = rooms[s, 1 : 1 + size, :] + 0.5 * corner


def exact(values):
    return [value.astype(bf16).astype(f32) for value in values]


def first_strips(cols, table, block, *refs):
    outs, strips = refs[:4], refs[4]
    size = block.shape[0]
    strips[0] = block[0].astype(f32)
    strips[2] = block[size - 1].astype(f32)
    strips[3] = block[:, 0:16, :].astype(f32)[:, 0, :]
    strips[1] = block[:, size - 16 :, :].astype(f32)[:, 15, :]
    send_strips(table, cols, strips, outs)


def first_bulk(block, weight, shifted, pre, hidden, slope, pairs, lower, upper):
    count, size, lanes = pre.shape
    c = lanes // 2
    for i in range(count):
        pairs[i, :, 0:c] = block[2 * i]
        pairs[i, :, c:] = block[2 * i + 1]
    fill_columns(shifted, pairs)
    bulk_conv(shifted, weight, lower, upper, pre, False)
    for i in range(count):
        value, rate = gelu_both(pre[i])
        hidden[i] = value.astype(bf16)
        slope[i] = rate.astype(bf16)


def first_edges(cols, table, *refs):
    received, weight, blocks = refs[:4], refs[4], refs[5:9]
    outs, hidden, slope, halo = refs[9:13], refs[13:17], refs[17:21], refs[21]
    rooms, strips, long = refs[22:28], refs[28], refs[29]
    take_strips(table, cols, received, halo)
    terms = halo_terms(halo_windows(halo, long), weight)
    edges = add_strips(load_edges(*blocks), terms, rooms)
    both = [gelu_both(edge) for edge in edges]
    values = exact([value for value, _ in both])
    for k in range(4):
        hidden[k][...] = values[k]
        slope[k][...] = both[k][1]
    edge_strips(values, strips)
    send_strips(table, cols, strips, outs)


def second_bulk(hidden, left, right, top, bottom, weight, cotangent, *refs):
    shifted, pre, out_field, delta, pairs, lower, upper = refs
    count, size, lanes = pre.shape
    c = lanes // 2
    pairs[...] = hidden[...].astype(f32)
    lay_edges(pairs, left, right, top, bottom)
    fill_columns(shifted, pairs)
    bulk_conv(shifted, weight, lower, upper, pre, False)
    for i in range(count):
        for parity in range(2):
            part = slice(parity * c, (parity + 1) * c)
            value, rate = gelu_both(pre[i, :, part])
            out_field[i, :, part] = value.astype(bf16)
            delta[i, :, part] = (cotangent[2 * i + parity].astype(f32) * rate).astype(bf16)


def second_edges(cols, table, *refs):
    received, weight, blocks, wanted = refs[:4], refs[4], refs[5:9], refs[9:13]
    outs, out_field, delta, halo = refs[13:17], refs[17:21], refs[21:25], refs[25]
    rooms, strips, long, grads = refs[26:32], refs[32], refs[33], refs[34]
    half, depth = blocks[0].shape[:2]
    take_strips(table, cols, received, halo)
    terms = halo_terms(halo_windows(halo, long), weight)
    edges = add_strips(load_edges(*blocks), terms, rooms)
    cots = []
    for ref, at in ((wanted[0], 0), (wanted[1], 16 - depth)):
        block = ref[...].astype(f32)
        block = block.reshape((half, 2) + block.shape[1:])[:, :, at : at + depth, :]
        cots.append(jnp.concatenate([block[:, 0], block[:, 1]], axis=-1))
    cots += [wanted[2][0].astype(f32), wanted[3][0].astype(f32)]
    both = [gelu_both(edge) for edge in edges]
    deltas = exact([cot * rate for cot, (_, rate) in zip(cots, both)])
    for k in range(4):
        out_field[k][...] = both[k][0]
        delta[k][...] = deltas[k]
    edge_strips(deltas, strips)
    halo_grads(strips, weight, long, grads)
    send_strips(table, cols, grads, outs)


def second_back(*refs):
    bulk_out, bulk_delta, out_edges, delta_edges, halo = (
        refs[0],
        refs[1],
        refs[2:6],
        refs[6:10],
        refs[10],
    )
    shifted, weight, bulk_slope = refs[11:14]
    out_field, grad_weight, grad_hidden, delta_first = refs[14:18]
    pairs, delta, lower, upper, moved, strips, long = refs[18:25]
    count, size, lanes = pairs.shape
    c = lanes // 2
    pairs[...] = bulk_out[...].astype(f32)
    lay_edges(pairs, *out_edges)
    for i in range(count):
        out_field[2 * i] = pairs[i, :, 0:c].astype(bf16)
        out_field[2 * i + 1] = pairs[i, :, c:].astype(bf16)
    pairs[...] = bulk_delta[...].astype(f32)
    lay_edges(pairs, *delta_edges)
    delta[...] = pairs[...].astype(bf16)
    bulk_weight_grad(shifted, delta, grad_weight)
    edge_strips([ref[...] for ref in delta_edges], strips)
    halo_weight_grad(halo_windows(halo, long), strips, grad_weight)
    fill_columns(moved, pairs)
    bulk_conv(moved, weight, lower, upper, grad_hidden, True)
    for i in range(count):
        delta_first[i] = (grad_hidden[i] * bulk_slope[i].astype(f32)).astype(bf16)


def first_back(cols, table, *refs):
    received, weight, blocks, slope, bulk_delta = (
        refs[:4],
        refs[4],
        refs[5:9],
        refs[9:13],
        refs[13],
    )
    halo, shifted, other_grad = refs[14:17]
    outs, delta, kept, given = refs[17:21], refs[21], refs[22], refs[23]
    rooms, strips, long, grads, back, pairs, grad_weight = (
        refs[24:30],
        refs[30],
        refs[31],
        refs[32],
        refs[33],
        refs[34],
        refs[35],
    )
    take_strips(table, cols, received, back)
    edges = add_strips(load_edges(*blocks), [back[s] for s in range(4)], rooms)
    deltas = exact([edge * rate[...] for edge, rate in zip(edges, slope)])
    edge_strips(deltas, strips)
    halo_grads(strips, weight, long, grads)
    send_strips(table, cols, grads, outs)
    pairs[...] = bulk_delta[...].astype(f32)
    lay_edges(pairs, *deltas)
    delta[...] = pairs[...].astype(bf16)
    bulk_weight_grad(shifted, delta, grad_weight)
    halo_weight_grad(halo_windows(halo, long), strips, grad_weight)
    core = lax.axis_index("tile") & 1
    for tap in range(grad_weight.shape[0]):
        one, two = grad_weight[tap], other_grad[tap]
        kept[tap] = jnp.where(core == 0, one, two)
        given[tap] = jnp.where(core == 0, two, one).astype(bf16)


def last_bulk(delta, weight, interior, pairs, moved, lower, upper):
    pairs[...] = delta[...].astype(f32)
    fill_columns(moved, pairs)
    bulk_conv(moved, weight, lower, upper, interior, True)


def last_edges(cols, table, *refs):
    received, interior, grad = refs[:4], refs[4], refs[5]
    rooms, back, pairs = refs[6:12], refs[12], refs[13]
    count, size, lanes = interior.shape
    c = lanes // 2
    take_strips(table, cols, received, back)
    edges = (
        interior[:, 0:8, :],
        interior[:, size - 8 :, :],
        interior[0, :, 0:c],
        interior[count - 1, :, c:],
    )
    edges = add_strips(edges, [back[s] for s in range(4)], rooms)
    pairs[...] = interior[...]
    lay_edges(pairs, *edges)
    for i in range(count):
        grad[2 * i] = pairs[i, :, 0:c].astype(bf16)
        grad[2 * i + 1] = pairs[i, :, c:].astype(bf16)


def flip_swap(block, mask_ens, mask_tile):
    ens, tile = lax.axis_size("ens"), lax.axis_size("tile")
    route = [
        (e * tile + t, (e ^ mask_ens) * tile + (t ^ mask_tile))
        for e in range(ens)
        for t in range(tile)
    ]
    return lax.ppermute(block, ("ens", "tile"), route)


def pick(parts, index):
    return lax.dynamic_index_in_dim(parts, index, 0, keepdims=False)


def all_sum(kept, given):
    tile = lax.axis_index("tile")
    rows, lanes = kept.shape
    part = kept + flip_swap(given, 0, 1).astype(f32)
    seat = lax.axis_index("ens") * 2 + (tile >> 1 & 1)
    quarters = part.reshape(4, rows // 4, lanes)
    sent = quarters.astype(bf16)
    part = pick(quarters, seat)
    for k in (1, 2, 3):
        part = part + flip_swap(pick(sent, seat ^ k), k >> 1, (k & 1) << 1).astype(f32)
    bit = 4
    while bit < lax.axis_size("tile"):
        own = part.astype(bf16)
        part = lax.reduce_precision(part, 8, 7)
        if bit * 2 < lax.axis_size("tile"):
            one, two, three = (flip_swap(own, 0, bit * k).astype(f32) for k in (1, 2, 3))
            part = (part + one) + (two + three)
            bit *= 4
        else:
            part = part + flip_swap(own, 0, bit).astype(f32)
            bit *= 2
    part = part.astype(bf16)
    whole = jnp.zeros((4,) + part.shape, part.dtype)
    whole = lax.dynamic_update_index_in_dim(whole, part, seat, 0)
    for k in (1, 2, 3):
        got = flip_swap(part, k >> 1, (k & 1) << 1)
        whole = lax.dynamic_update_index_in_dim(whole, got, seat ^ k, 0)
    half = whole.reshape(rows, lanes)
    other = flip_swap(half, 0, 1)
    first = (tile & 1) == 0
    return jnp.where(first, half, other), jnp.where(first, other, half)


def call(kernel, name, ins, outs, scratch, cost=0):
    whole = pl.BlockSpec(memory_space=pltpu.VMEM)
    return pl.pallas_call(
        kernel,
        name=name,
        grid=(1,),
        in_specs=[spec or whole for _, spec in ins],
        out_specs=[whole] * len(outs),
        out_shape=outs,
        scratch_shapes=scratch,
        compiler_params=pltpu.CompilerParams(vmem_limit_bytes=40 << 20),
        cost_estimate=pl.CostEstimate(flops=cost, bytes_accessed=2 << 20, transcendentals=0),
    )(*[array for array, _ in ins])


def local(fields, weight_first, weight_second, neighbours, cotangent):
    block, wanted = fields[0, 0], cotangent[0, 0]
    size, c = block.shape[0], block.shape[-1]
    half = size // 2
    count = lax.axis_size("tile")
    cols = max(4, count // 8)
    shape = weight_first.shape
    one, two = weight_first.reshape(9, c, c), weight_second.reshape(9, c, c)
    flops = 2 * size * size * 9 * c * c

    S = jax.ShapeDtypeStruct
    table = (neighbours, pl.BlockSpec(memory_space=pltpu.SMEM))
    sent = [S((size, c), bf16)] * 4
    halo = S((4, size, c), f32)
    edge = [S((half, 8, 2 * c), f32)] * 2 + [S((size, c), f32)] * 2
    pairs = lambda kind: S((half, size, 2 * c), kind)
    shifted = S(((half + 1) * size, 6 * c), bf16)
    V = lambda leaf: pltpu.VMEM(leaf.shape, leaf.dtype)
    ahead = [pltpu.VMEM((6 * c, 2 * c), bf16)] * 2
    back = [pltpu.VMEM((2 * c, 6 * c), bf16)] * 2
    rooms = [V(leaf) for leaf in edge] + [pltpu.VMEM((size, c), f32)] * 2
    long = pltpu.VMEM((4, size + 16, c), f32)
    whole = lambda arrays: [(array, None) for array in arrays]

    def edge_blocks(array):
        last = size // 8 - 1
        return [
            (array, pl.BlockSpec((half, 8, 2 * c), lambda step: (0, 0, 0))),
            (array, pl.BlockSpec((half, 8, 2 * c), lambda step: (0, last, 0))),
            (array, pl.BlockSpec((1, size, c), lambda step: (0, 0, 0))),
            (array, pl.BlockSpec((1, size, c), lambda step: (half - 1, 0, 1))),
        ]

    def image_edges(array):
        last = size // 16 - 1
        return [
            (array, pl.BlockSpec((size, 16, c), lambda step: (0, 0, 0))),
            (array, pl.BlockSpec((size, 16, c), lambda step: (0, last, 0))),
            (array, pl.BlockSpec((1, size, c), lambda step: (0, 0, 0))),
            (array, pl.BlockSpec((1, size, c), lambda step: (size - 1, 0, 0))),
        ]

    strips = call(
        functools.partial(first_strips, cols),
        "first_strips",
        [table, (block, None)],
        sent,
        [V(halo)],
    )
    strips = swap_all(strips, cols)
    shifted_one, pre_one, hidden, slope = call(
        first_bulk,
        "first_bulk",
        whole([block, one]),
        [shifted, pairs(f32), pairs(bf16), pairs(bf16)],
        [V(pairs(bf16))] + ahead,
        flops,
    )
    found = call(
        functools.partial(first_edges, cols),
        "first_edges",
        [table] + whole(strips) + [(one, None)] + edge_blocks(pre_one),
        sent + edge + edge + [halo],
        rooms + [V(halo), long],
    )
    strips, hidden_edges, slope_edges, halo_one = found[:4], found[4:8], found[8:12], found[12]
    strips = swap_all(strips, cols)
    shifted_two, pre_two, out_bulk, delta_bulk = call(
        second_bulk,
        "second_bulk",
        whole([hidden, *hidden_edges, two, wanted]),
        [shifted, pairs(f32), pairs(bf16), pairs(bf16)],
        [V(pairs(f32))] + ahead,
        flops,
    )
    found = call(
        functools.partial(second_edges, cols),
        "second_edges",
        [table] + whole(strips) + [(two, None)] + edge_blocks(pre_two) + image_edges(wanted),
        sent + edge + edge + [halo],
        rooms + [V(halo), long, V(halo)],
    )
    strips, out_edges, delta_edges, halo_two = found[:4], found[4:8], found[8:12], found[12]
    strips = swap_all(strips, cols)
    out_field, grad_two, grad_hidden, delta_one = call(
        second_back,
        "second_back",
        whole(
            [out_bulk, delta_bulk, *out_edges, *delta_edges, halo_two, shifted_two, two, slope]
        ),
        [S(block.shape, bf16), S((9, c, c), f32), pairs(f32), pairs(bf16)],
        [V(pairs(f32)), V(pairs(bf16))] + back + [V(shifted), V(halo), long],
        2 * flops,
    )
    found = call(
        functools.partial(first_back, cols),
        "first_back",
        [table]
        + whole(strips)
        + [(one, None)]
        + edge_blocks(grad_hidden)
        + whole([*slope_edges, delta_one, halo_one, shifted_one, grad_two]),
        sent + [pairs(bf16), S((9, c, c), f32), S((9, c, c), bf16)],
        rooms
        + [V(halo), long, V(halo), V(halo), V(pairs(f32)), pltpu.VMEM((9, c, c), f32)],
        flops,
    )
    strips, delta_one, kept, given = found[:4], *found[4:7]
    strips = swap_all(strips, cols)
    (interior,) = call(
        last_bulk,
        "last_bulk",
        whole([delta_one, one]),
        [pairs(f32)],
        [V(pairs(f32)), V(shifted)] + back,
        flops,
    )
    (grad_block,) = call(
        functools.partial(last_edges, cols),
        "last_edges",
        [table] + whole([*strips, interior]),
        [S(block.shape, bf16)],
        rooms + [V(halo), V(pairs(f32))],
    )
    grads = all_sum(kept.reshape(9 * c, c), given.reshape(9 * c, c))
    grad_first, grad_second = (grad.astype(f32).reshape(shape) for grad in grads)
    return (out_field[None, None], grad_block[None, None], grad_first, grad_second)


def solution(mesh):
    placed = (P("ens", "tile", None, None, None), P(), P(), P(), P("ens", "tile", None, None, None))
    return jax.shard_map(
        local,
        mesh=mesh,
        in_specs=placed,
        out_specs=(
            P("ens", "tile", None, None, None),
            P("ens", "tile", None, None, None),
            P(),
            P(),
        ),
        check_vma=False,
    )
```

time: 112 us -> 72.1 us (0.64)
  matrix products: 24.8 us -> 0 us
  Pallas kernels: 0 us -> 15.7 us
  other arithmetic: 12.2 us -> 2.02 us
  local copies, waits for them, and re-layouts: 10.5 us -> 2.9 us
  waiting for transfers between devices: 27.4 us -> 21.7 us
  starting transfers between devices: 34.3 us -> 28.7 us
  between operations: 2.26 us -> 0.82 us
    dot_general x74 -> x0, matrix products: 24.8 us -> none  [the longest x18 9.12 us: weight_grad(): jnp.dot(window.T, flat_delta, preferred_element_type=jnp.float32)]
    pallas_call x0 -> x9, Pallas kernels: none -> 15.7 us  [call(): pl.pallas_call(kernel, name=name, grid=(1,), in_specs=[spec or whole for...]
    ppermute x16, waiting for transfers between devices: 14.3 us -> 7.56 us  [swap_all(): lax.ppermute(block, 'tile', [(p, ways[p][k]) for p in range(count)])]
    ppermute x16, starting transfers between devices: 22.4 us -> 17 us  [swap_all(): lax.ppermute(block, 'tile', [(p, ways[p][k]) for p in range(count)])]
    convert_element_type x27 -> x2, other arithmetic: 3.32 us -> 0.08 us  [the longest x1 0.04 us: all_sum(): sent = quarters.astype(bf16)]
    unnamed x78 -> x11, local copies, waits for them, and re-layouts: 5.75 us -> 2.79 us
    slice x13 -> x0, local copies, waits for them, and re-layouts: 2.69 us -> none  [the longest x4 1.23 us: convolve(): padded[..., a:a + extent, b:b + extent, :].reshape(-1, padded.shape[-1])]
    concatenate x4 -> x0, other arithmetic: 1.88 us -> none  [the longest x2 1.05 us: assemble(): jnp.concatenate([left_col[..., :, None, :], block, right_col[..., :, None...]
  transfers between devices with their start and end apart: 27 -> 27, of which waited for: 12 -> 15; matrix products, arithmetic and copies ran while one was open for 6% -> 0% of each run, Pallas kernels for 0% -> 13%
where the time goes in v2:
time: 72.1 us; the launch traced here: 71.9 us
  starting transfers between devices  28.7 us (40%)
  waiting for transfers between devices  21.7 us (30%)
  Pallas kernels  15.7 us (22%)
  local copies, waits for them, and re-layouts  2.9 us (4%)
  other arithmetic  2.02 us (3%)
  between operations  0.82 us (1%)
    ppermute x16, starting transfers between devices, swap_all(): lax.ppermute(block, 'tile', [(p, ways[p][k]) for p in range(count)])  17 us
    pallas_call x9, Pallas kernels, call(): pl.pallas_call(kernel, name=name, grid=(1,), in_specs=[spec or whole for...  15.7 us
    ppermute x11, waiting for transfers between devices, flip_swap(): return lax.ppermute(block, ('ens', 'tile'), route)  14.2 us
    ppermute x11, starting transfers between devices, flip_swap(): return lax.ppermute(block, ('ens', 'tile'), route)  11.7 us
    ppermute x16, waiting for transfers between devices, swap_all(): lax.ppermute(block, 'tile', [(p, ways[p][k]) for p in range(count)])  7.56 us
    unnamed x11, local copies, waits for them, and re-layouts  2.79 us
    reshape x2, other arithmetic, local(): grad.astype(f32).reshape(shape)  1.72 us
  transfers between devices with their start and end apart: 27, of which 15 were waited for; matrix products, arithmetic and copies ran while one was open for 0% of the time, Pallas kernels for 13%

profile of v2, /device:TPU:0, one launch (start us, length us, event | category | flops | bytes accessed | tf_op | source)
XLA Modules:
  0.0 71.9 jit_solution(854462786464362404)
XLA Ops:
  0.6 0.8 %copy.10.table = s32[16,4]{1,0:T(8,128)S(1)} copy(s32[16,4]{0,1:T(4,128)} %param.8) | data formatting | bytes 512 | tf_op args[3]
  1.4 1.1 %copy-done.3 = bf16[1,1,48,48,128]{4,3,2,1,0:T(8,128)(2,1)S(1)} copy-done((bf16[1,1,48,48,128]{4,3,2,1,0:T(8,128)(2,1)S(1)}, bf16[1,1,48,48,128]{4,3,2,1,0:T(8,128)(2,1)}, u32[]{:S(2)}) %copy-start.3) | copy-done | bytes 589848
  2.5 0.9 %first_strips.1 = (bf16[48,128]{1,0:T(8,128)(2,1)S(1)}, bf16[48,128]{1,0:T(8,128)(2,1)S(1)}, bf16[48,128]{1,0:T(8,128)(2,1)S(1)}, bf16[48,128]{1,0:T(8,128)(2,1)S(1)}) custom-call(s32[16,4]{1,0:T(8,128)S(1)} %copy.10.table, bf16[48,48,128]{2,1,0:T(8,128)(2,1)S(1)} %bitcast.51), custom_call_target="tpu_custom_call" | custom-call | bytes 2097152 | tf_op jit(solution)/shard_map/first_strips/pallas_call | solution.py:482
  3.3 5.1 %collective-permute-start = (bf16[48,128]{1,0:T(8,128)(2,1)S(1)}, bf16[48,128]{1,0:T(8,128)(2,1)S(1)}, u32[]{:S(2)}, u32[]{:S(2)}) collective-permute-start(bf16[48,128]{1,0:T(8,128)(2,1)S(1)} %get-tuple-element.54), channel_id=1, source_target_pairs={{0,12},{1,13},{2,14},{3,15},{4,8},{5,9},{6,10},{7,11},{8,4},{9,5},... | collective-permute-start | bytes 36872 | tf_op jit(solution)/shard_map/ppermute | solution.py:65
  8.4 0.7 %collective-permute-start.2 = (bf16[48,128]{1,0:T(8,128)(2,1)S(1)}, bf16[48,128]{1,0:T(8,128)(2,1)S(1)}, u32[]{:S(2)}, u32[]{:S(2)}) collective-permute-start(bf16[48,128]{1,0:T(8,128)(2,1)S(1)} %get-tuple-element.56), channel_id=1, source_target_pairs={{0,15},{1,2},{2,1},{3,4},{4,3},{5,6},{6,5},{7,8},{8,7},{9,10},{10,... | collective-permute-start | bytes 36872 | tf_op jit(solution)/shard_map/ppermute | solution.py:65
  9.2 0.9 %collective-permute-start.3 = (bf16[48,128]{1,0:T(8,128)(2,1)S(1)}, bf16[48,128]{1,0:T(8,128)(2,1)S(1)}, u32[]{:S(2)}, u32[]{:S(2)}) collective-permute-start(bf16[48,128]{1,0:T(8,128)(2,1)S(1)} %get-tuple-element.57), channel_id=1, source_target_pairs={{0,1},{1,0},{2,3},{3,2},{4,5},{5,4},{6,7},{7,6},{8,9},{9,8},{10,11... | collective-permute-start | bytes 36872 | tf_op jit(solution)/shard_map/ppermute | solution.py:65
  10.1 1.0 %copy-done.1 = bf16[3,3,128,128]{3,2,1,0:T(8,128)(2,1)S(1)} copy-done((bf16[3,3,128,128]{3,2,1,0:T(8,128)(2,1)S(1)}, bf16[3,3,128,128]{3,2,1,0:T(8,128)(2,1)}, u32[]{:S(2)}) %copy-start.1) | copy-done | bytes 294936
  11.0 1.7 %first_bulk.1 = (bf16[1200,768]{1,0:T(8,128)(2,1)S(1)}, f32[24,48,256]{2,1,0:T(8,128)S(1)}, bf16[24,48,256]{2,1,0:T(8,128)(2,1)S(1)}, bf16[24,48,256]{2,1,0:T(8,128)(2,1)S(1)}) custom-call(bf16[48,48,128]{2,1,0:T(8,128)(2,1)S(1)} %bitcast.52, bf16[9,128,128]{2,1,0:T(8,128)(2,1)S(1)} %bitcast.47), custom_call_target="tpu_custom_call" | custom-call | flops 679477248 | bytes 2097152 | tf_op jit(solution)/shard_map/first_bulk/pallas_call | solution.py:482
  12.7 1.5 %collective-permute-done.2.refs_2_ = bf16[48,128]{1,0:T(8,128)(2,1)S(1)} collective-permute-done((bf16[48,128]{1,0:T(8,128)(2,1)S(1)}, bf16[48,128]{1,0:T(8,128)(2,1)S(1)}, u32[]{:S(2)}, u32[]{:S(2)}) %collective-permute-start.2) | collective-permute-done | bytes 12320 | tf_op jit(solution)/shard_map/ppermute | solution.py:65
  14.3 1.3 %first_edges.1 = (bf16[48,128]{1,0:T(8,128)(2,1)S(1)}, bf16[48,128]{1,0:T(8,128)(2,1)S(1)}, bf16[48,128]{1,0:T(8,128)(2,1)S(1)}, bf16[48,128]{1,0:T(8,128)(2,1)S...) custom-call(s32[16,4]{1,0:T(8,128)S(1)} %copy.10.table, ...), custom_call_target="tpu_custom_call" | custom-call | bytes 2097152 | tf_op jit(solution)/shard_map/first_edges/pallas_call | solution.py:482
  15.7 0.8 %collective-permute-start.5 = (bf16[48,128]{1,0:T(8,128)(2,1)S(1)}, bf16[48,128]{1,0:T(8,128)(2,1)S(1)}, u32[]{:S(2)}, u32[]{:S(2)}) collective-permute-start(bf16[48,128]{1,0:T(8,128)(2,1)S(1)} %get-tuple-element.66), channel_id=1, source_target_pairs={{0,4},{1,5},{2,6},{3,7},{4,0},{5,1},{6,2},{7,3},{8,12},{9,13},{10,... | collective-permute-start | bytes 36872 | tf_op jit(solution)/shard_map/ppermute | solution.py:65
  16.4 2.3 %collective-permute-start.6 = (bf16[48,128]{1,0:T(8,128)(2,1)S(1)}, bf16[48,128]{1,0:T(8,128)(2,1)S(1)}, u32[]{:S(2)}, u32[]{:S(2)}) collective-permute-start(bf16[48,128]{1,0:T(8,128)(2,1)S(1)} %get-tuple-element.67), channel_id=1, source_target_pairs={{0,15},{1,2},{2,1},{3,4},{4,3},{5,6},{6,5},{7,8},{8,7},{9,10},{10,... | collective-permute-start | bytes 36872 | tf_op jit(solution)/shard_map/ppermute | solution.py:65
  18.8 1.7 %second_bulk.1 = (bf16[1200,768]{1,0:T(8,128)(2,1)S(1)}, f32[24,48,256]{2,1,0:T(8,128)S(1)}, bf16[24,48,256]{2,1,0:T(8,128)(2,1)S(1)}, bf16[24,48,256]{2,1,0:T(8,128)(2,1)S(1)}) custom-call(bf16[24,48,256]{2,1,0:T(8,128)(2,1)S(1)} %get-tuple-element.53.hidden, f32[24,8,256]{2,1,0:T(8,128)S(1)} %get-tuple-element.59.left, ...), custom_call_target="tpu_custom_call" | custom-call | flops 679477248 | bytes 2097152 | tf_op jit(solution)/shard_map/second_bulk/pallas_call | solution.py:482
  20.5 0.7 collective-permute-done.4.refs_0_
  21.2 1.1 %collective-permute-done.6.refs_2_ = bf16[48,128]{1,0:T(8,128)(2,1)S(1)} collective-permute-done((bf16[48,128]{1,0:T(8,128)(2,1)S(1)}, bf16[48,128]{1,0:T(8,128)(2,1)S(1)}, u32[]{:S(2)}, u32[]{:S(2)}) %collective-permute-start.6) | collective-permute-done | bytes 12320 | tf_op jit(solution)/shard_map/ppermute | solution.py:65
  22.3 1.6 %second_edges.1 = (bf16[48,128]{1,0:T(8,128)(2,1)S(1)}, bf16[48,128]{1,0:T(8,128)(2,1)S(1)}, bf16[48,128]{1,0:T(8,128)(2,1)S(1)}, bf16[48,128]{1,0:T(8,128)(2,1)...) custom-call(s32[16,4]{1,0:T(8,128)S(1)} %copy.10.table, ...), custom_call_target="tpu_custom_call" | custom-call | bytes 2097152 | tf_op jit(solution)/shard_map/second_edges/pallas_call | solution.py:482
  23.8 2.4 %collective-permute-start.10 = (bf16[48,128]{1,0:T(8,128)(2,1)S(1)}, bf16[48,128]{1,0:T(8,128)(2,1)S(1)}, u32[]{:S(2)}, u32[]{:S(2)}) collective-permute-start(bf16[48,128]{1,0:T(8,128)(2,1)S(1)} %get-tuple-element.84), channel_id=1, source_target_pairs={{0,15},{1,2},{2,1},{3,4},{4,3},{5,6},{6,5},{7,8},{8,7},{9,10},{10,... | collective-permute-start | bytes 36872 | tf_op jit(solution)/shard_map/ppermute | solution.py:65
  26.2 0.5 collective-permute-start.9
  26.7 3.3 %second_back.1 = (bf16[48,48,128]{2,1,0:T(8,128)(2,1)}, f32[9,128,128]{2,1,0:T(8,128)S(1)}, f32[24,48,256]{2,1,0:T(8,128)S(1)}, bf16[24,48,256]{2,1,0:T(8,128)(2,1)S(1)}) custom-call(bf16[24,48,256]{2,1,0:T(8,128)(2,1)S(1)} %get-tuple-element.63.refs_0_, bf16[24,48,256]{2,1,0:T(8,128)(2,1)S(1)} %get-tuple-element.64.refs_1_, ...), custom_call_target="tpu_custom_call" | custom-call | flops 1358954496 | bytes 2097152 | tf_op jit(solution)/shard_map/second_back/pallas_call | solution.py:482
  30.0 1.7 %collective-permute-done.8.refs_0_ = bf16[48,128]{1,0:T(8,128)(2,1)S(1)} collective-permute-done((bf16[48,128]{1,0:T(8,128)(2,1)S(1)}, bf16[48,128]{1,0:T(8,128)(2,1)S(1)}, u32[]{:S(2)}, u32[]{:S(2)}) %collective-permute-start.8) | collective-permute-done | bytes 12320 | tf_op jit(solution)/shard_map/ppermute | solution.py:65
  31.7 2.4 %first_back.1 = (bf16[48,128]{1,0:T(8,128)(2,1)S(1)}, bf16[48,128]{1,0:T(8,128)(2,1)S(1)}, bf16[48,128]{1,0:T(8,128)(2,1)S(1)}, bf16[48,128]{1,0:T(8,128)(2,1)S(...) custom-call(s32[16,4]{1,0:T(8,128)S(1)} %copy.10.table, ...), custom_call_target="tpu_custom_call" | custom-call | flops 679477248 | bytes 2097152 | tf_op jit(solution)/shard_map/first_back/pallas_call | solution.py:482
  34.2 1.5 %collective-permute-done.16 = bf16[1152,128]{1,0:T(8,128)(2,1)S(1)} collective-permute-done((bf16[1152,128]{1,0:T(8,128)(2,1)S(1)}, bf16[1152,128]{1,0:T(8,128)(2,1)S(1)}, u32[]{:S(2)}, u32[]{:S(2)}) %collective-permute-start.16) | collective-permute-done | bytes 294944 | tf_op jit(solution)/shard_map/ppermute | solution.py:440
  35.9 1.4 %collective-permute-start.17 = (bf16[288,128]{1,0:T(8,128)(2,1)S(1)}, bf16[288,128]{1,0:T(8,128)(2,1)S(1)}, u32[]{:S(2)}, u32[]{:S(2)}) collective-permute-start(bf16[288,128]{1,0:T(8,128)(2,1)S(1)} %get-tuple-element.106), channel_id=1, source_target_pairs={{0,2},{1,3},{2,0},{3,1},{4,6},{5,7},{6,4},{7,5},{8,10},{9,11},{10,... | collective-permute-start | bytes 221192 | tf_op jit(solution)/shard_map/ppermute | solution.py:440
  37.3 1.5 %collective-permute-start.18 = (bf16[288,128]{1,0:T(8,128)(2,1)S(1)}, bf16[288,128]{1,0:T(8,128)(2,1)S(1)}, u32[]{:S(2)}, u32[]{:S(2)}) collective-permute-start(bf16[288,128]{1,0:T(8,128)(2,1)S(1)} %get-tuple-element.108), channel_id=1, source_target_pairs={{0,16},{1,17},{2,18},{3,19},{4,20},{5,21},{6,22},{7,23},{8,24},{9,... | collective-permute-start | bytes 221192 | tf_op jit(solution)/shard_map/ppermute | solution.py:440
  38.8 0.7 collective-permute-start.19
  39.5 0.9 %collective-permute-done.17 = bf16[288,128]{1,0:T(8,128)(2,1)S(1)} collective-permute-done((bf16[288,128]{1,0:T(8,128)(2,1)S(1)}, bf16[288,128]{1,0:T(8,128)(2,1)S(1)}, u32[]{:S(2)}, u32[]{:S(2)}) %collective-permute-start.17) | collective-permute-done | bytes 73760 | tf_op jit(solution)/shard_map/ppermute | solution.py:440
  40.3 1.8 %collective-permute-done.18 = bf16[288,128]{1,0:T(8,128)(2,1)S(1)} collective-permute-done((bf16[288,128]{1,0:T(8,128)(2,1)S(1)}, bf16[288,128]{1,0:T(8,128)(2,1)S(1)}, u32[]{:S(2)}, u32[]{:S(2)}) %collective-permute-start.18) | collective-permute-done | bytes 73760 | tf_op jit(solution)/shard_map/ppermute | solution.py:440
  42.2 1.9 %collective-permute-done.19 = bf16[288,128]{1,0:T(8,128)(2,1)S(1)} collective-permute-done((bf16[288,128]{1,0:T(8,128)(2,1)S(1)}, bf16[288,128]{1,0:T(8,128)(2,1)S(1)}, u32[]{:S(2)}, u32[]{:S(2)}) %collective-permute-start.19) | collective-permute-done | bytes 73760 | tf_op jit(solution)/shard_map/ppermute | solution.py:440
  44.1 1.7 %collective-permute-start.20 = (bf16[288,128]{1,0:T(8,128)(2,1)S(1)}, bf16[288,128]{1,0:T(8,128)(2,1)S(1)}, u32[]{:S(2)}, u32[]{:S(2)}) collective-permute-start(bf16[288,128]{1,0:T(8,128)(2,1)S(1)} %fusion.2), channel_id=1, source_target_pairs={{0,4},{1,5},{2,6},{3,7},{4,0},{5,1},{6,2},{7,3},{8,12},{9,13},{10,... | collective-permute-start | bytes 221192 | tf_op jit(solution)/shard_map/ppermute | solution.py:440
  45.8 0.7 collective-permute-start.21
  46.5 2.0 %collective-permute-start.22 = (bf16[288,128]{1,0:T(8,128)(2,1)S(1)}, bf16[288,128]{1,0:T(8,128)(2,1)S(1)}, u32[]{:S(2)}, u32[]{:S(2)}) collective-permute-start(bf16[288,128]{1,0:T(8,128)(2,1)S(1)} %fusion.2), channel_id=1, source_target_pairs={{0,12},{1,13},{2,14},{3,15},{4,8},{5,9},{6,10},{7,11},{8,4},{9,5},... | collective-permute-start | bytes 221192 | tf_op jit(solution)/shard_map/ppermute | solution.py:440
  48.5 1.0 %collective-permute-done.20 = bf16[288,128]{1,0:T(8,128)(2,1)S(1)} collective-permute-done((bf16[288,128]{1,0:T(8,128)(2,1)S(1)}, bf16[288,128]{1,0:T(8,128)(2,1)S(1)}, u32[]{:S(2)}, u32[]{:S(2)}) %collective-permute-start.20) | collective-permute-done | bytes 73760 | tf_op jit(solution)/shard_map/ppermute | solution.py:440
  49.6 3.3 %collective-permute-done.21 = bf16[288,128]{1,0:T(8,128)(2,1)S(1)} collective-permute-done((bf16[288,128]{1,0:T(8,128)(2,1)S(1)}, bf16[288,128]{1,0:T(8,128)(2,1)S(1)}, u32[]{:S(2)}, u32[]{:S(2)}) %collective-permute-start.21) | collective-permute-done | bytes 73760 | tf_op jit(solution)/shard_map/ppermute | solution.py:440
  53.0 1.2 %collective-permute-start.23 = (bf16[288,128]{1,0:T(8,128)(2,1)S(1)}, bf16[288,128]{1,0:T(8,128)(2,1)S(1)}, u32[]{:S(2)}, u32[]{:S(2)}) collective-permute-start(bf16[288,128]{1,0:T(8,128)(2,1)S(1)} %get-tuple-element.103), channel_id=1, source_target_pairs={{0,2},{1,3},{2,0},{3,1},{4,6},{5,7},{6,4},{7,5},{8,10},{9,11},{10,... | collective-permute-start | bytes 221192 | tf_op jit(solution)/shard_map/ppermute | solution.py:440
  54.2 0.9 %collective-permute-start.24 = (bf16[288,128]{1,0:T(8,128)(2,1)S(1)}, bf16[288,128]{1,0:T(8,128)(2,1)S(1)}, u32[]{:S(2)}, u32[]{:S(2)}) collective-permute-start(bf16[288,128]{1,0:T(8,128)(2,1)S(1)} %get-tuple-element.103), channel_id=1, source_target_pairs={{0,16},{1,17},{2,18},{3,19},{4,20},{5,21},{6,22},{7,23},{8,24},{9,... | collective-permute-start | bytes 221192 | tf_op jit(solution)/shard_map/ppermute | solution.py:440
  55.1 1.5 %collective-permute-start.25 = (bf16[288,128]{1,0:T(8,128)(2,1)S(1)}, bf16[288,128]{1,0:T(8,128)(2,1)S(1)}, u32[]{:S(2)}, u32[]{:S(2)}) collective-permute-start(bf16[288,128]{1,0:T(8,128)(2,1)S(1)} %get-tuple-element.103), channel_id=1, source_target_pairs={{0,18},{1,19},{2,16},{3,17},{4,22},{5,23},{6,20},{7,21},{8,26},{9,... | collective-permute-start | bytes 221192 | tf_op jit(solution)/shard_map/ppermute | solution.py:440
  56.6 0.9 %collective-permute-done.23 = bf16[288,128]{1,0:T(8,128)(2,1)S(1)} collective-permute-done((bf16[288,128]{1,0:T(8,128)(2,1)S(1)}, bf16[288,128]{1,0:T(8,128)(2,1)S(1)}, u32[]{:S(2)}, u32[]{:S(2)}) %collective-permute-start.23) | collective-permute-done | bytes 73760 | tf_op jit(solution)/shard_map/ppermute | solution.py:440
  57.5 1.1 %collective-permute-done.24 = bf16[288,128]{1,0:T(8,128)(2,1)S(1)} collective-permute-done((bf16[288,128]{1,0:T(8,128)(2,1)S(1)}, bf16[288,128]{1,0:T(8,128)(2,1)S(1)}, u32[]{:S(2)}, u32[]{:S(2)}) %collective-permute-start.24) | collective-permute-done | bytes 73760 | tf_op jit(solution)/shard_map/ppermute | solution.py:440
  58.6 1.7 %collective-permute-done.25 = bf16[288,128]{1,0:T(8,128)(2,1)S(1)} collective-permute-done((bf16[288,128]{1,0:T(8,128)(2,1)S(1)}, bf16[288,128]{1,0:T(8,128)(2,1)S(1)}, u32[]{:S(2)}, u32[]{:S(2)}) %collective-permute-start.25) | collective-permute-done | bytes 73760 | tf_op jit(solution)/shard_map/ppermute | solution.py:440
  60.4 1.8 %collective-permute-start.12 = (bf16[48,128]{1,0:T(8,128)(2,1)S(1)}, bf16[48,128]{1,0:T(8,128)(2,1)S(1)}, u32[]{:S(2)}, u32[]{:S(2)}) collective-permute-start(bf16[48,128]{1,0:T(8,128)(2,1)S(1)} %get-tuple-element.95), channel_id=1, source_target_pairs={{0,12},{1,13},{2,14},{3,15},{4,8},{5,9},{6,10},{7,11},{8,4},{9,5},... | collective-permute-start | bytes 36872 | tf_op jit(solution)/shard_map/ppermute | solution.py:65
  62.2 0.4 collective-permute-start.13
  62.6 2.0 %collective-permute-start.14 = (bf16[48,128]{1,0:T(8,128)(2,1)S(1)}, bf16[48,128]{1,0:T(8,128)(2,1)S(1)}, u32[]{:S(2)}, u32[]{:S(2)}) collective-permute-start(bf16[48,128]{1,0:T(8,128)(2,1)S(1)} %get-tuple-element.97), channel_id=1, source_target_pairs={{0,15},{1,2},{2,1},{3,4},{4,3},{5,6},{6,5},{7,8},{8,7},{9,10},{10,... | collective-permute-start | bytes 36872 | tf_op jit(solution)/shard_map/ppermute | solution.py:65
  64.6 1.2 %last_bulk.1.refs_4_ = f32[24,48,256]{2,1,0:T(8,128)S(1)} custom-call(bf16[24,48,256]{2,1,0:T(8,128)(2,1)S(1)} %get-tuple-element.99.delta, bf16[9,128,128]{2,1,0:T(8,128)(2,1)S(1)} %bitcast.50), custom_call_target="tpu_custom_call" | custom-call | flops 679477248 | bytes 2097152 | tf_op jit(solution)/shard_map/last_bulk/pallas_call | solution.py:482
  65.9 0.2 collective-permute-done.12.refs_0_
  66.1 2.4 %collective-permute-done.14.refs_2_ = bf16[48,128]{1,0:T(8,128)(2,1)S(1)} collective-permute-done((bf16[48,128]{1,0:T(8,128)(2,1)S(1)}, bf16[48,128]{1,0:T(8,128)(2,1)S(1)}, u32[]{:S(2)}, u32[]{:S(2)}) %collective-permute-start.14) | collective-permute-done | bytes 12320 | tf_op jit(solution)/shard_map/ppermute | solution.py:65
  68.4 1.7 %last_edges.1 = bf16[48,48,128]{2,1,0:T(8,128)(2,1)} custom-call(s32[16,4]{1,0:T(8,128)S(1)} %copy.10.table, bf16[48,128]{1,0:T(8,128)(2,1)S(1)} %collective-permute-done.12.refs_0_, bf16[48,128]{1,0:T(8,128)(2,1)S(1)} %collective-permute-done.13.refs_1_, bf16[48,128]{1,0:T(8,128)(2,1)S(1)} %collective-permute-done.14.refs_2_, ...), custom_call_target="tpu_custom_call" | custom-call | bytes 2097152 | tf_op jit(solution)/shard_map/last_edges/pallas_call | solution.py:482
  70.1 0.9 %convert.2 = f32[3,3,128,128]{3,2,1,0:T(8,128)} convert(bf16[3,3,128,128]{3,2,1,0:T(8,128)(2,1)S(1)} %bitcast.61) | non-fusion elementwise | flops 147456 | bytes 884736 | tf_op jit(solution)/shard_map/reshape | solution.py:620
  71.0 0.9 %convert.3 = f32[3,3,128,128]{3,2,1,0:T(8,128)} convert(bf16[3,3,128,128]{3,2,1,0:T(8,128)(2,1)S(1)} %bitcast.60) | non-fusion elementwise | flops 147456 | bytes 884736 | tf_op jit(solution)/shard_map/reshape | solution.py:620
  (38 shorter events, 0.7 us)
Async XLA Ops:
  1.4 1.1 %copy-start.3 = (bf16[1,1,48,48,128]{4,3,2,1,0:T(8,128)(2,1)S(1)}, bf16[1,1,48,48,128]{4,3,2,1,0:T(8,128)(2,1)}, u32[]{:S(2)}) copy-start(bf16[1,1,48,48,128]{4,3,2,1,0:T(8,128)(2,1)} %param.5) | copy-start | bytes 1769476
  3.3 9.4 %collective-permute-start = (bf16[48,128]{1,0:T(8,128)(2,1)S(1)}, bf16[48,128]{1,0:T(8,128)(2,1)S(1)}, u32[]{:S(2)}, u32[]{:S(2)}) collective-permute-start(bf16[48,128]{1,0:T(8,128)(2,1)S(1)} %get-tuple-element.54), channel_id=1, source_target_pairs={{0,12},{1,13},{2,14},{3,15},{4,8},{5,9},{6,10},{7,11},{8,4},{9,5},... | collective-permute-start | bytes 36872 | tf_op jit(solution)/shard_map/ppermute | solution.py:65
  8.4 4.3 %collective-permute-start.1 = (bf16[48,128]{1,0:T(8,128)(2,1)S(1)}, bf16[48,128]{1,0:T(8,128)(2,1)S(1)}, u32[]{:S(2)}, u32[]{:S(2)}) collective-permute-start(bf16[48,128]{1,0:T(8,128)(2,1)S(1)} %get-tuple-element.55), channel_id=1, source_target_pairs={{0,4},{1,5},{2,6},{3,7},{4,0},{5,1},{6,2},{7,3},{8,12},{9,13},{10,... | collective-permute-start | bytes 36872 | tf_op jit(solution)/shard_map/ppermute | solution.py:65
  8.4 5.8 %collective-permute-start.2 = (bf16[48,128]{1,0:T(8,128)(2,1)S(1)}, bf16[48,128]{1,0:T(8,128)(2,1)S(1)}, u32[]{:S(2)}, u32[]{:S(2)}) collective-permute-start(bf16[48,128]{1,0:T(8,128)(2,1)S(1)} %get-tuple-element.56), channel_id=1, source_target_pairs={{0,15},{1,2},{2,1},{3,4},{4,3},{5,6},{6,5},{7,8},{8,7},{9,10},{10,... | collective-permute-start | bytes 36872 | tf_op jit(solution)/shard_map/ppermute | solution.py:65
  9.2 5.1 %collective-permute-start.3 = (bf16[48,128]{1,0:T(8,128)(2,1)S(1)}, bf16[48,128]{1,0:T(8,128)(2,1)S(1)}, u32[]{:S(2)}, u32[]{:S(2)}) collective-permute-start(bf16[48,128]{1,0:T(8,128)(2,1)S(1)} %get-tuple-element.57), channel_id=1, source_target_pairs={{0,1},{1,0},{2,3},{3,2},{4,5},{5,4},{6,7},{7,6},{8,9},{9,8},{10,11... | collective-permute-start | bytes 36872 | tf_op jit(solution)/shard_map/ppermute | solution.py:65
  10.1 1.0 %copy-start.1 = (bf16[3,3,128,128]{3,2,1,0:T(8,128)(2,1)S(1)}, bf16[3,3,128,128]{3,2,1,0:T(8,128)(2,1)}, u32[]{:S(2)}) copy-start(bf16[3,3,128,128]{3,2,1,0:T(8,128)(2,1)} %param.6) | copy-start | bytes 884740
  14.3 4.5 %copy-start = (bf16[1,1,48,48,128]{4,3,2,1,0:T(8,128)(2,1)S(1)}, bf16[1,1,48,48,128]{4,3,2,1,0:T(8,128)(2,1)}, u32[]{:S(2)}) copy-start(bf16[1,1,48,48,128]{4,3,2,1,0:T(8,128)(2,1)} %param.9) | copy-start | bytes 1769476
  14.3 4.5 %copy-start.4 = (bf16[3,3,128,128]{3,2,1,0:T(8,128)(2,1)S(1)}, bf16[3,3,128,128]{3,2,1,0:T(8,128)(2,1)}, u32[]{:S(2)}) copy-start(bf16[3,3,128,128]{3,2,1,0:T(8,128)(2,1)} %param.7) | copy-start | bytes 884740
  15.6 5.6 %collective-permute-start.4 = (bf16[48,128]{1,0:T(8,128)(2,1)S(1)}, bf16[48,128]{1,0:T(8,128)(2,1)S(1)}, u32[]{:S(2)}, u32[]{:S(2)}) collective-permute-start(bf16[48,128]{1,0:T(8,128)(2,1)S(1)} %get-tuple-element.65), channel_id=1, source_target_pairs={{0,12},{1,13},{2,14},{3,15},{4,8},{5,9},{6,10},{7,11},{8,4},{9,5},... | collective-permute-start | bytes 36872 | tf_op jit(solution)/shard_map/ppermute | solution.py:65
  15.7 5.5 %collective-permute-start.5 = (bf16[48,128]{1,0:T(8,128)(2,1)S(1)}, bf16[48,128]{1,0:T(8,128)(2,1)S(1)}, u32[]{:S(2)}, u32[]{:S(2)}) collective-permute-start(bf16[48,128]{1,0:T(8,128)(2,1)S(1)} %get-tuple-element.66), channel_id=1, source_target_pairs={{0,4},{1,5},{2,6},{3,7},{4,0},{5,1},{6,2},{7,3},{8,12},{9,13},{10,... | collective-permute-start | bytes 36872 | tf_op jit(solution)/shard_map/ppermute | solution.py:65
  16.4 5.8 %collective-permute-start.6 = (bf16[48,128]{1,0:T(8,128)(2,1)S(1)}, bf16[48,128]{1,0:T(8,128)(2,1)S(1)}, u32[]{:S(2)}, u32[]{:S(2)}) collective-permute-start(bf16[48,128]{1,0:T(8,128)(2,1)S(1)} %get-tuple-element.67), channel_id=1, source_target_pairs={{0,15},{1,2},{2,1},{3,4},{4,3},{5,6},{6,5},{7,8},{8,7},{9,10},{10,... | collective-permute-start | bytes 36872 | tf_op jit(solution)/shard_map/ppermute | solution.py:65
  18.7 3.5 %collective-permute-start.7 = (bf16[48,128]{1,0:T(8,128)(2,1)S(1)}, bf16[48,128]{1,0:T(8,128)(2,1)S(1)}, u32[]{:S(2)}, u32[]{:S(2)}) collective-permute-start(bf16[48,128]{1,0:T(8,128)(2,1)S(1)} %get-tuple-element.68), channel_id=1, source_target_pairs={{0,1},{1,0},{2,3},{3,2},{4,5},{5,4},{6,7},{7,6},{8,9},{9,8},{10,11... | collective-permute-start | bytes 36872 | tf_op jit(solution)/shard_map/ppermute | solution.py:65
  23.8 6.2 %collective-permute-start.10 = (bf16[48,128]{1,0:T(8,128)(2,1)S(1)}, bf16[48,128]{1,0:T(8,128)(2,1)S(1)}, u32[]{:S(2)}, u32[]{:S(2)}) collective-permute-start(bf16[48,128]{1,0:T(8,128)(2,1)S(1)} %get-tuple-element.84), channel_id=1, source_target_pairs={{0,15},{1,2},{2,1},{3,4},{4,3},{5,6},{6,5},{7,8},{8,7},{9,10},{10,... | collective-permute-start | bytes 36872 | tf_op jit(solution)/shard_map/ppermute | solution.py:65
  26.2 3.8 %collective-permute-start.11 = (bf16[48,128]{1,0:T(8,128)(2,1)S(1)}, bf16[48,128]{1,0:T(8,128)(2,1)S(1)}, u32[]{:S(2)}, u32[]{:S(2)}) collective-permute-start(bf16[48,128]{1,0:T(8,128)(2,1)S(1)} %get-tuple-element.85), channel_id=1, source_target_pairs={{0,1},{1,0},{2,3},{3,2},{4,5},{5,4},{6,7},{7,6},{8,9},{9,8},{10,11... | collective-permute-start | bytes 36872 | tf_op jit(solution)/shard_map/ppermute | solution.py:65
  26.2 5.5 %collective-permute-start.8 = (bf16[48,128]{1,0:T(8,128)(2,1)S(1)}, bf16[48,128]{1,0:T(8,128)(2,1)S(1)}, u32[]{:S(2)}, u32[]{:S(2)}) collective-permute-start(bf16[48,128]{1,0:T(8,128)(2,1)S(1)} %get-tuple-element.82), channel_id=1, source_target_pairs={{0,12},{1,13},{2,14},{3,15},{4,8},{5,9},{6,10},{7,11},{8,4},{9,5},... | collective-permute-start | bytes 36872 | tf_op jit(solution)/shard_map/ppermute | solution.py:65
  26.2 5.5 %collective-permute-start.9 = (bf16[48,128]{1,0:T(8,128)(2,1)S(1)}, bf16[48,128]{1,0:T(8,128)(2,1)S(1)}, u32[]{:S(2)}, u32[]{:S(2)}) collective-permute-start(bf16[48,128]{1,0:T(8,128)(2,1)S(1)} %get-tuple-element.83), channel_id=1, source_target_pairs={{0,4},{1,5},{2,6},{3,7},{4,0},{5,1},{6,2},{7,3},{8,12},{9,13},{10,... | collective-permute-start | bytes 36872 | tf_op jit(solution)/shard_map/ppermute | solution.py:65
  26.7 5.0 %copy-start.2 = (bf16[3,3,128,128]{3,2,1,0:T(8,128)(2,1)S(1)}, bf16[3,3,128,128]{3,2,1,0:T(8,128)(2,1)}, u32[]{:S(2)}) copy-start(bf16[3,3,128,128]{3,2,1,0:T(8,128)(2,1)} %param.6) | copy-start | bytes 884740
  34.1 1.6 %collective-permute-start.16 = (bf16[1152,128]{1,0:T(8,128)(2,1)S(1)}, bf16[1152,128]{1,0:T(8,128)(2,1)S(1)}, u32[]{:S(2)}, u32[]{:S(2)}) collective-permute-start(bf16[1152,128]{1,0:T(8,128)(2,1)S(1)} %bitcast.56), channel_id=1, source_target_pairs={{0,1},{1,0},{2,3},{3,2},{4,5},{5,4},{6,7},{7,6},{8,9},{9,8},{10,11... | collective-permute-start | bytes 884744 | tf_op jit(solution)/shard_map/ppermute | solution.py:440
  35.9 4.4 %collective-permute-start.17 = (bf16[288,128]{1,0:T(8,128)(2,1)S(1)}, bf16[288,128]{1,0:T(8,128)(2,1)S(1)}, u32[]{:S(2)}, u32[]{:S(2)}) collective-permute-start(bf16[288,128]{1,0:T(8,128)(2,1)S(1)} %get-tuple-element.106), channel_id=1, source_target_pairs={{0,2},{1,3},{2,0},{3,1},{4,6},{5,7},{6,4},{7,5},{8,10},{9,11},{10,... | collective-permute-start | bytes 221192 | tf_op jit(solution)/shard_map/ppermute | solution.py:440
  37.3 4.9 %collective-permute-start.18 = (bf16[288,128]{1,0:T(8,128)(2,1)S(1)}, bf16[288,128]{1,0:T(8,128)(2,1)S(1)}, u32[]{:S(2)}, u32[]{:S(2)}) collective-permute-start(bf16[288,128]{1,0:T(8,128)(2,1)S(1)} %get-tuple-element.108), channel_id=1, source_target_pairs={{0,16},{1,17},{2,18},{3,19},{4,20},{5,21},{6,22},{7,23},{8,24},{9,... | collective-permute-start | bytes 221192 | tf_op jit(solution)/shard_map/ppermute | solution.py:440
  38.8 5.3 %collective-permute-start.19 = (bf16[288,128]{1,0:T(8,128)(2,1)S(1)}, bf16[288,128]{1,0:T(8,128)(2,1)S(1)}, u32[]{:S(2)}, u32[]{:S(2)}) collective-permute-start(bf16[288,128]{1,0:T(8,128)(2,1)S(1)} %get-tuple-element.107), channel_id=1, source_target_pairs={{0,18},{1,19},{2,16},{3,17},{4,22},{5,23},{6,20},{7,21},{8,26},{9,... | collective-permute-start | bytes 221192 | tf_op jit(solution)/shard_map/ppermute | solution.py:440
  44.1 5.5 %collective-permute-start.20 = (bf16[288,128]{1,0:T(8,128)(2,1)S(1)}, bf16[288,128]{1,0:T(8,128)(2,1)S(1)}, u32[]{:S(2)}, u32[]{:S(2)}) collective-permute-start(bf16[288,128]{1,0:T(8,128)(2,1)S(1)} %fusion.2), channel_id=1, source_target_pairs={{0,4},{1,5},{2,6},{3,7},{4,0},{5,1},{6,2},{7,3},{8,12},{9,13},{10,... | collective-permute-start | bytes 221192 | tf_op jit(solution)/shard_map/ppermute | solution.py:440
  45.8 7.1 %collective-permute-start.21 = (bf16[288,128]{1,0:T(8,128)(2,1)S(1)}, bf16[288,128]{1,0:T(8,128)(2,1)S(1)}, u32[]{:S(2)}, u32[]{:S(2)}) collective-permute-start(bf16[288,128]{1,0:T(8,128)(2,1)S(1)} %fusion.2), channel_id=1, source_target_pairs={{0,8},{1,9},{2,10},{3,11},{4,12},{5,13},{6,14},{7,15},{8,0},{9,1},... | collective-permute-start | bytes 221192 | tf_op jit(solution)/shard_map/ppermute | solution.py:440
  46.5 6.4 %collective-permute-start.22 = (bf16[288,128]{1,0:T(8,128)(2,1)S(1)}, bf16[288,128]{1,0:T(8,128)(2,1)S(1)}, u32[]{:S(2)}, u32[]{:S(2)}) collective-permute-start(bf16[288,128]{1,0:T(8,128)(2,1)S(1)} %fusion.2), channel_id=1, source_target_pairs={{0,12},{1,13},{2,14},{3,15},{4,8},{5,9},{6,10},{7,11},{8,4},{9,5},... | collective-permute-start | bytes 221192 | tf_op jit(solution)/shard_map/ppermute | solution.py:440
  53.0 4.4 %collective-permute-start.23 = (bf16[288,128]{1,0:T(8,128)(2,1)S(1)}, bf16[288,128]{1,0:T(8,128)(2,1)S(1)}, u32[]{:S(2)}, u32[]{:S(2)}) collective-permute-start(bf16[288,128]{1,0:T(8,128)(2,1)S(1)} %get-tuple-element.103), channel_id=1, source_target_pairs={{0,2},{1,3},{2,0},{3,1},{4,6},{5,7},{6,4},{7,5},{8,10},{9,11},{10,... | collective-permute-start | bytes 221192 | tf_op jit(solution)/shard_map/ppermute | solution.py:440
  54.2 4.4 %collective-permute-start.24 = (bf16[288,128]{1,0:T(8,128)(2,1)S(1)}, bf16[288,128]{1,0:T(8,128)(2,1)S(1)}, u32[]{:S(2)}, u32[]{:S(2)}) collective-permute-start(bf16[288,128]{1,0:T(8,128)(2,1)S(1)} %get-tuple-element.103), channel_id=1, source_target_pairs={{0,16},{1,17},{2,18},{3,19},{4,20},{5,21},{6,22},{7,23},{8,24},{9,... | collective-permute-start | bytes 221192 | tf_op jit(solution)/shard_map/ppermute | solution.py:440
  55.1 5.3 %collective-permute-start.25 = (bf16[288,128]{1,0:T(8,128)(2,1)S(1)}, bf16[288,128]{1,0:T(8,128)(2,1)S(1)}, u32[]{:S(2)}, u32[]{:S(2)}) collective-permute-start(bf16[288,128]{1,0:T(8,128)(2,1)S(1)} %get-tuple-element.103), channel_id=1, source_target_pairs={{0,18},{1,19},{2,16},{3,17},{4,22},{5,23},{6,20},{7,21},{8,26},{9,... | collective-permute-start | bytes 221192 | tf_op jit(solution)/shard_map/ppermute | solution.py:440
  60.3 9.8 %collective-permute-start.26 = (bf16[1152,128]{1,0:T(8,128)(2,1)S(1)}, bf16[1152,128]{1,0:T(8,128)(2,1)S(1)}, u32[]{:S(2)}, u32[]{:S(2)}) collective-permute-start(bf16[1152,128]{1,0:T(8,128)(2,1)S(1)} %bitcast.62), channel_id=1, source_target_pairs={{0,1},{1,0},{2,3},{3,2},{4,5},{5,4},{6,7},{7,6},{8,9},{9,8},{10,11... | collective-permute-start | bytes 884744 | tf_op jit(solution)/shard_map/ppermute | solution.py:440
  60.4 5.6 %collective-permute-start.12 = (bf16[48,128]{1,0:T(8,128)(2,1)S(1)}, bf16[48,128]{1,0:T(8,128)(2,1)S(1)}, u32[]{:S(2)}, u32[]{:S(2)}) collective-permute-start(bf16[48,128]{1,0:T(8,128)(2,1)S(1)} %get-tuple-element.95), channel_id=1, source_target_pairs={{0,12},{1,13},{2,14},{3,15},{4,8},{5,9},{6,10},{7,11},{8,4},{9,5},... | collective-permute-start | bytes 36872 | tf_op jit(solution)/shard_map/ppermute | solution.py:65
  62.2 3.8 %collective-permute-start.13 = (bf16[48,128]{1,0:T(8,128)(2,1)S(1)}, bf16[48,128]{1,0:T(8,128)(2,1)S(1)}, u32[]{:S(2)}, u32[]{:S(2)}) collective-permute-start(bf16[48,128]{1,0:T(8,128)(2,1)S(1)} %get-tuple-element.96), channel_id=1, source_target_pairs={{0,4},{1,5},{2,6},{3,7},{4,0},{5,1},{6,2},{7,3},{8,12},{9,13},{10,... | collective-permute-start | bytes 36872 | tf_op jit(solution)/shard_map/ppermute | solution.py:65
  62.6 5.8 %collective-permute-start.14 = (bf16[48,128]{1,0:T(8,128)(2,1)S(1)}, bf16[48,128]{1,0:T(8,128)(2,1)S(1)}, u32[]{:S(2)}, u32[]{:S(2)}) collective-permute-start(bf16[48,128]{1,0:T(8,128)(2,1)S(1)} %get-tuple-element.97), channel_id=1, source_target_pairs={{0,15},{1,2},{2,1},{3,4},{4,3},{5,6},{6,5},{7,8},{8,7},{9,10},{10,... | collective-permute-start | bytes 36872 | tf_op jit(solution)/shard_map/ppermute | solution.py:65
  64.6 3.8 %collective-permute-start.15 = (bf16[48,128]{1,0:T(8,128)(2,1)S(1)}, bf16[48,128]{1,0:T(8,128)(2,1)S(1)}, u32[]{:S(2)}, u32[]{:S(2)}) collective-permute-start(bf16[48,128]{1,0:T(8,128)(2,1)S(1)} %get-tuple-element.98), channel_id=1, source_target_pairs={{0,1},{1,0},{2,3},{3,2},{4,5},{5,4},{6,7},{7,6},{8,9},{9,8},{10,11... | collective-permute-start | bytes 36872 | tf_op jit(solution)/shard_map/ppermute | solution.py:65

commit v3 on v2

--- a/solution.py
+++ b/solution.py
@@ -29,41 +29,53 @@
     ]
 
 
-def links(table, cols):
+def write_links(table, cols, found):
     count = lax.axis_size("tile")
     me = lax.axis_index("tile")
-    found = []
-    for other in partners(me, count, cols):
+    for k, other in enumerate(partners(me, count, cols)):
         side, back = jnp.int32(0), jnp.int32(0)
         for s in range(1, 4):
-            side = jnp.where(table[me, s] == other, s, side)
-            back = jnp.where(table[other, s] == me, s, back)
-        found.append((side, (side >= 2) == (back >= 2)))
-    return found
-
-
-def send_strips(table, cols, strips, outs):
-    size = strips.shape[1]
+            side = jnp.where(table[s, me] == other, s, side)
+            back = jnp.where(table[s, other] == me, s, back)
+        turn = jnp.where((side >= 2) == (back >= 2), 1, 0)
+        found[k] = jnp.full(found.shape[1:], side, jnp.int32)
+        found[4 + k] = jnp.full(found.shape[1:], turn, jnp.int32)
+
+
+def send_strips(found, strips, outs):
+    _, size, c = strips.shape
     at_row = lax.broadcasted_iota(jnp.int32, (size, size), 0)
     at_col = lax.broadcasted_iota(jnp.int32, (size, size), 1)
-    for (side, turn), out in zip(links(table, cols), outs):
+    for k, out in enumerate(outs):
+        turn = found[4 + k][0:1, 0:size] == 1
         order = (at_col == jnp.where(turn, size - 1 - at_row, at_row)).astype(f32).astype(bf16)
-        out[...] = jnp.dot(order, strips[side].astype(bf16), preferred_element_type=f32).astype(
-            bf16
-        )
-
-
-def take_strips(table, cols, received, strips):
-    for (side, _), block in zip(links(table, cols), received):
-        strips[side] = block[...].astype(f32)
+        side = found[k][None]
+        chosen = jnp.zeros((size // 8, 8, c), f32)
+        for s in range(4):
+            chosen = jnp.where(side == s, strips[s].reshape(chosen.shape), chosen)
+        chosen = chosen.reshape(size, c).astype(bf16)
+        out[...] = jnp.dot(order, chosen, preferred_element_type=f32).astype(bf16)
+
+
+def take_strips(found, received, strips):
+    _, size, c = strips.shape
+    blocks = [block[...].astype(f32).reshape(size // 8, 8, c) for block in received]
+    for s in range(4):
+        taken = blocks[0]
+        for k in range(1, 4):
+            taken = jnp.where(found[k][None] == s, blocks[k], taken)
+        strips[s] = taken.reshape(size, c)
+
+
+def routes(cols):
+    count = lax.axis_size("tile")
+    return list(zip(*[partners(p, count, cols) for p in range(count)]))
 
 
 def swap_all(blocks, cols):
-    count = lax.axis_size("tile")
-    ways = [partners(p, count, cols) for p in range(count)]
     return [
-        lax.ppermute(block, "tile", [(p, ways[p][k]) for p in range(count)])
-        for k, block in enumerate(blocks)
+        lax.ppermute(block, "tile", list(enumerate(way)))
+        for block, way in zip(blocks, routes(cols))
     ]
 
 
@@ -257,14 +269,35 @@
     return [value.astype(bf16).astype(f32) for value in values]
 
 
-def first_strips(cols, table, block, *refs):
-    outs, strips = refs[:4], refs[4]
+def first_strips(cols, table, block, weight, *refs):
+    outs, found, held, held_weight = refs[:4], *refs[4:7]
+    strips, columns, rows, near, arrived = refs[7:12]
     size = block.shape[0]
-    strips[0] = block[0].astype(f32)
-    strips[2] = block[size - 1].astype(f32)
-    strips[3] = block[:, 0:16, :].astype(f32)[:, 0, :]
-    strips[1] = block[:, size - 16 :, :].astype(f32)[:, 15, :]
-    send_strips(table, cols, strips, outs)
+    pairs = [
+        (table, near),
+        (block.at[0], rows.at[0]),
+        (block.at[size - 1], rows.at[1]),
+        (block.at[:, pl.ds(0, 16), :], columns.at[0]),
+        (block.at[:, pl.ds(size - 16, 16), :], columns.at[1]),
+        (block, held),
+        (weight, held_weight),
+    ]
+    copies = [
+        pltpu.make_async_copy(source, target, arrived.at[k])
+        for k, (source, target) in enumerate(pairs)
+    ]
+    for copy in copies:
+        copy.start()
+    for copy in copies[:5]:
+        copy.wait()
+    write_links(near, cols, found)
+    strips[0] = rows[0].astype(f32)
+    strips[2] = rows[1].astype(f32)
+    strips[3] = columns[0].astype(f32)[:, 0, :]
+    strips[1] = columns[1].astype(f32)[:, 15, :]
+    send_strips(found, strips, outs)
+    for copy in copies[5:]:
+        copy.wait()
 
 
 def first_bulk(block, weight, shifted, pre, hidden, slope, pairs, lower, upper):
@@ -281,11 +314,11 @@
         slope[i] = rate.astype(bf16)
 
 
-def first_edges(cols, table, *refs):
+def first_edges(found, *refs):
     received, weight, blocks = refs[:4], refs[4], refs[5:9]
     outs, hidden, slope, halo = refs[9:13], refs[13:17], refs[17:21], refs[21]
     rooms, strips, long = refs[22:28], refs[28], refs[29]
-    take_strips(table, cols, received, halo)
+    take_strips(found, received, halo)
     terms = halo_terms(halo_windows(halo, long), weight)
     edges = add_strips(load_edges(*blocks), terms, rooms)
     both = [gelu_both(edge) for edge in edges]
@@ -294,7 +327,7 @@
         hidden[k][...] = values[k]
         slope[k][...] = both[k][1]
     edge_strips(values, strips)
-    send_strips(table, cols, strips, outs)
+    send_strips(found, strips, outs)
 
 
 def second_bulk(hidden, left, right, top, bottom, weight, cotangent, *refs):
@@ -313,12 +346,12 @@
             delta[i, :, part] = (cotangent[2 * i + parity].astype(f32) * rate).astype(bf16)
 
 
-def second_edges(cols, table, *refs):
+def second_edges(found, *refs):
     received, weight, blocks, wanted = refs[:4], refs[4], refs[5:9], refs[9:13]
     outs, out_field, delta, halo = refs[13:17], refs[17:21], refs[21:25], refs[25]
     rooms, strips, long, grads = refs[26:32], refs[32], refs[33], refs[34]
     half, depth = blocks[0].shape[:2]
-    take_strips(table, cols, received, halo)
+    take_strips(found, received, halo)
     terms = halo_terms(halo_windows(halo, long), weight)
     edges = add_strips(load_edges(*blocks), terms, rooms)
     cots = []
@@ -334,27 +367,15 @@
         delta[k][...] = deltas[k]
     edge_strips(deltas, strips)
     halo_grads(strips, weight, long, grads)
-    send_strips(table, cols, grads, outs)
+    send_strips(found, grads, outs)
 
 
 def second_back(*refs):
-    bulk_out, bulk_delta, out_edges, delta_edges, halo = (
-        refs[0],
-        refs[1],
-        refs[2:6],
-        refs[6:10],
-        refs[10],
-    )
-    shifted, weight, bulk_slope = refs[11:14]
-    out_field, grad_weight, grad_hidden, delta_first = refs[14:18]
-    pairs, delta, lower, upper, moved, strips, long = refs[18:25]
-    count, size, lanes = pairs.shape
-    c = lanes // 2
-    pairs[...] = bulk_out[...].astype(f32)
-    lay_edges(pairs, *out_edges)
-    for i in range(count):
-        out_field[2 * i] = pairs[i, :, 0:c].astype(bf16)
-        out_field[2 * i + 1] = pairs[i, :, c:].astype(bf16)
+    bulk_delta, delta_edges, halo = refs[0], refs[1:5], refs[5]
+    shifted, weight, bulk_slope = refs[6:9]
+    grad_weight, grad_hidden, delta_first = refs[9:12]
+    pairs, delta, lower, upper, moved, strips, long = refs[12:19]
+    count = pairs.shape[0]
     pairs[...] = bulk_delta[...].astype(f32)
     lay_edges(pairs, *delta_edges)
     delta[...] = pairs[...].astype(bf16)
@@ -367,31 +388,17 @@
         delta_first[i] = (grad_hidden[i] * bulk_slope[i].astype(f32)).astype(bf16)
 
 
-def first_back(cols, table, *refs):
-    received, weight, blocks, slope, bulk_delta = (
-        refs[:4],
-        refs[4],
-        refs[5:9],
-        refs[9:13],
-        refs[13],
-    )
-    halo, shifted, other_grad = refs[14:17]
-    outs, delta, kept, given = refs[17:21], refs[21], refs[22], refs[23]
-    rooms, strips, long, grads, back, pairs, grad_weight = (
-        refs[24:30],
-        refs[30],
-        refs[31],
-        refs[32],
-        refs[33],
-        refs[34],
-        refs[35],
-    )
-    take_strips(table, cols, received, back)
+def first_back(found, *refs):
+    received, blocks, slope, bulk_delta = refs[:4], refs[4:8], refs[8:12], refs[12]
+    halo, shifted, other_grad = refs[13:16]
+    delta, edges_out, kept, given = refs[16], refs[17:21], refs[21], refs[22]
+    rooms, strips, long, back, pairs, grad_weight = refs[23:29], *refs[29:34]
+    take_strips(found, received, back)
     edges = add_strips(load_edges(*blocks), [back[s] for s in range(4)], rooms)
     deltas = exact([edge * rate[...] for edge, rate in zip(edges, slope)])
+    for k in range(4):
+        edges_out[k][...] = deltas[k]
     edge_strips(deltas, strips)
-    halo_grads(strips, weight, long, grads)
-    send_strips(table, cols, grads, outs)
     pairs[...] = bulk_delta[...].astype(f32)
     lay_edges(pairs, *deltas)
     delta[...] = pairs[...].astype(bf16)
@@ -404,18 +411,34 @@
         given[tap] = jnp.where(core == 0, two, one).astype(bf16)
 
 
-def last_bulk(delta, weight, interior, pairs, moved, lower, upper):
+def first_returns(found, *refs):
+    edges, weight, outs = refs[:4], refs[4], refs[5:9]
+    strips, long, grads = refs[9:12]
+    edge_strips([edge[...] for edge in edges], strips)
+    halo_grads(strips, weight, long, grads)
+    send_strips(found, grads, outs)
+
+
+def last_bulk(delta, weight, bulk_out, *refs):
+    out_edges, interior, out_field, pairs, moved, lower, upper = refs[:4], *refs[4:10]
+    count, size, lanes = pairs.shape
+    c = lanes // 2
+    pairs[...] = bulk_out[...].astype(f32)
+    lay_edges(pairs, *out_edges)
+    for i in range(count):
+        out_field[2 * i] = pairs[i, :, 0:c].astype(bf16)
+        out_field[2 * i + 1] = pairs[i, :, c:].astype(bf16)
     pairs[...] = delta[...].astype(f32)
     fill_columns(moved, pairs)
     bulk_conv(moved, weight, lower, upper, interior, True)
 
 
-def last_edges(cols, table, *refs):
+def last_edges(found, *refs):
     received, interior, grad = refs[:4], refs[4], refs[5]
     rooms, back, pairs = refs[6:12], refs[12], refs[13]
     count, size, lanes = interior.shape
     c = lanes // 2
-    take_strips(table, cols, received, back)
+    take_strips(found, received, back)
     edges = (
         interior[:, 0:8, :],
         interior[:, size - 8 :, :],
@@ -444,40 +467,64 @@
     return lax.dynamic_index_in_dim(parts, index, 0, keepdims=False)
 
 
-def all_sum(kept, given):
+def summed_part(kept, given, riders, ways, beside):
     tile = lax.axis_index("tile")
     rows, lanes = kept.shape
-    part = kept + flip_swap(given, 0, 1).astype(f32)
+    carried = [None] * len(riders)
+
+    def swap(block, mask):
+        way = tuple(t ^ mask for t in range(lax.axis_size("tile")))
+        if way not in ways or carried[ways.index(way)] is not None:
+            return flip_swap(block, 0, mask)
+        k = ways.index(way)
+        both = flip_swap(jnp.concatenate([block, riders[k]]), 0, mask)
+        carried[k] = both[block.shape[0] :]
+        return both[: block.shape[0]]
+
+    given, riders = lax.optimization_barrier((flip_swap(given, 0, 1), riders))
+    part = kept + given.astype(f32)
     seat = lax.axis_index("ens") * 2 + (tile >> 1 & 1)
     quarters = part.reshape(4, rows // 4, lanes)
     sent = quarters.astype(bf16)
     part = pick(quarters, seat)
     for k in (1, 2, 3):
         part = part + flip_swap(pick(sent, seat ^ k), k >> 1, (k & 1) << 1).astype(f32)
+    part, beside = lax.optimization_barrier((part, beside))
     bit = 4
     while bit < lax.axis_size("tile"):
         own = part.astype(bf16)
         part = lax.reduce_precision(part, 8, 7)
         if bit * 2 < lax.axis_size("tile"):
-            one, two, three = (flip_swap(own, 0, bit * k).astype(f32) for k in (1, 2, 3))
+            one, two, three = (swap(own, bit * k).astype(f32) for k in (1, 2, 3))
             part = (part + one) + (two + three)
             bit *= 4
         else:
-            part = part + flip_swap(own, 0, bit).astype(f32)
+            part = part + swap(own, bit).astype(f32)
             bit *= 2
-    part = part.astype(bf16)
+    for k, way in enumerate(ways):
+        if carried[k] is None:
+            carried[k] = lax.ppermute(riders[k], "tile", list(enumerate(way)))
+    return part.astype(bf16), carried, beside
+
+
+def gather_quarters(part):
+    seat = lax.axis_index("ens") * 2 + (lax.axis_index("tile") >> 1 & 1)
     whole = jnp.zeros((4,) + part.shape, part.dtype)
     whole = lax.dynamic_update_index_in_dim(whole, part, seat, 0)
     for k in (1, 2, 3):
         got = flip_swap(part, k >> 1, (k & 1) << 1)
         whole = lax.dynamic_update_index_in_dim(whole, got, seat ^ k, 0)
-    half = whole.reshape(rows, lanes)
-    other = flip_swap(half, 0, 1)
-    first = (tile & 1) == 0
-    return jnp.where(first, half, other), jnp.where(first, other, half)
-
-
-def call(kernel, name, ins, outs, scratch, cost=0):
+    return whole.reshape(-1, part.shape[-1])
+
+
+def both_grads(half, other, first, second):
+    core = lax.axis_index("tile") & 1
+    one, two = half[...].astype(f32), other[...].astype(f32)
+    first[...] = jnp.where(core == 0, one, two)
+    second[...] = jnp.where(core == 0, two, one)
+
+
+def call(kernel, name, ins, outs, scratch, cost=0, room=16 << 20):
     whole = pl.BlockSpec(memory_space=pltpu.VMEM)
     return pl.pallas_call(
         kernel,
@@ -487,7 +534,7 @@
         out_specs=[whole] * len(outs),
         out_shape=outs,
         scratch_shapes=scratch,
-        compiler_params=pltpu.CompilerParams(vmem_limit_bytes=40 << 20),
+        compiler_params=pltpu.CompilerParams(vmem_limit_bytes=room),
         cost_estimate=pl.CostEstimate(flops=cost, bytes_accessed=2 << 20, transcendentals=0),
     )(*[array for array, _ in ins])
 
@@ -503,7 +550,6 @@
     flops = 2 * size * size * 9 * c * c
 
     S = jax.ShapeDtypeStruct
-    table = (neighbours, pl.BlockSpec(memory_space=pltpu.SMEM))
     sent = [S((size, c), bf16)] * 4
     halo = S((4, size, c), f32)
     edge = [S((half, 8, 2 * c), f32)] * 2 + [S((size, c), f32)] * 2
@@ -534,13 +580,17 @@
             (array, pl.BlockSpec((1, size, c), lambda step: (size - 1, 0, 0))),
         ]
 
-    strips = call(
+    far = pl.BlockSpec(memory_space=pl.ANY)
+    stay = lambda array: (pltpu.with_memory_space_constraint(array, pltpu.HBM), far)
+    *strips, found, block, one = call(
         functools.partial(first_strips, cols),
         "first_strips",
-        [table, (block, None)],
-        sent,
-        [V(halo)],
-    )
+        [stay(neighbours.T), stay(block), stay(one)],
+        sent + [S((8, 8, 128), jnp.int32), S(block.shape, bf16), S(one.shape, bf16)],
+        [V(halo), pltpu.VMEM((2, size, 16, c), bf16), pltpu.VMEM((2, size, c), bf16)]
+        + [pltpu.SMEM(neighbours.shape[::-1], jnp.int32), pltpu.SemaphoreType.DMA((7,))],
+    )
+    links = (found, None)
     strips = swap_all(strips, cols)
     shifted_one, pre_one, hidden, slope = call(
         first_bulk,
@@ -551,9 +601,9 @@
         flops,
     )
     found = call(
-        functools.partial(first_edges, cols),
+        first_edges,
         "first_edges",
-        [table] + whole(strips) + [(one, None)] + edge_blocks(pre_one),
+        [links] + whole(strips) + [(one, None)] + edge_blocks(pre_one),
         sent + edge + edge + [halo],
         rooms + [V(halo), long],
     )
@@ -568,56 +618,72 @@
         flops,
     )
     found = call(
-        functools.partial(second_edges, cols),
+        second_edges,
         "second_edges",
-        [table] + whole(strips) + [(two, None)] + edge_blocks(pre_two) + image_edges(wanted),
+        [links] + whole(strips) + [(two, None)] + edge_blocks(pre_two) + image_edges(wanted),
         sent + edge + edge + [halo],
         rooms + [V(halo), long, V(halo)],
     )
     strips, out_edges, delta_edges, halo_two = found[:4], found[4:8], found[8:12], found[12]
     strips = swap_all(strips, cols)
-    out_field, grad_two, grad_hidden, delta_one = call(
+    grad_two, grad_hidden, delta_one = call(
         second_back,
         "second_back",
         whole(
-            [out_bulk, delta_bulk, *out_edges, *delta_edges, halo_two, shifted_two, two, slope]
+            [delta_bulk, *delta_edges, halo_two, shifted_two, two, slope]
         ),
-        [S(block.shape, bf16), S((9, c, c), f32), pairs(f32), pairs(bf16)],
+        [S((9, c, c), f32), pairs(f32), pairs(bf16)],
         [V(pairs(f32)), V(pairs(bf16))] + back + [V(shifted), V(halo), long],
         2 * flops,
     )
     found = call(
-        functools.partial(first_back, cols),
+        first_back,
         "first_back",
-        [table]
+        [links]
         + whole(strips)
-        + [(one, None)]
         + edge_blocks(grad_hidden)
         + whole([*slope_edges, delta_one, halo_one, shifted_one, grad_two]),
-        sent + [pairs(bf16), S((9, c, c), f32), S((9, c, c), bf16)],
-        rooms
-        + [V(halo), long, V(halo), V(halo), V(pairs(f32)), pltpu.VMEM((9, c, c), f32)],
+        [pairs(bf16)] + edge + [S((9, c, c), f32), S((9, c, c), bf16)],
+        rooms + [V(halo), long, V(halo), V(pairs(f32)), pltpu.VMEM((9, c, c), f32)],
         flops,
     )
-    strips, delta_one, kept, given = found[:4], *found[4:7]
-    strips = swap_all(strips, cols)
-    (interior,) = call(
+    delta_one, delta_edges, kept, given = found[0], found[1:5], *found[5:]
+    strips = call(
+        first_returns,
+        "first_returns",
+        [links] + whole([*delta_edges, one]),
+        sent,
+        [V(halo), long, V(halo)],
+    )
+    interior, out_field = call(
         last_bulk,
         "last_bulk",
-        whole([delta_one, one]),
-        [pairs(f32)],
+        whole([delta_one, one, out_bulk, *out_edges]),
+        [pairs(f32), S(block.shape, bf16)],
         [V(pairs(f32)), V(shifted)] + back,
         flops,
     )
+    part, strips, interior = summed_part(
+        kept.reshape(9 * c, c), given.reshape(9 * c, c), strips, routes(cols), interior
+    )
+    part, strips = lax.optimization_barrier((part, strips))
     (grad_block,) = call(
-        functools.partial(last_edges, cols),
+        last_edges,
         "last_edges",
-        [table] + whole([*strips, interior]),
+        [links] + whole([*strips, interior]),
         [S(block.shape, bf16)],
         rooms + [V(halo), V(pairs(f32))],
     )
-    grads = all_sum(kept.reshape(9 * c, c), given.reshape(9 * c, c))
-    grad_first, grad_second = (grad.astype(f32).reshape(shape) for grad in grads)
+    half_grads = gather_quarters(part)
+    half_grads, grad_block = lax.optimization_barrier((half_grads, grad_block))
+    grads = call(
+        both_grads,
+        "both_grads",
+        whole([half_grads, flip_swap(half_grads, 0, 1)]),
+        [S((9 * c, c), f32)] * 2,
+        [],
+    )
+    grad_first, grad_second = (grad.reshape(shape) for grad in grads)
     return (out_field[None, None], grad_block[None, None], grad_first, grad_second)
 
 

time: 72.1 us -> 62.9 us (0.87)
  starting transfers between devices: 28.7 us -> 24.1 us
  local copies, waits for them, and re-layouts: 2.9 us -> 0.95 us
  waiting for transfers between devices: 21.7 us -> 20 us
  Pallas kernels: 15.7 us -> 14.7 us
    ppermute x16 -> x14, starting transfers between devices: 17 us -> 13.3 us  [the longest x12 12.6 us: swap_all(): lax.ppermute(block, 'tile', list(enumerate(way)))]
    unnamed x11 -> x6, local copies, waits for them, and re-layouts: 2.79 us -> 0.82 us
    add x1 -> x2, other arithmetic: 0.05 us -> 2 us  [the longest x1 1.06 us: summed_part(): part = kept + given.astype(f32)]
    reshape x2 -> x0, other arithmetic: 1.72 us -> none  [local(): grad.astype(f32).reshape(shape)]
    ppermute x16 -> x14, waiting for transfers between devices: 7.56 us -> 6.39 us  [the longest x12 6.39 us: swap_all(): lax.ppermute(block, 'tile', list(enumerate(way)))]
    pallas_call x9 -> x11, Pallas kernels: 15.7 us -> 14.7 us  [call(): pl.pallas_call(kernel, name=name, grid=(1,), in_specs=[spec or whole for...]
    ppermute x11, starting transfers between devices: 11.7 us -> 10.8 us  [flip_swap(): return lax.ppermute(block, ('ens', 'tile'), route)]
  transfers between devices with their start and end apart: 27 -> 25, of which waited for: 15 -> 14; matrix products, arithmetic and copies ran while one was open for 0% -> 0% of each run, Pallas kernels for 13% -> 15%
where the time goes in v3:
time: 62.9 us; the launch traced here: 62.7 us
  starting transfers between devices  24.1 us (38%)
  waiting for transfers between devices  20 us (32%)
  Pallas kernels  14.7 us (23%)
  other arithmetic  2.12 us (3%)
  local copies, waits for them, and re-layouts  0.95 us (2%)
  between operations  0.86 us (1%)
    pallas_call x11, Pallas kernels, call(): pl.pallas_call(kernel, name=name, grid=(1,), in_specs=[spec or whole for...  14.7 us
    ppermute x11, waiting for transfers between devices, flip_swap(): return lax.ppermute(block, ('ens', 'tile'), route)  13.6 us
    ppermute x12, starting transfers between devices, swap_all(): lax.ppermute(block, 'tile', list(enumerate(way)))  12.6 us
    ppermute x11, starting transfers between devices, flip_swap(): return lax.ppermute(block, ('ens', 'tile'), route)  10.8 us
    ppermute x12, waiting for transfers between devices, swap_all(): lax.ppermute(block, 'tile', list(enumerate(way)))  6.39 us
  transfers between devices with their start and end apart: 25, of which 14 were waited for; matrix products, arithmetic and copies ran while one was open for 0% of the time, Pallas kernels for 15%

profile of v3, /device:TPU:0, one launch (start us, length us, event | category | flops | bytes accessed | tf_op | source)
XLA Modules:
  0.0 62.7 jit_solution(5508522238257169198)
XLA Ops:
  0.6 1.4 %first_strips.1 = (bf16[48,128]{1,0:T(8,128)(2,1)S(1)}, bf16[48,128]{1,0:T(8,128)(2,1)S(1)}, bf16[48,128]{1,0:T(8,128)(2,1)S(1)}, bf16[48,128]{1,0:T(8,128)(2,1)...) custom-call(s32[4,16]{1,0:T(4,128)} %bitcast.50, ...), custom_call_target="tpu_custom_call" | custom-call | bytes 2097152 | tf_op jit(solution)/shard_map/first_strips/pallas_call | solution.py:529
  2.1 5.1 %collective-permute-start = (bf16[48,128]{1,0:T(8,128)(2,1)S(1)}, bf16[48,128]{1,0:T(8,128)(2,1)S(1)}, u32[]{:S(2)}, u32[]{:S(2)}) collective-permute-start(bf16[48,128]{1,0:T(8,128)(2,1)S(1)} %get-tuple-element.78), channel_id=1, source_target_pairs={{0,12},{1,13},{2,14},{3,15},{4,8},{5,9},{6,10},{7,11},{8,4},{9,5},... | collective-permute-start | bytes 36872 | tf_op jit(solution)/shard_map/ppermute | solution.py:77
  7.2 0.7 %collective-permute-start.2 = (bf16[48,128]{1,0:T(8,128)(2,1)S(1)}, bf16[48,128]{1,0:T(8,128)(2,1)S(1)}, u32[]{:S(2)}, u32[]{:S(2)}) collective-permute-start(bf16[48,128]{1,0:T(8,128)(2,1)S(1)} %get-tuple-element.80), channel_id=1, source_target_pairs={{0,15},{1,2},{2,1},{3,4},{4,3},{5,6},{6,5},{7,8},{8,7},{9,10},{10,... | collective-permute-start | bytes 36872 | tf_op jit(solution)/shard_map/ppermute | solution.py:77
  7.9 0.9 %collective-permute-start.3 = (bf16[48,128]{1,0:T(8,128)(2,1)S(1)}, bf16[48,128]{1,0:T(8,128)(2,1)S(1)}, u32[]{:S(2)}, u32[]{:S(2)}) collective-permute-start(bf16[48,128]{1,0:T(8,128)(2,1)S(1)} %get-tuple-element.81), channel_id=1, source_target_pairs={{0,1},{1,0},{2,3},{3,2},{4,5},{5,4},{6,7},{7,6},{8,9},{9,8},{10,11... | collective-permute-start | bytes 36872 | tf_op jit(solution)/shard_map/ppermute | solution.py:77
  8.8 1.7 %first_bulk.1 = (bf16[1200,768]{1,0:T(8,128)(2,1)S(1)}, f32[24,48,256]{2,1,0:T(8,128)S(1)}, bf16[24,48,256]{2,1,0:T(8,128)(2,1)S(1)}, bf16[24,48,256]{2,1,0:T(8,128)(2,1)S(1)}) custom-call(bf16[48,48,128]{2,1,0:T(8,128)(2,1)S(1)} %get-tuple-element.83.block, bf16[9,128,128]{2,1,0:T(8,128)(2,1)S(1)} %get-tuple-element.82.weight.refs_4_), custom_call_target="tpu_custom_call" | custom-call | flops 679477248 | bytes 2097152 | tf_op jit(solution)/shard_map/first_bulk/pallas_call | solution.py:529
  10.5 0.4 collective-permute-done.1.refs_1_
  10.9 2.1 %collective-permute-done.2.refs_2_ = bf16[48,128]{1,0:T(8,128)(2,1)S(1)} collective-permute-done((bf16[48,128]{1,0:T(8,128)(2,1)S(1)}, bf16[48,128]{1,0:T(8,128)(2,1)S(1)}, u32[]{:S(2)}, u32[]{:S(2)}) %collective-permute-start.2) | collective-permute-done | bytes 12320 | tf_op jit(solution)/shard_map/ppermute | solution.py:77
  13.0 0.6 first_edges.1
  13.6 0.1 collective-permute-start.4
  13.7 0.3 collective-permute-start.5
  14.0 2.1 %collective-permute-start.6 = (bf16[48,128]{1,0:T(8,128)(2,1)S(1)}, bf16[48,128]{1,0:T(8,128)(2,1)S(1)}, u32[]{:S(2)}, u32[]{:S(2)}) collective-permute-start(bf16[48,128]{1,0:T(8,128)(2,1)S(1)} %get-tuple-element.87), channel_id=1, source_target_pairs={{0,15},{1,2},{2,1},{3,4},{4,3},{5,6},{6,5},{7,8},{8,7},{9,10},{10,... | collective-permute-start | bytes 36872 | tf_op jit(solution)/shard_map/ppermute | solution.py:77
  16.1 1.7 %second_bulk.1 = (bf16[1200,768]{1,0:T(8,128)(2,1)S(1)}, f32[24,48,256]{2,1,0:T(8,128)S(1)}, bf16[24,48,256]{2,1,0:T(8,128)(2,1)S(1)}, bf16[24,48,256]{2,1,0:T(8,128)(2,1)S(1)}) custom-call(bf16[24,48,256]{2,1,0:T(8,128)(2,1)S(1)} %get-tuple-element.89.hidden, f32[24,8,256]{2,1,0:T(8,128)S(1)} %get-tuple-element.90.left, ...), custom_call_target="tpu_custom_call" | custom-call | flops 679477248 | bytes 2097152 | tf_op jit(solution)/shard_map/second_bulk/pallas_call | solution.py:529
  17.9 1.3 %collective-permute-done.4.refs_0_ = bf16[48,128]{1,0:T(8,128)(2,1)S(1)} collective-permute-done((bf16[48,128]{1,0:T(8,128)(2,1)S(1)}, bf16[48,128]{1,0:T(8,128)(2,1)S(1)}, u32[]{:S(2)}, u32[]{:S(2)}) %collective-permute-start.4) | collective-permute-done | bytes 12320 | tf_op jit(solution)/shard_map/ppermute | solution.py:77
  19.2 0.6 collective-permute-done.6.refs_2_
  19.8 0.9 %second_edges.1 = (bf16[48,128]{1,0:T(8,128)(2,1)S(1)}, bf16[48,128]{1,0:T(8,128)(2,1)S(1)}, bf16[48,128]{1,0:T(8,128)(2,1)S(1)}, bf16[48,128]{1,0:T(8,128)(2,1)...) custom-call(s32[8,8,128]{2,1,0:T(8,128)S(1)} %get-tuple-element.77.f, ...), custom_call_target="tpu_custom_call" | custom-call | bytes 2097152 | tf_op jit(solution)/shard_map/second_edges/pallas_call | solution.py:529
  20.7 2.2 %collective-permute-start.10 = (bf16[48,128]{1,0:T(8,128)(2,1)S(1)}, bf16[48,128]{1,0:T(8,128)(2,1)S(1)}, u32[]{:S(2)}, u32[]{:S(2)}) collective-permute-start(bf16[48,128]{1,0:T(8,128)(2,1)S(1)} %get-tuple-element.97), channel_id=1, source_target_pairs={{0,15},{1,2},{2,1},{3,4},{4,3},{5,6},{6,5},{7,8},{8,7},{9,10},{10,... | collective-permute-start | bytes 36872 | tf_op jit(solution)/shard_map/ppermute | solution.py:77
  22.9 1.1 %collective-permute-start.9 = (bf16[48,128]{1,0:T(8,128)(2,1)S(1)}, bf16[48,128]{1,0:T(8,128)(2,1)S(1)}, u32[]{:S(2)}, u32[]{:S(2)}) collective-permute-start(bf16[48,128]{1,0:T(8,128)(2,1)S(1)} %get-tuple-element.96), channel_id=1, source_target_pairs={{0,4},{1,5},{2,6},{3,7},{4,0},{5,1},{6,2},{7,3},{8,12},{9,13},{10,... | collective-permute-start | bytes 36872 | tf_op jit(solution)/shard_map/ppermute | solution.py:77
  24.1 2.4 %second_back.1 = (f32[9,128,128]{2,1,0:T(8,128)S(1)}, f32[24,48,256]{2,1,0:T(8,128)S(1)}, bf16[24,48,256]{2,1,0:T(8,128)(2,1)S(1)}) custom-call(bf16[24,48,256]{2,1,0:T(8,128)(2,1)S(1)} %get-tuple-element.99.refs_0_, f32[24,8,256]{2,1,0:T(8,128)S(1)} %get-tuple-element.100.refs_1_, f32[24,8,256]{2,1,0:T(8,128)S(1)} %get-tuple-element.101.refs_2_, ...), custom_call_target="tpu_custom_call" | custom-call | flops 1358954496 | bytes 2097152 | tf_op jit(solution)/shard_map/second_back/pallas_call | solution.py:529
  26.5 0.1 collective-permute-done.10.refs_2_
  26.6 1.8 %collective-permute-done.8.refs_0_ = bf16[48,128]{1,0:T(8,128)(2,1)S(1)} collective-permute-done((bf16[48,128]{1,0:T(8,128)(2,1)S(1)}, bf16[48,128]{1,0:T(8,128)(2,1)S(1)}, u32[]{:S(2)}, u32[]{:S(2)}) %collective-permute-start.8) | collective-permute-done | bytes 12320 | tf_op jit(solution)/shard_map/ppermute | solution.py:77
  28.4 1.4 %first_back.1 = (bf16[24,48,256]{2,1,0:T(8,128)(2,1)S(1)}, f32[24,8,256]{2,1,0:T(8,128)S(1)}, f32[24,8,256]{2,1,0:T(8,128)S(1)}, f32[48,128]{1,0:T(8,128)S(1)}, ...) custom-call(s32[8,8,128]{2,1,0:T(8,128)S(1)} %get-tuple-element.77.found, ...), custom_call_target="tpu_custom_call" | custom-call | flops 679477248 | bytes 2097152 | tf_op jit(solution)/shard_map/first_back/pallas_call | solution.py:529
  29.8 0.1 collective-permute-start.12
  29.9 0.4 first_returns.1
  30.4 1.2 %collective-permute-done.12 = bf16[1152,128]{1,0:T(8,128)(2,1)} collective-permute-done((bf16[1152,128]{1,0:T(8,128)(2,1)S(1)}, bf16[1152,128]{1,0:T(8,128)(2,1)}, u32[]{:S(2)}, u32[]{:S(2)}) %collective-permute-start.12) | collective-permute-done | bytes 294944 | tf_op jit(solution)/shard_map/ppermute | solution.py:463
  31.6 1.1 %bitcast_add_fusion = f32[1152,128]{1,0:T(8,128)S(1)} fusion(f32[9,128,128]{2,1,0:T(8,128)S(1)} %get-tuple-element.123, bf16[1152,128]{1,0:T(8,128)(2,1)} %collective-permute-done.12), kind=kLoop, calls=%fused_computation | loop fusion | flops 294912 | bytes 1474560 | tf_op jit(solution)/shard_map/add | solution.py:485
  32.7 0.8 %copy-done.2 = f32[1152,128]{1,0:T(8,128)} copy-done((f32[1152,128]{1,0:T(8,128)}, f32[1152,128]{1,0:T(8,128)S(1)}, u32[]{:S(2)}) %copy-start.2) | copy-done | bytes 589848
  33.6 1.5 %collective-permute-start.13 = (bf16[288,128]{1,0:T(8,128)(2,1)S(1)}, bf16[288,128]{1,0:T(8,128)(2,1)S(1)}, u32[]{:S(2)}, u32[]{:S(2)}) collective-permute-start(bf16[288,128]{1,0:T(8,128)(2,1)S(1)} %get-tuple-element.150), channel_id=1, source_target_pairs={{0,2},{1,3},{2,0},{3,1},{4,6},{5,7},{6,4},{7,5},{8,10},{9,11},{10,... | collective-permute-start | bytes 221192 | tf_op jit(solution)/shard_map/ppermute | solution.py:463
  35.1 1.5 %collective-permute-start.14 = (bf16[288,128]{1,0:T(8,128)(2,1)S(1)}, bf16[288,128]{1,0:T(8,128)(2,1)S(1)}, u32[]{:S(2)}, u32[]{:S(2)}) collective-permute-start(bf16[288,128]{1,0:T(8,128)(2,1)S(1)} %get-tuple-element.152), channel_id=1, source_target_pairs={{0,16},{1,17},{2,18},{3,19},{4,20},{5,21},{6,22},{7,23},{8,24},{9,... | collective-permute-start | bytes 221192 | tf_op jit(solution)/shard_map/ppermute | solution.py:463
  36.6 0.5 collective-permute-start.15
  37.1 2.1 %last_bulk.1 = (f32[24,48,256]{2,1,0:T(8,128)S(1)}, bf16[48,48,128]{2,1,0:T(8,128)(2,1)}) custom-call(bf16[24,48,256]{2,1,0:T(8,128)(2,1)S(1)} %get-tuple-element.116.delta, bf16[9,128,128]{2,1,0:T(8,128)(2,1)S(1)} %get-tuple-element.82.weight.refs_4_, bf16[24,48,256]{2,1,0:T(8,128)(2,1)S(1)} %get-tuple-element.117.bulk_out, ...), custom_call_target="tpu_custom_call" | custom-call | flops 679477248 | bytes 2097152 | tf_op jit(solution)/shard_map/last_bulk/pallas_call | solution.py:529
  39.2 1.0 %collective-permute-done.14 = bf16[288,128]{1,0:T(8,128)(2,1)S(1)} collective-permute-done((bf16[288,128]{1,0:T(8,128)(2,1)S(1)}, bf16[288,128]{1,0:T(8,128)(2,1)S(1)}, u32[]{:S(2)}, u32[]{:S(2)}) %collective-permute-start.14) | collective-permute-done | bytes 73760 | tf_op jit(solution)/shard_map/ppermute | solution.py:463
  40.2 1.7 %collective-permute-done.15 = bf16[288,128]{1,0:T(8,128)(2,1)S(1)} collective-permute-done((bf16[288,128]{1,0:T(8,128)(2,1)S(1)}, bf16[288,128]{1,0:T(8,128)(2,1)S(1)}, u32[]{:S(2)}, u32[]{:S(2)}) %collective-permute-start.15) | collective-permute-done | bytes 73760 | tf_op jit(solution)/shard_map/ppermute | solution.py:463
  41.8 0.9 %fusion.1 = f32[288,128]{1,0:T(8,128)S(1)} fusion(bf16[288,128]{1,0:T(8,128)(2,1)S(1)} %collective-permute-done.15, bf16[288,128]{1,0:T(8,128)(2,1)S(1)} %collective-permute-done.14, bf16[288,128]{1,0:T(8,128)(2,1)S(1)} %collective-permute-done.13, f32[4,288,128]{2,1,0:T(8,128)} %bitcast.46, s32[]{:T(128)S(6)} %select_n.19), kind=kLoop, calls=%fused_computation.3 | loop fusion | flops 221184 | bytes 516100 | tf_op jit(solution)/shard_map/add | solution.py:491
  42.8 0.8 %collective-permute-start.16 = (bf16[336,128]{1,0:T(8,128)(2,1)S(1)}, bf16[336,128]{1,0:T(8,128)(2,1)S(1)}, u32[]{:S(2)}, u32[]{:S(2)}) collective-permute-start(bf16[336,128]{1,0:T(8,128)(2,1)S(1)} %get-tuple-element.153), channel_id=1, source_target_pairs={{0,4},{1,5},{2,6},{3,7},{4,0},{5,1},{6,2},{7,3},{8,12},{9,13},{10,... | collective-permute-start | bytes 258056 | tf_op jit(solution)/shard_map/ppermute | solution.py:463
  43.7 1.2 %collective-permute-start.18 = (bf16[336,128]{1,0:T(8,128)(2,1)S(1)}, bf16[336,128]{1,0:T(8,128)(2,1)S(1)}, u32[]{:S(2)}, u32[]{:S(2)}) collective-permute-start(bf16[336,128]{1,0:T(8,128)(2,1)S(1)} %get-tuple-element.154), channel_id=1, source_target_pairs={{0,12},{1,13},{2,14},{3,15},{4,8},{5,9},{6,10},{7,11},{8,4},{9,5},... | collective-permute-start | bytes 258056 | tf_op jit(solution)/shard_map/ppermute | solution.py:463
  44.9 1.5 %collective-permute-start.17 = (bf16[288,128]{1,0:T(8,128)(2,1)S(1)}, bf16[288,128]{1,0:T(8,128)(2,1)S(1)}, u32[]{:S(2)}, u32[]{:S(2)}) collective-permute-start(bf16[288,128]{1,0:T(8,128)(2,1)S(1)} %convert_element_type.35), channel_id=1, source_target_pairs={{0,8},{1,9},{2,10},{3,11},{4,12},{5,13},{6,14},{7,15},{8,0},{9,1},... | collective-permute-start | bytes 221192 | tf_op jit(solution)/shard_map/ppermute | solution.py:463
  46.4 0.8 %collective-permute-start.20 = (bf16[48,128]{1,0:T(8,128)(2,1)S(1)}, bf16[48,128]{1,0:T(8,128)(2,1)S(1)}, u32[]{:S(2)}, u32[]{:S(2)}) collective-permute-start(bf16[48,128]{1,0:T(8,128)(2,1)S(1)} %get-tuple-element.139), channel_id=1, source_target_pairs={{0,1},{1,0},{2,3},{3,2},{4,5},{5,4},{6,7},{7,6},{8,9},{9,8},{10,11... | collective-permute-start | bytes 36872 | tf_op jit(solution)/shard_map/ppermute | solution.py:506
  47.1 5.2 %collective-permute-done.17 = bf16[288,128]{1,0:T(8,128)(2,1)S(1)} collective-permute-done((bf16[288,128]{1,0:T(8,128)(2,1)S(1)}, bf16[288,128]{1,0:T(8,128)(2,1)S(1)}, u32[]{:S(2)}, u32[]{:S(2)}) %collective-permute-start.17) | collective-permute-done | bytes 73760 | tf_op jit(solution)/shard_map/ppermute | solution.py:463
  52.5 1.4 %collective-permute-start.21 = (bf16[288,128]{1,0:T(8,128)(2,1)S(1)}, bf16[288,128]{1,0:T(8,128)(2,1)S(1)}, u32[]{:S(2)}, u32[]{:S(2)}) collective-permute-start(bf16[288,128]{1,0:T(8,128)(2,1)S(1)} %add_convert_fusion), channel_id=1, source_target_pairs={{0,2},{1,3},{2,0},{3,1},{4,6},{5,7},{6,4},{7,5},{8,10},{9,11},{10,... | collective-permute-start | bytes 221192 | tf_op jit(solution)/shard_map/ppermute | solution.py:463
  53.9 0.8 %collective-permute-start.22 = (bf16[288,128]{1,0:T(8,128)(2,1)S(1)}, bf16[288,128]{1,0:T(8,128)(2,1)S(1)}, u32[]{:S(2)}, u32[]{:S(2)}) collective-permute-start(bf16[288,128]{1,0:T(8,128)(2,1)S(1)} %add_convert_fusion), channel_id=1, source_target_pairs={{0,16},{1,17},{2,18},{3,19},{4,20},{5,21},{6,22},{7,23},{8,24},{9,... | collective-permute-start | bytes 221192 | tf_op jit(solution)/shard_map/ppermute | solution.py:463
  54.7 1.3 %collective-permute-start.23 = (bf16[288,128]{1,0:T(8,128)(2,1)S(1)}, bf16[288,128]{1,0:T(8,128)(2,1)S(1)}, u32[]{:S(2)}, u32[]{:S(2)}) collective-permute-start(bf16[288,128]{1,0:T(8,128)(2,1)S(1)} %add_convert_fusion), channel_id=1, source_target_pairs={{0,18},{1,19},{2,16},{3,17},{4,22},{5,23},{6,20},{7,21},{8,26},{9,... | collective-permute-start | bytes 221192 | tf_op jit(solution)/shard_map/ppermute | solution.py:463
  56.1 1.0 %last_edges.1 = bf16[48,48,128]{2,1,0:T(8,128)(2,1)} custom-call(s32[8,8,128]{2,1,0:T(8,128)S(1)} %get-tuple-element.77.found, bf16[48,128]{1,0:T(8,128)(2,1)S(1)} %slice.18.refs_0_, bf16[48,128]{1,0:T(8,128)(2,1)S(1)} %slice.19.refs_1_, bf16[48,128]{1,0:T(8,128)(2,1)S(1)} %collective-permute-done.19.refs_2_, ...), custom_call_target="tpu_custom_call" | custom-call | bytes 2097152 | tf_op jit(solution)/shard_map/last_edges/pallas_call | solution.py:529
  57.1 0.5 collective-permute-done.21
  57.6 0.6 collective-permute-done.22
  58.2 1.7 %collective-permute-done.23 = bf16[288,128]{1,0:T(8,128)(2,1)S(1)} collective-permute-done((bf16[288,128]{1,0:T(8,128)(2,1)S(1)}, bf16[288,128]{1,0:T(8,128)(2,1)S(1)}, u32[]{:S(2)}, u32[]{:S(2)}) %collective-permute-start.23) | collective-permute-done | bytes 73760 | tf_op jit(solution)/shard_map/ppermute | solution.py:463
  60.0 0.1 collective-permute-start.24
  60.1 1.6 %collective-permute-done.24.other = bf16[1152,128]{1,0:T(8,128)(2,1)S(1)} collective-permute-done((bf16[1152,128]{1,0:T(8,128)(2,1)S(1)}, bf16[1152,128]{1,0:T(8,128)(2,1)S(1)}, u32[]{:S(2)}, u32[]{:S(2)}) %collective-permute-start.24) | collective-permute-done | bytes 294944 | tf_op jit(solution)/shard_map/ppermute | solution.py:463
  61.6 1.1 %both_grads.1 = (f32[1152,128]{1,0:T(8,128)}, f32[1152,128]{1,0:T(8,128)}) custom-call(bf16[1152,128]{1,0:T(8,128)(2,1)S(1)} %bitcast.40, bf16[1152,128]{1,0:T(8,128)(2,1)S(1)} %collective-permute-done.24.other), custom_call_target="tpu_custom_call" | custom-call | bytes 2097152 | tf_op jit(solution)/shard_map/both_grads/pallas_call | solution.py:529
  (33 shorter events, 0.3 us)
Async XLA Ops:
  2.1 8.4 %collective-permute-start = (bf16[48,128]{1,0:T(8,128)(2,1)S(1)}, bf16[48,128]{1,0:T(8,128)(2,1)S(1)}, u32[]{:S(2)}, u32[]{:S(2)}) collective-permute-start(bf16[48,128]{1,0:T(8,128)(2,1)S(1)} %get-tuple-element.78), channel_id=1, source_target_pairs={{0,12},{1,13},{2,14},{3,15},{4,8},{5,9},{6,10},{7,11},{8,4},{9,5},... | collective-permute-start | bytes 36872 | tf_op jit(solution)/shard_map/ppermute | solution.py:77
  7.2 3.7 %collective-permute-start.1 = (bf16[48,128]{1,0:T(8,128)(2,1)S(1)}, bf16[48,128]{1,0:T(8,128)(2,1)S(1)}, u32[]{:S(2)}, u32[]{:S(2)}) collective-permute-start(bf16[48,128]{1,0:T(8,128)(2,1)S(1)} %get-tuple-element.79), channel_id=1, source_target_pairs={{0,4},{1,5},{2,6},{3,7},{4,0},{5,1},{6,2},{7,3},{8,12},{9,13},{10,... | collective-permute-start | bytes 36872 | tf_op jit(solution)/shard_map/ppermute | solution.py:77
  7.2 5.8 %collective-permute-start.2 = (bf16[48,128]{1,0:T(8,128)(2,1)S(1)}, bf16[48,128]{1,0:T(8,128)(2,1)S(1)}, u32[]{:S(2)}, u32[]{:S(2)}) collective-permute-start(bf16[48,128]{1,0:T(8,128)(2,1)S(1)} %get-tuple-element.80), channel_id=1, source_target_pairs={{0,15},{1,2},{2,1},{3,4},{4,3},{5,6},{6,5},{7,8},{8,7},{9,10},{10,... | collective-permute-start | bytes 36872 | tf_op jit(solution)/shard_map/ppermute | solution.py:77
  7.9 5.1 %collective-permute-start.3 = (bf16[48,128]{1,0:T(8,128)(2,1)S(1)}, bf16[48,128]{1,0:T(8,128)(2,1)S(1)}, u32[]{:S(2)}, u32[]{:S(2)}) collective-permute-start(bf16[48,128]{1,0:T(8,128)(2,1)S(1)} %get-tuple-element.81), channel_id=1, source_target_pairs={{0,1},{1,0},{2,3},{3,2},{4,5},{5,4},{6,7},{7,6},{8,9},{9,8},{10,11... | collective-permute-start | bytes 36872 | tf_op jit(solution)/shard_map/ppermute | solution.py:77
  13.0 3.1 %copy-start = (bf16[1,1,48,48,128]{4,3,2,1,0:T(8,128)(2,1)S(1)}, bf16[1,1,48,48,128]{4,3,2,1,0:T(8,128)(2,1)}, u32[]{:S(2)}) copy-start(bf16[1,1,48,48,128]{4,3,2,1,0:T(8,128)(2,1)} %param.9) | copy-start | bytes 1769476
  13.0 3.1 %copy-start.1 = (bf16[3,3,128,128]{3,2,1,0:T(8,128)(2,1)S(1)}, bf16[3,3,128,128]{3,2,1,0:T(8,128)(2,1)}, u32[]{:S(2)}) copy-start(bf16[3,3,128,128]{3,2,1,0:T(8,128)(2,1)} %param.7) | copy-start | bytes 884740
  13.6 5.6 %collective-permute-start.4 = (bf16[48,128]{1,0:T(8,128)(2,1)S(1)}, bf16[48,128]{1,0:T(8,128)(2,1)S(1)}, u32[]{:S(2)}, u32[]{:S(2)}) collective-permute-start(bf16[48,128]{1,0:T(8,128)(2,1)S(1)} %get-tuple-element.85), channel_id=1, source_target_pairs={{0,12},{1,13},{2,14},{3,15},{4,8},{5,9},{6,10},{7,11},{8,4},{9,5},... | collective-permute-start | bytes 36872 | tf_op jit(solution)/shard_map/ppermute | solution.py:77
  13.7 5.5 %collective-permute-start.5 = (bf16[48,128]{1,0:T(8,128)(2,1)S(1)}, bf16[48,128]{1,0:T(8,128)(2,1)S(1)}, u32[]{:S(2)}, u32[]{:S(2)}) collective-permute-start(bf16[48,128]{1,0:T(8,128)(2,1)S(1)} %get-tuple-element.86), channel_id=1, source_target_pairs={{0,4},{1,5},{2,6},{3,7},{4,0},{5,1},{6,2},{7,3},{8,12},{9,13},{10,... | collective-permute-start | bytes 36872 | tf_op jit(solution)/shard_map/ppermute | solution.py:77
  14.0 5.8 %collective-permute-start.6 = (bf16[48,128]{1,0:T(8,128)(2,1)S(1)}, bf16[48,128]{1,0:T(8,128)(2,1)S(1)}, u32[]{:S(2)}, u32[]{:S(2)}) collective-permute-start(bf16[48,128]{1,0:T(8,128)(2,1)S(1)} %get-tuple-element.87), channel_id=1, source_target_pairs={{0,15},{1,2},{2,1},{3,4},{4,3},{5,6},{6,5},{7,8},{8,7},{9,10},{10,... | collective-permute-start | bytes 36872 | tf_op jit(solution)/shard_map/ppermute | solution.py:77
  16.1 3.7 %collective-permute-start.7 = (bf16[48,128]{1,0:T(8,128)(2,1)S(1)}, bf16[48,128]{1,0:T(8,128)(2,1)S(1)}, u32[]{:S(2)}, u32[]{:S(2)}) collective-permute-start(bf16[48,128]{1,0:T(8,128)(2,1)S(1)} %get-tuple-element.88), channel_id=1, source_target_pairs={{0,1},{1,0},{2,3},{3,2},{4,5},{5,4},{6,7},{7,6},{8,9},{9,8},{10,11... | collective-permute-start | bytes 36872 | tf_op jit(solution)/shard_map/ppermute | solution.py:77
  20.7 5.9 %collective-permute-start.10 = (bf16[48,128]{1,0:T(8,128)(2,1)S(1)}, bf16[48,128]{1,0:T(8,128)(2,1)S(1)}, u32[]{:S(2)}, u32[]{:S(2)}) collective-permute-start(bf16[48,128]{1,0:T(8,128)(2,1)S(1)} %get-tuple-element.97), channel_id=1, source_target_pairs={{0,15},{1,2},{2,1},{3,4},{4,3},{5,6},{6,5},{7,8},{8,7},{9,10},{10,... | collective-permute-start | bytes 36872 | tf_op jit(solution)/shard_map/ppermute | solution.py:77
  22.9 3.7 %collective-permute-start.11 = (bf16[48,128]{1,0:T(8,128)(2,1)S(1)}, bf16[48,128]{1,0:T(8,128)(2,1)S(1)}, u32[]{:S(2)}, u32[]{:S(2)}) collective-permute-start(bf16[48,128]{1,0:T(8,128)(2,1)S(1)} %get-tuple-element.98), channel_id=1, source_target_pairs={{0,1},{1,0},{2,3},{3,2},{4,5},{5,4},{6,7},{7,6},{8,9},{9,8},{10,11... | collective-permute-start | bytes 36872 | tf_op jit(solution)/shard_map/ppermute | solution.py:77
  22.9 5.5 %collective-permute-start.8 = (bf16[48,128]{1,0:T(8,128)(2,1)S(1)}, bf16[48,128]{1,0:T(8,128)(2,1)S(1)}, u32[]{:S(2)}, u32[]{:S(2)}) collective-permute-start(bf16[48,128]{1,0:T(8,128)(2,1)S(1)} %get-tuple-element.95), channel_id=1, source_target_pairs={{0,12},{1,13},{2,14},{3,15},{4,8},{5,9},{6,10},{7,11},{8,4},{9,5},... | collective-permute-start | bytes 36872 | tf_op jit(solution)/shard_map/ppermute | solution.py:77
  22.9 5.5 %collective-permute-start.9 = (bf16[48,128]{1,0:T(8,128)(2,1)S(1)}, bf16[48,128]{1,0:T(8,128)(2,1)S(1)}, u32[]{:S(2)}, u32[]{:S(2)}) collective-permute-start(bf16[48,128]{1,0:T(8,128)(2,1)S(1)} %get-tuple-element.96), channel_id=1, source_target_pairs={{0,4},{1,5},{2,6},{3,7},{4,0},{5,1},{6,2},{7,3},{8,12},{9,13},{10,... | collective-permute-start | bytes 36872 | tf_op jit(solution)/shard_map/ppermute | solution.py:77
  29.8 1.8 %collective-permute-start.12 = (bf16[1152,128]{1,0:T(8,128)(2,1)S(1)}, bf16[1152,128]{1,0:T(8,128)(2,1)}, u32[]{:S(2)}, u32[]{:S(2)}) collective-permute-start(bf16[1152,128]{1,0:T(8,128)(2,1)S(1)} %bitcast.44), channel_id=1, source_target_pairs={{0,1},{1,0},{2,3},{3,2},{4,5},{5,4},{6,7},{7,6},{8,9},{9,8},{10,11... | collective-permute-start | bytes 884744 | tf_op jit(solution)/shard_map/ppermute | solution.py:463
  32.7 0.8 %copy-start.2 = (f32[1152,128]{1,0:T(8,128)}, f32[1152,128]{1,0:T(8,128)S(1)}, u32[]{:S(2)}) copy-start(f32[1152,128]{1,0:T(8,128)S(1)} %bitcast_add_fusion) | copy-start | bytes 1769476
  33.6 5.6 %collective-permute-start.13 = (bf16[288,128]{1,0:T(8,128)(2,1)S(1)}, bf16[288,128]{1,0:T(8,128)(2,1)S(1)}, u32[]{:S(2)}, u32[]{:S(2)}) collective-permute-start(bf16[288,128]{1,0:T(8,128)(2,1)S(1)} %get-tuple-element.150), channel_id=1, source_target_pairs={{0,2},{1,3},{2,0},{3,1},{4,6},{5,7},{6,4},{7,5},{8,10},{9,11},{10,... | collective-permute-start | bytes 221192 | tf_op jit(solution)/shard_map/ppermute | solution.py:463
  35.1 5.1 %collective-permute-start.14 = (bf16[288,128]{1,0:T(8,128)(2,1)S(1)}, bf16[288,128]{1,0:T(8,128)(2,1)S(1)}, u32[]{:S(2)}, u32[]{:S(2)}) collective-permute-start(bf16[288,128]{1,0:T(8,128)(2,1)S(1)} %get-tuple-element.152), channel_id=1, source_target_pairs={{0,16},{1,17},{2,18},{3,19},{4,20},{5,21},{6,22},{7,23},{8,24},{9,... | collective-permute-start | bytes 221192 | tf_op jit(solution)/shard_map/ppermute | solution.py:463
  36.6 5.3 %collective-permute-start.15 = (bf16[288,128]{1,0:T(8,128)(2,1)S(1)}, bf16[288,128]{1,0:T(8,128)(2,1)S(1)}, u32[]{:S(2)}, u32[]{:S(2)}) collective-permute-start(bf16[288,128]{1,0:T(8,128)(2,1)S(1)} %get-tuple-element.151), channel_id=1, source_target_pairs={{0,18},{1,19},{2,16},{3,17},{4,22},{5,23},{6,20},{7,21},{8,26},{9,... | collective-permute-start | bytes 221192 | tf_op jit(solution)/shard_map/ppermute | solution.py:463
  42.8 9.6 %collective-permute-start.16 = (bf16[336,128]{1,0:T(8,128)(2,1)S(1)}, bf16[336,128]{1,0:T(8,128)(2,1)S(1)}, u32[]{:S(2)}, u32[]{:S(2)}) collective-permute-start(bf16[336,128]{1,0:T(8,128)(2,1)S(1)} %get-tuple-element.153), channel_id=1, source_target_pairs={{0,4},{1,5},{2,6},{3,7},{4,0},{5,1},{6,2},{7,3},{8,12},{9,13},{10,... | collective-permute-start | bytes 258056 | tf_op jit(solution)/shard_map/ppermute | solution.py:463
  43.7 8.7 %collective-permute-start.18 = (bf16[336,128]{1,0:T(8,128)(2,1)S(1)}, bf16[336,128]{1,0:T(8,128)(2,1)S(1)}, u32[]{:S(2)}, u32[]{:S(2)}) collective-permute-start(bf16[336,128]{1,0:T(8,128)(2,1)S(1)} %get-tuple-element.154), channel_id=1, source_target_pairs={{0,12},{1,13},{2,14},{3,15},{4,8},{5,9},{6,10},{7,11},{8,4},{9,5},... | collective-permute-start | bytes 258056 | tf_op jit(solution)/shard_map/ppermute | solution.py:463
  44.9 7.5 %collective-permute-start.17 = (bf16[288,128]{1,0:T(8,128)(2,1)S(1)}, bf16[288,128]{1,0:T(8,128)(2,1)S(1)}, u32[]{:S(2)}, u32[]{:S(2)}) collective-permute-start(bf16[288,128]{1,0:T(8,128)(2,1)S(1)} %convert_element_type.35), channel_id=1, source_target_pairs={{0,8},{1,9},{2,10},{3,11},{4,12},{5,13},{6,14},{7,15},{8,0},{9,1},... | collective-permute-start | bytes 221192 | tf_op jit(solution)/shard_map/ppermute | solution.py:463
  46.4 6.1 %collective-permute-start.19 = (bf16[48,128]{1,0:T(8,128)(2,1)S(1)}, bf16[48,128]{1,0:T(8,128)(2,1)S(1)}, u32[]{:S(2)}, u32[]{:S(2)}) collective-permute-start(bf16[48,128]{1,0:T(8,128)(2,1)S(1)} %get-tuple-element.138), channel_id=1, source_target_pairs={{0,15},{1,2},{2,1},{3,4},{4,3},{5,6},{6,5},{7,8},{8,7},{9,10},{10,... | collective-permute-start | bytes 36872 | tf_op jit(solution)/shard_map/ppermute | solution.py:506
  46.4 6.1 %collective-permute-start.20 = (bf16[48,128]{1,0:T(8,128)(2,1)S(1)}, bf16[48,128]{1,0:T(8,128)(2,1)S(1)}, u32[]{:S(2)}, u32[]{:S(2)}) collective-permute-start(bf16[48,128]{1,0:T(8,128)(2,1)S(1)} %get-tuple-element.139), channel_id=1, source_target_pairs={{0,1},{1,0},{2,3},{3,2},{4,5},{5,4},{6,7},{7,6},{8,9},{9,8},{10,11... | collective-permute-start | bytes 36872 | tf_op jit(solution)/shard_map/ppermute | solution.py:506
  52.5 5.1 %collective-permute-start.21 = (bf16[288,128]{1,0:T(8,128)(2,1)S(1)}, bf16[288,128]{1,0:T(8,128)(2,1)S(1)}, u32[]{:S(2)}, u32[]{:S(2)}) collective-permute-start(bf16[288,128]{1,0:T(8,128)(2,1)S(1)} %add_convert_fusion), channel_id=1, source_target_pairs={{0,2},{1,3},{2,0},{3,1},{4,6},{5,7},{6,4},{7,5},{8,10},{9,11},{10,... | collective-permute-start | bytes 221192 | tf_op jit(solution)/shard_map/ppermute | solution.py:463
  53.9 4.4 %collective-permute-start.22 = (bf16[288,128]{1,0:T(8,128)(2,1)S(1)}, bf16[288,128]{1,0:T(8,128)(2,1)S(1)}, u32[]{:S(2)}, u32[]{:S(2)}) collective-permute-start(bf16[288,128]{1,0:T(8,128)(2,1)S(1)} %add_convert_fusion), channel_id=1, source_target_pairs={{0,16},{1,17},{2,18},{3,19},{4,20},{5,21},{6,22},{7,23},{8,24},{9,... | collective-permute-start | bytes 221192 | tf_op jit(solution)/shard_map/ppermute | solution.py:463
  54.7 5.3 %collective-permute-start.23 = (bf16[288,128]{1,0:T(8,128)(2,1)S(1)}, bf16[288,128]{1,0:T(8,128)(2,1)S(1)}, u32[]{:S(2)}, u32[]{:S(2)}) collective-permute-start(bf16[288,128]{1,0:T(8,128)(2,1)S(1)} %add_convert_fusion), channel_id=1, source_target_pairs={{0,18},{1,19},{2,16},{3,17},{4,22},{5,23},{6,20},{7,21},{8,26},{9,... | collective-permute-start | bytes 221192 | tf_op jit(solution)/shard_map/ppermute | solution.py:463
  60.0 1.6 %collective-permute-start.24 = (bf16[1152,128]{1,0:T(8,128)(2,1)S(1)}, bf16[1152,128]{1,0:T(8,128)(2,1)S(1)}, u32[]{:S(2)}, u32[]{:S(2)}) collective-permute-start(bf16[1152,128]{1,0:T(8,128)(2,1)S(1)} %bitcast.39), channel_id=1, source_target_pairs={{0,1},{1,0},{2,3},{3,2},{4,5},{5,4},{6,7},{7,6},{8,9},{9,8},{10,11... | collective-permute-start | bytes 884744 | tf_op jit(solution)/shard_map/ppermute | solution.py:463

commit v4 on v3

--- a/solution.py
+++ b/solution.py
@@ -453,77 +453,6 @@
         grad[2 * i + 1] = pairs[i, :, c:].astype(bf16)
 
 
-def flip_swap(block, mask_ens, mask_tile):
-    ens, tile = lax.axis_size("ens"), lax.axis_size("tile")
-    route = [
-        (e * tile + t, (e ^ mask_ens) * tile + (t ^ mask_tile))
-        for e in range(ens)
-        for t in range(tile)
-    ]
-    return lax.ppermute(block, ("ens", "tile"), route)
-
-
-def pick(parts, index):
-    return lax.dynamic_index_in_dim(parts, index, 0, keepdims=False)
-
-
-def summed_part(kept, given, riders, ways, beside):
-    tile = lax.axis_index("tile")
-    rows, lanes = kept.shape
-    carried = [None] * len(riders)
-
-    def swap(block, mask):
-        way = tuple(t ^ mask for t in range(lax.axis_size("tile")))
-        if way not in ways or carried[ways.index(way)] is not None:
-            return flip_swap(block, 0, mask)
-        k = ways.index(way)
-        both = flip_swap(jnp.concatenate([block, riders[k]]), 0, mask)
-        carried[k] = both[block.shape[0] :]
-        return both[: block.shape[0]]
-
-    given, riders = lax.optimization_barrier((flip_swap(given, 0, 1), riders))
-    part = kept + given.astype(f32)
-    seat = lax.axis_index("ens") * 2 + (tile >> 1 & 1)
-    quarters = part.reshape(4, rows // 4, lanes)
-    sent = quarters.astype(bf16)
-    part = pick(quarters, seat)
-    for k in (1, 2, 3):
-        part = part + flip_swap(pick(sent, seat ^ k), k >> 1, (k & 1) << 1).astype(f32)
-    part, beside = lax.optimization_barrier((part, beside))
-    bit = 4
-    while bit < lax.axis_size("tile"):
-        own = part.astype(bf16)
-        part = lax.reduce_precision(part, 8, 7)
-        if bit * 2 < lax.axis_size("tile"):
-            one, two, three = (swap(own, bit * k).astype(f32) for k in (1, 2, 3))
-            part = (part + one) + (two + three)
-            bit *= 4
-        else:
-            part = part + swap(own, bit).astype(f32)
-            bit *= 2
-    for k, way in enumerate(ways):
-        if carried[k] is None:
-            carried[k] = lax.ppermute(riders[k], "tile", list(enumerate(way)))
-    return part.astype(bf16), carried, beside
-
-
-def gather_quarters(part):
-    seat = lax.axis_index("ens") * 2 + (lax.axis_index("tile") >> 1 & 1)
-    whole = jnp.zeros((4,) + part.shape, part.dtype)
-    whole = lax.dynamic_update_index_in_dim(whole, part, seat, 0)
-    for k in (1, 2, 3):
-        got = flip_swap(part, k >> 1, (k & 1) << 1)
-        whole = lax.dynamic_update_index_in_dim(whole, got, seat ^ k, 0)
-    return whole.reshape(-1, part.shape[-1])
-
-
-def both_grads(half, other, first, second):
-    core = lax.axis_index("tile") & 1
-    one, two = half[...].astype(f32), other[...].astype(f32)
-    first[...] = jnp.where(core == 0, one, two)
-    second[...] = jnp.where(core == 0, two, one)
-
-
 def call(kernel, name, ins, outs, scratch, cost=0, room=16 << 20):
     whole = pl.BlockSpec(memory_space=pltpu.VMEM)
     return pl.pallas_call(
@@ -539,6 +468,108 @@
     )(*[array for array, _ in ins])
 
 
+def flip_swap(block, mask_ens, mask_tile):
+    ens, tile = lax.axis_size("ens"), lax.axis_size("tile")
+    route = [
+        (e * tile + t, (e ^ mask_ens) * tile + (t ^ mask_tile))
+        for e in range(ens)
+        for t in range(tile)
+    ]
+    return lax.ppermute(block, ("ens", "tile"), route)
+
+
+def seat_of():
+    return lax.axis_index("ens") * 2 + (lax.axis_index("tile") >> 1 & 1)
+
+
+def share_out(kept, given, own, *sent):
+    rows = own.shape[0]
+    seat = seat_of()
+    quarter = lambda at: pl.ds(pl.multiple_of(at * rows, rows), rows)
+    add = lambda at: kept[quarter(at), :] + given[quarter(at), :].astype(f32)
+    own[...] = add(seat)
+    for k, block in enumerate(sent):
+        block[...] = add(seat ^ (k + 1)).astype(bf16)
+
+
+def add_up(count, loads, base, *refs):
+    got, riders = refs[:count], refs[count : count + loads]
+    total, loaded, came = refs[count + loads], refs[count + loads + 1 :][:loads], refs[count + 2 * loads + 1 :]
+    rows = base.shape[0]
+    terms = [base[...].astype(f32)] + [block[0:rows].astype(f32) for block in got]
+    while len(terms) > 1:
+        terms = [terms[i] + terms[i + 1] for i in range(0, len(terms), 2)]
+    total[...] = terms[0].astype(bf16)
+    for block, rider in zip(loaded, riders):
+        block[0:rows] = terms[0].astype(bf16)
+        block[rows:] = rider[...]
+    for block, place in zip([block for block in got if block.shape[0] > rows], came):
+        place[...] = block[rows:]
+
+
+def summed_part(kept, given, riders, ways, beside):
+    tiles = lax.axis_size("tile")
+    rows, lanes = kept.shape[0] // 4, kept.shape[1]
+    groups, bit = [], 4
+    while bit < tiles:
+        groups.append([bit, 2 * bit, 3 * bit] if 2 * bit < tiles else [bit])
+        bit *= 4
+    S = jax.ShapeDtypeStruct
+    given, riders = lax.optimization_barrier((flip_swap(given, 0, 1), riders))
+    base, *sent = call(
+        share_out,
+        "share_out",
+        [(kept, None), (given, None)],
+        [S((rows, lanes), f32)] + [S((rows, lanes), bf16)] * 3,
+        [],
+    )
+    got = [flip_swap(block, k >> 1, (k & 1) << 1) for k, block in zip((1, 2, 3), sent)]
+    carried, coming = {}, []
+    for n, masks in enumerate(groups + [[]]):
+        aboard = {}
+        for mask in masks:
+            way = tuple(t ^ mask for t in range(tiles))
+            if way in ways:
+                aboard[mask] = ways.index(way)
+        loads = [riders[k] for k in aboard.values()]
+        found = call(
+            functools.partial(add_up, len(got), len(loads)),
+            "add_up",
+            [(block, None) for block in (base, *got, *loads)],
+            [S((rows, lanes), bf16)]
+            + [S((rows + load.shape[0], lanes), bf16) for load in loads]
+            + [S(riders[k].shape, bf16) for k in coming],
+            [],
+        )
+        if n == 0:
+            found, beside = lax.optimization_barrier((found, beside))
+        base, loaded = found[0], dict(zip(aboard, found[1 : 1 + len(loads)]))
+        carried.update(zip(coming, found[1 + len(loads) :]))
+        got = [flip_swap(loaded.get(mask, base), 0, mask) for mask in masks]
+        coming = list(aboard.values())
+    for k, way in enumerate(ways):
+        if k not in carried:
+            carried[k] = lax.ppermute(riders[k], "tile", list(enumerate(way)))
+    return base, [carried[k] for k in range(len(ways))], beside
+
+
+def gather_quarters(part):
+    seat = seat_of()
+    whole = jnp.zeros((4,) + part.shape, part.dtype)
+    whole = lax.dynamic_update_index_in_dim(whole, part, seat, 0)
+    for k in (1, 2, 3):
+        got = flip_swap(part, k >> 1, (k & 1) << 1)
+        whole = lax.dynamic_update_index_in_dim(whole, got, seat ^ k, 0)
+    return whole.reshape(-1, part.shape[-1])
+
+
+def both_grads(half, other, first, second):
+    core = lax.axis_index("tile") & 1
+    one, two = half[...].astype(f32), other[...].astype(f32)
+    first[...] = jnp.where(core == 0, one, two)
+    second[...] = jnp.where(core == 0, two, one)
+
+
 def local(fields, weight_first, weight_second, neighbours, cotangent):
     block, wanted = fields[0, 0], cotangent[0, 0]
     size, c = block.shape[0], block.shape[-1]

time: 62.9 us -> 59.9 us (0.952)
  other arithmetic: 2.12 us -> 0 us
  local copies, waits for them, and re-layouts: 0.95 us -> 0.11 us
    add x2 -> x0, other arithmetic: 2 us -> none  [the longest x1 1.06 us: summed_part(): part = kept + given.astype(f32)]
    unnamed x6 -> x4, local copies, waits for them, and re-layouts: 0.82 us -> 0.01 us
    pallas_call x11 -> x14, Pallas kernels: 14.7 us -> 14.8 us  [call(): pl.pallas_call(kernel, name=name, grid=(1,), in_specs=[spec or whole for...]
  transfers between devices with their start and end apart: 25 -> 25, of which waited for: 14 -> 14; matrix products, arithmetic and copies ran while one was open for 0% -> 0% of each run, Pallas kernels for 15% -> 16%
where the time goes in v4:
time: 59.9 us; the launch traced here: 59.7 us
  starting transfers between devices  24.1 us (40%)
  waiting for transfers between devices  19.8 us (33%)
  Pallas kernels  14.8 us (25%)
  between operations  0.79 us (1%)
    pallas_call x14, Pallas kernels, call(): pl.pallas_call(kernel, name=name, grid=(1,), in_specs=[spec or whole for...  14.8 us
    ppermute x11, waiting for transfers between devices, flip_swap(): return lax.ppermute(block, ('ens', 'tile'), route)  13.4 us
    ppermute x12, starting transfers between devices, swap_all(): lax.ppermute(block, 'tile', list(enumerate(way)))  12.6 us
    ppermute x11, starting transfers between devices, flip_swap(): return lax.ppermute(block, ('ens', 'tile'), route)  10.8 us
    ppermute x12, waiting for transfers between devices, swap_all(): lax.ppermute(block, 'tile', list(enumerate(way)))  6.41 us
  transfers between devices with their start and end apart: 25, of which 14 were waited for; matrix products, arithmetic and copies ran while one was open for 0% of the time, Pallas kernels for 16%

profile of v4, /device:TPU:0, one launch (start us, length us, event | category | flops | bytes accessed | tf_op | source)
XLA Modules:
  0.0 59.7 jit_solution(3706045562920698287)
XLA Ops:
  0.6 1.4 %first_strips.1 = (bf16[48,128]{1,0:T(8,128)(2,1)S(1)}, bf16[48,128]{1,0:T(8,128)(2,1)S(1)}, bf16[48,128]{1,0:T(8,128)(2,1)S(1)}, bf16[48,128]{1,0:T(8,128)(2,1)...) custom-call(s32[4,16]{1,0:T(4,128)} %bitcast.35, ...), custom_call_target="tpu_custom_call" | custom-call | bytes 2097152 | tf_op jit(solution)/shard_map/first_strips/pallas_call | solution.py:458
  2.1 5.1 %collective-permute-start = (bf16[48,128]{1,0:T(8,128)(2,1)S(1)}, bf16[48,128]{1,0:T(8,128)(2,1)S(1)}, u32[]{:S(2)}, u32[]{:S(2)}) collective-permute-start(bf16[48,128]{1,0:T(8,128)(2,1)S(1)} %get-tuple-element.90), channel_id=1, source_target_pairs={{0,12},{1,13},{2,14},{3,15},{4,8},{5,9},{6,10},{7,11},{8,4},{9,5},... | collective-permute-start | bytes 36872 | tf_op jit(solution)/shard_map/ppermute | solution.py:77
  7.2 0.0 collective-permute-start.1
  7.2 0.7 %collective-permute-start.2 = (bf16[48,128]{1,0:T(8,128)(2,1)S(1)}, bf16[48,128]{1,0:T(8,128)(2,1)S(1)}, u32[]{:S(2)}, u32[]{:S(2)}) collective-permute-start(bf16[48,128]{1,0:T(8,128)(2,1)S(1)} %get-tuple-element.92), channel_id=1, source_target_pairs={{0,15},{1,2},{2,1},{3,4},{4,3},{5,6},{6,5},{7,8},{8,7},{9,10},{10,... | collective-permute-start | bytes 36872 | tf_op jit(solution)/shard_map/ppermute | solution.py:77
  7.9 0.9 %collective-permute-start.3 = (bf16[48,128]{1,0:T(8,128)(2,1)S(1)}, bf16[48,128]{1,0:T(8,128)(2,1)S(1)}, u32[]{:S(2)}, u32[]{:S(2)}) collective-permute-start(bf16[48,128]{1,0:T(8,128)(2,1)S(1)} %get-tuple-element.93), channel_id=1, source_target_pairs={{0,1},{1,0},{2,3},{3,2},{4,5},{5,4},{6,7},{7,6},{8,9},{9,8},{10,11... | collective-permute-start | bytes 36872 | tf_op jit(solution)/shard_map/ppermute | solution.py:77
  8.8 1.7 %first_bulk.1 = (bf16[1200,768]{1,0:T(8,128)(2,1)S(1)}, f32[24,48,256]{2,1,0:T(8,128)S(1)}, bf16[24,48,256]{2,1,0:T(8,128)(2,1)S(1)}, bf16[24,48,256]{2,1,0:T(8,128)(2,1)S(1)}) custom-call(bf16[48,48,128]{2,1,0:T(8,128)(2,1)S(1)} %get-tuple-element.95.block, bf16[9,128,128]{2,1,0:T(8,128)(2,1)S(1)} %get-tuple-element.94.weight.refs_4_), custom_call_target="tpu_custom_call" | custom-call | flops 679477248 | bytes 2097152 | tf_op jit(solution)/shard_map/first_bulk/pallas_call | solution.py:458
  10.5 0.4 collective-permute-done.1.refs_1_
  10.9 2.1 %collective-permute-done.2.refs_2_ = bf16[48,128]{1,0:T(8,128)(2,1)S(1)} collective-permute-done((bf16[48,128]{1,0:T(8,128)(2,1)S(1)}, bf16[48,128]{1,0:T(8,128)(2,1)S(1)}, u32[]{:S(2)}, u32[]{:S(2)}) %collective-permute-start.2) | collective-permute-done | bytes 12320 | tf_op jit(solution)/shard_map/ppermute | solution.py:77
  13.0 0.6 %first_edges.1 = (bf16[48,128]{1,0:T(8,128)(2,1)S(1)}, bf16[48,128]{1,0:T(8,128)(2,1)S(1)}, bf16[48,128]{1,0:T(8,128)(2,1)S(1)}, bf16[48,128]{1,0:T(8,128)(2,1)S...) custom-call(s32[8,8,128]{2,1,0:T(8,128)S(1)} %get-tuple-element.89.f, ...), custom_call_target="tpu_custom_call" | custom-call | bytes 2097152 | tf_op jit(solution)/shard_map/first_edges/pallas_call | solution.py:458
  13.6 0.1 collective-permute-start.4
  13.7 0.3 collective-permute-start.5
  14.0 2.1 %collective-permute-start.6 = (bf16[48,128]{1,0:T(8,128)(2,1)S(1)}, bf16[48,128]{1,0:T(8,128)(2,1)S(1)}, u32[]{:S(2)}, u32[]{:S(2)}) collective-permute-start(bf16[48,128]{1,0:T(8,128)(2,1)S(1)} %get-tuple-element.99), channel_id=1, source_target_pairs={{0,15},{1,2},{2,1},{3,4},{4,3},{5,6},{6,5},{7,8},{8,7},{9,10},{10,... | collective-permute-start | bytes 36872 | tf_op jit(solution)/shard_map/ppermute | solution.py:77
  16.1 1.7 %second_bulk.1 = (bf16[1200,768]{1,0:T(8,128)(2,1)S(1)}, f32[24,48,256]{2,1,0:T(8,128)S(1)}, bf16[24,48,256]{2,1,0:T(8,128)(2,1)S(1)}, bf16[24,48,256]{2,1,0:T(8,128)(2,1)S(1)}) custom-call(bf16[24,48,256]{2,1,0:T(8,128)(2,1)S(1)} %get-tuple-element.101.hidden, f32[24,8,256]{2,1,0:T(8,128)S(1)} %get-tuple-element.102.left, ...), custom_call_target="tpu_custom_call" | custom-call | flops 679477248 | bytes 2097152 | tf_op jit(solution)/shard_map/second_bulk/pallas_call | solution.py:458
  17.9 1.3 %collective-permute-done.4.refs_0_ = bf16[48,128]{1,0:T(8,128)(2,1)S(1)} collective-permute-done((bf16[48,128]{1,0:T(8,128)(2,1)S(1)}, bf16[48,128]{1,0:T(8,128)(2,1)S(1)}, u32[]{:S(2)}, u32[]{:S(2)}) %collective-permute-start.4) | collective-permute-done | bytes 12320 | tf_op jit(solution)/shard_map/ppermute | solution.py:77
  19.2 0.6 %collective-permute-done.6.refs_2_ = bf16[48,128]{1,0:T(8,128)(2,1)S(1)} collective-permute-done((bf16[48,128]{1,0:T(8,128)(2,1)S(1)}, bf16[48,128]{1,0:T(8,128)(2,1)S(1)}, u32[]{:S(2)}, u32[]{:S(2)}) %collective-permute-start.6) | collective-permute-done | bytes 12320 | tf_op jit(solution)/shard_map/ppermute | solution.py:77
  19.8 0.9 %second_edges.1 = (bf16[48,128]{1,0:T(8,128)(2,1)S(1)}, bf16[48,128]{1,0:T(8,128)(2,1)S(1)}, bf16[48,128]{1,0:T(8,128)(2,1)S(1)}, bf16[48,128]{1,0:T(8,128)(2,1)...) custom-call(s32[8,8,128]{2,1,0:T(8,128)S(1)} %get-tuple-element.89.f, ...), custom_call_target="tpu_custom_call" | custom-call | bytes 2097152 | tf_op jit(solution)/shard_map/second_edges/pallas_call | solution.py:458
  20.7 2.2 %collective-permute-start.10 = (bf16[48,128]{1,0:T(8,128)(2,1)S(1)}, bf16[48,128]{1,0:T(8,128)(2,1)S(1)}, u32[]{:S(2)}, u32[]{:S(2)}) collective-permute-start(bf16[48,128]{1,0:T(8,128)(2,1)S(1)} %get-tuple-element.109), channel_id=1, source_target_pairs={{0,15},{1,2},{2,1},{3,4},{4,3},{5,6},{6,5},{7,8},{8,7},{9,10},{10,... | collective-permute-start | bytes 36872 | tf_op jit(solution)/shard_map/ppermute | solution.py:77
  22.9 0.0 collective-permute-start.8
  22.9 1.1 %collective-permute-start.9 = (bf16[48,128]{1,0:T(8,128)(2,1)S(1)}, bf16[48,128]{1,0:T(8,128)(2,1)S(1)}, u32[]{:S(2)}, u32[]{:S(2)}) collective-permute-start(bf16[48,128]{1,0:T(8,128)(2,1)S(1)} %get-tuple-element.108), channel_id=1, source_target_pairs={{0,4},{1,5},{2,6},{3,7},{4,0},{5,1},{6,2},{7,3},{8,12},{9,13},{10,... | collective-permute-start | bytes 36872 | tf_op jit(solution)/shard_map/ppermute | solution.py:77
  24.1 2.4 %second_back.1 = (f32[9,128,128]{2,1,0:T(8,128)S(1)}, f32[24,48,256]{2,1,0:T(8,128)S(1)}, bf16[24,48,256]{2,1,0:T(8,128)(2,1)S(1)}) custom-call(bf16[24,48,256]{2,1,0:T(8,128)(2,1)S(1)} %get-tuple-element.111.refs_0_, f32[24,8,256]{2,1,0:T(8,128)S(1)} %get-tuple-element.112.refs_1_, f32[24,8,256]{2,1,0:T(8,128)S(1)} %get-tuple-element.113.refs_2_, ...), custom_call_target="tpu_custom_call" | custom-call | flops 1358954496 | bytes 2097152 | tf_op jit(solution)/shard_map/second_back/pallas_call | solution.py:458
  26.4 0.2 collective-permute-done.10.refs_2_
  26.6 1.8 %collective-permute-done.8.refs_0_ = bf16[48,128]{1,0:T(8,128)(2,1)S(1)} collective-permute-done((bf16[48,128]{1,0:T(8,128)(2,1)S(1)}, bf16[48,128]{1,0:T(8,128)(2,1)S(1)}, u32[]{:S(2)}, u32[]{:S(2)}) %collective-permute-start.8) | collective-permute-done | bytes 12320 | tf_op jit(solution)/shard_map/ppermute | solution.py:77
  28.4 1.4 %first_back.1 = (bf16[24,48,256]{2,1,0:T(8,128)(2,1)S(1)}, f32[24,8,256]{2,1,0:T(8,128)S(1)}, f32[24,8,256]{2,1,0:T(8,128)S(1)}, f32[48,128]{1,0:T(8,128)S(1)}, ...) custom-call(s32[8,8,128]{2,1,0:T(8,128)S(1)} %get-tuple-element.89.found, ...), custom_call_target="tpu_custom_call" | custom-call | flops 679477248 | bytes 2097152 | tf_op jit(solution)/shard_map/first_back/pallas_call | solution.py:458
  29.8 0.1 collective-permute-start.12
  29.9 0.5 first_returns.1
  30.4 1.1 %collective-permute-done.12.given = bf16[1152,128]{1,0:T(8,128)(2,1)S(1)} collective-permute-done((bf16[1152,128]{1,0:T(8,128)(2,1)S(1)}, bf16[1152,128]{1,0:T(8,128)(2,1)S(1)}, u32[]{:S(2)}, u32[]{:S(2)}) %collective-permute-start.12) | collective-permute-done | bytes 294944 | tf_op jit(solution)/shard_map/ppermute | solution.py:478
  31.5 0.1 share_out.1
  31.5 1.5 %collective-permute-start.13 = (bf16[288,128]{1,0:T(8,128)(2,1)S(1)}, bf16[288,128]{1,0:T(8,128)(2,1)S(1)}, u32[]{:S(2)}, u32[]{:S(2)}) collective-permute-start(bf16[288,128]{1,0:T(8,128)(2,1)S(1)} %get-tuple-element.147), channel_id=1, source_target_pairs={{0,2},{1,3},{2,0},{3,1},{4,6},{5,7},{6,4},{7,5},{8,10},{9,11},{10,... | collective-permute-start | bytes 221192 | tf_op jit(solution)/shard_map/ppermute | solution.py:478
  33.1 1.5 %collective-permute-start.14 = (bf16[288,128]{1,0:T(8,128)(2,1)S(1)}, bf16[288,128]{1,0:T(8,128)(2,1)S(1)}, u32[]{:S(2)}, u32[]{:S(2)}) collective-permute-start(bf16[288,128]{1,0:T(8,128)(2,1)S(1)} %get-tuple-element.148), channel_id=1, source_target_pairs={{0,16},{1,17},{2,18},{3,19},{4,20},{5,21},{6,22},{7,23},{8,24},{9,... | collective-permute-start | bytes 221192 | tf_op jit(solution)/shard_map/ppermute | solution.py:478
  34.6 0.5 collective-permute-start.15
  35.1 2.1 %last_bulk.1 = (f32[24,48,256]{2,1,0:T(8,128)S(1)}, bf16[48,48,128]{2,1,0:T(8,128)(2,1)}) custom-call(bf16[24,48,256]{2,1,0:T(8,128)(2,1)S(1)} %get-tuple-element.128.delta, bf16[9,128,128]{2,1,0:T(8,128)(2,1)S(1)} %get-tuple-element.94.weight.refs_4_, bf16[24,48,256]{2,1,0:T(8,128)(2,1)S(1)} %get-tuple-element.129.bulk_out, ...), custom_call_target="tpu_custom_call" | custom-call | flops 679477248 | bytes 2097152 | tf_op jit(solution)/shard_map/last_bulk/pallas_call | solution.py:458
  37.1 1.0 %collective-permute-done.14.refs_1_ = bf16[288,128]{1,0:T(8,128)(2,1)S(1)} collective-permute-done((bf16[288,128]{1,0:T(8,128)(2,1)S(1)}, bf16[288,128]{1,0:T(8,128)(2,1)S(1)}, u32[]{:S(2)}, u32[]{:S(2)}) %collective-permute-start.14) | collective-permute-done | bytes 73760 | tf_op jit(solution)/shard_map/ppermute | solution.py:478
  38.1 1.7 %collective-permute-done.15.refs_2_ = bf16[288,128]{1,0:T(8,128)(2,1)S(1)} collective-permute-done((bf16[288,128]{1,0:T(8,128)(2,1)S(1)}, bf16[288,128]{1,0:T(8,128)(2,1)S(1)}, u32[]{:S(2)}, u32[]{:S(2)}) %collective-permute-start.15) | collective-permute-done | bytes 73760 | tf_op jit(solution)/shard_map/ppermute | solution.py:478
  39.9 0.8 %collective-permute-start.16 = (bf16[336,128]{1,0:T(8,128)(2,1)S(1)}, bf16[336,128]{1,0:T(8,128)(2,1)S(1)}, u32[]{:S(2)}, u32[]{:S(2)}) collective-permute-start(bf16[336,128]{1,0:T(8,128)(2,1)S(1)} %get-tuple-element.157), channel_id=1, source_target_pairs={{0,4},{1,5},{2,6},{3,7},{4,0},{5,1},{6,2},{7,3},{8,12},{9,13},{10,... | collective-permute-start | bytes 258056 | tf_op jit(solution)/shard_map/ppermute | solution.py:478
  40.7 1.2 %collective-permute-start.18 = (bf16[336,128]{1,0:T(8,128)(2,1)S(1)}, bf16[336,128]{1,0:T(8,128)(2,1)S(1)}, u32[]{:S(2)}, u32[]{:S(2)}) collective-permute-start(bf16[336,128]{1,0:T(8,128)(2,1)S(1)} %get-tuple-element.158), channel_id=1, source_target_pairs={{0,12},{1,13},{2,14},{3,15},{4,8},{5,9},{6,10},{7,11},{8,4},{9,5},... | collective-permute-start | bytes 258056 | tf_op jit(solution)/shard_map/ppermute | solution.py:478
  41.9 1.5 %collective-permute-start.17 = (bf16[288,128]{1,0:T(8,128)(2,1)S(1)}, bf16[288,128]{1,0:T(8,128)(2,1)S(1)}, u32[]{:S(2)}, u32[]{:S(2)}) collective-permute-start(bf16[288,128]{1,0:T(8,128)(2,1)S(1)} %get-tuple-element.156.base), channel_id=1, source_target_pairs={{0,8},{1,9},{2,10},{3,11},{4,12},{5,13},{6,14},{7,15},{8,0},{9,1},... | collective-permute-start | bytes 221192 | tf_op jit(solution)/shard_map/ppermute | solution.py:478
  43.4 0.8 %collective-permute-start.20 = (bf16[48,128]{1,0:T(8,128)(2,1)S(1)}, bf16[48,128]{1,0:T(8,128)(2,1)S(1)}, u32[]{:S(2)}, u32[]{:S(2)}) collective-permute-start(bf16[48,128]{1,0:T(8,128)(2,1)S(1)} %get-tuple-element.163), channel_id=1, source_target_pairs={{0,1},{1,0},{2,3},{3,2},{4,5},{5,4},{6,7},{7,6},{8,9},{9,8},{10,11... | collective-permute-start | bytes 36872 | tf_op jit(solution)/shard_map/ppermute | solution.py:552
  44.2 5.2 %collective-permute-done.17.refs_1_ = bf16[288,128]{1,0:T(8,128)(2,1)S(1)} collective-permute-done((bf16[288,128]{1,0:T(8,128)(2,1)S(1)}, bf16[288,128]{1,0:T(8,128)(2,1)S(1)}, u32[]{:S(2)}, u32[]{:S(2)}) %collective-permute-start.17) | collective-permute-done | bytes 73760 | tf_op jit(solution)/shard_map/ppermute | solution.py:478
  49.5 1.4 %collective-permute-start.21 = (bf16[288,128]{1,0:T(8,128)(2,1)S(1)}, bf16[288,128]{1,0:T(8,128)(2,1)S(1)}, u32[]{:S(2)}, u32[]{:S(2)}) collective-permute-start(bf16[288,128]{1,0:T(8,128)(2,1)S(1)} %get-tuple-element.164), channel_id=1, source_target_pairs={{0,2},{1,3},{2,0},{3,1},{4,6},{5,7},{6,4},{7,5},{8,10},{9,11},{10,... | collective-permute-start | bytes 221192 | tf_op jit(solution)/shard_map/ppermute | solution.py:478
  50.9 0.8 %collective-permute-start.22 = (bf16[288,128]{1,0:T(8,128)(2,1)S(1)}, bf16[288,128]{1,0:T(8,128)(2,1)S(1)}, u32[]{:S(2)}, u32[]{:S(2)}) collective-permute-start(bf16[288,128]{1,0:T(8,128)(2,1)S(1)} %get-tuple-element.164), channel_id=1, source_target_pairs={{0,16},{1,17},{2,18},{3,19},{4,20},{5,21},{6,22},{7,23},{8,24},{9,... | collective-permute-start | bytes 221192 | tf_op jit(solution)/shard_map/ppermute | solution.py:478
  51.7 1.3 %collective-permute-start.23 = (bf16[288,128]{1,0:T(8,128)(2,1)S(1)}, bf16[288,128]{1,0:T(8,128)(2,1)S(1)}, u32[]{:S(2)}, u32[]{:S(2)}) collective-permute-start(bf16[288,128]{1,0:T(8,128)(2,1)S(1)} %get-tuple-element.164), channel_id=1, source_target_pairs={{0,18},{1,19},{2,16},{3,17},{4,22},{5,23},{6,20},{7,21},{8,26},{9,... | collective-permute-start | bytes 221192 | tf_op jit(solution)/shard_map/ppermute | solution.py:478
  53.1 1.0 %last_edges.1 = bf16[48,48,128]{2,1,0:T(8,128)(2,1)} custom-call(s32[8,8,128]{2,1,0:T(8,128)S(1)} %get-tuple-element.89.found, bf16[48,128]{1,0:T(8,128)(2,1)S(1)} %get-tuple-element.165.refs_0_, bf16[48,128]{1,0:T(8,128)(2,1)S(1)} %get-tuple-element.166.refs_1_, bf16[48,128]{1,0:T(8,128)(2,1)S(1)} %collective-permute-done.19.refs_2_, ...), custom_call_target="tpu_custom_call" | custom-call | bytes 2097152 | tf_op jit(solution)/shard_map/last_edges/pallas_call | solution.py:458
  54.0 0.5 collective-permute-done.21
  54.6 0.7 %collective-permute-done.22 = bf16[288,128]{1,0:T(8,128)(2,1)S(1)} collective-permute-done((bf16[288,128]{1,0:T(8,128)(2,1)S(1)}, bf16[288,128]{1,0:T(8,128)(2,1)S(1)}, u32[]{:S(2)}, u32[]{:S(2)}) %collective-permute-start.22) | collective-permute-done | bytes 73760 | tf_op jit(solution)/shard_map/ppermute | solution.py:478
  55.2 1.7 %collective-permute-done.23 = bf16[288,128]{1,0:T(8,128)(2,1)S(1)} collective-permute-done((bf16[288,128]{1,0:T(8,128)(2,1)S(1)}, bf16[288,128]{1,0:T(8,128)(2,1)S(1)}, u32[]{:S(2)}, u32[]{:S(2)}) %collective-permute-start.23) | collective-permute-done | bytes 73760 | tf_op jit(solution)/shard_map/ppermute | solution.py:478
  57.0 0.1 collective-permute-start.24
  57.0 1.6 %collective-permute-done.24.other = bf16[1152,128]{1,0:T(8,128)(2,1)S(1)} collective-permute-done((bf16[1152,128]{1,0:T(8,128)(2,1)S(1)}, bf16[1152,128]{1,0:T(8,128)(2,1)S(1)}, u32[]{:S(2)}, u32[]{:S(2)}) %collective-permute-start.24) | collective-permute-done | bytes 294944 | tf_op jit(solution)/shard_map/ppermute | solution.py:478
  58.6 1.1 %both_grads.1 = (f32[1152,128]{1,0:T(8,128)}, f32[1152,128]{1,0:T(8,128)}) custom-call(bf16[1152,128]{1,0:T(8,128)(2,1)S(1)} %bitcast.26, bf16[1152,128]{1,0:T(8,128)(2,1)S(1)} %collective-permute-done.24.other), custom_call_target="tpu_custom_call" | custom-call | bytes 2097152 | tf_op jit(solution)/shard_map/both_grads/pallas_call | solution.py:458
  (25 shorter events, 0.2 us)
Async XLA Ops:
  2.1 8.4 %collective-permute-start = (bf16[48,128]{1,0:T(8,128)(2,1)S(1)}, bf16[48,128]{1,0:T(8,128)(2,1)S(1)}, u32[]{:S(2)}, u32[]{:S(2)}) collective-permute-start(bf16[48,128]{1,0:T(8,128)(2,1)S(1)} %get-tuple-element.90), channel_id=1, source_target_pairs={{0,12},{1,13},{2,14},{3,15},{4,8},{5,9},{6,10},{7,11},{8,4},{9,5},... | collective-permute-start | bytes 36872 | tf_op jit(solution)/shard_map/ppermute | solution.py:77
  7.2 3.7 %collective-permute-start.1 = (bf16[48,128]{1,0:T(8,128)(2,1)S(1)}, bf16[48,128]{1,0:T(8,128)(2,1)S(1)}, u32[]{:S(2)}, u32[]{:S(2)}) collective-permute-start(bf16[48,128]{1,0:T(8,128)(2,1)S(1)} %get-tuple-element.91), channel_id=1, source_target_pairs={{0,4},{1,5},{2,6},{3,7},{4,0},{5,1},{6,2},{7,3},{8,12},{9,13},{10,... | collective-permute-start | bytes 36872 | tf_op jit(solution)/shard_map/ppermute | solution.py:77
  7.2 5.8 %collective-permute-start.2 = (bf16[48,128]{1,0:T(8,128)(2,1)S(1)}, bf16[48,128]{1,0:T(8,128)(2,1)S(1)}, u32[]{:S(2)}, u32[]{:S(2)}) collective-permute-start(bf16[48,128]{1,0:T(8,128)(2,1)S(1)} %get-tuple-element.92), channel_id=1, source_target_pairs={{0,15},{1,2},{2,1},{3,4},{4,3},{5,6},{6,5},{7,8},{8,7},{9,10},{10,... | collective-permute-start | bytes 36872 | tf_op jit(solution)/shard_map/ppermute | solution.py:77
  7.9 5.1 %collective-permute-start.3 = (bf16[48,128]{1,0:T(8,128)(2,1)S(1)}, bf16[48,128]{1,0:T(8,128)(2,1)S(1)}, u32[]{:S(2)}, u32[]{:S(2)}) collective-permute-start(bf16[48,128]{1,0:T(8,128)(2,1)S(1)} %get-tuple-element.93), channel_id=1, source_target_pairs={{0,1},{1,0},{2,3},{3,2},{4,5},{5,4},{6,7},{7,6},{8,9},{9,8},{10,11... | collective-permute-start | bytes 36872 | tf_op jit(solution)/shard_map/ppermute | solution.py:77
  13.0 3.1 %copy-start = (bf16[1,1,48,48,128]{4,3,2,1,0:T(8,128)(2,1)S(1)}, bf16[1,1,48,48,128]{4,3,2,1,0:T(8,128)(2,1)}, u32[]{:S(2)}) copy-start(bf16[1,1,48,48,128]{4,3,2,1,0:T(8,128)(2,1)} %param.9) | copy-start | bytes 1769476
  13.0 3.1 %copy-start.1 = (bf16[3,3,128,128]{3,2,1,0:T(8,128)(2,1)S(1)}, bf16[3,3,128,128]{3,2,1,0:T(8,128)(2,1)}, u32[]{:S(2)}) copy-start(bf16[3,3,128,128]{3,2,1,0:T(8,128)(2,1)} %param.7) | copy-start | bytes 884740
  13.6 5.6 %collective-permute-start.4 = (bf16[48,128]{1,0:T(8,128)(2,1)S(1)}, bf16[48,128]{1,0:T(8,128)(2,1)S(1)}, u32[]{:S(2)}, u32[]{:S(2)}) collective-permute-start(bf16[48,128]{1,0:T(8,128)(2,1)S(1)} %get-tuple-element.97), channel_id=1, source_target_pairs={{0,12},{1,13},{2,14},{3,15},{4,8},{5,9},{6,10},{7,11},{8,4},{9,5},... | collective-permute-start | bytes 36872 | tf_op jit(solution)/shard_map/ppermute | solution.py:77
  13.7 5.5 %collective-permute-start.5 = (bf16[48,128]{1,0:T(8,128)(2,1)S(1)}, bf16[48,128]{1,0:T(8,128)(2,1)S(1)}, u32[]{:S(2)}, u32[]{:S(2)}) collective-permute-start(bf16[48,128]{1,0:T(8,128)(2,1)S(1)} %get-tuple-element.98), channel_id=1, source_target_pairs={{0,4},{1,5},{2,6},{3,7},{4,0},{5,1},{6,2},{7,3},{8,12},{9,13},{10,... | collective-permute-start | bytes 36872 | tf_op jit(solution)/shard_map/ppermute | solution.py:77
  14.0 5.8 %collective-permute-start.6 = (bf16[48,128]{1,0:T(8,128)(2,1)S(1)}, bf16[48,128]{1,0:T(8,128)(2,1)S(1)}, u32[]{:S(2)}, u32[]{:S(2)}) collective-permute-start(bf16[48,128]{1,0:T(8,128)(2,1)S(1)} %get-tuple-element.99), channel_id=1, source_target_pairs={{0,15},{1,2},{2,1},{3,4},{4,3},{5,6},{6,5},{7,8},{8,7},{9,10},{10,... | collective-permute-start | bytes 36872 | tf_op jit(solution)/shard_map/ppermute | solution.py:77
  16.1 3.7 %collective-permute-start.7 = (bf16[48,128]{1,0:T(8,128)(2,1)S(1)}, bf16[48,128]{1,0:T(8,128)(2,1)S(1)}, u32[]{:S(2)}, u32[]{:S(2)}) collective-permute-start(bf16[48,128]{1,0:T(8,128)(2,1)S(1)} %get-tuple-element.100), channel_id=1, source_target_pairs={{0,1},{1,0},{2,3},{3,2},{4,5},{5,4},{6,7},{7,6},{8,9},{9,8},{10,11... | collective-permute-start | bytes 36872 | tf_op jit(solution)/shard_map/ppermute | solution.py:77
  20.7 5.9 %collective-permute-start.10 = (bf16[48,128]{1,0:T(8,128)(2,1)S(1)}, bf16[48,128]{1,0:T(8,128)(2,1)S(1)}, u32[]{:S(2)}, u32[]{:S(2)}) collective-permute-start(bf16[48,128]{1,0:T(8,128)(2,1)S(1)} %get-tuple-element.109), channel_id=1, source_target_pairs={{0,15},{1,2},{2,1},{3,4},{4,3},{5,6},{6,5},{7,8},{8,7},{9,10},{10,... | collective-permute-start | bytes 36872 | tf_op jit(solution)/shard_map/ppermute | solution.py:77
  22.9 3.7 %collective-permute-start.11 = (bf16[48,128]{1,0:T(8,128)(2,1)S(1)}, bf16[48,128]{1,0:T(8,128)(2,1)S(1)}, u32[]{:S(2)}, u32[]{:S(2)}) collective-permute-start(bf16[48,128]{1,0:T(8,128)(2,1)S(1)} %get-tuple-element.110), channel_id=1, source_target_pairs={{0,1},{1,0},{2,3},{3,2},{4,5},{5,4},{6,7},{7,6},{8,9},{9,8},{10,11... | collective-permute-start | bytes 36872 | tf_op jit(solution)/shard_map/ppermute | solution.py:77
  22.9 5.5 %collective-permute-start.8 = (bf16[48,128]{1,0:T(8,128)(2,1)S(1)}, bf16[48,128]{1,0:T(8,128)(2,1)S(1)}, u32[]{:S(2)}, u32[]{:S(2)}) collective-permute-start(bf16[48,128]{1,0:T(8,128)(2,1)S(1)} %get-tuple-element.107), channel_id=1, source_target_pairs={{0,12},{1,13},{2,14},{3,15},{4,8},{5,9},{6,10},{7,11},{8,4},{9,5},... | collective-permute-start | bytes 36872 | tf_op jit(solution)/shard_map/ppermute | solution.py:77
  22.9 5.5 %collective-permute-start.9 = (bf16[48,128]{1,0:T(8,128)(2,1)S(1)}, bf16[48,128]{1,0:T(8,128)(2,1)S(1)}, u32[]{:S(2)}, u32[]{:S(2)}) collective-permute-start(bf16[48,128]{1,0:T(8,128)(2,1)S(1)} %get-tuple-element.108), channel_id=1, source_target_pairs={{0,4},{1,5},{2,6},{3,7},{4,0},{5,1},{6,2},{7,3},{8,12},{9,13},{10,... | collective-permute-start | bytes 36872 | tf_op jit(solution)/shard_map/ppermute | solution.py:77
  29.8 1.6 %collective-permute-start.12 = (bf16[1152,128]{1,0:T(8,128)(2,1)S(1)}, bf16[1152,128]{1,0:T(8,128)(2,1)S(1)}, u32[]{:S(2)}, u32[]{:S(2)}) collective-permute-start(bf16[1152,128]{1,0:T(8,128)(2,1)S(1)} %bitcast.31), channel_id=1, source_target_pairs={{0,1},{1,0},{2,3},{3,2},{4,5},{5,4},{6,7},{7,6},{8,9},{9,8},{10,11... | collective-permute-start | bytes 884744 | tf_op jit(solution)/shard_map/ppermute | solution.py:478
  31.5 5.6 %collective-permute-start.13 = (bf16[288,128]{1,0:T(8,128)(2,1)S(1)}, bf16[288,128]{1,0:T(8,128)(2,1)S(1)}, u32[]{:S(2)}, u32[]{:S(2)}) collective-permute-start(bf16[288,128]{1,0:T(8,128)(2,1)S(1)} %get-tuple-element.147), channel_id=1, source_target_pairs={{0,2},{1,3},{2,0},{3,1},{4,6},{5,7},{6,4},{7,5},{8,10},{9,11},{10,... | collective-permute-start | bytes 221192 | tf_op jit(solution)/shard_map/ppermute | solution.py:478
  33.1 5.1 %collective-permute-start.14 = (bf16[288,128]{1,0:T(8,128)(2,1)S(1)}, bf16[288,128]{1,0:T(8,128)(2,1)S(1)}, u32[]{:S(2)}, u32[]{:S(2)}) collective-permute-start(bf16[288,128]{1,0:T(8,128)(2,1)S(1)} %get-tuple-element.148), channel_id=1, source_target_pairs={{0,16},{1,17},{2,18},{3,19},{4,20},{5,21},{6,22},{7,23},{8,24},{9,... | collective-permute-start | bytes 221192 | tf_op jit(solution)/shard_map/ppermute | solution.py:478
  34.6 5.3 %collective-permute-start.15 = (bf16[288,128]{1,0:T(8,128)(2,1)S(1)}, bf16[288,128]{1,0:T(8,128)(2,1)S(1)}, u32[]{:S(2)}, u32[]{:S(2)}) collective-permute-start(bf16[288,128]{1,0:T(8,128)(2,1)S(1)} %get-tuple-element.149), channel_id=1, source_target_pairs={{0,18},{1,19},{2,16},{3,17},{4,22},{5,23},{6,20},{7,21},{8,26},{9,... | collective-permute-start | bytes 221192 | tf_op jit(solution)/shard_map/ppermute | solution.py:478
  39.9 9.5 %collective-permute-start.16 = (bf16[336,128]{1,0:T(8,128)(2,1)S(1)}, bf16[336,128]{1,0:T(8,128)(2,1)S(1)}, u32[]{:S(2)}, u32[]{:S(2)}) collective-permute-start(bf16[336,128]{1,0:T(8,128)(2,1)S(1)} %get-tuple-element.157), channel_id=1, source_target_pairs={{0,4},{1,5},{2,6},{3,7},{4,0},{5,1},{6,2},{7,3},{8,12},{9,13},{10,... | collective-permute-start | bytes 258056 | tf_op jit(solution)/shard_map/ppermute | solution.py:478
  40.7 8.7 %collective-permute-start.18 = (bf16[336,128]{1,0:T(8,128)(2,1)S(1)}, bf16[336,128]{1,0:T(8,128)(2,1)S(1)}, u32[]{:S(2)}, u32[]{:S(2)}) collective-permute-start(bf16[336,128]{1,0:T(8,128)(2,1)S(1)} %get-tuple-element.158), channel_id=1, source_target_pairs={{0,12},{1,13},{2,14},{3,15},{4,8},{5,9},{6,10},{7,11},{8,4},{9,5},... | collective-permute-start | bytes 258056 | tf_op jit(solution)/shard_map/ppermute | solution.py:478
  41.9 7.5 %collective-permute-start.17 = (bf16[288,128]{1,0:T(8,128)(2,1)S(1)}, bf16[288,128]{1,0:T(8,128)(2,1)S(1)}, u32[]{:S(2)}, u32[]{:S(2)}) collective-permute-start(bf16[288,128]{1,0:T(8,128)(2,1)S(1)} %get-tuple-element.156.base), channel_id=1, source_target_pairs={{0,8},{1,9},{2,10},{3,11},{4,12},{5,13},{6,14},{7,15},{8,0},{9,1},... | collective-permute-start | bytes 221192 | tf_op jit(solution)/shard_map/ppermute | solution.py:478
  43.4 6.0 %collective-permute-start.19 = (bf16[48,128]{1,0:T(8,128)(2,1)S(1)}, bf16[48,128]{1,0:T(8,128)(2,1)S(1)}, u32[]{:S(2)}, u32[]{:S(2)}) collective-permute-start(bf16[48,128]{1,0:T(8,128)(2,1)S(1)} %get-tuple-element.162), channel_id=1, source_target_pairs={{0,15},{1,2},{2,1},{3,4},{4,3},{5,6},{6,5},{7,8},{8,7},{9,10},{10,... | collective-permute-start | bytes 36872 | tf_op jit(solution)/shard_map/ppermute | solution.py:552
  43.4 6.0 %collective-permute-start.20 = (bf16[48,128]{1,0:T(8,128)(2,1)S(1)}, bf16[48,128]{1,0:T(8,128)(2,1)S(1)}, u32[]{:S(2)}, u32[]{:S(2)}) collective-permute-start(bf16[48,128]{1,0:T(8,128)(2,1)S(1)} %get-tuple-element.163), channel_id=1, source_target_pairs={{0,1},{1,0},{2,3},{3,2},{4,5},{5,4},{6,7},{7,6},{8,9},{9,8},{10,11... | collective-permute-start | bytes 36872 | tf_op jit(solution)/shard_map/ppermute | solution.py:552
  49.5 5.1 %collective-permute-start.21 = (bf16[288,128]{1,0:T(8,128)(2,1)S(1)}, bf16[288,128]{1,0:T(8,128)(2,1)S(1)}, u32[]{:S(2)}, u32[]{:S(2)}) collective-permute-start(bf16[288,128]{1,0:T(8,128)(2,1)S(1)} %get-tuple-element.164), channel_id=1, source_target_pairs={{0,2},{1,3},{2,0},{3,1},{4,6},{5,7},{6,4},{7,5},{8,10},{9,11},{10,... | collective-permute-start | bytes 221192 | tf_op jit(solution)/shard_map/ppermute | solution.py:478
  50.9 4.4 %collective-permute-start.22 = (bf16[288,128]{1,0:T(8,128)(2,1)S(1)}, bf16[288,128]{1,0:T(8,128)(2,1)S(1)}, u32[]{:S(2)}, u32[]{:S(2)}) collective-permute-start(bf16[288,128]{1,0:T(8,128)(2,1)S(1)} %get-tuple-element.164), channel_id=1, source_target_pairs={{0,16},{1,17},{2,18},{3,19},{4,20},{5,21},{6,22},{7,23},{8,24},{9,... | collective-permute-start | bytes 221192 | tf_op jit(solution)/shard_map/ppermute | solution.py:478
  51.7 5.3 %collective-permute-start.23 = (bf16[288,128]{1,0:T(8,128)(2,1)S(1)}, bf16[288,128]{1,0:T(8,128)(2,1)S(1)}, u32[]{:S(2)}, u32[]{:S(2)}) collective-permute-start(bf16[288,128]{1,0:T(8,128)(2,1)S(1)} %get-tuple-element.164), channel_id=1, source_target_pairs={{0,18},{1,19},{2,16},{3,17},{4,22},{5,23},{6,20},{7,21},{8,26},{9,... | collective-permute-start | bytes 221192 | tf_op jit(solution)/shard_map/ppermute | solution.py:478
  57.0 1.6 %collective-permute-start.24 = (bf16[1152,128]{1,0:T(8,128)(2,1)S(1)}, bf16[1152,128]{1,0:T(8,128)(2,1)S(1)}, u32[]{:S(2)}, u32[]{:S(2)}) collective-permute-start(bf16[1152,128]{1,0:T(8,128)(2,1)S(1)} %bitcast.25), channel_id=1, source_target_pairs={{0,1},{1,0},{2,3},{3,2},{4,5},{5,4},{6,7},{7,6},{8,9},{9,8},{10,11... | collective-permute-start | bytes 884744 | tf_op jit(solution)/shard_map/ppermute | solution.py:478

commit v5 on v4

--- a/solution.py
+++ b/solution.py
@@ -288,9 +288,10 @@
     ]
     for copy in copies:
         copy.start()
-    for copy in copies[:5]:
+    copies[0].wait()
+    write_links(near, cols, found)
+    for copy in copies[1:5]:
         copy.wait()
-    write_links(near, cols, found)
     strips[0] = rows[0].astype(f32)
     strips[2] = rows[1].astype(f32)
     strips[3] = columns[0].astype(f32)[:, 0, :]
@@ -489,7 +490,7 @@
     add = lambda at: kept[quarter(at), :] + given[quarter(at), :].astype(f32)
     own[...] = add(seat)
     for k, block in enumerate(sent):
-        block[...] = add(seat ^ (k + 1)).astype(bf16)
+        block[...] = add(seat ^ (3, 2, 1)[k]).astype(bf16)
 
 
 def add_up(count, loads, base, *refs):
@@ -512,7 +513,7 @@
     rows, lanes = kept.shape[0] // 4, kept.shape[1]
     groups, bit = [], 4
     while bit < tiles:
-        groups.append([bit, 2 * bit, 3 * bit] if 2 * bit < tiles else [bit])
+        groups.append([3 * bit, 2 * bit, bit] if 2 * bit < tiles else [bit])
         bit *= 4
     S = jax.ShapeDtypeStruct
     given, riders = lax.optimization_barrier((flip_swap(given, 0, 1), riders))
@@ -523,7 +524,7 @@
         [S((rows, lanes), f32)] + [S((rows, lanes), bf16)] * 3,
         [],
     )
-    got = [flip_swap(block, k >> 1, (k & 1) << 1) for k, block in zip((1, 2, 3), sent)]
+    got = [flip_swap(block, k >> 1, (k & 1) << 1) for k, block in zip((3, 2, 1), sent)]
     carried, coming = {}, []
     for n, masks in enumerate(groups + [[]]):
         aboard = {}
@@ -554,20 +555,18 @@
 
 
 def gather_quarters(part):
-    seat = seat_of()
-    whole = jnp.zeros((4,) + part.shape, part.dtype)
-    whole = lax.dynamic_update_index_in_dim(whole, part, seat, 0)
-    for k in (1, 2, 3):
-        got = flip_swap(part, k >> 1, (k & 1) << 1)
-        whole = lax.dynamic_update_index_in_dim(whole, got, seat ^ k, 0)
-    return whole.reshape(-1, part.shape[-1])
-
-
-def both_grads(half, other, first, second):
-    core = lax.axis_index("tile") & 1
-    one, two = half[...].astype(f32), other[...].astype(f32)
-    first[...] = jnp.where(core == 0, one, two)
-    second[...] = jnp.where(core == 0, two, one)
+    return [part] + [flip_swap(part, k >> 1, (k & 1) << 1) for k in (1, 2, 3)]
+
+
+def both_grads(*refs):
+    mine, others, first, second = refs[:4], refs[4:8], refs[8], refs[9]
+    rows = mine[0].shape[0]
+    core, seat = lax.axis_index("tile") & 1, seat_of()
+    for k in range(4):
+        place = pl.ds(pl.multiple_of((seat ^ k) * rows, rows), rows)
+        one, two = mine[k][...].astype(f32), others[k][...].astype(f32)
+        first[place, :] = jnp.where(core == 0, one, two)
+        second[place, :] = jnp.where(core == 0, two, one)
 
 
 def local(fields, weight_first, weight_second, neighbours, cotangent):
@@ -705,12 +704,13 @@
         [S(block.shape, bf16)],
         rooms + [V(halo), V(pairs(f32))],
     )
-    half_grads = gather_quarters(part)
-    half_grads, grad_block = lax.optimization_barrier((half_grads, grad_block))
+    quarters = gather_quarters(part)
+    others = [flip_swap(quarter, 0, 1) for quarter in quarters]
+    others, grad_block = lax.optimization_barrier((others, grad_block))
     grads = call(
         both_grads,
         "both_grads",
-        whole([half_grads, flip_swap(half_grads, 0, 1)]),
+        whole([*quarters, *others]),
         [S((9 * c, c), f32)] * 2,
         [],
     )

time: 59.9 us -> 58.3 us (0.973)
  waiting for transfers between devices: 19.8 us -> 16.5 us
  starting transfers between devices: 24.1 us -> 26.1 us
    ppermute x11 -> x14, waiting for transfers between devices: 13.4 us -> 7.85 us  [flip_swap(): return lax.ppermute(block, ('ens', 'tile'), route)]
    ppermute x2, waiting for transfers between devices: 0.01 us -> 1.55 us  [summed_part(): carried[k] = lax.ppermute(riders[k], 'tile', list(enumerate(way)))]
    ppermute x11 -> x14, starting transfers between devices: 10.8 us -> 12 us  [flip_swap(): return lax.ppermute(block, ('ens', 'tile'), route)]
    ppermute x12, waiting for transfers between devices: 6.41 us -> 7.1 us  [swap_all(): lax.ppermute(block, 'tile', list(enumerate(way)))]
  transfers between devices with their start and end apart: 25 -> 28, of which waited for: 14 -> 15; matrix products, arithmetic and copies ran while one was open for 0% -> 0% of each run, Pallas kernels for 16% -> 16%
where the time goes in v5:
time: 58.3 us; the launch traced here: 58.2 us
  starting transfers between devices  26.1 us (45%)
  waiting for transfers between devices  16.5 us (28%)
  Pallas kernels  14.8 us (25%)
  between operations  0.77 us (1%)
    pallas_call x14, Pallas kernels, call(): pl.pallas_call(kernel, name=name, grid=(1,), in_specs=[spec or whole for...  14.8 us
    ppermute x12, starting transfers between devices, swap_all(): lax.ppermute(block, 'tile', list(enumerate(way)))  12.9 us
    ppermute x14, starting transfers between devices, flip_swap(): return lax.ppermute(block, ('ens', 'tile'), route)  12 us
    ppermute x14, waiting for transfers between devices, flip_swap(): return lax.ppermute(block, ('ens', 'tile'), route)  7.85 us
    ppermute x12, waiting for transfers between devices, swap_all(): lax.ppermute(block, 'tile', list(enumerate(way)))  7.1 us
    ppermute x2, waiting for transfers between devices, summed_part(): carried[k] = lax.ppermute(riders[k], 'tile', list(enumerate(way)))  1.55 us
    ppermute x2, starting transfers between devices, summed_part(): carried[k] = lax.ppermute(riders[k], 'tile', list(enumerate(way)))  1.17 us
  transfers between devices with their start and end apart: 28, of which 15 were waited for; matrix products, arithmetic and copies ran while one was open for 0% of the time, Pallas kernels for 16%

profile of v5, /device:TPU:0, one launch (start us, length us, event | category | flops | bytes accessed | tf_op | source)
XLA Modules:
  0.0 58.2 jit_solution(17034892549884723462)
XLA Ops:
  0.6 1.4 %first_strips.1 = (bf16[48,128]{1,0:T(8,128)(2,1)S(1)}, bf16[48,128]{1,0:T(8,128)(2,1)S(1)}, bf16[48,128]{1,0:T(8,128)(2,1)S(1)}, bf16[48,128]{1,0:T(8,128)(2,1)...) custom-call(s32[4,16]{1,0:T(4,128)} %bitcast.24, ...), custom_call_target="tpu_custom_call" | custom-call | bytes 2097152 | tf_op jit(solution)/shard_map/first_strips/pallas_call | solution.py:459
  2.1 5.1 %collective-permute-start = (bf16[48,128]{1,0:T(8,128)(2,1)S(1)}, bf16[48,128]{1,0:T(8,128)(2,1)S(1)}, u32[]{:S(2)}, u32[]{:S(2)}) collective-permute-start(bf16[48,128]{1,0:T(8,128)(2,1)S(1)} %get-tuple-element.93), channel_id=1, source_target_pairs={{0,12},{1,13},{2,14},{3,15},{4,8},{5,9},{6,10},{7,11},{8,4},{9,5},... | collective-permute-start | bytes 36872 | tf_op jit(solution)/shard_map/ppermute | solution.py:77
  7.2 0.7 %collective-permute-start.2 = (bf16[48,128]{1,0:T(8,128)(2,1)S(1)}, bf16[48,128]{1,0:T(8,128)(2,1)S(1)}, u32[]{:S(2)}, u32[]{:S(2)}) collective-permute-start(bf16[48,128]{1,0:T(8,128)(2,1)S(1)} %get-tuple-element.95), channel_id=1, source_target_pairs={{0,15},{1,2},{2,1},{3,4},{4,3},{5,6},{6,5},{7,8},{8,7},{9,10},{10,... | collective-permute-start | bytes 36872 | tf_op jit(solution)/shard_map/ppermute | solution.py:77
  7.9 0.9 %collective-permute-start.3 = (bf16[48,128]{1,0:T(8,128)(2,1)S(1)}, bf16[48,128]{1,0:T(8,128)(2,1)S(1)}, u32[]{:S(2)}, u32[]{:S(2)}) collective-permute-start(bf16[48,128]{1,0:T(8,128)(2,1)S(1)} %get-tuple-element.96), channel_id=1, source_target_pairs={{0,1},{1,0},{2,3},{3,2},{4,5},{5,4},{6,7},{7,6},{8,9},{9,8},{10,11... | collective-permute-start | bytes 36872 | tf_op jit(solution)/shard_map/ppermute | solution.py:77
  8.8 1.7 %first_bulk.1 = (bf16[1200,768]{1,0:T(8,128)(2,1)S(1)}, f32[24,48,256]{2,1,0:T(8,128)S(1)}, bf16[24,48,256]{2,1,0:T(8,128)(2,1)S(1)}, bf16[24,48,256]{2,1,0:T(8,128)(2,1)S(1)}) custom-call(bf16[48,48,128]{2,1,0:T(8,128)(2,1)S(1)} %get-tuple-element.98.block, bf16[9,128,128]{2,1,0:T(8,128)(2,1)S(1)} %get-tuple-element.97.weight.refs_4_), custom_call_target="tpu_custom_call" | custom-call | flops 679477248 | bytes 2097152 | tf_op jit(solution)/shard_map/first_bulk/pallas_call | solution.py:459
  10.5 0.4 collective-permute-done.1.refs_1_
  10.9 2.1 %collective-permute-done.2.refs_2_ = bf16[48,128]{1,0:T(8,128)(2,1)S(1)} collective-permute-done((bf16[48,128]{1,0:T(8,128)(2,1)S(1)}, bf16[48,128]{1,0:T(8,128)(2,1)S(1)}, u32[]{:S(2)}, u32[]{:S(2)}) %collective-permute-start.2) | collective-permute-done | bytes 12320 | tf_op jit(solution)/shard_map/ppermute | solution.py:77
  13.0 0.6 %first_edges.1 = (bf16[48,128]{1,0:T(8,128)(2,1)S(1)}, bf16[48,128]{1,0:T(8,128)(2,1)S(1)}, bf16[48,128]{1,0:T(8,128)(2,1)S(1)}, bf16[48,128]{1,0:T(8,128)(2,1)S...) custom-call(s32[8,8,128]{2,1,0:T(8,128)S(1)} %get-tuple-element.92.f, ...), custom_call_target="tpu_custom_call" | custom-call | bytes 2097152 | tf_op jit(solution)/shard_map/first_edges/pallas_call | solution.py:459
  13.6 0.1 collective-permute-start.4
  13.7 0.3 collective-permute-start.5
  14.0 2.1 %collective-permute-start.6 = (bf16[48,128]{1,0:T(8,128)(2,1)S(1)}, bf16[48,128]{1,0:T(8,128)(2,1)S(1)}, u32[]{:S(2)}, u32[]{:S(2)}) collective-permute-start(bf16[48,128]{1,0:T(8,128)(2,1)S(1)} %get-tuple-element.102), channel_id=1, source_target_pairs={{0,15},{1,2},{2,1},{3,4},{4,3},{5,6},{6,5},{7,8},{8,7},{9,10},{10,... | collective-permute-start | bytes 36872 | tf_op jit(solution)/shard_map/ppermute | solution.py:77
  16.1 1.7 %second_bulk.1 = (bf16[1200,768]{1,0:T(8,128)(2,1)S(1)}, f32[24,48,256]{2,1,0:T(8,128)S(1)}, bf16[24,48,256]{2,1,0:T(8,128)(2,1)S(1)}, bf16[24,48,256]{2,1,0:T(8,128)(2,1)S(1)}) custom-call(bf16[24,48,256]{2,1,0:T(8,128)(2,1)S(1)} %get-tuple-element.104.hidden, f32[24,8,256]{2,1,0:T(8,128)S(1)} %get-tuple-element.105.left, ...), custom_call_target="tpu_custom_call" | custom-call | flops 679477248 | bytes 2097152 | tf_op jit(solution)/shard_map/second_bulk/pallas_call | solution.py:459
  17.9 1.3 %collective-permute-done.4.refs_0_ = bf16[48,128]{1,0:T(8,128)(2,1)S(1)} collective-permute-done((bf16[48,128]{1,0:T(8,128)(2,1)S(1)}, bf16[48,128]{1,0:T(8,128)(2,1)S(1)}, u32[]{:S(2)}, u32[]{:S(2)}) %collective-permute-start.4) | collective-permute-done | bytes 12320 | tf_op jit(solution)/shard_map/ppermute | solution.py:77
  19.2 0.6 %collective-permute-done.6.refs_2_ = bf16[48,128]{1,0:T(8,128)(2,1)S(1)} collective-permute-done((bf16[48,128]{1,0:T(8,128)(2,1)S(1)}, bf16[48,128]{1,0:T(8,128)(2,1)S(1)}, u32[]{:S(2)}, u32[]{:S(2)}) %collective-permute-start.6) | collective-permute-done | bytes 12320 | tf_op jit(solution)/shard_map/ppermute | solution.py:77
  19.8 0.9 %second_edges.1 = (bf16[48,128]{1,0:T(8,128)(2,1)S(1)}, bf16[48,128]{1,0:T(8,128)(2,1)S(1)}, bf16[48,128]{1,0:T(8,128)(2,1)S(1)}, bf16[48,128]{1,0:T(8,128)(2,1)...) custom-call(s32[8,8,128]{2,1,0:T(8,128)S(1)} %get-tuple-element.92.f, ...), custom_call_target="tpu_custom_call" | custom-call | bytes 2097152 | tf_op jit(solution)/shard_map/second_edges/pallas_call | solution.py:459
  20.7 1.8 %collective-permute-start.8 = (bf16[48,128]{1,0:T(8,128)(2,1)S(1)}, bf16[48,128]{1,0:T(8,128)(2,1)S(1)}, u32[]{:S(2)}, u32[]{:S(2)}) collective-permute-start(bf16[48,128]{1,0:T(8,128)(2,1)S(1)} %get-tuple-element.110), channel_id=1, source_target_pairs={{0,12},{1,13},{2,14},{3,15},{4,8},{5,9},{6,10},{7,11},{8,4},{9,5},... | collective-permute-start | bytes 36872 | tf_op jit(solution)/shard_map/ppermute | solution.py:77
  22.5 1.1 %collective-permute-start.9 = (bf16[48,128]{1,0:T(8,128)(2,1)S(1)}, bf16[48,128]{1,0:T(8,128)(2,1)S(1)}, u32[]{:S(2)}, u32[]{:S(2)}) collective-permute-start(bf16[48,128]{1,0:T(8,128)(2,1)S(1)} %get-tuple-element.111), channel_id=1, source_target_pairs={{0,4},{1,5},{2,6},{3,7},{4,0},{5,1},{6,2},{7,3},{8,12},{9,13},{10,... | collective-permute-start | bytes 36872 | tf_op jit(solution)/shard_map/ppermute | solution.py:77
  23.6 0.8 %collective-permute-start.10 = (bf16[48,128]{1,0:T(8,128)(2,1)S(1)}, bf16[48,128]{1,0:T(8,128)(2,1)S(1)}, u32[]{:S(2)}, u32[]{:S(2)}) collective-permute-start(bf16[48,128]{1,0:T(8,128)(2,1)S(1)} %get-tuple-element.112), channel_id=1, source_target_pairs={{0,15},{1,2},{2,1},{3,4},{4,3},{5,6},{6,5},{7,8},{8,7},{9,10},{10,... | collective-permute-start | bytes 36872 | tf_op jit(solution)/shard_map/ppermute | solution.py:77
  24.4 2.4 %second_back.1 = (f32[9,128,128]{2,1,0:T(8,128)S(1)}, f32[24,48,256]{2,1,0:T(8,128)S(1)}, bf16[24,48,256]{2,1,0:T(8,128)(2,1)S(1)}) custom-call(bf16[24,48,256]{2,1,0:T(8,128)(2,1)S(1)} %get-tuple-element.114.refs_0_, f32[24,8,256]{2,1,0:T(8,128)S(1)} %get-tuple-element.115.refs_1_, f32[24,8,256]{2,1,0:T(8,128)S(1)} %get-tuple-element.116.refs_2_, ...), custom_call_target="tpu_custom_call" | custom-call | flops 1358954496 | bytes 2097152 | tf_op jit(solution)/shard_map/second_back/pallas_call | solution.py:459
  26.8 2.6 %collective-permute-done.10.refs_2_ = bf16[48,128]{1,0:T(8,128)(2,1)S(1)} collective-permute-done((bf16[48,128]{1,0:T(8,128)(2,1)S(1)}, bf16[48,128]{1,0:T(8,128)(2,1)S(1)}, u32[]{:S(2)}, u32[]{:S(2)}) %collective-permute-start.10) | collective-permute-done | bytes 12320 | tf_op jit(solution)/shard_map/ppermute | solution.py:77
  29.5 1.4 %first_back.1 = (bf16[24,48,256]{2,1,0:T(8,128)(2,1)S(1)}, f32[24,8,256]{2,1,0:T(8,128)S(1)}, f32[24,8,256]{2,1,0:T(8,128)S(1)}, f32[48,128]{1,0:T(8,128)S(1)}, ...) custom-call(s32[8,8,128]{2,1,0:T(8,128)S(1)} %get-tuple-element.92.found, ...), custom_call_target="tpu_custom_call" | custom-call | flops 679477248 | bytes 2097152 | tf_op jit(solution)/shard_map/first_back/pallas_call | solution.py:459
  30.9 0.1 collective-permute-start.12
  30.9 0.5 first_returns.1
  31.4 1.1 %collective-permute-done.12.given = bf16[1152,128]{1,0:T(8,128)(2,1)S(1)} collective-permute-done((bf16[1152,128]{1,0:T(8,128)(2,1)S(1)}, bf16[1152,128]{1,0:T(8,128)(2,1)S(1)}, u32[]{:S(2)}, u32[]{:S(2)}) %collective-permute-start.12) | collective-permute-done | bytes 294944 | tf_op jit(solution)/shard_map/ppermute | solution.py:479
  32.5 0.1 share_out.1
  32.6 0.1 collective-permute-start.13
  32.7 1.5 %collective-permute-start.14 = (bf16[288,128]{1,0:T(8,128)(2,1)S(1)}, bf16[288,128]{1,0:T(8,128)(2,1)S(1)}, u32[]{:S(2)}, u32[]{:S(2)}) collective-permute-start(bf16[288,128]{1,0:T(8,128)(2,1)S(1)} %get-tuple-element.151), channel_id=1, source_target_pairs={{0,16},{1,17},{2,18},{3,19},{4,20},{5,21},{6,22},{7,23},{8,24},{9,... | collective-permute-start | bytes 221192 | tf_op jit(solution)/shard_map/ppermute | solution.py:479
  34.2 1.9 %collective-permute-start.15 = (bf16[288,128]{1,0:T(8,128)(2,1)S(1)}, bf16[288,128]{1,0:T(8,128)(2,1)S(1)}, u32[]{:S(2)}, u32[]{:S(2)}) collective-permute-start(bf16[288,128]{1,0:T(8,128)(2,1)S(1)} %get-tuple-element.152), channel_id=1, source_target_pairs={{0,2},{1,3},{2,0},{3,1},{4,6},{5,7},{6,4},{7,5},{8,10},{9,11},{10,... | collective-permute-start | bytes 221192 | tf_op jit(solution)/shard_map/ppermute | solution.py:479
  36.1 2.0 %last_bulk.1 = (f32[24,48,256]{2,1,0:T(8,128)S(1)}, bf16[48,48,128]{2,1,0:T(8,128)(2,1)}) custom-call(bf16[24,48,256]{2,1,0:T(8,128)(2,1)S(1)} %get-tuple-element.131.delta, bf16[9,128,128]{2,1,0:T(8,128)(2,1)S(1)} %get-tuple-element.97.weight.refs_4_, bf16[24,48,256]{2,1,0:T(8,128)(2,1)S(1)} %get-tuple-element.132.bulk_out, ...), custom_call_target="tpu_custom_call" | custom-call | flops 679477248 | bytes 2097152 | tf_op jit(solution)/shard_map/last_bulk/pallas_call | solution.py:459
  38.2 0.2 collective-permute-done.13.refs_0_
  38.4 1.0 %collective-permute-done.15.refs_2_ = bf16[288,128]{1,0:T(8,128)(2,1)S(1)} collective-permute-done((bf16[288,128]{1,0:T(8,128)(2,1)S(1)}, bf16[288,128]{1,0:T(8,128)(2,1)S(1)}, u32[]{:S(2)}, u32[]{:S(2)}) %collective-permute-start.15) | collective-permute-done | bytes 73760 | tf_op jit(solution)/shard_map/ppermute | solution.py:479
  39.5 1.1 %collective-permute-start.16 = (bf16[336,128]{1,0:T(8,128)(2,1)S(1)}, bf16[336,128]{1,0:T(8,128)(2,1)S(1)}, u32[]{:S(2)}, u32[]{:S(2)}) collective-permute-start(bf16[336,128]{1,0:T(8,128)(2,1)S(1)} %get-tuple-element.160), channel_id=1, source_target_pairs={{0,12},{1,13},{2,14},{3,15},{4,8},{5,9},{6,10},{7,11},{8,4},{9,5},... | collective-permute-start | bytes 258056 | tf_op jit(solution)/shard_map/ppermute | solution.py:479
  40.6 3.3 %collective-permute-start.17 = (bf16[288,128]{1,0:T(8,128)(2,1)S(1)}, bf16[288,128]{1,0:T(8,128)(2,1)S(1)}, u32[]{:S(2)}, u32[]{:S(2)}) collective-permute-start(bf16[288,128]{1,0:T(8,128)(2,1)S(1)} %get-tuple-element.159.base), channel_id=1, source_target_pairs={{0,8},{1,9},{2,10},{3,11},{4,12},{5,13},{6,14},{7,15},{8,0},{9,1},... | collective-permute-start | bytes 221192 | tf_op jit(solution)/shard_map/ppermute | solution.py:479
  43.9 0.1 collective-permute-start.19
  44.0 1.1 %collective-permute-start.20 = (bf16[48,128]{1,0:T(8,128)(2,1)S(1)}, bf16[48,128]{1,0:T(8,128)(2,1)S(1)}, u32[]{:S(2)}, u32[]{:S(2)}) collective-permute-start(bf16[48,128]{1,0:T(8,128)(2,1)S(1)} %get-tuple-element.166), channel_id=1, source_target_pairs={{0,1},{1,0},{2,3},{3,2},{4,5},{5,4},{6,7},{7,6},{8,9},{9,8},{10,11... | collective-permute-start | bytes 36872 | tf_op jit(solution)/shard_map/ppermute | solution.py:553
  45.1 3.0 %collective-permute-done.17.refs_1_ = bf16[288,128]{1,0:T(8,128)(2,1)S(1)} collective-permute-done((bf16[288,128]{1,0:T(8,128)(2,1)S(1)}, bf16[288,128]{1,0:T(8,128)(2,1)S(1)}, u32[]{:S(2)}, u32[]{:S(2)}) %collective-permute-start.17) | collective-permute-done | bytes 73760 | tf_op jit(solution)/shard_map/ppermute | solution.py:479
  48.1 0.1 collective-permute-done.18.refs_2_
  48.2 1.5 %collective-permute-done.19.refs_2_ = bf16[48,128]{1,0:T(8,128)(2,1)S(1)} collective-permute-done((bf16[48,128]{1,0:T(8,128)(2,1)S(1)}, bf16[48,128]{1,0:T(8,128)(2,1)S(1)}, u32[]{:S(2)}, u32[]{:S(2)}) %collective-permute-start.19) | collective-permute-done | bytes 12320 | tf_op jit(solution)/shard_map/ppermute | solution.py:553
  49.8 0.2 collective-permute-start.26
  49.9 1.3 %collective-permute-start.24 = (bf16[288,128]{1,0:T(8,128)(2,1)S(1)}, bf16[288,128]{1,0:T(8,128)(2,1)S(1)}, u32[]{:S(2)}, u32[]{:S(2)}) collective-permute-start(bf16[288,128]{1,0:T(8,128)(2,1)S(1)} %get-tuple-element.167.refs_0_), channel_id=1, source_target_pairs={{0,16},{1,17},{2,18},{3,19},{4,20},{5,21},{6,22},{7,23},{8,24},{9,... | collective-permute-start | bytes 221192 | tf_op jit(solution)/shard_map/ppermute | solution.py:479
  51.2 2.0 %collective-permute-start.22 = (bf16[288,128]{1,0:T(8,128)(2,1)S(1)}, bf16[288,128]{1,0:T(8,128)(2,1)S(1)}, u32[]{:S(2)}, u32[]{:S(2)}) collective-permute-start(bf16[288,128]{1,0:T(8,128)(2,1)S(1)} %get-tuple-element.167.refs_0_), channel_id=1, source_target_pairs={{0,2},{1,3},{2,0},{3,1},{4,6},{5,7},{6,4},{7,5},{8,10},{9,11},{10,... | collective-permute-start | bytes 221192 | tf_op jit(solution)/shard_map/ppermute | solution.py:479
  53.2 1.8 %collective-permute-done.26.refs_3_ = bf16[288,128]{1,0:T(8,128)(2,1)S(1)} collective-permute-done((bf16[288,128]{1,0:T(8,128)(2,1)S(1)}, bf16[288,128]{1,0:T(8,128)(2,1)S(1)}, u32[]{:S(2)}, u32[]{:S(2)}) %collective-permute-start.26) | collective-permute-done | bytes 73760 | tf_op jit(solution)/shard_map/ppermute | solution.py:479
  55.0 0.1 collective-permute-done.24.refs_2_
  55.1 0.4 collective-permute-start.25
  55.5 0.3 collective-permute-done.22.refs_1_
  55.8 1.0 %last_edges.1 = bf16[48,48,128]{2,1,0:T(8,128)(2,1)} custom-call(s32[8,8,128]{2,1,0:T(8,128)S(1)} %get-tuple-element.92.found, bf16[48,128]{1,0:T(8,128)(2,1)S(1)} %get-tuple-element.168.refs_0_, bf16[48,128]{1,0:T(8,128)(2,1)S(1)} %get-tuple-element.169.refs_1_, bf16[48,128]{1,0:T(8,128)(2,1)S(1)} %collective-permute-done.19.refs_2_, ...), custom_call_target="tpu_custom_call" | custom-call | bytes 2097152 | tf_op jit(solution)/shard_map/last_edges/pallas_call | solution.py:459
  56.8 0.3 collective-permute-done.23.refs_5_
  57.1 1.1 %both_grads.1 = (f32[1152,128]{1,0:T(8,128)}, f32[1152,128]{1,0:T(8,128)}) custom-call(bf16[288,128]{1,0:T(8,128)(2,1)S(1)} %get-tuple-element.167.refs_0_, bf16[288,128]{1,0:T(8,128)(2,1)S(1)} %collective-permute-done.22.refs_1_, bf16[288,128]{1,0:T(8,128)(2,1)S(1)} %collective-permute-done.24.refs_2_, ...), custom_call_target="tpu_custom_call" | custom-call | bytes 2097152 | tf_op jit(solution)/shard_map/both_grads/pallas_call | solution.py:459
  (26 shorter events, 0.1 us)
Async XLA Ops:
  2.1 8.4 %collective-permute-start = (bf16[48,128]{1,0:T(8,128)(2,1)S(1)}, bf16[48,128]{1,0:T(8,128)(2,1)S(1)}, u32[]{:S(2)}, u32[]{:S(2)}) collective-permute-start(bf16[48,128]{1,0:T(8,128)(2,1)S(1)} %get-tuple-element.93), channel_id=1, source_target_pairs={{0,12},{1,13},{2,14},{3,15},{4,8},{5,9},{6,10},{7,11},{8,4},{9,5},... | collective-permute-start | bytes 36872 | tf_op jit(solution)/shard_map/ppermute | solution.py:77
  7.2 3.7 %collective-permute-start.1 = (bf16[48,128]{1,0:T(8,128)(2,1)S(1)}, bf16[48,128]{1,0:T(8,128)(2,1)S(1)}, u32[]{:S(2)}, u32[]{:S(2)}) collective-permute-start(bf16[48,128]{1,0:T(8,128)(2,1)S(1)} %get-tuple-element.94), channel_id=1, source_target_pairs={{0,4},{1,5},{2,6},{3,7},{4,0},{5,1},{6,2},{7,3},{8,12},{9,13},{10,... | collective-permute-start | bytes 36872 | tf_op jit(solution)/shard_map/ppermute | solution.py:77
  7.2 5.8 %collective-permute-start.2 = (bf16[48,128]{1,0:T(8,128)(2,1)S(1)}, bf16[48,128]{1,0:T(8,128)(2,1)S(1)}, u32[]{:S(2)}, u32[]{:S(2)}) collective-permute-start(bf16[48,128]{1,0:T(8,128)(2,1)S(1)} %get-tuple-element.95), channel_id=1, source_target_pairs={{0,15},{1,2},{2,1},{3,4},{4,3},{5,6},{6,5},{7,8},{8,7},{9,10},{10,... | collective-permute-start | bytes 36872 | tf_op jit(solution)/shard_map/ppermute | solution.py:77
  7.9 5.1 %collective-permute-start.3 = (bf16[48,128]{1,0:T(8,128)(2,1)S(1)}, bf16[48,128]{1,0:T(8,128)(2,1)S(1)}, u32[]{:S(2)}, u32[]{:S(2)}) collective-permute-start(bf16[48,128]{1,0:T(8,128)(2,1)S(1)} %get-tuple-element.96), channel_id=1, source_target_pairs={{0,1},{1,0},{2,3},{3,2},{4,5},{5,4},{6,7},{7,6},{8,9},{9,8},{10,11... | collective-permute-start | bytes 36872 | tf_op jit(solution)/shard_map/ppermute | solution.py:77
  13.0 3.1 %copy-start = (bf16[1,1,48,48,128]{4,3,2,1,0:T(8,128)(2,1)S(1)}, bf16[1,1,48,48,128]{4,3,2,1,0:T(8,128)(2,1)}, u32[]{:S(2)}) copy-start(bf16[1,1,48,48,128]{4,3,2,1,0:T(8,128)(2,1)} %param.9) | copy-start | bytes 1769476
  13.0 3.1 %copy-start.1 = (bf16[3,3,128,128]{3,2,1,0:T(8,128)(2,1)S(1)}, bf16[3,3,128,128]{3,2,1,0:T(8,128)(2,1)}, u32[]{:S(2)}) copy-start(bf16[3,3,128,128]{3,2,1,0:T(8,128)(2,1)} %param.7) | copy-start | bytes 884740
  13.6 5.6 %collective-permute-start.4 = (bf16[48,128]{1,0:T(8,128)(2,1)S(1)}, bf16[48,128]{1,0:T(8,128)(2,1)S(1)}, u32[]{:S(2)}, u32[]{:S(2)}) collective-permute-start(bf16[48,128]{1,0:T(8,128)(2,1)S(1)} %get-tuple-element.100), channel_id=1, source_target_pairs={{0,12},{1,13},{2,14},{3,15},{4,8},{5,9},{6,10},{7,11},{8,4},{9,5},... | collective-permute-start | bytes 36872 | tf_op jit(solution)/shard_map/ppermute | solution.py:77
  13.7 5.5 %collective-permute-start.5 = (bf16[48,128]{1,0:T(8,128)(2,1)S(1)}, bf16[48,128]{1,0:T(8,128)(2,1)S(1)}, u32[]{:S(2)}, u32[]{:S(2)}) collective-permute-start(bf16[48,128]{1,0:T(8,128)(2,1)S(1)} %get-tuple-element.101), channel_id=1, source_target_pairs={{0,4},{1,5},{2,6},{3,7},{4,0},{5,1},{6,2},{7,3},{8,12},{9,13},{10,... | collective-permute-start | bytes 36872 | tf_op jit(solution)/shard_map/ppermute | solution.py:77
  14.0 5.8 %collective-permute-start.6 = (bf16[48,128]{1,0:T(8,128)(2,1)S(1)}, bf16[48,128]{1,0:T(8,128)(2,1)S(1)}, u32[]{:S(2)}, u32[]{:S(2)}) collective-permute-start(bf16[48,128]{1,0:T(8,128)(2,1)S(1)} %get-tuple-element.102), channel_id=1, source_target_pairs={{0,15},{1,2},{2,1},{3,4},{4,3},{5,6},{6,5},{7,8},{8,7},{9,10},{10,... | collective-permute-start | bytes 36872 | tf_op jit(solution)/shard_map/ppermute | solution.py:77
  16.1 3.7 %collective-permute-start.7 = (bf16[48,128]{1,0:T(8,128)(2,1)S(1)}, bf16[48,128]{1,0:T(8,128)(2,1)S(1)}, u32[]{:S(2)}, u32[]{:S(2)}) collective-permute-start(bf16[48,128]{1,0:T(8,128)(2,1)S(1)} %get-tuple-element.103), channel_id=1, source_target_pairs={{0,1},{1,0},{2,3},{3,2},{4,5},{5,4},{6,7},{7,6},{8,9},{9,8},{10,11... | collective-permute-start | bytes 36872 | tf_op jit(solution)/shard_map/ppermute | solution.py:77
  20.7 6.1 %collective-permute-start.8 = (bf16[48,128]{1,0:T(8,128)(2,1)S(1)}, bf16[48,128]{1,0:T(8,128)(2,1)S(1)}, u32[]{:S(2)}, u32[]{:S(2)}) collective-permute-start(bf16[48,128]{1,0:T(8,128)(2,1)S(1)} %get-tuple-element.110), channel_id=1, source_target_pairs={{0,12},{1,13},{2,14},{3,15},{4,8},{5,9},{6,10},{7,11},{8,4},{9,5},... | collective-permute-start | bytes 36872 | tf_op jit(solution)/shard_map/ppermute | solution.py:77
  22.5 4.3 %collective-permute-start.9 = (bf16[48,128]{1,0:T(8,128)(2,1)S(1)}, bf16[48,128]{1,0:T(8,128)(2,1)S(1)}, u32[]{:S(2)}, u32[]{:S(2)}) collective-permute-start(bf16[48,128]{1,0:T(8,128)(2,1)S(1)} %get-tuple-element.111), channel_id=1, source_target_pairs={{0,4},{1,5},{2,6},{3,7},{4,0},{5,1},{6,2},{7,3},{8,12},{9,13},{10,... | collective-permute-start | bytes 36872 | tf_op jit(solution)/shard_map/ppermute | solution.py:77
  23.6 5.8 %collective-permute-start.10 = (bf16[48,128]{1,0:T(8,128)(2,1)S(1)}, bf16[48,128]{1,0:T(8,128)(2,1)S(1)}, u32[]{:S(2)}, u32[]{:S(2)}) collective-permute-start(bf16[48,128]{1,0:T(8,128)(2,1)S(1)} %get-tuple-element.112), channel_id=1, source_target_pairs={{0,15},{1,2},{2,1},{3,4},{4,3},{5,6},{6,5},{7,8},{8,7},{9,10},{10,... | collective-permute-start | bytes 36872 | tf_op jit(solution)/shard_map/ppermute | solution.py:77
  24.4 5.1 %collective-permute-start.11 = (bf16[48,128]{1,0:T(8,128)(2,1)S(1)}, bf16[48,128]{1,0:T(8,128)(2,1)S(1)}, u32[]{:S(2)}, u32[]{:S(2)}) collective-permute-start(bf16[48,128]{1,0:T(8,128)(2,1)S(1)} %get-tuple-element.113), channel_id=1, source_target_pairs={{0,1},{1,0},{2,3},{3,2},{4,5},{5,4},{6,7},{7,6},{8,9},{9,8},{10,11... | collective-permute-start | bytes 36872 | tf_op jit(solution)/shard_map/ppermute | solution.py:77
  30.9 1.6 %collective-permute-start.12 = (bf16[1152,128]{1,0:T(8,128)(2,1)S(1)}, bf16[1152,128]{1,0:T(8,128)(2,1)S(1)}, u32[]{:S(2)}, u32[]{:S(2)}) collective-permute-start(bf16[1152,128]{1,0:T(8,128)(2,1)S(1)} %bitcast.20), channel_id=1, source_target_pairs={{0,1},{1,0},{2,3},{3,2},{4,5},{5,4},{6,7},{7,6},{8,9},{9,8},{10,11... | collective-permute-start | bytes 884744 | tf_op jit(solution)/shard_map/ppermute | solution.py:479
  32.6 5.8 %collective-permute-start.13 = (bf16[288,128]{1,0:T(8,128)(2,1)S(1)}, bf16[288,128]{1,0:T(8,128)(2,1)S(1)}, u32[]{:S(2)}, u32[]{:S(2)}) collective-permute-start(bf16[288,128]{1,0:T(8,128)(2,1)S(1)} %get-tuple-element.150), channel_id=1, source_target_pairs={{0,18},{1,19},{2,16},{3,17},{4,22},{5,23},{6,20},{7,21},{8,26},{9,... | collective-permute-start | bytes 221192 | tf_op jit(solution)/shard_map/ppermute | solution.py:479
  32.7 5.7 %collective-permute-start.14 = (bf16[288,128]{1,0:T(8,128)(2,1)S(1)}, bf16[288,128]{1,0:T(8,128)(2,1)S(1)}, u32[]{:S(2)}, u32[]{:S(2)}) collective-permute-start(bf16[288,128]{1,0:T(8,128)(2,1)S(1)} %get-tuple-element.151), channel_id=1, source_target_pairs={{0,16},{1,17},{2,18},{3,19},{4,20},{5,21},{6,22},{7,23},{8,24},{9,... | collective-permute-start | bytes 221192 | tf_op jit(solution)/shard_map/ppermute | solution.py:479
  34.2 5.2 %collective-permute-start.15 = (bf16[288,128]{1,0:T(8,128)(2,1)S(1)}, bf16[288,128]{1,0:T(8,128)(2,1)S(1)}, u32[]{:S(2)}, u32[]{:S(2)}) collective-permute-start(bf16[288,128]{1,0:T(8,128)(2,1)S(1)} %get-tuple-element.152), channel_id=1, source_target_pairs={{0,2},{1,3},{2,0},{3,1},{4,6},{5,7},{6,4},{7,5},{8,10},{9,11},{10,... | collective-permute-start | bytes 221192 | tf_op jit(solution)/shard_map/ppermute | solution.py:479
  39.5 8.6 %collective-permute-start.16 = (bf16[336,128]{1,0:T(8,128)(2,1)S(1)}, bf16[336,128]{1,0:T(8,128)(2,1)S(1)}, u32[]{:S(2)}, u32[]{:S(2)}) collective-permute-start(bf16[336,128]{1,0:T(8,128)(2,1)S(1)} %get-tuple-element.160), channel_id=1, source_target_pairs={{0,12},{1,13},{2,14},{3,15},{4,8},{5,9},{6,10},{7,11},{8,4},{9,5},... | collective-permute-start | bytes 258056 | tf_op jit(solution)/shard_map/ppermute | solution.py:479
  40.6 7.6 %collective-permute-start.18 = (bf16[336,128]{1,0:T(8,128)(2,1)S(1)}, bf16[336,128]{1,0:T(8,128)(2,1)S(1)}, u32[]{:S(2)}, u32[]{:S(2)}) collective-permute-start(bf16[336,128]{1,0:T(8,128)(2,1)S(1)} %get-tuple-element.161), channel_id=1, source_target_pairs={{0,4},{1,5},{2,6},{3,7},{4,0},{5,1},{6,2},{7,3},{8,12},{9,13},{10,... | collective-permute-start | bytes 258056 | tf_op jit(solution)/shard_map/ppermute | solution.py:479
  40.6 7.5 %collective-permute-start.17 = (bf16[288,128]{1,0:T(8,128)(2,1)S(1)}, bf16[288,128]{1,0:T(8,128)(2,1)S(1)}, u32[]{:S(2)}, u32[]{:S(2)}) collective-permute-start(bf16[288,128]{1,0:T(8,128)(2,1)S(1)} %get-tuple-element.159.base), channel_id=1, source_target_pairs={{0,8},{1,9},{2,10},{3,11},{4,12},{5,13},{6,14},{7,15},{8,0},{9,1},... | collective-permute-start | bytes 221192 | tf_op jit(solution)/shard_map/ppermute | solution.py:479
  43.9 5.8 %collective-permute-start.19 = (bf16[48,128]{1,0:T(8,128)(2,1)S(1)}, bf16[48,128]{1,0:T(8,128)(2,1)S(1)}, u32[]{:S(2)}, u32[]{:S(2)}) collective-permute-start(bf16[48,128]{1,0:T(8,128)(2,1)S(1)} %get-tuple-element.165), channel_id=1, source_target_pairs={{0,15},{1,2},{2,1},{3,4},{4,3},{5,6},{6,5},{7,8},{8,7},{9,10},{10,... | collective-permute-start | bytes 36872 | tf_op jit(solution)/shard_map/ppermute | solution.py:553
  44.0 5.7 %collective-permute-start.20 = (bf16[48,128]{1,0:T(8,128)(2,1)S(1)}, bf16[48,128]{1,0:T(8,128)(2,1)S(1)}, u32[]{:S(2)}, u32[]{:S(2)}) collective-permute-start(bf16[48,128]{1,0:T(8,128)(2,1)S(1)} %get-tuple-element.166), channel_id=1, source_target_pairs={{0,1},{1,0},{2,3},{3,2},{4,5},{5,4},{6,7},{7,6},{8,9},{9,8},{10,11... | collective-permute-start | bytes 36872 | tf_op jit(solution)/shard_map/ppermute | solution.py:553
  49.8 5.3 %collective-permute-start.26 = (bf16[288,128]{1,0:T(8,128)(2,1)S(1)}, bf16[288,128]{1,0:T(8,128)(2,1)S(1)}, u32[]{:S(2)}, u32[]{:S(2)}) collective-permute-start(bf16[288,128]{1,0:T(8,128)(2,1)S(1)} %get-tuple-element.167.refs_0_), channel_id=1, source_target_pairs={{0,18},{1,19},{2,16},{3,17},{4,22},{5,23},{6,20},{7,21},{8,26},{9,... | collective-permute-start | bytes 221192 | tf_op jit(solution)/shard_map/ppermute | solution.py:479
  49.9 5.2 %collective-permute-start.24 = (bf16[288,128]{1,0:T(8,128)(2,1)S(1)}, bf16[288,128]{1,0:T(8,128)(2,1)S(1)}, u32[]{:S(2)}, u32[]{:S(2)}) collective-permute-start(bf16[288,128]{1,0:T(8,128)(2,1)S(1)} %get-tuple-element.167.refs_0_), channel_id=1, source_target_pairs={{0,16},{1,17},{2,18},{3,19},{4,20},{5,21},{6,22},{7,23},{8,24},{9,... | collective-permute-start | bytes 221192 | tf_op jit(solution)/shard_map/ppermute | solution.py:479
  51.2 4.5 %collective-permute-start.22 = (bf16[288,128]{1,0:T(8,128)(2,1)S(1)}, bf16[288,128]{1,0:T(8,128)(2,1)S(1)}, u32[]{:S(2)}, u32[]{:S(2)}) collective-permute-start(bf16[288,128]{1,0:T(8,128)(2,1)S(1)} %get-tuple-element.167.refs_0_), channel_id=1, source_target_pairs={{0,2},{1,3},{2,0},{3,1},{4,6},{5,7},{6,4},{7,5},{8,10},{9,11},{10,... | collective-permute-start | bytes 221192 | tf_op jit(solution)/shard_map/ppermute | solution.py:479
  53.2 3.5 %collective-permute-start.21 = (bf16[288,128]{1,0:T(8,128)(2,1)S(1)}, bf16[288,128]{1,0:T(8,128)(2,1)S(1)}, u32[]{:S(2)}, u32[]{:S(2)}) collective-permute-start(bf16[288,128]{1,0:T(8,128)(2,1)S(1)} %get-tuple-element.167.refs_0_), channel_id=1, source_target_pairs={{0,1},{1,0},{2,3},{3,2},{4,5},{5,4},{6,7},{7,6},{8,9},{9,8},{10,11... | collective-permute-start | bytes 221192 | tf_op jit(solution)/shard_map/ppermute | solution.py:479
  55.0 1.7 %collective-permute-start.27 = (bf16[288,128]{1,0:T(8,128)(2,1)S(1)}, bf16[288,128]{1,0:T(8,128)(2,1)S(1)}, u32[]{:S(2)}, u32[]{:S(2)}) collective-permute-start(bf16[288,128]{1,0:T(8,128)(2,1)S(1)} %collective-permute-done.26.refs_3_), channel_id=1, source_target_pairs={{0,1},{1,0},{2,3},{3,2},{4,5},{5,4},{6,7},{7,6},{8,9},{9,8},{10,11... | collective-permute-start | bytes 221192 | tf_op jit(solution)/shard_map/ppermute | solution.py:479
  55.1 1.7 %collective-permute-start.25 = (bf16[288,128]{1,0:T(8,128)(2,1)S(1)}, bf16[288,128]{1,0:T(8,128)(2,1)S(1)}, u32[]{:S(2)}, u32[]{:S(2)}) collective-permute-start(bf16[288,128]{1,0:T(8,128)(2,1)S(1)} %collective-permute-done.24.refs_2_), channel_id=1, source_target_pairs={{0,1},{1,0},{2,3},{3,2},{4,5},{5,4},{6,7},{7,6},{8,9},{9,8},{10,11... | collective-permute-start | bytes 221192 | tf_op jit(solution)/shard_map/ppermute | solution.py:479
  55.8 1.3 %collective-permute-start.23 = (bf16[288,128]{1,0:T(8,128)(2,1)S(1)}, bf16[288,128]{1,0:T(8,128)(2,1)S(1)}, u32[]{:S(2)}, u32[]{:S(2)}) collective-permute-start(bf16[288,128]{1,0:T(8,128)(2,1)S(1)} %collective-permute-done.22.refs_1_), channel_id=1, source_target_pairs={{0,1},{1,0},{2,3},{3,2},{4,5},{5,4},{6,7},{7,6},{8,9},{9,8},{10,11... | collective-permute-start | bytes 221192 | tf_op jit(solution)/shard_map/ppermute | solution.py:479

commit v6 on v5

--- a/solution.py
+++ b/solution.py
@@ -40,26 +40,43 @@
         turn = jnp.where((side >= 2) == (back >= 2), 1, 0)
         found[k] = jnp.full(found.shape[1:], side, jnp.int32)
         found[4 + k] = jnp.full(found.shape[1:], turn, jnp.int32)
+        found[8 + k] = jnp.full(found.shape[1:], back, jnp.int32)
+
+
+def masked(found, block):
+    wide = jnp.concatenate([found] * (block.shape[-1] // found.shape[-1]), axis=1)
+    return wide[None]
+
+
+def choose(found, strips):
+    _, size, c = strips.shape
+    chosen = strips[0].reshape(size // 8, 8, c)
+    for s in range(1, 4):
+        here = masked(found, chosen) == s
+        chosen = jnp.where(here, strips[s].reshape(chosen.shape), chosen)
+    return chosen.reshape(size, c)
 
 
 def send_strips(found, strips, outs):
-    _, size, c = strips.shape
+    _, size, lanes = strips.shape
+    c = outs[0].shape[-1]
     at_row = lax.broadcasted_iota(jnp.int32, (size, size), 0)
     at_col = lax.broadcasted_iota(jnp.int32, (size, size), 1)
     for k, out in enumerate(outs):
         turn = found[4 + k][0:1, 0:size] == 1
         order = (at_col == jnp.where(turn, size - 1 - at_row, at_row)).astype(f32).astype(bf16)
-        side = found[k][None]
-        chosen = jnp.zeros((size // 8, 8, c), f32)
-        for s in range(4):
-            chosen = jnp.where(side == s, strips[s].reshape(chosen.shape), chosen)
-        chosen = chosen.reshape(size, c).astype(bf16)
-        out[...] = jnp.dot(order, chosen, preferred_element_type=f32).astype(bf16)
-
-
-def take_strips(found, received, strips):
+        chosen = choose(found[k], strips).astype(bf16)
+        turned = jnp.dot(order, chosen, preferred_element_type=f32).astype(bf16)
+        for part in range(lanes // c):
+            out[part * size : (part + 1) * size] = turned[:, part * c : (part + 1) * c]
+
+
+def take_strips(found, received, strips, last=False):
     _, size, c = strips.shape
-    blocks = [block[...].astype(f32).reshape(size // 8, 8, c) for block in received]
+    blocks = []
+    for block in received:
+        row = block.shape[0] - size if last else 0
+        blocks.append(block[row : row + size].astype(f32).reshape(size // 8, 8, c))
     for s in range(4):
         taken = blocks[0]
         for k in range(1, 4):
@@ -225,6 +242,75 @@
     return windows
 
 
+def rim_ends(strips, rooms, ends):
+    size = strips.shape[1]
+    last = size - 1
+    ne, nw = rooms[0, 8 + size : 9 + size, :], rooms[0, 7:8, :]
+    se, sw = rooms[2, 8 + size : 9 + size, :], rooms[2, 7:8, :]
+    across = lambda at: (strips[3, at : at + 1, :], strips[1, at : at + 1, :])
+    along = lambda at: (strips[0, at : at + 1, :], strips[2, at : at + 1, :])
+    ends[...] = jnp.zeros_like(ends)
+    for side, rows in enumerate(
+        (
+            ((nw, ne), across(0), across(1)),
+            ((ne, se), along(last), along(last - 1)),
+            ((sw, se), across(last), across(last - 1)),
+            ((nw, sw), along(0), along(1)),
+        )
+    ):
+        for depth, (before, after) in enumerate(rows):
+            for turned, pair in enumerate(((before, after), (after, before))):
+                ends[side, turned, 2 * depth : 2 * depth + 1, :] = pair[0]
+                ends[side, turned, 2 * depth + 1 : 2 * depth + 2, :] = pair[1]
+
+
+def rim_weight_grad(found, own, near, carried, grads, room, out):
+    _, size, c = own.shape
+    windows, deltas = [], []
+    for k in range(4):
+        ends = carried[k][2 * size :].astype(f32)
+        rows = (
+            choose(found[k], own),
+            near[k][0:size].astype(f32),
+            near[k][size : 2 * size].astype(f32),
+        )
+        for depth, row in enumerate(rows):
+            room[depth, 7:8, :] = ends[2 * depth : 2 * depth + 1]
+            room[depth, 8 : 8 + size, :] = row
+            room[depth, 8 + size : 9 + size, :] = ends[2 * depth + 1 : 2 * depth + 2]
+        part = [
+            [room[d, 7 + b : 7 + b + size, :].reshape(size // 8, 8, c) for b in range(3)]
+            for d in range(3)
+        ]
+        turned = found[4 + k][None] == 1
+        back = found[8 + k][None]
+        swap = lambda here, one, two: (jnp.where(here, two, one), jnp.where(here, one, two))
+        for d in range(3):
+            part[d][0], part[d][2] = swap(turned, part[d][0], part[d][2])
+        for b in range(3):
+            inward = (back == 1) | (back == 2)
+            part[0][b], part[2][b] = swap(inward, part[0][b], part[2][b])
+        for a, b in ((0, 1), (0, 2), (1, 2)):
+            upright = (back & 1) == 1
+            part[a][b], part[b][a] = swap(upright, part[a][b], part[b][a])
+        windows.append(
+            jnp.concatenate(
+                [part[a][b].reshape(size, c).astype(bf16) for a in range(3) for b in range(3)],
+                axis=1,
+            )
+        )
+        delta = choose(found[k], grads).astype(bf16).astype(f32)
+        deltas.append((delta * carried[k][size : 2 * size].astype(f32)).astype(bf16))
+    term = lax.dot_general(
+        jnp.concatenate(windows, axis=0),
+        jnp.concatenate(deltas, axis=0),
+        TN,
+        preferred_element_type=f32,
+    )
+    for tap in range(9):
+        out[tap] += term[tap * c : (tap + 1) * c]
+
+
 side_taps = ((0, 1, 2), (2, 5, 8), (6, 7, 8), (0, 3, 6))
 
 
@@ -270,13 +356,13 @@
 
 
 def first_strips(cols, table, block, weight, *refs):
-    outs, found, held, held_weight = refs[:4], *refs[4:7]
-    strips, columns, rows, near, arrived = refs[7:12]
-    size = block.shape[0]
+    outs, found, held, held_weight, own = refs[:4], *refs[4:8]
+    strips, columns, rows, near, arrived = refs[8:13]
+    size, c = own.shape[1:]
     pairs = [
         (table, near),
-        (block.at[0], rows.at[0]),
-        (block.at[size - 1], rows.at[1]),
+        (block.at[pl.ds(0, 2)], rows.at[0]),
+        (block.at[pl.ds(size - 2, 2)], rows.at[1]),
         (block.at[:, pl.ds(0, 16), :], columns.at[0]),
         (block.at[:, pl.ds(size - 16, 16), :], columns.at[1]),
         (block, held),
@@ -292,10 +378,16 @@
     write_links(near, cols, found)
     for copy in copies[1:5]:
         copy.wait()
-    strips[0] = rows[0].astype(f32)
-    strips[2] = rows[1].astype(f32)
-    strips[3] = columns[0].astype(f32)[:, 0, :]
-    strips[1] = columns[1].astype(f32)[:, 15, :]
+    left, right = columns[0].astype(f32), columns[1].astype(f32)
+    for side, edge, second in (
+        (0, rows[0, 0].astype(f32), rows[0, 1].astype(f32)),
+        (1, right[:, 15, :], right[:, 14, :]),
+        (2, rows[1, 1].astype(f32), rows[1, 0].astype(f32)),
+        (3, left[:, 0, :], left[:, 1, :]),
+    ):
+        own[side] = edge
+        strips[side, :, 0:c] = edge
+        strips[side, :, c:] = second
     send_strips(found, strips, outs)
     for copy in copies[5:]:
         copy.wait()
@@ -318,7 +410,8 @@
 def first_edges(found, *refs):
     received, weight, blocks = refs[:4], refs[4], refs[5:9]
     outs, hidden, slope, halo = refs[9:13], refs[13:17], refs[17:21], refs[21]
-    rooms, strips, long = refs[22:28], refs[28], refs[29]
+    rooms, strips, long, ends, narrow = refs[22:28], *refs[28:32]
+    size, c = halo.shape[1:]
     take_strips(found, received, halo)
     terms = halo_terms(halo_windows(halo, long), weight)
     edges = add_strips(load_edges(*blocks), terms, rooms)
@@ -327,8 +420,16 @@
     for k in range(4):
         hidden[k][...] = values[k]
         slope[k][...] = both[k][1]
-    edge_strips(values, strips)
+    for k, edges in enumerate((values, [rate for _, rate in both])):
+        edge_strips(edges, narrow)
+        strips[:, :, k * c : (k + 1) * c] = narrow[...]
+    rim_ends(halo, long, ends)
     send_strips(found, strips, outs)
+    for k, out in enumerate(outs):
+        straight = choose(found[k], ends.at[:, 0])
+        turned = choose(found[k], ends.at[:, 1])
+        here = jnp.concatenate([found[4 + k]] * 2, axis=0) == 1
+        out[2 * size :] = jnp.where(here, turned, straight).astype(bf16)
 
 
 def second_bulk(hidden, left, right, top, bottom, weight, cotangent, *refs):
@@ -349,8 +450,8 @@
 
 def second_edges(found, *refs):
     received, weight, blocks, wanted = refs[:4], refs[4], refs[5:9], refs[9:13]
-    outs, out_field, delta, halo = refs[13:17], refs[17:21], refs[21:25], refs[25]
-    rooms, strips, long, grads = refs[26:32], refs[32], refs[33], refs[34]
+    outs, out_field, delta, halo, grads = refs[13:17], refs[17:21], refs[21:25], *refs[25:27]
+    rooms, strips, long = refs[27:33], refs[33], refs[34]
     half, depth = blocks[0].shape[:2]
     take_strips(found, received, halo)
     terms = halo_terms(halo_windows(halo, long), weight)
@@ -389,22 +490,19 @@
         delta_first[i] = (grad_hidden[i] * bulk_slope[i].astype(f32)).astype(bf16)
 
 
-def first_back(found, *refs):
-    received, blocks, slope, bulk_delta = refs[:4], refs[4:8], refs[8:12], refs[12]
-    halo, shifted, other_grad = refs[13:16]
-    delta, edges_out, kept, given = refs[16], refs[17:21], refs[21], refs[22]
-    rooms, strips, long, back, pairs, grad_weight = refs[23:29], *refs[29:34]
-    take_strips(found, received, back)
-    edges = add_strips(load_edges(*blocks), [back[s] for s in range(4)], rooms)
-    deltas = exact([edge * rate[...] for edge, rate in zip(edges, slope)])
-    for k in range(4):
-        edges_out[k][...] = deltas[k]
-    edge_strips(deltas, strips)
+def first_grads(found, *refs):
+    blocks, slope, bulk_delta, halo, shifted, other_grad = refs[:4], refs[4:8], *refs[8:12]
+    own, near, carried, grads = refs[12], refs[13:17], refs[17:21], refs[21]
+    delta, kept, given = refs[22:25]
+    pairs, strips, long, grad_weight, room = refs[25:30]
+    edges = [edge * rate[...] for edge, rate in zip(load_edges(*blocks), slope)]
     pairs[...] = bulk_delta[...].astype(f32)
-    lay_edges(pairs, *deltas)
+    lay_edges(pairs, *edges)
     delta[...] = pairs[...].astype(bf16)
     bulk_weight_grad(shifted, delta, grad_weight)
+    edge_strips(edges, strips)
     halo_weight_grad(halo_windows(halo, long), strips, grad_weight)
+    rim_weight_grad(found, own, near, carried, grads, room, grad_weight)
     core = lax.axis_index("tile") & 1
     for tap in range(grad_weight.shape[0]):
         one, two = grad_weight[tap], other_grad[tap]
@@ -412,16 +510,23 @@
         given[tap] = jnp.where(core == 0, two, one).astype(bf16)
 
 
-def first_returns(found, *refs):
-    edges, weight, outs = refs[:4], refs[4], refs[5:9]
-    strips, long, grads = refs[9:12]
-    edge_strips([edge[...] for edge in edges], strips)
+def first_back(found, *refs):
+    received, weight, blocks, slope = refs[:4], refs[4], refs[5:9], refs[9:13]
+    outs, delta = refs[13:17], refs[17:21]
+    rooms, strips, long, grads, back = refs[21:27], *refs[27:31]
+    take_strips(found, received, back, True)
+    edges = add_strips(load_edges(*blocks), [back[s] for s in range(4)], rooms)
+    deltas = exact([edge * rate[...] for edge, rate in zip(edges, slope)])
+    for k in range(4):
+        delta[k][...] = deltas[k]
+    edge_strips(deltas, strips)
     halo_grads(strips, weight, long, grads)
     send_strips(found, grads, outs)
 
 
 def last_bulk(delta, weight, bulk_out, *refs):
-    out_edges, interior, out_field, pairs, moved, lower, upper = refs[:4], *refs[4:10]
+    delta_edges, out_edges, interior, out_field = refs[:4], refs[4:8], *refs[8:10]
+    pairs, moved, lower, upper = refs[10:14]
     count, size, lanes = pairs.shape
     c = lanes // 2
     pairs[...] = bulk_out[...].astype(f32)
@@ -430,6 +535,7 @@
         out_field[2 * i] = pairs[i, :, 0:c].astype(bf16)
         out_field[2 * i + 1] = pairs[i, :, c:].astype(bf16)
     pairs[...] = delta[...].astype(f32)
+    lay_edges(pairs, *delta_edges)
     fill_columns(moved, pairs)
     bulk_conv(moved, weight, lower, upper, interior, True)
 
@@ -439,7 +545,7 @@
     rooms, back, pairs = refs[6:12], refs[12], refs[13]
     count, size, lanes = interior.shape
     c = lanes // 2
-    take_strips(found, received, back)
+    take_strips(found, received, back, True)
     edges = (
         interior[:, 0:8, :],
         interior[:, size - 8 :, :],
@@ -480,22 +586,27 @@
 
 
 def seat_of():
-    return lax.axis_index("ens") * 2 + (lax.axis_index("tile") >> 1 & 1)
-
-
-def share_out(kept, given, own, *sent):
+    return lax.axis_index("tile") >> 2 & 3
+
+
+def share_out(loads, kept, given, *refs):
+    riders, own, sent = refs[: sum(loads)], refs[sum(loads)], refs[sum(loads) + 1 :]
     rows = own.shape[0]
     seat = seat_of()
     quarter = lambda at: pl.ds(pl.multiple_of(at * rows, rows), rows)
     add = lambda at: kept[quarter(at), :] + given[quarter(at), :].astype(f32)
     own[...] = add(seat)
+    taken = 0
     for k, block in enumerate(sent):
-        block[...] = add(seat ^ (3, 2, 1)[k]).astype(bf16)
+        block[0:rows] = add(seat ^ (3 - k)).astype(bf16)
+        if loads[k]:
+            block[rows:] = riders[taken][...]
+            taken += 1
 
 
 def add_up(count, loads, base, *refs):
-    got, riders = refs[:count], refs[count : count + loads]
-    total, loaded, came = refs[count + loads], refs[count + loads + 1 :][:loads], refs[count + 2 * loads + 1 :]
+    got, riders, total = refs[:count], refs[count : count + loads], refs[count + loads]
+    loaded = refs[count + loads + 1 :]
     rows = base.shape[0]
     terms = [base[...].astype(f32)] + [block[0:rows].astype(f32) for block in got]
     while len(terms) > 1:
@@ -504,67 +615,81 @@
     for block, rider in zip(loaded, riders):
         block[0:rows] = terms[0].astype(bf16)
         block[rows:] = rider[...]
-    for block, place in zip([block for block in got if block.shape[0] > rows], came):
-        place[...] = block[rows:]
-
-
-def summed_part(kept, given, riders, ways, beside):
+
+
+def line_masks():
+    return [12, 8, 4]
+
+
+def aboard(ways):
     tiles = lax.axis_size("tile")
+    line = [tuple(t ^ mask for t in range(tiles)) for mask in line_masks()]
+    return [ways.index(way) if way in ways else None for way in line]
+
+
+def swap_line(blocks, riders, ways):
+    riding = aboard(ways)
+    got = [flip_swap(block, 0, mask) for block, mask in zip(blocks, line_masks())]
+    came = [
+        got[riding.index(k)] if k in riding else lax.ppermute(rider, "tile", list(enumerate(way)))
+        for k, (rider, way) in enumerate(zip(riders, ways))
+    ]
+    return got, came
+
+
+def scatter_line(kept, given, riders, ways):
     rows, lanes = kept.shape[0] // 4, kept.shape[1]
-    groups, bit = [], 4
+    S = jax.ShapeDtypeStruct
+    given, riders = lax.optimization_barrier((flip_swap(given, 0, 1), riders))
+    loads = [k is not None for k in aboard(ways)]
+    taken = [riders[k] for k in aboard(ways) if k is not None]
+    own, *sent = call(
+        functools.partial(share_out, loads),
+        "share_out",
+        [(block, None) for block in (kept, given, *taken)],
+        [S((rows, lanes), f32)]
+        + [S((rows + load * riders[0].shape[0], lanes), bf16) for load in loads],
+        [],
+    )
+    got, came = swap_line(sent, riders, ways)
+    return own, got, came
+
+
+def sum_rest(own, got, riders, ways):
+    tiles = lax.axis_size("tile")
+    groups, bit = [[(1, 2), (1, 0), (0, 2)]], 16
     while bit < tiles:
-        groups.append([3 * bit, 2 * bit, bit] if 2 * bit < tiles else [bit])
+        groups.append([(0, 3 * bit), (0, 2 * bit), (0, bit)] if 2 * bit < tiles else [(0, bit)])
         bit *= 4
     S = jax.ShapeDtypeStruct
-    given, riders = lax.optimization_barrier((flip_swap(given, 0, 1), riders))
-    base, *sent = call(
-        share_out,
-        "share_out",
-        [(kept, None), (given, None)],
-        [S((rows, lanes), f32)] + [S((rows, lanes), bf16)] * 3,
-        [],
-    )
-    got = [flip_swap(block, k >> 1, (k & 1) << 1) for k, block in zip((3, 2, 1), sent)]
-    carried, coming = {}, []
-    for n, masks in enumerate(groups + [[]]):
-        aboard = {}
-        for mask in masks:
-            way = tuple(t ^ mask for t in range(tiles))
-            if way in ways:
-                aboard[mask] = ways.index(way)
-        loads = [riders[k] for k in aboard.values()]
-        found = call(
-            functools.partial(add_up, len(got), len(loads)),
+    riding = aboard(ways)
+    for masks in groups + [None]:
+        taken = [riders[k] for k in riding if k is not None] if masks is None else []
+        own, *loaded = call(
+            functools.partial(add_up, len(got), len(taken)),
             "add_up",
-            [(block, None) for block in (base, *got, *loads)],
-            [S((rows, lanes), bf16)]
-            + [S((rows + load.shape[0], lanes), bf16) for load in loads]
-            + [S(riders[k].shape, bf16) for k in coming],
+            [(block, None) for block in (own, *got, *taken)],
+            [S(own.shape, bf16)]
+            + [S((own.shape[0] + rider.shape[0], own.shape[1]), bf16) for rider in taken],
             [],
         )
-        if n == 0:
-            found, beside = lax.optimization_barrier((found, beside))
-        base, loaded = found[0], dict(zip(aboard, found[1 : 1 + len(loads)]))
-        carried.update(zip(coming, found[1 + len(loads) :]))
-        got = [flip_swap(loaded.get(mask, base), 0, mask) for mask in masks]
-        coming = list(aboard.values())
-    for k, way in enumerate(ways):
-        if k not in carried:
-            carried[k] = lax.ppermute(riders[k], "tile", list(enumerate(way)))
-    return base, [carried[k] for k in range(len(ways))], beside
-
-
-def gather_quarters(part):
-    return [part] + [flip_swap(part, k >> 1, (k & 1) << 1) for k in (1, 2, 3)]
-
-
-def both_grads(*refs):
-    mine, others, first, second = refs[:4], refs[4:8], refs[8], refs[9]
-    rows = mine[0].shape[0]
+        if masks is not None:
+            got = [flip_swap(own, *mask) for mask in masks]
+    return own, [own if k is None else loaded.pop(0) for k in riding]
+
+
+def stack(*refs):
+    rows = refs[0].shape[0]
+    for k in range(4):
+        refs[4][k] = refs[k][0:rows]
+
+
+def both_grads(mine, others, first, second):
+    rows = mine.shape[1]
     core, seat = lax.axis_index("tile") & 1, seat_of()
     for k in range(4):
         place = pl.ds(pl.multiple_of((seat ^ k) * rows, rows), rows)
-        one, two = mine[k][...].astype(f32), others[k][...].astype(f32)
+        one, two = mine[k].astype(f32), others[k].astype(f32)
         first[place, :] = jnp.where(core == 0, one, two)
         second[place, :] = jnp.where(core == 0, two, one)
 
@@ -610,18 +735,20 @@
             (array, pl.BlockSpec((1, size, c), lambda step: (size - 1, 0, 0))),
         ]
 
+    wide = pltpu.VMEM((4, size, 2 * c), f32)
     far = pl.BlockSpec(memory_space=pl.ANY)
     stay = lambda array: (pltpu.with_memory_space_constraint(array, pltpu.HBM), far)
-    *strips, found, block, one = call(
+    *strips, found, block, one, own = call(
         functools.partial(first_strips, cols),
         "first_strips",
         [stay(neighbours.T), stay(block), stay(one)],
-        sent + [S((8, 8, 128), jnp.int32), S(block.shape, bf16), S(one.shape, bf16)],
-        [V(halo), pltpu.VMEM((2, size, 16, c), bf16), pltpu.VMEM((2, size, c), bf16)]
+        [S((2 * size, c), bf16)] * 4
+        + [S((12, 8, 128), jnp.int32), S(block.shape, bf16), S(one.shape, bf16), halo],
+        [wide, pltpu.VMEM((2, size, 16, c), bf16), pltpu.VMEM((2, 2, size, c), bf16)]
         + [pltpu.SMEM(neighbours.shape[::-1], jnp.int32), pltpu.SemaphoreType.DMA((7,))],
     )
     links = (found, None)
-    strips = swap_all(strips, cols)
+    near = swap_all(strips, cols)
     shifted_one, pre_one, hidden, slope = call(
         first_bulk,
         "first_bulk",
@@ -633,12 +760,12 @@
     found = call(
         first_edges,
         "first_edges",
-        [links] + whole(strips) + [(one, None)] + edge_blocks(pre_one),
-        sent + edge + edge + [halo],
-        rooms + [V(halo), long],
+        [links] + whole(near) + [(one, None)] + edge_blocks(pre_one),
+        [S((2 * size + 16, c), bf16)] * 4 + edge + edge + [halo],
+        rooms + [wide, long, pltpu.VMEM((4, 2, 16, c), f32), V(halo)],
     )
     strips, hidden_edges, slope_edges, halo_one = found[:4], found[4:8], found[8:12], found[12]
-    strips = swap_all(strips, cols)
+    carried = swap_all(strips, cols)
     shifted_two, pre_two, out_bulk, delta_bulk = call(
         second_bulk,
         "second_bulk",
@@ -650,53 +777,56 @@
     found = call(
         second_edges,
         "second_edges",
-        [links] + whole(strips) + [(two, None)] + edge_blocks(pre_two) + image_edges(wanted),
-        sent + edge + edge + [halo],
-        rooms + [V(halo), long, V(halo)],
-    )
-    strips, out_edges, delta_edges, halo_two = found[:4], found[4:8], found[8:12], found[12]
-    strips = swap_all(strips, cols)
+        [links] + whole(carried) + [(two, None)] + edge_blocks(pre_two) + image_edges(wanted),
+        sent + edge + edge + [halo, halo],
+        rooms + [V(halo), long],
+    )
+    strips, out_edges, delta_edges, halo_two, grads = found[:4], found[4:8], found[8:12], *found[12:]
     grad_two, grad_hidden, delta_one = call(
         second_back,
         "second_back",
-        whole(
-            [delta_bulk, *delta_edges, halo_two, shifted_two, two, slope]
-        ),
+        whole([delta_bulk, *delta_edges, halo_two, shifted_two, two, slope]),
         [S((9, c, c), f32), pairs(f32), pairs(bf16)],
         [V(pairs(f32)), V(pairs(bf16))] + back + [V(shifted), V(halo), long],
         2 * flops,
     )
+    delta_one, kept, given = call(
+        first_grads,
+        "first_grads",
+        [links]
+        + edge_blocks(grad_hidden)
+        + whole([*slope_edges, delta_one, halo_one, shifted_one, grad_two])
+        + whole([own, *near, *carried, grads]),
+        [pairs(bf16), S((9, c, c), f32), S((9, c, c), bf16)],
+        [V(pairs(f32)), V(halo), long, pltpu.VMEM((9, c, c), f32)]
+        + [pltpu.VMEM((3, size + 16, c), f32)],
+        flops,
+    )
+    ways = routes(cols)
+    quarter, got, strips = scatter_line(
+        kept.reshape(9 * c, c), given.reshape(9 * c, c), strips, ways
+    )
     found = call(
         first_back,
         "first_back",
-        [links]
-        + whole(strips)
-        + edge_blocks(grad_hidden)
-        + whole([*slope_edges, delta_one, halo_one, shifted_one, grad_two]),
-        [pairs(bf16)] + edge + [S((9, c, c), f32), S((9, c, c), bf16)],
-        rooms + [V(halo), long, V(halo), V(pairs(f32)), pltpu.VMEM((9, c, c), f32)],
-        flops,
-    )
-    delta_one, delta_edges, kept, given = found[0], found[1:5], *found[5:]
-    strips = call(
-        first_returns,
-        "first_returns",
-        [links] + whole([*delta_edges, one]),
-        sent,
-        [V(halo), long, V(halo)],
-    )
+        [links] + whole(strips) + [(one, None)] + edge_blocks(grad_hidden) + whole(slope_edges),
+        sent + edge,
+        rooms + [V(halo), long, V(halo), V(halo)],
+    )
+    strips, delta_edges = found[:4], found[4:8]
     interior, out_field = call(
         last_bulk,
         "last_bulk",
-        whole([delta_one, one, out_bulk, *out_edges]),
+        whole([delta_one, one, out_bulk, *delta_edges, *out_edges]),
         [pairs(f32), S(block.shape, bf16)],
         [V(pairs(f32)), V(shifted)] + back,
         flops,
     )
-    part, strips, interior = summed_part(
-        kept.reshape(9 * c, c), given.reshape(9 * c, c), strips, routes(cols), interior
-    )
-    part, strips = lax.optimization_barrier((part, strips))
+    quarter, blocks = sum_rest(quarter, got, strips, ways)
+    quarter, blocks, strips, interior = lax.optimization_barrier(
+        (quarter, blocks, strips, interior)
+    )
+    got, strips = lax.optimization_barrier(swap_line(blocks, strips, ways))
     (grad_block,) = call(
         last_edges,
         "last_edges",
@@ -704,13 +834,13 @@
         [S(block.shape, bf16)],
         rooms + [V(halo), V(pairs(f32))],
     )
-    quarters = gather_quarters(part)
-    others = [flip_swap(quarter, 0, 1) for quarter in quarters]
-    others, grad_block = lax.optimization_barrier((others, grad_block))
+    quarters = [quarter, *got[::-1]]
+    (stacked,) = call(stack, "stack", whole(quarters), [S((4, *quarter.shape), bf16)], [])
+    others, grad_block = lax.optimization_barrier((flip_swap(stacked, 0, 1), grad_block))
     grads = call(
         both_grads,
         "both_grads",
-        whole([*quarters, *others]),
+        whole([stacked, others]),
         [S((9 * c, c), f32)] * 2,
         [],
     )

time: 58.3 us -> 58.1 us (level)
  starting transfers between devices: 26.1 us -> 24.5 us
  waiting for transfers between devices: 16.5 us -> 17.5 us
    ppermute x12 -> x8, starting transfers between devices: 12.9 us -> 9.24 us  [swap_all(): lax.ppermute(block, 'tile', list(enumerate(way)))]
    ppermute x2 -> x4, waiting for transfers between devices: 1.55 us -> 4.56 us  [swap_line(): lax.ppermute(rider, 'tile', list(enumerate(way)))]
    ppermute x12 -> x8, waiting for transfers between devices: 7.1 us -> 4.77 us  [swap_all(): lax.ppermute(block, 'tile', list(enumerate(way)))]
    ppermute x2 -> x4, starting transfers between devices: 1.17 us -> 2.63 us  [swap_line(): lax.ppermute(rider, 'tile', list(enumerate(way)))]
    ppermute x14 -> x11, starting transfers between devices: 12 us -> 12.6 us  [flip_swap(): return lax.ppermute(block, ('ens', 'tile'), route)]
    ppermute x14 -> x11, waiting for transfers between devices: 7.85 us -> 8.17 us  [flip_swap(): return lax.ppermute(block, ('ens', 'tile'), route)]
    pallas_call x14 -> x15, Pallas kernels: 14.8 us -> 15.1 us  [call(): pl.pallas_call(kernel, name=name, grid=(1,), in_specs=[spec or whole for...]
  transfers between devices with their start and end apart: 28 -> 23, of which waited for: 15 -> 9; matrix products, arithmetic and copies ran while one was open for 0% -> 0% of each run, Pallas kernels for 16% -> 12%
where the time goes in v6:
time: 58.1 us; the launch traced here: 57.9 us
  starting transfers between devices  24.5 us (42%)
  waiting for transfers between devices  17.5 us (30%)
  Pallas kernels  15.1 us (26%)
  between operations  0.78 us (1%)
    pallas_call x15, Pallas kernels, call(): pl.pallas_call(kernel, name=name, grid=(1,), in_specs=[spec or whole for...  15.1 us
    ppermute x11, starting transfers between devices, flip_swap(): return lax.ppermute(block, ('ens', 'tile'), route)  12.6 us
    ppermute x8, starting transfers between devices, swap_all(): lax.ppermute(block, 'tile', list(enumerate(way)))  9.24 us
    ppermute x11, waiting for transfers between devices, flip_swap(): return lax.ppermute(block, ('ens', 'tile'), route)  8.17 us
    ppermute x8, waiting for transfers between devices, swap_all(): lax.ppermute(block, 'tile', list(enumerate(way)))  4.77 us
    ppermute x4, waiting for transfers between devices, swap_line(): lax.ppermute(rider, 'tile', list(enumerate(way)))  4.56 us
    ppermute x4, starting transfers between devices, swap_line(): lax.ppermute(rider, 'tile', list(enumerate(way)))  2.63 us
  transfers between devices with their start and end apart: 23, of which 9 were waited for; matrix products, arithmetic and copies ran while one was open for 0% of the time, Pallas kernels for 12%

profile of v6, /device:TPU:0, one launch (start us, length us, event | category | flops | bytes accessed | tf_op | source)
XLA Modules:
  0.0 57.9 jit_solution(14271430058185831002)
XLA Ops:
  0.6 1.4 %first_strips.1 = (bf16[96,128]{1,0:T(8,128)(2,1)S(1)}, bf16[96,128]{1,0:T(8,128)(2,1)S(1)}, bf16[96,128]{1,0:T(8,128)(2,1)S(1)}, bf16[96,128]{1,0:T(8,128)(2,1)...) custom-call(s32[4,16]{1,0:T(4,128)} %bitcast.24, ...), custom_call_target="tpu_custom_call" | custom-call | bytes 2097152 | tf_op jit(solution)/shard_map/first_strips/pallas_call | solution.py:565
  2.1 5.1 %collective-permute-start = (bf16[96,128]{1,0:T(8,128)(2,1)S(1)}, bf16[96,128]{1,0:T(8,128)(2,1)S(1)}, u32[]{:S(2)}, u32[]{:S(2)}) collective-permute-start(bf16[96,128]{1,0:T(8,128)(2,1)S(1)} %get-tuple-element.97), channel_id=1, source_target_pairs={{0,12},{1,13},{2,14},{3,15},{4,8},{5,9},{6,10},{7,11},{8,4},{9,5},... | collective-permute-start | bytes 73736 | tf_op jit(solution)/shard_map/ppermute | solution.py:94
  7.2 0.0 collective-permute-start.1
  7.2 0.7 %collective-permute-start.2 = (bf16[96,128]{1,0:T(8,128)(2,1)S(1)}, bf16[96,128]{1,0:T(8,128)(2,1)S(1)}, u32[]{:S(2)}, u32[]{:S(2)}) collective-permute-start(bf16[96,128]{1,0:T(8,128)(2,1)S(1)} %get-tuple-element.99), channel_id=1, source_target_pairs={{0,15},{1,2},{2,1},{3,4},{4,3},{5,6},{6,5},{7,8},{8,7},{9,10},{10,... | collective-permute-start | bytes 73736 | tf_op jit(solution)/shard_map/ppermute | solution.py:94
  7.9 0.9 %collective-permute-start.3 = (bf16[96,128]{1,0:T(8,128)(2,1)S(1)}, bf16[96,128]{1,0:T(8,128)(2,1)S(1)}, u32[]{:S(2)}, u32[]{:S(2)}) collective-permute-start(bf16[96,128]{1,0:T(8,128)(2,1)S(1)} %get-tuple-element.100), channel_id=1, source_target_pairs={{0,1},{1,0},{2,3},{3,2},{4,5},{5,4},{6,7},{7,6},{8,9},{9,8},{10,11... | collective-permute-start | bytes 73736 | tf_op jit(solution)/shard_map/ppermute | solution.py:94
  8.8 1.7 %first_bulk.1 = (bf16[1200,768]{1,0:T(8,128)(2,1)S(1)}, f32[24,48,256]{2,1,0:T(8,128)S(1)}, bf16[24,48,256]{2,1,0:T(8,128)(2,1)S(1)}, bf16[24,48,256]{2,1,0:T(8,128)(2,1)S(1)}) custom-call(bf16[48,48,128]{2,1,0:T(8,128)(2,1)S(1)} %get-tuple-element.94.block, bf16[9,128,128]{2,1,0:T(8,128)(2,1)S(1)} %get-tuple-element.95.weight.refs_4_), custom_call_target="tpu_custom_call" | custom-call | flops 679477248 | bytes 2097152 | tf_op jit(solution)/shard_map/first_bulk/pallas_call | solution.py:565
  10.5 0.5 collective-permute-done.1.refs_1_.refs_14_
  11.0 2.1 %collective-permute-done.2.refs_2_.refs_15_ = bf16[96,128]{1,0:T(8,128)(2,1)S(1)} collective-permute-done((bf16[96,128]{1,0:T(8,128)(2,1)S(1)}, bf16[96,128]{1,0:T(8,128)(2,1)S(1)}, u32[]{:S(2)}, u32[]{:S(2)}) %collective-permute-start.2) | collective-permute-done | bytes 24608 | tf_op jit(solution)/shard_map/ppermute | solution.py:94
  13.1 0.7 %first_edges.1 = (bf16[112,128]{1,0:T(8,128)(2,1)S(1)}, bf16[112,128]{1,0:T(8,128)(2,1)S(1)}, bf16[112,128]{1,0:T(8,128)(2,1)S(1)}, bf16[112,128]{1,0:T(8,128)(2...) custom-call(s32[12,8,128]{2,1,0:T(8,128)S(1)} %get-tuple-element.93., ...), custom_call_target="tpu_custom_call" | custom-call | bytes 2097152 | tf_op jit(solution)/shard_map/first_edges/pallas_call | solution.py:565
  13.8 0.1 collective-permute-start.4
  13.9 0.3 collective-permute-start.5
  14.2 2.1 %collective-permute-start.6 = (bf16[112,128]{1,0:T(8,128)(2,1)S(1)}, bf16[112,128]{1,0:T(8,128)(2,1)S(1)}, u32[]{:S(2)}, u32[]{:S(2)}) collective-permute-start(bf16[112,128]{1,0:T(8,128)(2,1)S(1)} %get-tuple-element.109), channel_id=1, source_target_pairs={{0,15},{1,2},{2,1},{3,4},{4,3},{5,6},{6,5},{7,8},{8,7},{9,10},{10,... | collective-permute-start | bytes 86024 | tf_op jit(solution)/shard_map/ppermute | solution.py:94
  16.3 1.7 %second_bulk.1 = (bf16[1200,768]{1,0:T(8,128)(2,1)S(1)}, f32[24,48,256]{2,1,0:T(8,128)S(1)}, bf16[24,48,256]{2,1,0:T(8,128)(2,1)S(1)}, bf16[24,48,256]{2,1,0:T(8,128)(2,1)S(1)}) custom-call(bf16[24,48,256]{2,1,0:T(8,128)(2,1)S(1)} %get-tuple-element.96.hidden, f32[24,8,256]{2,1,0:T(8,128)S(1)} %get-tuple-element.102.left, ...), custom_call_target="tpu_custom_call" | custom-call | flops 679477248 | bytes 2097152 | tf_op jit(solution)/shard_map/second_bulk/pallas_call | solution.py:565
  18.0 1.5 %collective-permute-done.4.refs_0_.refs_17_ = bf16[112,128]{1,0:T(8,128)(2,1)S(1)} collective-permute-done((bf16[112,128]{1,0:T(8,128)(2,1)S(1)}, bf16[112,128]{1,0:T(8,128)(2,1)S(1)}, u32[]{:S(2)}, u32[]{:S(2)}) %collective-permute-start.4) | collective-permute-done | bytes 28704 | tf_op jit(solution)/shard_map/ppermute | solution.py:94
  19.6 0.6 %collective-permute-done.6.refs_2_.refs_19_ = bf16[112,128]{1,0:T(8,128)(2,1)S(1)} collective-permute-done((bf16[112,128]{1,0:T(8,128)(2,1)S(1)}, bf16[112,128]{1,0:T(8,128)(2,1)S(1)}, u32[]{:S(2)}, u32[]{:S(2)}) %collective-permute-start.6) | collective-permute-done | bytes 28704 | tf_op jit(solution)/shard_map/ppermute | solution.py:94
  20.2 0.0 collective-permute-done.7.refs_3_.refs_20_
  20.2 0.9 %second_edges.1 = (bf16[48,128]{1,0:T(8,128)(2,1)S(1)}, bf16[48,128]{1,0:T(8,128)(2,1)S(1)}, bf16[48,128]{1,0:T(8,128)(2,1)S(1)}, bf16[48,128]{1,0:T(8,128)(2,1)...) custom-call(s32[12,8,128]{2,1,0:T(8,128)S(1)} %get-tuple-element.93., ...), custom_call_target="tpu_custom_call" | custom-call | bytes 2097152 | tf_op jit(solution)/shard_map/second_edges/pallas_call | solution.py:565
  21.1 2.4 %second_back.1 = (f32[9,128,128]{2,1,0:T(8,128)S(1)}, f32[24,48,256]{2,1,0:T(8,128)S(1)}, bf16[24,48,256]{2,1,0:T(8,128)(2,1)S(1)}) custom-call(bf16[24,48,256]{2,1,0:T(8,128)(2,1)S(1)} %get-tuple-element.106.refs_0_, f32[24,8,256]{2,1,0:T(8,128)S(1)} %get-tuple-element.112.refs_1_, f32[24,8,256]{2,1,0:T(8,128)S(1)} %get-tuple-element.113.refs_2_, ...), custom_call_target="tpu_custom_call" | custom-call | flops 1358954496 | bytes 2097152 | tf_op jit(solution)/shard_map/second_back/pallas_call | solution.py:565
  23.5 1.6 %first_grads.1 = (bf16[24,48,256]{2,1,0:T(8,128)(2,1)S(1)}, f32[9,128,128]{2,1,0:T(8,128)S(1)}, bf16[9,128,128]{2,1,0:T(8,128)(2,1)S(1)}) custom-call(s32[12,8,128]{2,1,0:T(8,128)S(1)} %get-tuple-element.93.found, f32[24,48,256]{2,1,0:T(8,128)S(1)} %get-tuple-element.119.refs_0_.refs_1_.refs_2_.refs_3_.refs_5_.refs_6_.refs_7_.refs_8_, ...), custom_call_target="tpu_custom_call" | custom-call | flops 679477248 | bytes 2097152 | tf_op jit(solution)/shard_map/first_grads/pallas_call | solution.py:565
  25.1 0.1 collective-permute-start.8
  25.2 1.6 %collective-permute-done.8.given = bf16[1152,128]{1,0:T(8,128)(2,1)S(1)} collective-permute-done((bf16[1152,128]{1,0:T(8,128)(2,1)S(1)}, bf16[1152,128]{1,0:T(8,128)(2,1)S(1)}, u32[]{:S(2)}, u32[]{:S(2)}) %collective-permute-start.8) | collective-permute-done | bytes 294944 | tf_op jit(solution)/shard_map/ppermute | solution.py:585
  26.8 0.1 share_out.1
  26.8 1.8 %collective-permute-start.9 = (bf16[336,128]{1,0:T(8,128)(2,1)S(1)}, bf16[336,128]{1,0:T(8,128)(2,1)S(1)}, u32[]{:S(2)}, u32[]{:S(2)}) collective-permute-start(bf16[336,128]{1,0:T(8,128)(2,1)S(1)} %get-tuple-element.141), channel_id=1, source_target_pairs={{0,12},{1,13},{2,14},{3,15},{4,8},{5,9},{6,10},{7,11},{8,4},{9,5},... | collective-permute-start | bytes 258056 | tf_op jit(solution)/shard_map/ppermute | solution.py:585
  28.6 1.1 %collective-permute-start.10 = (bf16[336,128]{1,0:T(8,128)(2,1)S(1)}, bf16[336,128]{1,0:T(8,128)(2,1)S(1)}, u32[]{:S(2)}, u32[]{:S(2)}) collective-permute-start(bf16[336,128]{1,0:T(8,128)(2,1)S(1)} %get-tuple-element.142), channel_id=1, source_target_pairs={{0,4},{1,5},{2,6},{3,7},{4,0},{5,1},{6,2},{7,3},{8,12},{9,13},{10,... | collective-permute-start | bytes 258056 | tf_op jit(solution)/shard_map/ppermute | solution.py:585
  29.7 1.5 %collective-permute-start.13 = (bf16[288,128]{1,0:T(8,128)(2,1)S(1)}, bf16[288,128]{1,0:T(8,128)(2,1)S(1)}, u32[]{:S(2)}, u32[]{:S(2)}) collective-permute-start(bf16[288,128]{1,0:T(8,128)(2,1)S(1)} %get-tuple-element.155), channel_id=1, source_target_pairs={{0,8},{1,9},{2,10},{3,11},{4,12},{5,13},{6,14},{7,15},{8,0},{9,1},... | collective-permute-start | bytes 221192 | tf_op jit(solution)/shard_map/ppermute | solution.py:585
  31.3 1.3 %collective-permute-start.11 = (bf16[48,128]{1,0:T(8,128)(2,1)S(1)}, bf16[48,128]{1,0:T(8,128)(2,1)S(1)}, u32[]{:S(2)}, u32[]{:S(2)}) collective-permute-start(bf16[48,128]{1,0:T(8,128)(2,1)S(1)} %get-tuple-element.143), channel_id=1, source_target_pairs={{0,15},{1,2},{2,1},{3,4},{4,3},{5,6},{6,5},{7,8},{8,7},{9,10},{10,... | collective-permute-start | bytes 36872 | tf_op jit(solution)/shard_map/ppermute | solution.py:634
  32.6 4.5 %collective-permute-done.13.refs_1_ = bf16[288,128]{1,0:T(8,128)(2,1)S(1)} collective-permute-done((bf16[288,128]{1,0:T(8,128)(2,1)S(1)}, bf16[288,128]{1,0:T(8,128)(2,1)S(1)}, u32[]{:S(2)}, u32[]{:S(2)}) %collective-permute-start.13) | collective-permute-done | bytes 73760 | tf_op jit(solution)/shard_map/ppermute | solution.py:585
  37.0 0.0 collective-permute-done.10.refs_1_.refs_2_
  37.1 0.9 %collective-permute-start.16 = (bf16[288,128]{1,0:T(8,128)(2,1)S(1)}, bf16[288,128]{1,0:T(8,128)(2,1)S(1)}, u32[]{:S(2)}, u32[]{:S(2)}) collective-permute-start(bf16[288,128]{1,0:T(8,128)(2,1)S(1)} %add_up.2.base), channel_id=1, source_target_pairs={{0,2},{1,3},{2,0},{3,1},{4,6},{5,7},{6,4},{7,5},{8,10},{9,11},{10,... | collective-permute-start | bytes 221192 | tf_op jit(solution)/shard_map/ppermute | solution.py:585
  37.9 1.5 %collective-permute-start.15 = (bf16[288,128]{1,0:T(8,128)(2,1)S(1)}, bf16[288,128]{1,0:T(8,128)(2,1)S(1)}, u32[]{:S(2)}, u32[]{:S(2)}) collective-permute-start(bf16[288,128]{1,0:T(8,128)(2,1)S(1)} %add_up.2.base), channel_id=1, source_target_pairs={{0,16},{1,17},{2,18},{3,19},{4,20},{5,21},{6,22},{7,23},{8,24},{9,... | collective-permute-start | bytes 221192 | tf_op jit(solution)/shard_map/ppermute | solution.py:585
  39.4 1.2 %collective-permute-start.14 = (bf16[288,128]{1,0:T(8,128)(2,1)S(1)}, bf16[288,128]{1,0:T(8,128)(2,1)S(1)}, u32[]{:S(2)}, u32[]{:S(2)}) collective-permute-start(bf16[288,128]{1,0:T(8,128)(2,1)S(1)} %add_up.2.base), channel_id=1, source_target_pairs={{0,18},{1,19},{2,16},{3,17},{4,22},{5,23},{6,20},{7,21},{8,26},{9,... | collective-permute-start | bytes 221192 | tf_op jit(solution)/shard_map/ppermute | solution.py:585
  40.6 0.0 collective-permute-done.11.refs_2_
  40.6 0.0 collective-permute-done.12.refs_3_
  40.6 0.5 first_back.1
  41.1 2.0 %last_bulk.1 = (f32[24,48,256]{2,1,0:T(8,128)S(1)}, bf16[48,48,128]{2,1,0:T(8,128)(2,1)}) custom-call(bf16[24,48,256]{2,1,0:T(8,128)(2,1)S(1)} %get-tuple-element.130.delta, bf16[9,128,128]{2,1,0:T(8,128)(2,1)S(1)} %get-tuple-element.95.weight.refs_4_, bf16[24,48,256]{2,1,0:T(8,128)(2,1)S(1)} %get-tuple-element.131.bulk_out, ...), custom_call_target="tpu_custom_call" | custom-call | flops 679477248 | bytes 2097152 | tf_op jit(solution)/shard_map/last_bulk/pallas_call | solution.py:565
  43.1 0.0 collective-permute-done.16.refs_2_
  43.1 0.0 collective-permute-done.15.refs_1_
  43.1 1.5 %collective-permute-done.14.refs_0_ = bf16[288,128]{1,0:T(8,128)(2,1)S(1)} collective-permute-done((bf16[288,128]{1,0:T(8,128)(2,1)S(1)}, bf16[288,128]{1,0:T(8,128)(2,1)S(1)}, u32[]{:S(2)}, u32[]{:S(2)}) %collective-permute-start.14) | collective-permute-done | bytes 73760 | tf_op jit(solution)/shard_map/ppermute | solution.py:585
  44.7 2.2 %collective-permute-start.17 = (bf16[336,128]{1,0:T(8,128)(2,1)S(1)}, bf16[336,128]{1,0:T(8,128)(2,1)S(1)}, u32[]{:S(2)}, u32[]{:S(2)}) collective-permute-start(bf16[336,128]{1,0:T(8,128)(2,1)S(1)} %get-tuple-element.165), channel_id=1, source_target_pairs={{0,12},{1,13},{2,14},{3,15},{4,8},{5,9},{6,10},{7,11},{8,4},{9,5},... | collective-permute-start | bytes 258056 | tf_op jit(solution)/shard_map/ppermute | solution.py:585
  46.9 0.0 collective-permute-start.19
  46.9 2.3 %collective-permute-start.18 = (bf16[288,128]{1,0:T(8,128)(2,1)S(1)}, bf16[288,128]{1,0:T(8,128)(2,1)S(1)}, u32[]{:S(2)}, u32[]{:S(2)}) collective-permute-start(bf16[288,128]{1,0:T(8,128)(2,1)S(1)} %get-tuple-element.166.refs_0_), channel_id=1, source_target_pairs={{0,8},{1,9},{2,10},{3,11},{4,12},{5,13},{6,14},{7,15},{8,0},{9,1},... | collective-permute-start | bytes 221192 | tf_op jit(solution)/shard_map/ppermute | solution.py:585
  49.2 0.2 collective-permute-start.20
  49.4 1.1 %collective-permute-start.21 = (bf16[48,128]{1,0:T(8,128)(2,1)S(1)}, bf16[48,128]{1,0:T(8,128)(2,1)S(1)}, u32[]{:S(2)}, u32[]{:S(2)}) collective-permute-start(bf16[48,128]{1,0:T(8,128)(2,1)S(1)} %get-tuple-element.169), channel_id=1, source_target_pairs={{0,1},{1,0},{2,3},{3,2},{4,5},{5,4},{6,7},{7,6},{8,9},{9,8},{10,11... | collective-permute-start | bytes 36872 | tf_op jit(solution)/shard_map/ppermute | solution.py:634
  50.5 4.5 %collective-permute-done.20.refs_2_ = bf16[48,128]{1,0:T(8,128)(2,1)S(1)} collective-permute-done((bf16[48,128]{1,0:T(8,128)(2,1)S(1)}, bf16[48,128]{1,0:T(8,128)(2,1)S(1)}, u32[]{:S(2)}, u32[]{:S(2)}) %collective-permute-start.20) | collective-permute-done | bytes 12320 | tf_op jit(solution)/shard_map/ppermute | solution.py:634
  55.1 0.1 collective-permute-start.22
  55.2 1.0 %last_edges.1 = bf16[48,48,128]{2,1,0:T(8,128)(2,1)} custom-call(s32[12,8,128]{2,1,0:T(8,128)S(1)} %get-tuple-element.93.found, bf16[336,128]{1,0:T(8,128)(2,1)S(1)} %collective-permute-done.17.refs_3_.refs_0_, bf16[336,128]{1,0:T(8,128)(2,1)S(1)} %collective-permute-done.19.refs_1_, bf16[48,128]{1,0:T(8,128)(2,1)S(1)} %collective-permute-done.20.refs_2_, ...), custom_call_target="tpu_custom_call" | custom-call | bytes 2097152 | tf_op jit(solution)/shard_map/last_edges/pallas_call | solution.py:565
  56.2 0.6 %collective-permute-done.22.others = bf16[4,288,128]{2,1,0:T(8,128)(2,1)S(1)} collective-permute-done((bf16[4,288,128]{2,1,0:T(8,128)(2,1)S(1)}, bf16[4,288,128]{2,1,0:T(8,128)(2,1)S(1)}, u32[]{:S(2)}, u32[]{:S(2)}) %collective-permute-start.22) | collective-permute-done | bytes 294944 | tf_op jit(solution)/shard_map/ppermute | solution.py:585
  56.8 1.1 %both_grads.1 = (f32[1152,128]{1,0:T(8,128)}, f32[1152,128]{1,0:T(8,128)}) custom-call(bf16[4,288,128]{2,1,0:T(8,128)(2,1)S(1)} %stack.1.mine, bf16[4,288,128]{2,1,0:T(8,128)(2,1)S(1)} %collective-permute-done.22.others), custom_call_target="tpu_custom_call" | custom-call | bytes 2097152 | tf_op jit(solution)/shard_map/both_grads/pallas_call | solution.py:565
  (17 shorter events, 0.1 us)
Async XLA Ops:
  2.1 8.4 %collective-permute-start = (bf16[96,128]{1,0:T(8,128)(2,1)S(1)}, bf16[96,128]{1,0:T(8,128)(2,1)S(1)}, u32[]{:S(2)}, u32[]{:S(2)}) collective-permute-start(bf16[96,128]{1,0:T(8,128)(2,1)S(1)} %get-tuple-element.97), channel_id=1, source_target_pairs={{0,12},{1,13},{2,14},{3,15},{4,8},{5,9},{6,10},{7,11},{8,4},{9,5},... | collective-permute-start | bytes 73736 | tf_op jit(solution)/shard_map/ppermute | solution.py:94
  7.2 3.8 %collective-permute-start.1 = (bf16[96,128]{1,0:T(8,128)(2,1)S(1)}, bf16[96,128]{1,0:T(8,128)(2,1)S(1)}, u32[]{:S(2)}, u32[]{:S(2)}) collective-permute-start(bf16[96,128]{1,0:T(8,128)(2,1)S(1)} %get-tuple-element.98), channel_id=1, source_target_pairs={{0,4},{1,5},{2,6},{3,7},{4,0},{5,1},{6,2},{7,3},{8,12},{9,13},{10,... | collective-permute-start | bytes 73736 | tf_op jit(solution)/shard_map/ppermute | solution.py:94
  7.2 5.9 %collective-permute-start.2 = (bf16[96,128]{1,0:T(8,128)(2,1)S(1)}, bf16[96,128]{1,0:T(8,128)(2,1)S(1)}, u32[]{:S(2)}, u32[]{:S(2)}) collective-permute-start(bf16[96,128]{1,0:T(8,128)(2,1)S(1)} %get-tuple-element.99), channel_id=1, source_target_pairs={{0,15},{1,2},{2,1},{3,4},{4,3},{5,6},{6,5},{7,8},{8,7},{9,10},{10,... | collective-permute-start | bytes 73736 | tf_op jit(solution)/shard_map/ppermute | solution.py:94
  7.9 5.2 %collective-permute-start.3 = (bf16[96,128]{1,0:T(8,128)(2,1)S(1)}, bf16[96,128]{1,0:T(8,128)(2,1)S(1)}, u32[]{:S(2)}, u32[]{:S(2)}) collective-permute-start(bf16[96,128]{1,0:T(8,128)(2,1)S(1)} %get-tuple-element.100), channel_id=1, source_target_pairs={{0,1},{1,0},{2,3},{3,2},{4,5},{5,4},{6,7},{7,6},{8,9},{9,8},{10,11... | collective-permute-start | bytes 73736 | tf_op jit(solution)/shard_map/ppermute | solution.py:94
  13.1 3.2 %copy-start = (bf16[1,1,48,48,128]{4,3,2,1,0:T(8,128)(2,1)S(1)}, bf16[1,1,48,48,128]{4,3,2,1,0:T(8,128)(2,1)}, u32[]{:S(2)}) copy-start(bf16[1,1,48,48,128]{4,3,2,1,0:T(8,128)(2,1)} %param.9) | copy-start | bytes 1769476
  13.1 3.2 %copy-start.1 = (bf16[3,3,128,128]{3,2,1,0:T(8,128)(2,1)S(1)}, bf16[3,3,128,128]{3,2,1,0:T(8,128)(2,1)}, u32[]{:S(2)}) copy-start(bf16[3,3,128,128]{3,2,1,0:T(8,128)(2,1)} %param.7) | copy-start | bytes 884740
  13.8 5.7 %collective-permute-start.4 = (bf16[112,128]{1,0:T(8,128)(2,1)S(1)}, bf16[112,128]{1,0:T(8,128)(2,1)S(1)}, u32[]{:S(2)}, u32[]{:S(2)}) collective-permute-start(bf16[112,128]{1,0:T(8,128)(2,1)S(1)} %get-tuple-element.107), channel_id=1, source_target_pairs={{0,12},{1,13},{2,14},{3,15},{4,8},{5,9},{6,10},{7,11},{8,4},{9,5},... | collective-permute-start | bytes 86024 | tf_op jit(solution)/shard_map/ppermute | solution.py:94
  13.9 5.7 %collective-permute-start.5 = (bf16[112,128]{1,0:T(8,128)(2,1)S(1)}, bf16[112,128]{1,0:T(8,128)(2,1)S(1)}, u32[]{:S(2)}, u32[]{:S(2)}) collective-permute-start(bf16[112,128]{1,0:T(8,128)(2,1)S(1)} %get-tuple-element.108), channel_id=1, source_target_pairs={{0,4},{1,5},{2,6},{3,7},{4,0},{5,1},{6,2},{7,3},{8,12},{9,13},{10,... | collective-permute-start | bytes 86024 | tf_op jit(solution)/shard_map/ppermute | solution.py:94
  14.2 6.0 %collective-permute-start.6 = (bf16[112,128]{1,0:T(8,128)(2,1)S(1)}, bf16[112,128]{1,0:T(8,128)(2,1)S(1)}, u32[]{:S(2)}, u32[]{:S(2)}) collective-permute-start(bf16[112,128]{1,0:T(8,128)(2,1)S(1)} %get-tuple-element.109), channel_id=1, source_target_pairs={{0,15},{1,2},{2,1},{3,4},{4,3},{5,6},{6,5},{7,8},{8,7},{9,10},{10,... | collective-permute-start | bytes 86024 | tf_op jit(solution)/shard_map/ppermute | solution.py:94
  16.3 3.9 %collective-permute-start.7 = (bf16[112,128]{1,0:T(8,128)(2,1)S(1)}, bf16[112,128]{1,0:T(8,128)(2,1)S(1)}, u32[]{:S(2)}, u32[]{:S(2)}) collective-permute-start(bf16[112,128]{1,0:T(8,128)(2,1)S(1)} %get-tuple-element.110), channel_id=1, source_target_pairs={{0,1},{1,0},{2,3},{3,2},{4,5},{5,4},{6,7},{7,6},{8,9},{9,8},{10,11... | collective-permute-start | bytes 86024 | tf_op jit(solution)/shard_map/ppermute | solution.py:94
  25.1 1.6 %collective-permute-start.8 = (bf16[1152,128]{1,0:T(8,128)(2,1)S(1)}, bf16[1152,128]{1,0:T(8,128)(2,1)S(1)}, u32[]{:S(2)}, u32[]{:S(2)}) collective-permute-start(bf16[1152,128]{1,0:T(8,128)(2,1)S(1)} %bitcast.20), channel_id=1, source_target_pairs={{0,1},{1,0},{2,3},{3,2},{4,5},{5,4},{6,7},{7,6},{8,9},{9,8},{10,11... | collective-permute-start | bytes 884744 | tf_op jit(solution)/shard_map/ppermute | solution.py:585
  26.8 10.2 %collective-permute-start.9 = (bf16[336,128]{1,0:T(8,128)(2,1)S(1)}, bf16[336,128]{1,0:T(8,128)(2,1)S(1)}, u32[]{:S(2)}, u32[]{:S(2)}) collective-permute-start(bf16[336,128]{1,0:T(8,128)(2,1)S(1)} %get-tuple-element.141), channel_id=1, source_target_pairs={{0,12},{1,13},{2,14},{3,15},{4,8},{5,9},{6,10},{7,11},{8,4},{9,5},... | collective-permute-start | bytes 258056 | tf_op jit(solution)/shard_map/ppermute | solution.py:585
  28.6 8.4 %collective-permute-start.10 = (bf16[336,128]{1,0:T(8,128)(2,1)S(1)}, bf16[336,128]{1,0:T(8,128)(2,1)S(1)}, u32[]{:S(2)}, u32[]{:S(2)}) collective-permute-start(bf16[336,128]{1,0:T(8,128)(2,1)S(1)} %get-tuple-element.142), channel_id=1, source_target_pairs={{0,4},{1,5},{2,6},{3,7},{4,0},{5,1},{6,2},{7,3},{8,12},{9,13},{10,... | collective-permute-start | bytes 258056 | tf_op jit(solution)/shard_map/ppermute | solution.py:585
  29.7 7.3 %collective-permute-start.13 = (bf16[288,128]{1,0:T(8,128)(2,1)S(1)}, bf16[288,128]{1,0:T(8,128)(2,1)S(1)}, u32[]{:S(2)}, u32[]{:S(2)}) collective-permute-start(bf16[288,128]{1,0:T(8,128)(2,1)S(1)} %get-tuple-element.155), channel_id=1, source_target_pairs={{0,8},{1,9},{2,10},{3,11},{4,12},{5,13},{6,14},{7,15},{8,0},{9,1},... | collective-permute-start | bytes 221192 | tf_op jit(solution)/shard_map/ppermute | solution.py:585
  31.3 9.3 %collective-permute-start.11 = (bf16[48,128]{1,0:T(8,128)(2,1)S(1)}, bf16[48,128]{1,0:T(8,128)(2,1)S(1)}, u32[]{:S(2)}, u32[]{:S(2)}) collective-permute-start(bf16[48,128]{1,0:T(8,128)(2,1)S(1)} %get-tuple-element.143), channel_id=1, source_target_pairs={{0,15},{1,2},{2,1},{3,4},{4,3},{5,6},{6,5},{7,8},{8,7},{9,10},{10,... | collective-permute-start | bytes 36872 | tf_op jit(solution)/shard_map/ppermute | solution.py:634
  32.6 8.1 %collective-permute-start.12 = (bf16[48,128]{1,0:T(8,128)(2,1)S(1)}, bf16[48,128]{1,0:T(8,128)(2,1)S(1)}, u32[]{:S(2)}, u32[]{:S(2)}) collective-permute-start(bf16[48,128]{1,0:T(8,128)(2,1)S(1)} %get-tuple-element.144), channel_id=1, source_target_pairs={{0,1},{1,0},{2,3},{3,2},{4,5},{5,4},{6,7},{7,6},{8,9},{9,8},{10,11... | collective-permute-start | bytes 36872 | tf_op jit(solution)/shard_map/ppermute | solution.py:634
  37.1 6.1 %collective-permute-start.16 = (bf16[288,128]{1,0:T(8,128)(2,1)S(1)}, bf16[288,128]{1,0:T(8,128)(2,1)S(1)}, u32[]{:S(2)}, u32[]{:S(2)}) collective-permute-start(bf16[288,128]{1,0:T(8,128)(2,1)S(1)} %add_up.2.base), channel_id=1, source_target_pairs={{0,2},{1,3},{2,0},{3,1},{4,6},{5,7},{6,4},{7,5},{8,10},{9,11},{10,... | collective-permute-start | bytes 221192 | tf_op jit(solution)/shard_map/ppermute | solution.py:585
  37.9 5.2 %collective-permute-start.15 = (bf16[288,128]{1,0:T(8,128)(2,1)S(1)}, bf16[288,128]{1,0:T(8,128)(2,1)S(1)}, u32[]{:S(2)}, u32[]{:S(2)}) collective-permute-start(bf16[288,128]{1,0:T(8,128)(2,1)S(1)} %add_up.2.base), channel_id=1, source_target_pairs={{0,16},{1,17},{2,18},{3,19},{4,20},{5,21},{6,22},{7,23},{8,24},{9,... | collective-permute-start | bytes 221192 | tf_op jit(solution)/shard_map/ppermute | solution.py:585
  39.4 5.3 %collective-permute-start.14 = (bf16[288,128]{1,0:T(8,128)(2,1)S(1)}, bf16[288,128]{1,0:T(8,128)(2,1)S(1)}, u32[]{:S(2)}, u32[]{:S(2)}) collective-permute-start(bf16[288,128]{1,0:T(8,128)(2,1)S(1)} %add_up.2.base), channel_id=1, source_target_pairs={{0,18},{1,19},{2,16},{3,17},{4,22},{5,23},{6,20},{7,21},{8,26},{9,... | collective-permute-start | bytes 221192 | tf_op jit(solution)/shard_map/ppermute | solution.py:585
  44.7 10.4 %collective-permute-start.17 = (bf16[336,128]{1,0:T(8,128)(2,1)S(1)}, bf16[336,128]{1,0:T(8,128)(2,1)S(1)}, u32[]{:S(2)}, u32[]{:S(2)}) collective-permute-start(bf16[336,128]{1,0:T(8,128)(2,1)S(1)} %get-tuple-element.165), channel_id=1, source_target_pairs={{0,12},{1,13},{2,14},{3,15},{4,8},{5,9},{6,10},{7,11},{8,4},{9,5},... | collective-permute-start | bytes 258056 | tf_op jit(solution)/shard_map/ppermute | solution.py:585
  46.9 8.2 %collective-permute-start.19 = (bf16[336,128]{1,0:T(8,128)(2,1)S(1)}, bf16[336,128]{1,0:T(8,128)(2,1)S(1)}, u32[]{:S(2)}, u32[]{:S(2)}) collective-permute-start(bf16[336,128]{1,0:T(8,128)(2,1)S(1)} %get-tuple-element.167), channel_id=1, source_target_pairs={{0,4},{1,5},{2,6},{3,7},{4,0},{5,1},{6,2},{7,3},{8,12},{9,13},{10,... | collective-permute-start | bytes 258056 | tf_op jit(solution)/shard_map/ppermute | solution.py:585
  46.9 8.2 %collective-permute-start.18 = (bf16[288,128]{1,0:T(8,128)(2,1)S(1)}, bf16[288,128]{1,0:T(8,128)(2,1)S(1)}, u32[]{:S(2)}, u32[]{:S(2)}) collective-permute-start(bf16[288,128]{1,0:T(8,128)(2,1)S(1)} %get-tuple-element.166.refs_0_), channel_id=1, source_target_pairs={{0,8},{1,9},{2,10},{3,11},{4,12},{5,13},{6,14},{7,15},{8,0},{9,1},... | collective-permute-start | bytes 221192 | tf_op jit(solution)/shard_map/ppermute | solution.py:585
  49.2 5.9 %collective-permute-start.20 = (bf16[48,128]{1,0:T(8,128)(2,1)S(1)}, bf16[48,128]{1,0:T(8,128)(2,1)S(1)}, u32[]{:S(2)}, u32[]{:S(2)}) collective-permute-start(bf16[48,128]{1,0:T(8,128)(2,1)S(1)} %get-tuple-element.168), channel_id=1, source_target_pairs={{0,15},{1,2},{2,1},{3,4},{4,3},{5,6},{6,5},{7,8},{8,7},{9,10},{10,... | collective-permute-start | bytes 36872 | tf_op jit(solution)/shard_map/ppermute | solution.py:634
  49.4 5.7 %collective-permute-start.21 = (bf16[48,128]{1,0:T(8,128)(2,1)S(1)}, bf16[48,128]{1,0:T(8,128)(2,1)S(1)}, u32[]{:S(2)}, u32[]{:S(2)}) collective-permute-start(bf16[48,128]{1,0:T(8,128)(2,1)S(1)} %get-tuple-element.169), channel_id=1, source_target_pairs={{0,1},{1,0},{2,3},{3,2},{4,5},{5,4},{6,7},{7,6},{8,9},{9,8},{10,11... | collective-permute-start | bytes 36872 | tf_op jit(solution)/shard_map/ppermute | solution.py:634
  55.1 1.6 %collective-permute-start.22 = (bf16[4,288,128]{2,1,0:T(8,128)(2,1)S(1)}, bf16[4,288,128]{2,1,0:T(8,128)(2,1)S(1)}, u32[]{:S(2)}, u32[]{:S(2)}) collective-permute-start(bf16[4,288,128]{2,1,0:T(8,128)(2,1)S(1)} %stack.1.mine), channel_id=1, source_target_pairs={{0,1},{1,0},{2,3},{3,2},{4,5},{5,4},{6,7},{7,6},{8,9},{9,8},{10,11... | collective-permute-start | bytes 884744 | tf_op jit(solution)/shard_map/ppermute | solution.py:585

commit v7 on v6

--- a/solution.py
+++ b/solution.py
@@ -23,8 +23,8 @@
     odd, row_odd = index & 1, (index // cols) & 1
     return [
         (index + cols * (2 * row_odd - 1) + count) % count,
+        (index - 1 + 2 * odd + count) % count,
         (index + cols * (1 - 2 * row_odd) + count) % count,
-        (index - 1 + 2 * odd + count) % count,
         (index + 1 - 2 * odd + count) % count,
     ]
 
@@ -657,7 +657,7 @@
 
 def sum_rest(own, got, riders, ways):
     tiles = lax.axis_size("tile")
-    groups, bit = [[(1, 2), (1, 0), (0, 2)]], 16
+    groups, bit = [[(0, 2), (1, 0), (1, 2)]], 16
     while bit < tiles:
         groups.append([(0, 3 * bit), (0, 2 * bit), (0, bit)] if 2 * bit < tiles else [(0, bit)])
         bit *= 4

time: 58.1 us -> 56.4 us (0.971)
  waiting for transfers between devices: 17.5 us -> 14.9 us
  starting transfers between devices: 24.5 us -> 25.4 us
    ppermute x11, waiting for transfers between devices: 8.17 us -> 6.87 us  [flip_swap(): return lax.ppermute(block, ('ens', 'tile'), route)]
    ppermute x8, waiting for transfers between devices: 4.77 us -> 3.57 us  [swap_all(): lax.ppermute(block, 'tile', list(enumerate(way)))]
    ppermute x8, starting transfers between devices: 9.24 us -> 10.2 us  [swap_all(): lax.ppermute(block, 'tile', list(enumerate(way)))]
where the time goes in v7:
time: 56.4 us; the launch traced here: 56.2 us
  starting transfers between devices  25.4 us (45%)
  Pallas kernels  15.1 us (27%)
  waiting for transfers between devices  14.9 us (26%)
  between operations  0.78 us (1%)
    pallas_call x15, Pallas kernels, call(): pl.pallas_call(kernel, name=name, grid=(1,), in_specs=[spec or whole for...  15.1 us
    ppermute x11, starting transfers between devices, flip_swap(): return lax.ppermute(block, ('ens', 'tile'), route)  12.6 us
    ppermute x8, starting transfers between devices, swap_all(): lax.ppermute(block, 'tile', list(enumerate(way)))  10.2 us
    ppermute x11, waiting for transfers between devices, flip_swap(): return lax.ppermute(block, ('ens', 'tile'), route)  6.87 us
    ppermute x4, waiting for transfers between devices, swap_line(): lax.ppermute(rider, 'tile', list(enumerate(way)))  4.48 us
    ppermute x8, waiting for transfers between devices, swap_all(): lax.ppermute(block, 'tile', list(enumerate(way)))  3.57 us
    ppermute x4, starting transfers between devices, swap_line(): lax.ppermute(rider, 'tile', list(enumerate(way)))  2.54 us
  transfers between devices with their start and end apart: 23, of which 9 were waited for; matrix products, arithmetic and copies ran while one was open for 0% of the time, Pallas kernels for 12%

profile of v7, /device:TPU:0, one launch (start us, length us, event | category | flops | bytes accessed | tf_op | source)
XLA Modules:
  0.0 56.2 jit_solution(16066284812848920612)
XLA Ops:
  0.6 1.4 %first_strips.1 = (bf16[96,128]{1,0:T(8,128)(2,1)S(1)}, bf16[96,128]{1,0:T(8,128)(2,1)S(1)}, bf16[96,128]{1,0:T(8,128)(2,1)S(1)}, bf16[96,128]{1,0:T(8,128)(2,1)...) custom-call(s32[4,16]{1,0:T(4,128)} %bitcast.24, ...), custom_call_target="tpu_custom_call" | custom-call | bytes 2097152 | tf_op jit(solution)/shard_map/first_strips/pallas_call | solution.py:565
  2.1 5.1 %collective-permute-start = (bf16[96,128]{1,0:T(8,128)(2,1)S(1)}, bf16[96,128]{1,0:T(8,128)(2,1)S(1)}, u32[]{:S(2)}, u32[]{:S(2)}) collective-permute-start(bf16[96,128]{1,0:T(8,128)(2,1)S(1)} %get-tuple-element.97), channel_id=1, source_target_pairs={{0,12},{1,13},{2,14},{3,15},{4,8},{5,9},{6,10},{7,11},{8,4},{9,5},... | collective-permute-start | bytes 73736 | tf_op jit(solution)/shard_map/ppermute | solution.py:94
  7.2 0.5 collective-permute-start.1
  7.7 1.7 %collective-permute-start.2 = (bf16[96,128]{1,0:T(8,128)(2,1)S(1)}, bf16[96,128]{1,0:T(8,128)(2,1)S(1)}, u32[]{:S(2)}, u32[]{:S(2)}) collective-permute-start(bf16[96,128]{1,0:T(8,128)(2,1)S(1)} %get-tuple-element.99), channel_id=1, source_target_pairs={{0,4},{1,5},{2,6},{3,7},{4,0},{5,1},{6,2},{7,3},{8,12},{9,13},{10,... | collective-permute-start | bytes 73736 | tf_op jit(solution)/shard_map/ppermute | solution.py:94
  9.3 1.7 %first_bulk.1 = (bf16[1200,768]{1,0:T(8,128)(2,1)S(1)}, f32[24,48,256]{2,1,0:T(8,128)S(1)}, bf16[24,48,256]{2,1,0:T(8,128)(2,1)S(1)}, bf16[24,48,256]{2,1,0:T(8,128)(2,1)S(1)}) custom-call(bf16[48,48,128]{2,1,0:T(8,128)(2,1)S(1)} %get-tuple-element.94.block, bf16[9,128,128]{2,1,0:T(8,128)(2,1)S(1)} %get-tuple-element.95.weight.refs_4_), custom_call_target="tpu_custom_call" | custom-call | flops 679477248 | bytes 2097152 | tf_op jit(solution)/shard_map/first_bulk/pallas_call | solution.py:565
  11.0 0.0 collective-permute-done.refs_0_.refs_13_
  11.0 2.1 %collective-permute-done.1.refs_1_.refs_14_ = bf16[96,128]{1,0:T(8,128)(2,1)S(1)} collective-permute-done((bf16[96,128]{1,0:T(8,128)(2,1)S(1)}, bf16[96,128]{1,0:T(8,128)(2,1)S(1)}, u32[]{:S(2)}, u32[]{:S(2)}) %collective-permute-start.1) | collective-permute-done | bytes 24608 | tf_op jit(solution)/shard_map/ppermute | solution.py:94
  13.1 0.0 collective-permute-done.2.refs_2_.refs_15_
  13.1 0.0 collective-permute-done.3.refs_3_.refs_16_
  13.1 0.0 copy-start.1
  13.2 0.7 %first_edges.1 = (bf16[112,128]{1,0:T(8,128)(2,1)S(1)}, bf16[112,128]{1,0:T(8,128)(2,1)S(1)}, bf16[112,128]{1,0:T(8,128)(2,1)S(1)}, bf16[112,128]{1,0:T(8,128)(2...) custom-call(s32[12,8,128]{2,1,0:T(8,128)S(1)} %get-tuple-element.93., ...), custom_call_target="tpu_custom_call" | custom-call | bytes 2097152 | tf_op jit(solution)/shard_map/first_edges/pallas_call | solution.py:565
  13.8 0.1 collective-permute-start.4
  13.9 1.8 %collective-permute-start.5 = (bf16[112,128]{1,0:T(8,128)(2,1)S(1)}, bf16[112,128]{1,0:T(8,128)(2,1)S(1)}, u32[]{:S(2)}, u32[]{:S(2)}) collective-permute-start(bf16[112,128]{1,0:T(8,128)(2,1)S(1)} %get-tuple-element.108), channel_id=1, source_target_pairs={{0,15},{1,2},{2,1},{3,4},{4,3},{5,6},{6,5},{7,8},{8,7},{9,10},{10,... | collective-permute-start | bytes 86024 | tf_op jit(solution)/shard_map/ppermute | solution.py:94
  15.8 1.0 %collective-permute-start.6 = (bf16[112,128]{1,0:T(8,128)(2,1)S(1)}, bf16[112,128]{1,0:T(8,128)(2,1)S(1)}, u32[]{:S(2)}, u32[]{:S(2)}) collective-permute-start(bf16[112,128]{1,0:T(8,128)(2,1)S(1)} %get-tuple-element.109), channel_id=1, source_target_pairs={{0,4},{1,5},{2,6},{3,7},{4,0},{5,1},{6,2},{7,3},{8,12},{9,13},{10,... | collective-permute-start | bytes 86024 | tf_op jit(solution)/shard_map/ppermute | solution.py:94
  16.8 1.7 %second_bulk.1 = (bf16[1200,768]{1,0:T(8,128)(2,1)S(1)}, f32[24,48,256]{2,1,0:T(8,128)S(1)}, bf16[24,48,256]{2,1,0:T(8,128)(2,1)S(1)}, bf16[24,48,256]{2,1,0:T(8,128)(2,1)S(1)}) custom-call(bf16[24,48,256]{2,1,0:T(8,128)(2,1)S(1)} %get-tuple-element.96.hidden, f32[24,8,256]{2,1,0:T(8,128)S(1)} %get-tuple-element.102.left, ...), custom_call_target="tpu_custom_call" | custom-call | flops 679477248 | bytes 2097152 | tf_op jit(solution)/shard_map/second_bulk/pallas_call | solution.py:565
  18.5 1.1 %collective-permute-done.4.refs_0_.refs_17_ = bf16[112,128]{1,0:T(8,128)(2,1)S(1)} collective-permute-done((bf16[112,128]{1,0:T(8,128)(2,1)S(1)}, bf16[112,128]{1,0:T(8,128)(2,1)S(1)}, u32[]{:S(2)}, u32[]{:S(2)}) %collective-permute-start.4) | collective-permute-done | bytes 28704 | tf_op jit(solution)/shard_map/ppermute | solution.py:94
  19.6 0.4 collective-permute-done.5.refs_1_.refs_18_
  20.0 0.0 collective-permute-done.6.refs_2_.refs_19_
  20.0 0.0 collective-permute-done.7.refs_3_.refs_20_
  20.0 0.9 %second_edges.1 = (bf16[48,128]{1,0:T(8,128)(2,1)S(1)}, bf16[48,128]{1,0:T(8,128)(2,1)S(1)}, bf16[48,128]{1,0:T(8,128)(2,1)S(1)}, bf16[48,128]{1,0:T(8,128)(2,1)...) custom-call(s32[12,8,128]{2,1,0:T(8,128)S(1)} %get-tuple-element.93., ...), custom_call_target="tpu_custom_call" | custom-call | bytes 2097152 | tf_op jit(solution)/shard_map/second_edges/pallas_call | solution.py:565
  20.9 2.4 %second_back.1 = (f32[9,128,128]{2,1,0:T(8,128)S(1)}, f32[24,48,256]{2,1,0:T(8,128)S(1)}, bf16[24,48,256]{2,1,0:T(8,128)(2,1)S(1)}) custom-call(bf16[24,48,256]{2,1,0:T(8,128)(2,1)S(1)} %get-tuple-element.106.refs_0_, f32[24,8,256]{2,1,0:T(8,128)S(1)} %get-tuple-element.112.refs_1_, f32[24,8,256]{2,1,0:T(8,128)S(1)} %get-tuple-element.113.refs_2_, ...), custom_call_target="tpu_custom_call" | custom-call | flops 1358954496 | bytes 2097152 | tf_op jit(solution)/shard_map/second_back/pallas_call | solution.py:565
  23.3 1.6 %first_grads.1 = (bf16[24,48,256]{2,1,0:T(8,128)(2,1)S(1)}, f32[9,128,128]{2,1,0:T(8,128)S(1)}, bf16[9,128,128]{2,1,0:T(8,128)(2,1)S(1)}) custom-call(s32[12,8,128]{2,1,0:T(8,128)S(1)} %get-tuple-element.93.found, f32[24,48,256]{2,1,0:T(8,128)S(1)} %get-tuple-element.119.refs_0_.refs_1_.refs_2_.refs_3_.refs_5_.refs_6_.refs_7_.refs_8_, ...), custom_call_target="tpu_custom_call" | custom-call | flops 679477248 | bytes 2097152 | tf_op jit(solution)/shard_map/first_grads/pallas_call | solution.py:565
  24.9 0.1 collective-permute-start.8
  25.0 1.6 %collective-permute-done.8.given = bf16[1152,128]{1,0:T(8,128)(2,1)S(1)} collective-permute-done((bf16[1152,128]{1,0:T(8,128)(2,1)S(1)}, bf16[1152,128]{1,0:T(8,128)(2,1)S(1)}, u32[]{:S(2)}, u32[]{:S(2)}) %collective-permute-start.8) | collective-permute-done | bytes 294944 | tf_op jit(solution)/shard_map/ppermute | solution.py:585
  26.5 0.1 share_out.1
  26.6 2.0 %collective-permute-start.9 = (bf16[336,128]{1,0:T(8,128)(2,1)S(1)}, bf16[336,128]{1,0:T(8,128)(2,1)S(1)}, u32[]{:S(2)}, u32[]{:S(2)}) collective-permute-start(bf16[336,128]{1,0:T(8,128)(2,1)S(1)} %get-tuple-element.141), channel_id=1, source_target_pairs={{0,12},{1,13},{2,14},{3,15},{4,8},{5,9},{6,10},{7,11},{8,4},{9,5},... | collective-permute-start | bytes 258056 | tf_op jit(solution)/shard_map/ppermute | solution.py:585
  28.6 2.4 %collective-permute-start.13 = (bf16[288,128]{1,0:T(8,128)(2,1)S(1)}, bf16[288,128]{1,0:T(8,128)(2,1)S(1)}, u32[]{:S(2)}, u32[]{:S(2)}) collective-permute-start(bf16[288,128]{1,0:T(8,128)(2,1)S(1)} %get-tuple-element.155), channel_id=1, source_target_pairs={{0,8},{1,9},{2,10},{3,11},{4,12},{5,13},{6,14},{7,15},{8,0},{9,1},... | collective-permute-start | bytes 221192 | tf_op jit(solution)/shard_map/ppermute | solution.py:585
  31.1 1.2 %collective-permute-start.10 = (bf16[48,128]{1,0:T(8,128)(2,1)S(1)}, bf16[48,128]{1,0:T(8,128)(2,1)S(1)}, u32[]{:S(2)}, u32[]{:S(2)}) collective-permute-start(bf16[48,128]{1,0:T(8,128)(2,1)S(1)} %get-tuple-element.142), channel_id=1, source_target_pairs={{0,15},{1,2},{2,1},{3,4},{4,3},{5,6},{6,5},{7,8},{8,7},{9,10},{10,... | collective-permute-start | bytes 36872 | tf_op jit(solution)/shard_map/ppermute | solution.py:634
  32.3 0.0 collective-permute-start.12
  32.3 3.2 %collective-permute-done.13.refs_1_ = bf16[288,128]{1,0:T(8,128)(2,1)S(1)} collective-permute-done((bf16[288,128]{1,0:T(8,128)(2,1)S(1)}, bf16[288,128]{1,0:T(8,128)(2,1)S(1)}, u32[]{:S(2)}, u32[]{:S(2)}) %collective-permute-start.13) | collective-permute-done | bytes 73760 | tf_op jit(solution)/shard_map/ppermute | solution.py:585
  35.5 0.9 %collective-permute-done.11.refs_2_ = bf16[336,128]{1,0:T(8,128)(2,1)S(1)} collective-permute-done((bf16[336,128]{1,0:T(8,128)(2,1)S(1)}, bf16[336,128]{1,0:T(8,128)(2,1)S(1)}, u32[]{:S(2)}, u32[]{:S(2)}) %collective-permute-start.11) | collective-permute-done | bytes 86048 | tf_op jit(solution)/shard_map/ppermute | solution.py:585
  36.4 1.6 %collective-permute-start.16 = (bf16[288,128]{1,0:T(8,128)(2,1)S(1)}, bf16[288,128]{1,0:T(8,128)(2,1)S(1)}, u32[]{:S(2)}, u32[]{:S(2)}) collective-permute-start(bf16[288,128]{1,0:T(8,128)(2,1)S(1)} %add_up.2.base), channel_id=1, source_target_pairs={{0,18},{1,19},{2,16},{3,17},{4,22},{5,23},{6,20},{7,21},{8,26},{9,... | collective-permute-start | bytes 221192 | tf_op jit(solution)/shard_map/ppermute | solution.py:585
  38.0 0.5 collective-permute-start.15
  38.6 1.4 %collective-permute-start.14 = (bf16[288,128]{1,0:T(8,128)(2,1)S(1)}, bf16[288,128]{1,0:T(8,128)(2,1)S(1)}, u32[]{:S(2)}, u32[]{:S(2)}) collective-permute-start(bf16[288,128]{1,0:T(8,128)(2,1)S(1)} %add_up.2.base), channel_id=1, source_target_pairs={{0,2},{1,3},{2,0},{3,1},{4,6},{5,7},{6,4},{7,5},{8,10},{9,11},{10,... | collective-permute-start | bytes 221192 | tf_op jit(solution)/shard_map/ppermute | solution.py:585
  39.9 0.0 collective-permute-done.10.refs_1_
  40.0 0.5 first_back.1
  40.4 2.0 %last_bulk.1 = (f32[24,48,256]{2,1,0:T(8,128)S(1)}, bf16[48,48,128]{2,1,0:T(8,128)(2,1)}) custom-call(bf16[24,48,256]{2,1,0:T(8,128)(2,1)S(1)} %get-tuple-element.130.delta, bf16[9,128,128]{2,1,0:T(8,128)(2,1)S(1)} %get-tuple-element.95.weight.refs_4_, bf16[24,48,256]{2,1,0:T(8,128)(2,1)S(1)} %get-tuple-element.131.bulk_out, ...), custom_call_target="tpu_custom_call" | custom-call | flops 679477248 | bytes 2097152 | tf_op jit(solution)/shard_map/last_bulk/pallas_call | solution.py:565
  42.5 0.0 collective-permute-done.15.refs_1_
  42.5 0.6 %collective-permute-done.14.refs_0_ = bf16[288,128]{1,0:T(8,128)(2,1)S(1)} collective-permute-done((bf16[288,128]{1,0:T(8,128)(2,1)S(1)}, bf16[288,128]{1,0:T(8,128)(2,1)S(1)}, u32[]{:S(2)}, u32[]{:S(2)}) %collective-permute-start.14) | collective-permute-done | bytes 73760 | tf_op jit(solution)/shard_map/ppermute | solution.py:585
  43.1 2.7 %collective-permute-start.17 = (bf16[336,128]{1,0:T(8,128)(2,1)S(1)}, bf16[336,128]{1,0:T(8,128)(2,1)S(1)}, u32[]{:S(2)}, u32[]{:S(2)}) collective-permute-start(bf16[336,128]{1,0:T(8,128)(2,1)S(1)} %get-tuple-element.165), channel_id=1, source_target_pairs={{0,12},{1,13},{2,14},{3,15},{4,8},{5,9},{6,10},{7,11},{8,4},{9,5},... | collective-permute-start | bytes 258056 | tf_op jit(solution)/shard_map/ppermute | solution.py:585
  45.8 1.7 %collective-permute-start.18 = (bf16[288,128]{1,0:T(8,128)(2,1)S(1)}, bf16[288,128]{1,0:T(8,128)(2,1)S(1)}, u32[]{:S(2)}, u32[]{:S(2)}) collective-permute-start(bf16[288,128]{1,0:T(8,128)(2,1)S(1)} %get-tuple-element.166.refs_0_), channel_id=1, source_target_pairs={{0,8},{1,9},{2,10},{3,11},{4,12},{5,13},{6,14},{7,15},{8,0},{9,1},... | collective-permute-start | bytes 221192 | tf_op jit(solution)/shard_map/ppermute | solution.py:585
  47.6 0.2 collective-permute-start.20
  47.8 1.1 %collective-permute-start.21 = (bf16[48,128]{1,0:T(8,128)(2,1)S(1)}, bf16[48,128]{1,0:T(8,128)(2,1)S(1)}, u32[]{:S(2)}, u32[]{:S(2)}) collective-permute-start(bf16[48,128]{1,0:T(8,128)(2,1)S(1)} %get-tuple-element.169), channel_id=1, source_target_pairs={{0,1},{1,0},{2,3},{3,2},{4,5},{5,4},{6,7},{7,6},{8,9},{9,8},{10,11... | collective-permute-start | bytes 36872 | tf_op jit(solution)/shard_map/ppermute | solution.py:634
  48.9 4.5 %collective-permute-done.20.refs_1_ = bf16[48,128]{1,0:T(8,128)(2,1)S(1)} collective-permute-done((bf16[48,128]{1,0:T(8,128)(2,1)S(1)}, bf16[48,128]{1,0:T(8,128)(2,1)S(1)}, u32[]{:S(2)}, u32[]{:S(2)}) %collective-permute-start.20) | collective-permute-done | bytes 12320 | tf_op jit(solution)/shard_map/ppermute | solution.py:634
  53.4 0.1 collective-permute-start.22
  53.5 1.0 %last_edges.1 = bf16[48,48,128]{2,1,0:T(8,128)(2,1)} custom-call(s32[12,8,128]{2,1,0:T(8,128)S(1)} %get-tuple-element.93.found, bf16[336,128]{1,0:T(8,128)(2,1)S(1)} %collective-permute-done.17.refs_3_.refs_0_, bf16[48,128]{1,0:T(8,128)(2,1)S(1)} %collective-permute-done.20.refs_1_, bf16[336,128]{1,0:T(8,128)(2,1)S(1)} %collective-permute-done.19.refs_1_.refs_2_, ...), custom_call_target="tpu_custom_call" | custom-call | bytes 2097152 | tf_op jit(solution)/shard_map/last_edges/pallas_call | solution.py:565
  54.5 0.6 %collective-permute-done.22.others = bf16[4,288,128]{2,1,0:T(8,128)(2,1)S(1)} collective-permute-done((bf16[4,288,128]{2,1,0:T(8,128)(2,1)S(1)}, bf16[4,288,128]{2,1,0:T(8,128)(2,1)S(1)}, u32[]{:S(2)}, u32[]{:S(2)}) %collective-permute-start.22) | collective-permute-done | bytes 294944 | tf_op jit(solution)/shard_map/ppermute | solution.py:585
  55.1 1.1 %both_grads.1 = (f32[1152,128]{1,0:T(8,128)}, f32[1152,128]{1,0:T(8,128)}) custom-call(bf16[4,288,128]{2,1,0:T(8,128)(2,1)S(1)} %stack.1.mine, bf16[4,288,128]{2,1,0:T(8,128)(2,1)S(1)} %collective-permute-done.22.others), custom_call_target="tpu_custom_call" | custom-call | bytes 2097152 | tf_op jit(solution)/shard_map/both_grads/pallas_call | solution.py:565
  (17 shorter events, 0.1 us)
Async XLA Ops:
  2.1 8.9 %collective-permute-start = (bf16[96,128]{1,0:T(8,128)(2,1)S(1)}, bf16[96,128]{1,0:T(8,128)(2,1)S(1)}, u32[]{:S(2)}, u32[]{:S(2)}) collective-permute-start(bf16[96,128]{1,0:T(8,128)(2,1)S(1)} %get-tuple-element.97), channel_id=1, source_target_pairs={{0,12},{1,13},{2,14},{3,15},{4,8},{5,9},{6,10},{7,11},{8,4},{9,5},... | collective-permute-start | bytes 73736 | tf_op jit(solution)/shard_map/ppermute | solution.py:94
  7.2 5.9 %collective-permute-start.1 = (bf16[96,128]{1,0:T(8,128)(2,1)S(1)}, bf16[96,128]{1,0:T(8,128)(2,1)S(1)}, u32[]{:S(2)}, u32[]{:S(2)}) collective-permute-start(bf16[96,128]{1,0:T(8,128)(2,1)S(1)} %get-tuple-element.98), channel_id=1, source_target_pairs={{0,15},{1,2},{2,1},{3,4},{4,3},{5,6},{6,5},{7,8},{8,7},{9,10},{10,... | collective-permute-start | bytes 73736 | tf_op jit(solution)/shard_map/ppermute | solution.py:94
  7.7 5.5 %collective-permute-start.2 = (bf16[96,128]{1,0:T(8,128)(2,1)S(1)}, bf16[96,128]{1,0:T(8,128)(2,1)S(1)}, u32[]{:S(2)}, u32[]{:S(2)}) collective-permute-start(bf16[96,128]{1,0:T(8,128)(2,1)S(1)} %get-tuple-element.99), channel_id=1, source_target_pairs={{0,4},{1,5},{2,6},{3,7},{4,0},{5,1},{6,2},{7,3},{8,12},{9,13},{10,... | collective-permute-start | bytes 73736 | tf_op jit(solution)/shard_map/ppermute | solution.py:94
  9.3 3.8 %collective-permute-start.3 = (bf16[96,128]{1,0:T(8,128)(2,1)S(1)}, bf16[96,128]{1,0:T(8,128)(2,1)S(1)}, u32[]{:S(2)}, u32[]{:S(2)}) collective-permute-start(bf16[96,128]{1,0:T(8,128)(2,1)S(1)} %get-tuple-element.100), channel_id=1, source_target_pairs={{0,1},{1,0},{2,3},{3,2},{4,5},{5,4},{6,7},{7,6},{8,9},{9,8},{10,11... | collective-permute-start | bytes 73736 | tf_op jit(solution)/shard_map/ppermute | solution.py:94
  13.1 3.7 %copy-start = (bf16[1,1,48,48,128]{4,3,2,1,0:T(8,128)(2,1)S(1)}, bf16[1,1,48,48,128]{4,3,2,1,0:T(8,128)(2,1)}, u32[]{:S(2)}) copy-start(bf16[1,1,48,48,128]{4,3,2,1,0:T(8,128)(2,1)} %param.9) | copy-start | bytes 1769476
  13.1 3.7 %copy-start.1 = (bf16[3,3,128,128]{3,2,1,0:T(8,128)(2,1)S(1)}, bf16[3,3,128,128]{3,2,1,0:T(8,128)(2,1)}, u32[]{:S(2)}) copy-start(bf16[3,3,128,128]{3,2,1,0:T(8,128)(2,1)} %param.7) | copy-start | bytes 884740
  13.8 5.8 %collective-permute-start.4 = (bf16[112,128]{1,0:T(8,128)(2,1)S(1)}, bf16[112,128]{1,0:T(8,128)(2,1)S(1)}, u32[]{:S(2)}, u32[]{:S(2)}) collective-permute-start(bf16[112,128]{1,0:T(8,128)(2,1)S(1)} %get-tuple-element.107), channel_id=1, source_target_pairs={{0,12},{1,13},{2,14},{3,15},{4,8},{5,9},{6,10},{7,11},{8,4},{9,5},... | collective-permute-start | bytes 86024 | tf_op jit(solution)/shard_map/ppermute | solution.py:94
  13.9 6.1 %collective-permute-start.5 = (bf16[112,128]{1,0:T(8,128)(2,1)S(1)}, bf16[112,128]{1,0:T(8,128)(2,1)S(1)}, u32[]{:S(2)}, u32[]{:S(2)}) collective-permute-start(bf16[112,128]{1,0:T(8,128)(2,1)S(1)} %get-tuple-element.108), channel_id=1, source_target_pairs={{0,15},{1,2},{2,1},{3,4},{4,3},{5,6},{6,5},{7,8},{8,7},{9,10},{10,... | collective-permute-start | bytes 86024 | tf_op jit(solution)/shard_map/ppermute | solution.py:94
  15.8 4.2 %collective-permute-start.6 = (bf16[112,128]{1,0:T(8,128)(2,1)S(1)}, bf16[112,128]{1,0:T(8,128)(2,1)S(1)}, u32[]{:S(2)}, u32[]{:S(2)}) collective-permute-start(bf16[112,128]{1,0:T(8,128)(2,1)S(1)} %get-tuple-element.109), channel_id=1, source_target_pairs={{0,4},{1,5},{2,6},{3,7},{4,0},{5,1},{6,2},{7,3},{8,12},{9,13},{10,... | collective-permute-start | bytes 86024 | tf_op jit(solution)/shard_map/ppermute | solution.py:94
  16.8 3.2 %collective-permute-start.7 = (bf16[112,128]{1,0:T(8,128)(2,1)S(1)}, bf16[112,128]{1,0:T(8,128)(2,1)S(1)}, u32[]{:S(2)}, u32[]{:S(2)}) collective-permute-start(bf16[112,128]{1,0:T(8,128)(2,1)S(1)} %get-tuple-element.110), channel_id=1, source_target_pairs={{0,1},{1,0},{2,3},{3,2},{4,5},{5,4},{6,7},{7,6},{8,9},{9,8},{10,11... | collective-permute-start | bytes 86024 | tf_op jit(solution)/shard_map/ppermute | solution.py:94
  24.9 1.6 %collective-permute-start.8 = (bf16[1152,128]{1,0:T(8,128)(2,1)S(1)}, bf16[1152,128]{1,0:T(8,128)(2,1)S(1)}, u32[]{:S(2)}, u32[]{:S(2)}) collective-permute-start(bf16[1152,128]{1,0:T(8,128)(2,1)S(1)} %bitcast.20), channel_id=1, source_target_pairs={{0,1},{1,0},{2,3},{3,2},{4,5},{5,4},{6,7},{7,6},{8,9},{9,8},{10,11... | collective-permute-start | bytes 884744 | tf_op jit(solution)/shard_map/ppermute | solution.py:585
  26.6 8.9 %collective-permute-start.9 = (bf16[336,128]{1,0:T(8,128)(2,1)S(1)}, bf16[336,128]{1,0:T(8,128)(2,1)S(1)}, u32[]{:S(2)}, u32[]{:S(2)}) collective-permute-start(bf16[336,128]{1,0:T(8,128)(2,1)S(1)} %get-tuple-element.141), channel_id=1, source_target_pairs={{0,12},{1,13},{2,14},{3,15},{4,8},{5,9},{6,10},{7,11},{8,4},{9,5},... | collective-permute-start | bytes 258056 | tf_op jit(solution)/shard_map/ppermute | solution.py:585
  28.6 7.7 %collective-permute-start.11 = (bf16[336,128]{1,0:T(8,128)(2,1)S(1)}, bf16[336,128]{1,0:T(8,128)(2,1)S(1)}, u32[]{:S(2)}, u32[]{:S(2)}) collective-permute-start(bf16[336,128]{1,0:T(8,128)(2,1)S(1)} %get-tuple-element.143), channel_id=1, source_target_pairs={{0,4},{1,5},{2,6},{3,7},{4,0},{5,1},{6,2},{7,3},{8,12},{9,13},{10,... | collective-permute-start | bytes 258056 | tf_op jit(solution)/shard_map/ppermute | solution.py:585
  28.6 6.8 %collective-permute-start.13 = (bf16[288,128]{1,0:T(8,128)(2,1)S(1)}, bf16[288,128]{1,0:T(8,128)(2,1)S(1)}, u32[]{:S(2)}, u32[]{:S(2)}) collective-permute-start(bf16[288,128]{1,0:T(8,128)(2,1)S(1)} %get-tuple-element.155), channel_id=1, source_target_pairs={{0,8},{1,9},{2,10},{3,11},{4,12},{5,13},{6,14},{7,15},{8,0},{9,1},... | collective-permute-start | bytes 221192 | tf_op jit(solution)/shard_map/ppermute | solution.py:585
  31.1 8.9 %collective-permute-start.10 = (bf16[48,128]{1,0:T(8,128)(2,1)S(1)}, bf16[48,128]{1,0:T(8,128)(2,1)S(1)}, u32[]{:S(2)}, u32[]{:S(2)}) collective-permute-start(bf16[48,128]{1,0:T(8,128)(2,1)S(1)} %get-tuple-element.142), channel_id=1, source_target_pairs={{0,15},{1,2},{2,1},{3,4},{4,3},{5,6},{6,5},{7,8},{8,7},{9,10},{10,... | collective-permute-start | bytes 36872 | tf_op jit(solution)/shard_map/ppermute | solution.py:634
  32.3 7.7 %collective-permute-start.12 = (bf16[48,128]{1,0:T(8,128)(2,1)S(1)}, bf16[48,128]{1,0:T(8,128)(2,1)S(1)}, u32[]{:S(2)}, u32[]{:S(2)}) collective-permute-start(bf16[48,128]{1,0:T(8,128)(2,1)S(1)} %get-tuple-element.144), channel_id=1, source_target_pairs={{0,1},{1,0},{2,3},{3,2},{4,5},{5,4},{6,7},{7,6},{8,9},{9,8},{10,11... | collective-permute-start | bytes 36872 | tf_op jit(solution)/shard_map/ppermute | solution.py:634
  36.4 6.1 %collective-permute-start.16 = (bf16[288,128]{1,0:T(8,128)(2,1)S(1)}, bf16[288,128]{1,0:T(8,128)(2,1)S(1)}, u32[]{:S(2)}, u32[]{:S(2)}) collective-permute-start(bf16[288,128]{1,0:T(8,128)(2,1)S(1)} %add_up.2.base), channel_id=1, source_target_pairs={{0,18},{1,19},{2,16},{3,17},{4,22},{5,23},{6,20},{7,21},{8,26},{9,... | collective-permute-start | bytes 221192 | tf_op jit(solution)/shard_map/ppermute | solution.py:585
  38.0 4.5 %collective-permute-start.15 = (bf16[288,128]{1,0:T(8,128)(2,1)S(1)}, bf16[288,128]{1,0:T(8,128)(2,1)S(1)}, u32[]{:S(2)}, u32[]{:S(2)}) collective-permute-start(bf16[288,128]{1,0:T(8,128)(2,1)S(1)} %add_up.2.base), channel_id=1, source_target_pairs={{0,16},{1,17},{2,18},{3,19},{4,20},{5,21},{6,22},{7,23},{8,24},{9,... | collective-permute-start | bytes 221192 | tf_op jit(solution)/shard_map/ppermute | solution.py:585
  38.6 4.5 %collective-permute-start.14 = (bf16[288,128]{1,0:T(8,128)(2,1)S(1)}, bf16[288,128]{1,0:T(8,128)(2,1)S(1)}, u32[]{:S(2)}, u32[]{:S(2)}) collective-permute-start(bf16[288,128]{1,0:T(8,128)(2,1)S(1)} %add_up.2.base), channel_id=1, source_target_pairs={{0,2},{1,3},{2,0},{3,1},{4,6},{5,7},{6,4},{7,5},{8,10},{9,11},{10,... | collective-permute-start | bytes 221192 | tf_op jit(solution)/shard_map/ppermute | solution.py:585
  43.1 10.3 %collective-permute-start.17 = (bf16[336,128]{1,0:T(8,128)(2,1)S(1)}, bf16[336,128]{1,0:T(8,128)(2,1)S(1)}, u32[]{:S(2)}, u32[]{:S(2)}) collective-permute-start(bf16[336,128]{1,0:T(8,128)(2,1)S(1)} %get-tuple-element.165), channel_id=1, source_target_pairs={{0,12},{1,13},{2,14},{3,15},{4,8},{5,9},{6,10},{7,11},{8,4},{9,5},... | collective-permute-start | bytes 258056 | tf_op jit(solution)/shard_map/ppermute | solution.py:585
  45.8 7.6 %collective-permute-start.19 = (bf16[336,128]{1,0:T(8,128)(2,1)S(1)}, bf16[336,128]{1,0:T(8,128)(2,1)S(1)}, u32[]{:S(2)}, u32[]{:S(2)}) collective-permute-start(bf16[336,128]{1,0:T(8,128)(2,1)S(1)} %get-tuple-element.167), channel_id=1, source_target_pairs={{0,4},{1,5},{2,6},{3,7},{4,0},{5,1},{6,2},{7,3},{8,12},{9,13},{10,... | collective-permute-start | bytes 258056 | tf_op jit(solution)/shard_map/ppermute | solution.py:585
  45.8 7.6 %collective-permute-start.18 = (bf16[288,128]{1,0:T(8,128)(2,1)S(1)}, bf16[288,128]{1,0:T(8,128)(2,1)S(1)}, u32[]{:S(2)}, u32[]{:S(2)}) collective-permute-start(bf16[288,128]{1,0:T(8,128)(2,1)S(1)} %get-tuple-element.166.refs_0_), channel_id=1, source_target_pairs={{0,8},{1,9},{2,10},{3,11},{4,12},{5,13},{6,14},{7,15},{8,0},{9,1},... | collective-permute-start | bytes 221192 | tf_op jit(solution)/shard_map/ppermute | solution.py:585
  47.6 5.8 %collective-permute-start.20 = (bf16[48,128]{1,0:T(8,128)(2,1)S(1)}, bf16[48,128]{1,0:T(8,128)(2,1)S(1)}, u32[]{:S(2)}, u32[]{:S(2)}) collective-permute-start(bf16[48,128]{1,0:T(8,128)(2,1)S(1)} %get-tuple-element.168), channel_id=1, source_target_pairs={{0,15},{1,2},{2,1},{3,4},{4,3},{5,6},{6,5},{7,8},{8,7},{9,10},{10,... | collective-permute-start | bytes 36872 | tf_op jit(solution)/shard_map/ppermute | solution.py:634
  47.8 5.6 %collective-permute-start.21 = (bf16[48,128]{1,0:T(8,128)(2,1)S(1)}, bf16[48,128]{1,0:T(8,128)(2,1)S(1)}, u32[]{:S(2)}, u32[]{:S(2)}) collective-permute-start(bf16[48,128]{1,0:T(8,128)(2,1)S(1)} %get-tuple-element.169), channel_id=1, source_target_pairs={{0,1},{1,0},{2,3},{3,2},{4,5},{5,4},{6,7},{7,6},{8,9},{9,8},{10,11... | collective-permute-start | bytes 36872 | tf_op jit(solution)/shard_map/ppermute | solution.py:634
  53.4 1.6 %collective-permute-start.22 = (bf16[4,288,128]{2,1,0:T(8,128)(2,1)S(1)}, bf16[4,288,128]{2,1,0:T(8,128)(2,1)S(1)}, u32[]{:S(2)}, u32[]{:S(2)}) collective-permute-start(bf16[4,288,128]{2,1,0:T(8,128)(2,1)S(1)} %stack.1.mine), channel_id=1, source_target_pairs={{0,1},{1,0},{2,3},{3,2},{4,5},{5,4},{6,7},{7,6},{8,9},{9,8},{10,11... | collective-permute-start | bytes 884744 | tf_op jit(solution)/shard_map/ppermute | solution.py:585

commit v8 on v7

--- a/solution.py
+++ b/solution.py
@@ -598,7 +598,7 @@
     own[...] = add(seat)
     taken = 0
     for k, block in enumerate(sent):
-        block[0:rows] = add(seat ^ (3 - k)).astype(bf16)
+        block[0:rows] = add(seat ^ (k + 1)).astype(bf16)
         if loads[k]:
             block[rows:] = riders[taken][...]
             taken += 1
@@ -618,7 +618,7 @@
 
 
 def line_masks():
-    return [12, 8, 4]
+    return [4, 8, 12]
 
 
 def aboard(ways):
@@ -834,7 +834,7 @@
         [S(block.shape, bf16)],
         rooms + [V(halo), V(pairs(f32))],
     )
-    quarters = [quarter, *got[::-1]]
+    quarters = [quarter, *got]
     (stacked,) = call(stack, "stack", whole(quarters), [S((4, *quarter.shape), bf16)], [])
     others, grad_block = lax.optimization_barrier((flip_swap(stacked, 0, 1), grad_block))
     grads = call(

time: 56.4 us -> 55.7 us (0.988)
  starting transfers between devices: 25.4 us -> 24.5 us
    ppermute x11, starting transfers between devices: 12.6 us -> 11.7 us  [flip_swap(): return lax.ppermute(block, ('ens', 'tile'), route)]
  transfers between devices with their start and end apart: 23 -> 23, of which waited for: 9 -> 10; matrix products, arithmetic and copies ran while one was open for 0% -> 0% of each run, Pallas kernels for 12% -> 12%
where the time goes in v8:
time: 55.7 us; the launch traced here: 55.5 us
  starting transfers between devices  24.5 us (44%)
  waiting for transfers between devices  15.2 us (27%)
  Pallas kernels  15.1 us (27%)
  between operations  0.76 us (1%)
    pallas_call x15, Pallas kernels, call(): pl.pallas_call(kernel, name=name, grid=(1,), in_specs=[spec or whole for...  15.1 us
    ppermute x11, starting transfers between devices, flip_swap(): return lax.ppermute(block, ('ens', 'tile'), route)  11.7 us
    ppermute x8, starting transfers between devices, swap_all(): lax.ppermute(block, 'tile', list(enumerate(way)))  10.2 us
    ppermute x11, waiting for transfers between devices, flip_swap(): return lax.ppermute(block, ('ens', 'tile'), route)  7.01 us
    ppermute x4, waiting for transfers between devices, swap_line(): lax.ppermute(rider, 'tile', list(enumerate(way)))  4.58 us
    ppermute x8, waiting for transfers between devices, swap_all(): lax.ppermute(block, 'tile', list(enumerate(way)))  3.57 us
    ppermute x4, starting transfers between devices, swap_line(): lax.ppermute(rider, 'tile', list(enumerate(way)))  2.54 us
  transfers between devices with their start and end apart: 23, of which 10 were waited for; matrix products, arithmetic and copies ran while one was open for 0% of the time, Pallas kernels for 12%

profile of v8, /device:TPU:0, one launch (start us, length us, event | category | flops | bytes accessed | tf_op | source)
XLA Modules:
  0.0 55.5 jit_solution(11622179034708631116)
XLA Ops:
  0.6 1.4 %first_strips.1 = (bf16[96,128]{1,0:T(8,128)(2,1)S(1)}, bf16[96,128]{1,0:T(8,128)(2,1)S(1)}, bf16[96,128]{1,0:T(8,128)(2,1)S(1)}, bf16[96,128]{1,0:T(8,128)(2,1)...) custom-call(s32[4,16]{1,0:T(4,128)} %bitcast.24, ...), custom_call_target="tpu_custom_call" | custom-call | bytes 2097152 | tf_op jit(solution)/shard_map/first_strips/pallas_call | solution.py:565
  2.1 5.1 %collective-permute-start = (bf16[96,128]{1,0:T(8,128)(2,1)S(1)}, bf16[96,128]{1,0:T(8,128)(2,1)S(1)}, u32[]{:S(2)}, u32[]{:S(2)}) collective-permute-start(bf16[96,128]{1,0:T(8,128)(2,1)S(1)} %get-tuple-element.97), channel_id=1, source_target_pairs={{0,12},{1,13},{2,14},{3,15},{4,8},{5,9},{6,10},{7,11},{8,4},{9,5},... | collective-permute-start | bytes 73736 | tf_op jit(solution)/shard_map/ppermute | solution.py:94
  7.2 0.5 collective-permute-start.1
  7.7 1.7 %collective-permute-start.2 = (bf16[96,128]{1,0:T(8,128)(2,1)S(1)}, bf16[96,128]{1,0:T(8,128)(2,1)S(1)}, u32[]{:S(2)}, u32[]{:S(2)}) collective-permute-start(bf16[96,128]{1,0:T(8,128)(2,1)S(1)} %get-tuple-element.99), channel_id=1, source_target_pairs={{0,4},{1,5},{2,6},{3,7},{4,0},{5,1},{6,2},{7,3},{8,12},{9,13},{10,... | collective-permute-start | bytes 73736 | tf_op jit(solution)/shard_map/ppermute | solution.py:94
  9.3 1.7 %first_bulk.1 = (bf16[1200,768]{1,0:T(8,128)(2,1)S(1)}, f32[24,48,256]{2,1,0:T(8,128)S(1)}, bf16[24,48,256]{2,1,0:T(8,128)(2,1)S(1)}, bf16[24,48,256]{2,1,0:T(8,128)(2,1)S(1)}) custom-call(bf16[48,48,128]{2,1,0:T(8,128)(2,1)S(1)} %get-tuple-element.94.block, bf16[9,128,128]{2,1,0:T(8,128)(2,1)S(1)} %get-tuple-element.95.weight.refs_4_), custom_call_target="tpu_custom_call" | custom-call | flops 679477248 | bytes 2097152 | tf_op jit(solution)/shard_map/first_bulk/pallas_call | solution.py:565
  11.0 0.0 collective-permute-done.refs_0_.refs_13_
  11.0 2.1 %collective-permute-done.1.refs_1_.refs_14_ = bf16[96,128]{1,0:T(8,128)(2,1)S(1)} collective-permute-done((bf16[96,128]{1,0:T(8,128)(2,1)S(1)}, bf16[96,128]{1,0:T(8,128)(2,1)S(1)}, u32[]{:S(2)}, u32[]{:S(2)}) %collective-permute-start.1) | collective-permute-done | bytes 24608 | tf_op jit(solution)/shard_map/ppermute | solution.py:94
  13.1 0.0 collective-permute-done.2.refs_2_.refs_15_
  13.1 0.0 copy-start.1
  13.2 0.7 %first_edges.1 = (bf16[112,128]{1,0:T(8,128)(2,1)S(1)}, bf16[112,128]{1,0:T(8,128)(2,1)S(1)}, bf16[112,128]{1,0:T(8,128)(2,1)S(1)}, bf16[112,128]{1,0:T(8,128)(2...) custom-call(s32[12,8,128]{2,1,0:T(8,128)S(1)} %get-tuple-element.93., ...), custom_call_target="tpu_custom_call" | custom-call | bytes 2097152 | tf_op jit(solution)/shard_map/first_edges/pallas_call | solution.py:565
  13.8 0.1 collective-permute-start.4
  13.9 1.8 %collective-permute-start.5 = (bf16[112,128]{1,0:T(8,128)(2,1)S(1)}, bf16[112,128]{1,0:T(8,128)(2,1)S(1)}, u32[]{:S(2)}, u32[]{:S(2)}) collective-permute-start(bf16[112,128]{1,0:T(8,128)(2,1)S(1)} %get-tuple-element.108), channel_id=1, source_target_pairs={{0,15},{1,2},{2,1},{3,4},{4,3},{5,6},{6,5},{7,8},{8,7},{9,10},{10,... | collective-permute-start | bytes 86024 | tf_op jit(solution)/shard_map/ppermute | solution.py:94
  15.8 1.0 %collective-permute-start.6 = (bf16[112,128]{1,0:T(8,128)(2,1)S(1)}, bf16[112,128]{1,0:T(8,128)(2,1)S(1)}, u32[]{:S(2)}, u32[]{:S(2)}) collective-permute-start(bf16[112,128]{1,0:T(8,128)(2,1)S(1)} %get-tuple-element.109), channel_id=1, source_target_pairs={{0,4},{1,5},{2,6},{3,7},{4,0},{5,1},{6,2},{7,3},{8,12},{9,13},{10,... | collective-permute-start | bytes 86024 | tf_op jit(solution)/shard_map/ppermute | solution.py:94
  16.8 1.7 %second_bulk.1 = (bf16[1200,768]{1,0:T(8,128)(2,1)S(1)}, f32[24,48,256]{2,1,0:T(8,128)S(1)}, bf16[24,48,256]{2,1,0:T(8,128)(2,1)S(1)}, bf16[24,48,256]{2,1,0:T(8,128)(2,1)S(1)}) custom-call(bf16[24,48,256]{2,1,0:T(8,128)(2,1)S(1)} %get-tuple-element.96.hidden, f32[24,8,256]{2,1,0:T(8,128)S(1)} %get-tuple-element.102.left, ...), custom_call_target="tpu_custom_call" | custom-call | flops 679477248 | bytes 2097152 | tf_op jit(solution)/shard_map/second_bulk/pallas_call | solution.py:565
  18.5 1.1 %collective-permute-done.4.refs_0_.refs_17_ = bf16[112,128]{1,0:T(8,128)(2,1)S(1)} collective-permute-done((bf16[112,128]{1,0:T(8,128)(2,1)S(1)}, bf16[112,128]{1,0:T(8,128)(2,1)S(1)}, u32[]{:S(2)}, u32[]{:S(2)}) %collective-permute-start.4) | collective-permute-done | bytes 28704 | tf_op jit(solution)/shard_map/ppermute | solution.py:94
  19.6 0.4 collective-permute-done.5.refs_1_.refs_18_
  20.0 0.0 collective-permute-done.6.refs_2_.refs_19_
  20.0 0.9 %second_edges.1 = (bf16[48,128]{1,0:T(8,128)(2,1)S(1)}, bf16[48,128]{1,0:T(8,128)(2,1)S(1)}, bf16[48,128]{1,0:T(8,128)(2,1)S(1)}, bf16[48,128]{1,0:T(8,128)(2,1)...) custom-call(s32[12,8,128]{2,1,0:T(8,128)S(1)} %get-tuple-element.93., ...), custom_call_target="tpu_custom_call" | custom-call | bytes 2097152 | tf_op jit(solution)/shard_map/second_edges/pallas_call | solution.py:565
  20.9 2.4 %second_back.1 = (f32[9,128,128]{2,1,0:T(8,128)S(1)}, f32[24,48,256]{2,1,0:T(8,128)S(1)}, bf16[24,48,256]{2,1,0:T(8,128)(2,1)S(1)}) custom-call(bf16[24,48,256]{2,1,0:T(8,128)(2,1)S(1)} %get-tuple-element.106.refs_0_, f32[24,8,256]{2,1,0:T(8,128)S(1)} %get-tuple-element.112.refs_1_, f32[24,8,256]{2,1,0:T(8,128)S(1)} %get-tuple-element.113.refs_2_, ...), custom_call_target="tpu_custom_call" | custom-call | flops 1358954496 | bytes 2097152 | tf_op jit(solution)/shard_map/second_back/pallas_call | solution.py:565
  23.3 1.6 %first_grads.1 = (bf16[24,48,256]{2,1,0:T(8,128)(2,1)S(1)}, f32[9,128,128]{2,1,0:T(8,128)S(1)}, bf16[9,128,128]{2,1,0:T(8,128)(2,1)S(1)}) custom-call(s32[12,8,128]{2,1,0:T(8,128)S(1)} %get-tuple-element.93.found, f32[24,48,256]{2,1,0:T(8,128)S(1)} %get-tuple-element.119.refs_0_.refs_1_.refs_2_.refs_3_.refs_5_.refs_6_.refs_7_.refs_8_, ...), custom_call_target="tpu_custom_call" | custom-call | flops 679477248 | bytes 2097152 | tf_op jit(solution)/shard_map/first_grads/pallas_call | solution.py:565
  24.9 0.1 collective-permute-start.8
  25.0 1.6 %collective-permute-done.8.given = bf16[1152,128]{1,0:T(8,128)(2,1)S(1)} collective-permute-done((bf16[1152,128]{1,0:T(8,128)(2,1)S(1)}, bf16[1152,128]{1,0:T(8,128)(2,1)S(1)}, u32[]{:S(2)}, u32[]{:S(2)}) %collective-permute-start.8) | collective-permute-done | bytes 294944 | tf_op jit(solution)/shard_map/ppermute | solution.py:585
  26.5 0.1 share_out.1
  26.6 2.0 %collective-permute-start.9 = (bf16[336,128]{1,0:T(8,128)(2,1)S(1)}, bf16[336,128]{1,0:T(8,128)(2,1)S(1)}, u32[]{:S(2)}, u32[]{:S(2)}) collective-permute-start(bf16[336,128]{1,0:T(8,128)(2,1)S(1)} %get-tuple-element.141), channel_id=1, source_target_pairs={{0,12},{1,13},{2,14},{3,15},{4,8},{5,9},{6,10},{7,11},{8,4},{9,5},... | collective-permute-start | bytes 258056 | tf_op jit(solution)/shard_map/ppermute | solution.py:585
  28.6 2.4 %collective-permute-start.13 = (bf16[288,128]{1,0:T(8,128)(2,1)S(1)}, bf16[288,128]{1,0:T(8,128)(2,1)S(1)}, u32[]{:S(2)}, u32[]{:S(2)}) collective-permute-start(bf16[288,128]{1,0:T(8,128)(2,1)S(1)} %get-tuple-element.155), channel_id=1, source_target_pairs={{0,8},{1,9},{2,10},{3,11},{4,12},{5,13},{6,14},{7,15},{8,0},{9,1},... | collective-permute-start | bytes 221192 | tf_op jit(solution)/shard_map/ppermute | solution.py:585
  31.1 1.2 %collective-permute-start.10 = (bf16[48,128]{1,0:T(8,128)(2,1)S(1)}, bf16[48,128]{1,0:T(8,128)(2,1)S(1)}, u32[]{:S(2)}, u32[]{:S(2)}) collective-permute-start(bf16[48,128]{1,0:T(8,128)(2,1)S(1)} %get-tuple-element.142), channel_id=1, source_target_pairs={{0,15},{1,2},{2,1},{3,4},{4,3},{5,6},{6,5},{7,8},{8,7},{9,10},{10,... | collective-permute-start | bytes 36872 | tf_op jit(solution)/shard_map/ppermute | solution.py:634
  32.3 0.0 collective-permute-start.12
  32.3 3.2 %collective-permute-done.13.refs_1_ = bf16[288,128]{1,0:T(8,128)(2,1)S(1)} collective-permute-done((bf16[288,128]{1,0:T(8,128)(2,1)S(1)}, bf16[288,128]{1,0:T(8,128)(2,1)S(1)}, u32[]{:S(2)}, u32[]{:S(2)}) %collective-permute-start.13) | collective-permute-done | bytes 73760 | tf_op jit(solution)/shard_map/ppermute | solution.py:585
  35.5 0.9 %collective-permute-done.11.refs_2_.refs_0_ = bf16[336,128]{1,0:T(8,128)(2,1)S(1)} collective-permute-done((bf16[336,128]{1,0:T(8,128)(2,1)S(1)}, bf16[336,128]{1,0:T(8,128)(2,1)S(1)}, u32[]{:S(2)}, u32[]{:S(2)}) %collective-permute-start.11) | collective-permute-done | bytes 86048 | tf_op jit(solution)/shard_map/ppermute | solution.py:585
  36.4 1.6 %collective-permute-start.16 = (bf16[288,128]{1,0:T(8,128)(2,1)S(1)}, bf16[288,128]{1,0:T(8,128)(2,1)S(1)}, u32[]{:S(2)}, u32[]{:S(2)}) collective-permute-start(bf16[288,128]{1,0:T(8,128)(2,1)S(1)} %add_up.2.base), channel_id=1, source_target_pairs={{0,18},{1,19},{2,16},{3,17},{4,22},{5,23},{6,20},{7,21},{8,26},{9,... | collective-permute-start | bytes 221192 | tf_op jit(solution)/shard_map/ppermute | solution.py:585
  38.0 0.5 collective-permute-start.15
  38.6 1.4 %collective-permute-start.14 = (bf16[288,128]{1,0:T(8,128)(2,1)S(1)}, bf16[288,128]{1,0:T(8,128)(2,1)S(1)}, u32[]{:S(2)}, u32[]{:S(2)}) collective-permute-start(bf16[288,128]{1,0:T(8,128)(2,1)S(1)} %add_up.2.base), channel_id=1, source_target_pairs={{0,2},{1,3},{2,0},{3,1},{4,6},{5,7},{6,4},{7,5},{8,10},{9,11},{10,... | collective-permute-start | bytes 221192 | tf_op jit(solution)/shard_map/ppermute | solution.py:585
  40.0 0.5 first_back.1
  40.4 2.0 %last_bulk.1 = (f32[24,48,256]{2,1,0:T(8,128)S(1)}, bf16[48,48,128]{2,1,0:T(8,128)(2,1)}) custom-call(bf16[24,48,256]{2,1,0:T(8,128)(2,1)S(1)} %get-tuple-element.130.delta, bf16[9,128,128]{2,1,0:T(8,128)(2,1)S(1)} %get-tuple-element.95.weight.refs_4_, bf16[24,48,256]{2,1,0:T(8,128)(2,1)S(1)} %get-tuple-element.131.bulk_out, ...), custom_call_target="tpu_custom_call" | custom-call | flops 679477248 | bytes 2097152 | tf_op jit(solution)/shard_map/last_bulk/pallas_call | solution.py:565
  42.5 0.0 collective-permute-done.15.refs_1_
  42.5 0.6 %collective-permute-done.14.refs_0_ = bf16[288,128]{1,0:T(8,128)(2,1)S(1)} collective-permute-done((bf16[288,128]{1,0:T(8,128)(2,1)S(1)}, bf16[288,128]{1,0:T(8,128)(2,1)S(1)}, u32[]{:S(2)}, u32[]{:S(2)}) %collective-permute-start.14) | collective-permute-done | bytes 73760 | tf_op jit(solution)/shard_map/ppermute | solution.py:585
  43.1 0.5 collective-permute-start.17
  43.7 2.5 %collective-permute-start.19 = (bf16[336,128]{1,0:T(8,128)(2,1)S(1)}, bf16[336,128]{1,0:T(8,128)(2,1)S(1)}, u32[]{:S(2)}, u32[]{:S(2)}) collective-permute-start(bf16[336,128]{1,0:T(8,128)(2,1)S(1)} %get-tuple-element.167), channel_id=1, source_target_pairs={{0,12},{1,13},{2,14},{3,15},{4,8},{5,9},{6,10},{7,11},{8,4},{9,5},... | collective-permute-start | bytes 258056 | tf_op jit(solution)/shard_map/ppermute | solution.py:585
  46.1 0.5 collective-permute-start.18
  46.7 0.2 collective-permute-start.20
  46.9 1.1 %collective-permute-start.21 = (bf16[48,128]{1,0:T(8,128)(2,1)S(1)}, bf16[48,128]{1,0:T(8,128)(2,1)S(1)}, u32[]{:S(2)}, u32[]{:S(2)}) collective-permute-start(bf16[48,128]{1,0:T(8,128)(2,1)S(1)} %get-tuple-element.169), channel_id=1, source_target_pairs={{0,1},{1,0},{2,3},{3,2},{4,5},{5,4},{6,7},{7,6},{8,9},{9,8},{10,11... | collective-permute-start | bytes 36872 | tf_op jit(solution)/shard_map/ppermute | solution.py:634
  48.0 4.6 %collective-permute-done.20.refs_1_ = bf16[48,128]{1,0:T(8,128)(2,1)S(1)} collective-permute-done((bf16[48,128]{1,0:T(8,128)(2,1)S(1)}, bf16[48,128]{1,0:T(8,128)(2,1)S(1)}, u32[]{:S(2)}, u32[]{:S(2)}) %collective-permute-start.20) | collective-permute-done | bytes 12320 | tf_op jit(solution)/shard_map/ppermute | solution.py:634
  52.6 0.0 collective-permute-done.21.refs_3_
  52.6 0.1 collective-permute-done.18.refs_2_
  52.8 0.1 collective-permute-start.22
  52.9 1.0 %last_edges.1 = bf16[48,48,128]{2,1,0:T(8,128)(2,1)} custom-call(s32[12,8,128]{2,1,0:T(8,128)S(1)} %get-tuple-element.93.found, bf16[336,128]{1,0:T(8,128)(2,1)S(1)} %collective-permute-done.19.refs_3_.refs_0_, bf16[48,128]{1,0:T(8,128)(2,1)S(1)} %collective-permute-done.20.refs_1_, bf16[336,128]{1,0:T(8,128)(2,1)S(1)} %collective-permute-done.17.refs_1_.refs_2_, ...), custom_call_target="tpu_custom_call" | custom-call | bytes 2097152 | tf_op jit(solution)/shard_map/last_edges/pallas_call | solution.py:565
  53.8 0.6 %collective-permute-done.22.others = bf16[4,288,128]{2,1,0:T(8,128)(2,1)S(1)} collective-permute-done((bf16[4,288,128]{2,1,0:T(8,128)(2,1)S(1)}, bf16[4,288,128]{2,1,0:T(8,128)(2,1)S(1)}, u32[]{:S(2)}, u32[]{:S(2)}) %collective-permute-start.22) | collective-permute-done | bytes 294944 | tf_op jit(solution)/shard_map/ppermute | solution.py:585
  54.4 1.1 %both_grads.1 = (f32[1152,128]{1,0:T(8,128)}, f32[1152,128]{1,0:T(8,128)}) custom-call(bf16[4,288,128]{2,1,0:T(8,128)(2,1)S(1)} %stack.1.mine, bf16[4,288,128]{2,1,0:T(8,128)(2,1)S(1)} %collective-permute-done.22.others), custom_call_target="tpu_custom_call" | custom-call | bytes 2097152 | tf_op jit(solution)/shard_map/both_grads/pallas_call | solution.py:565
  (17 shorter events, 0.1 us)
Async XLA Ops:
  2.1 8.9 %collective-permute-start = (bf16[96,128]{1,0:T(8,128)(2,1)S(1)}, bf16[96,128]{1,0:T(8,128)(2,1)S(1)}, u32[]{:S(2)}, u32[]{:S(2)}) collective-permute-start(bf16[96,128]{1,0:T(8,128)(2,1)S(1)} %get-tuple-element.97), channel_id=1, source_target_pairs={{0,12},{1,13},{2,14},{3,15},{4,8},{5,9},{6,10},{7,11},{8,4},{9,5},... | collective-permute-start | bytes 73736 | tf_op jit(solution)/shard_map/ppermute | solution.py:94
  7.2 5.9 %collective-permute-start.1 = (bf16[96,128]{1,0:T(8,128)(2,1)S(1)}, bf16[96,128]{1,0:T(8,128)(2,1)S(1)}, u32[]{:S(2)}, u32[]{:S(2)}) collective-permute-start(bf16[96,128]{1,0:T(8,128)(2,1)S(1)} %get-tuple-element.98), channel_id=1, source_target_pairs={{0,15},{1,2},{2,1},{3,4},{4,3},{5,6},{6,5},{7,8},{8,7},{9,10},{10,... | collective-permute-start | bytes 73736 | tf_op jit(solution)/shard_map/ppermute | solution.py:94
  7.7 5.5 %collective-permute-start.2 = (bf16[96,128]{1,0:T(8,128)(2,1)S(1)}, bf16[96,128]{1,0:T(8,128)(2,1)S(1)}, u32[]{:S(2)}, u32[]{:S(2)}) collective-permute-start(bf16[96,128]{1,0:T(8,128)(2,1)S(1)} %get-tuple-element.99), channel_id=1, source_target_pairs={{0,4},{1,5},{2,6},{3,7},{4,0},{5,1},{6,2},{7,3},{8,12},{9,13},{10,... | collective-permute-start | bytes 73736 | tf_op jit(solution)/shard_map/ppermute | solution.py:94
  9.3 3.8 %collective-permute-start.3 = (bf16[96,128]{1,0:T(8,128)(2,1)S(1)}, bf16[96,128]{1,0:T(8,128)(2,1)S(1)}, u32[]{:S(2)}, u32[]{:S(2)}) collective-permute-start(bf16[96,128]{1,0:T(8,128)(2,1)S(1)} %get-tuple-element.100), channel_id=1, source_target_pairs={{0,1},{1,0},{2,3},{3,2},{4,5},{5,4},{6,7},{7,6},{8,9},{9,8},{10,11... | collective-permute-start | bytes 73736 | tf_op jit(solution)/shard_map/ppermute | solution.py:94
  13.1 3.7 %copy-start = (bf16[1,1,48,48,128]{4,3,2,1,0:T(8,128)(2,1)S(1)}, bf16[1,1,48,48,128]{4,3,2,1,0:T(8,128)(2,1)}, u32[]{:S(2)}) copy-start(bf16[1,1,48,48,128]{4,3,2,1,0:T(8,128)(2,1)} %param.9) | copy-start | bytes 1769476
  13.1 3.7 %copy-start.1 = (bf16[3,3,128,128]{3,2,1,0:T(8,128)(2,1)S(1)}, bf16[3,3,128,128]{3,2,1,0:T(8,128)(2,1)}, u32[]{:S(2)}) copy-start(bf16[3,3,128,128]{3,2,1,0:T(8,128)(2,1)} %param.7) | copy-start | bytes 884740
  13.8 5.8 %collective-permute-start.4 = (bf16[112,128]{1,0:T(8,128)(2,1)S(1)}, bf16[112,128]{1,0:T(8,128)(2,1)S(1)}, u32[]{:S(2)}, u32[]{:S(2)}) collective-permute-start(bf16[112,128]{1,0:T(8,128)(2,1)S(1)} %get-tuple-element.107), channel_id=1, source_target_pairs={{0,12},{1,13},{2,14},{3,15},{4,8},{5,9},{6,10},{7,11},{8,4},{9,5},... | collective-permute-start | bytes 86024 | tf_op jit(solution)/shard_map/ppermute | solution.py:94
  13.9 6.1 %collective-permute-start.5 = (bf16[112,128]{1,0:T(8,128)(2,1)S(1)}, bf16[112,128]{1,0:T(8,128)(2,1)S(1)}, u32[]{:S(2)}, u32[]{:S(2)}) collective-permute-start(bf16[112,128]{1,0:T(8,128)(2,1)S(1)} %get-tuple-element.108), channel_id=1, source_target_pairs={{0,15},{1,2},{2,1},{3,4},{4,3},{5,6},{6,5},{7,8},{8,7},{9,10},{10,... | collective-permute-start | bytes 86024 | tf_op jit(solution)/shard_map/ppermute | solution.py:94
  15.8 4.2 %collective-permute-start.6 = (bf16[112,128]{1,0:T(8,128)(2,1)S(1)}, bf16[112,128]{1,0:T(8,128)(2,1)S(1)}, u32[]{:S(2)}, u32[]{:S(2)}) collective-permute-start(bf16[112,128]{1,0:T(8,128)(2,1)S(1)} %get-tuple-element.109), channel_id=1, source_target_pairs={{0,4},{1,5},{2,6},{3,7},{4,0},{5,1},{6,2},{7,3},{8,12},{9,13},{10,... | collective-permute-start | bytes 86024 | tf_op jit(solution)/shard_map/ppermute | solution.py:94
  16.8 3.2 %collective-permute-start.7 = (bf16[112,128]{1,0:T(8,128)(2,1)S(1)}, bf16[112,128]{1,0:T(8,128)(2,1)S(1)}, u32[]{:S(2)}, u32[]{:S(2)}) collective-permute-start(bf16[112,128]{1,0:T(8,128)(2,1)S(1)} %get-tuple-element.110), channel_id=1, source_target_pairs={{0,1},{1,0},{2,3},{3,2},{4,5},{5,4},{6,7},{7,6},{8,9},{9,8},{10,11... | collective-permute-start | bytes 86024 | tf_op jit(solution)/shard_map/ppermute | solution.py:94
  24.9 1.6 %collective-permute-start.8 = (bf16[1152,128]{1,0:T(8,128)(2,1)S(1)}, bf16[1152,128]{1,0:T(8,128)(2,1)S(1)}, u32[]{:S(2)}, u32[]{:S(2)}) collective-permute-start(bf16[1152,128]{1,0:T(8,128)(2,1)S(1)} %bitcast.20), channel_id=1, source_target_pairs={{0,1},{1,0},{2,3},{3,2},{4,5},{5,4},{6,7},{7,6},{8,9},{9,8},{10,11... | collective-permute-start | bytes 884744 | tf_op jit(solution)/shard_map/ppermute | solution.py:585
  26.6 8.9 %collective-permute-start.9 = (bf16[336,128]{1,0:T(8,128)(2,1)S(1)}, bf16[336,128]{1,0:T(8,128)(2,1)S(1)}, u32[]{:S(2)}, u32[]{:S(2)}) collective-permute-start(bf16[336,128]{1,0:T(8,128)(2,1)S(1)} %get-tuple-element.141), channel_id=1, source_target_pairs={{0,12},{1,13},{2,14},{3,15},{4,8},{5,9},{6,10},{7,11},{8,4},{9,5},... | collective-permute-start | bytes 258056 | tf_op jit(solution)/shard_map/ppermute | solution.py:585
  28.6 7.7 %collective-permute-start.11 = (bf16[336,128]{1,0:T(8,128)(2,1)S(1)}, bf16[336,128]{1,0:T(8,128)(2,1)S(1)}, u32[]{:S(2)}, u32[]{:S(2)}) collective-permute-start(bf16[336,128]{1,0:T(8,128)(2,1)S(1)} %get-tuple-element.143), channel_id=1, source_target_pairs={{0,4},{1,5},{2,6},{3,7},{4,0},{5,1},{6,2},{7,3},{8,12},{9,13},{10,... | collective-permute-start | bytes 258056 | tf_op jit(solution)/shard_map/ppermute | solution.py:585
  28.6 6.8 %collective-permute-start.13 = (bf16[288,128]{1,0:T(8,128)(2,1)S(1)}, bf16[288,128]{1,0:T(8,128)(2,1)S(1)}, u32[]{:S(2)}, u32[]{:S(2)}) collective-permute-start(bf16[288,128]{1,0:T(8,128)(2,1)S(1)} %get-tuple-element.155), channel_id=1, source_target_pairs={{0,8},{1,9},{2,10},{3,11},{4,12},{5,13},{6,14},{7,15},{8,0},{9,1},... | collective-permute-start | bytes 221192 | tf_op jit(solution)/shard_map/ppermute | solution.py:585
  31.1 8.9 %collective-permute-start.10 = (bf16[48,128]{1,0:T(8,128)(2,1)S(1)}, bf16[48,128]{1,0:T(8,128)(2,1)S(1)}, u32[]{:S(2)}, u32[]{:S(2)}) collective-permute-start(bf16[48,128]{1,0:T(8,128)(2,1)S(1)} %get-tuple-element.142), channel_id=1, source_target_pairs={{0,15},{1,2},{2,1},{3,4},{4,3},{5,6},{6,5},{7,8},{8,7},{9,10},{10,... | collective-permute-start | bytes 36872 | tf_op jit(solution)/shard_map/ppermute | solution.py:634
  32.3 7.7 %collective-permute-start.12 = (bf16[48,128]{1,0:T(8,128)(2,1)S(1)}, bf16[48,128]{1,0:T(8,128)(2,1)S(1)}, u32[]{:S(2)}, u32[]{:S(2)}) collective-permute-start(bf16[48,128]{1,0:T(8,128)(2,1)S(1)} %get-tuple-element.144), channel_id=1, source_target_pairs={{0,1},{1,0},{2,3},{3,2},{4,5},{5,4},{6,7},{7,6},{8,9},{9,8},{10,11... | collective-permute-start | bytes 36872 | tf_op jit(solution)/shard_map/ppermute | solution.py:634
  36.4 6.1 %collective-permute-start.16 = (bf16[288,128]{1,0:T(8,128)(2,1)S(1)}, bf16[288,128]{1,0:T(8,128)(2,1)S(1)}, u32[]{:S(2)}, u32[]{:S(2)}) collective-permute-start(bf16[288,128]{1,0:T(8,128)(2,1)S(1)} %add_up.2.base), channel_id=1, source_target_pairs={{0,18},{1,19},{2,16},{3,17},{4,22},{5,23},{6,20},{7,21},{8,26},{9,... | collective-permute-start | bytes 221192 | tf_op jit(solution)/shard_map/ppermute | solution.py:585
  38.0 4.5 %collective-permute-start.15 = (bf16[288,128]{1,0:T(8,128)(2,1)S(1)}, bf16[288,128]{1,0:T(8,128)(2,1)S(1)}, u32[]{:S(2)}, u32[]{:S(2)}) collective-permute-start(bf16[288,128]{1,0:T(8,128)(2,1)S(1)} %add_up.2.base), channel_id=1, source_target_pairs={{0,16},{1,17},{2,18},{3,19},{4,20},{5,21},{6,22},{7,23},{8,24},{9,... | collective-permute-start | bytes 221192 | tf_op jit(solution)/shard_map/ppermute | solution.py:585
  38.6 4.5 %collective-permute-start.14 = (bf16[288,128]{1,0:T(8,128)(2,1)S(1)}, bf16[288,128]{1,0:T(8,128)(2,1)S(1)}, u32[]{:S(2)}, u32[]{:S(2)}) collective-permute-start(bf16[288,128]{1,0:T(8,128)(2,1)S(1)} %add_up.2.base), channel_id=1, source_target_pairs={{0,2},{1,3},{2,0},{3,1},{4,6},{5,7},{6,4},{7,5},{8,10},{9,11},{10,... | collective-permute-start | bytes 221192 | tf_op jit(solution)/shard_map/ppermute | solution.py:585
  43.1 9.6 %collective-permute-start.17 = (bf16[336,128]{1,0:T(8,128)(2,1)S(1)}, bf16[336,128]{1,0:T(8,128)(2,1)S(1)}, u32[]{:S(2)}, u32[]{:S(2)}) collective-permute-start(bf16[336,128]{1,0:T(8,128)(2,1)S(1)} %get-tuple-element.165), channel_id=1, source_target_pairs={{0,4},{1,5},{2,6},{3,7},{4,0},{5,1},{6,2},{7,3},{8,12},{9,13},{10,... | collective-permute-start | bytes 258056 | tf_op jit(solution)/shard_map/ppermute | solution.py:585
  43.7 9.1 %collective-permute-start.19 = (bf16[336,128]{1,0:T(8,128)(2,1)S(1)}, bf16[336,128]{1,0:T(8,128)(2,1)S(1)}, u32[]{:S(2)}, u32[]{:S(2)}) collective-permute-start(bf16[336,128]{1,0:T(8,128)(2,1)S(1)} %get-tuple-element.167), channel_id=1, source_target_pairs={{0,12},{1,13},{2,14},{3,15},{4,8},{5,9},{6,10},{7,11},{8,4},{9,5},... | collective-permute-start | bytes 258056 | tf_op jit(solution)/shard_map/ppermute | solution.py:585
  46.1 6.6 %collective-permute-start.18 = (bf16[288,128]{1,0:T(8,128)(2,1)S(1)}, bf16[288,128]{1,0:T(8,128)(2,1)S(1)}, u32[]{:S(2)}, u32[]{:S(2)}) collective-permute-start(bf16[288,128]{1,0:T(8,128)(2,1)S(1)} %get-tuple-element.166.refs_0_), channel_id=1, source_target_pairs={{0,8},{1,9},{2,10},{3,11},{4,12},{5,13},{6,14},{7,15},{8,0},{9,1},... | collective-permute-start | bytes 221192 | tf_op jit(solution)/shard_map/ppermute | solution.py:585
  46.7 5.9 %collective-permute-start.20 = (bf16[48,128]{1,0:T(8,128)(2,1)S(1)}, bf16[48,128]{1,0:T(8,128)(2,1)S(1)}, u32[]{:S(2)}, u32[]{:S(2)}) collective-permute-start(bf16[48,128]{1,0:T(8,128)(2,1)S(1)} %get-tuple-element.168), channel_id=1, source_target_pairs={{0,15},{1,2},{2,1},{3,4},{4,3},{5,6},{6,5},{7,8},{8,7},{9,10},{10,... | collective-permute-start | bytes 36872 | tf_op jit(solution)/shard_map/ppermute | solution.py:634
  46.9 5.7 %collective-permute-start.21 = (bf16[48,128]{1,0:T(8,128)(2,1)S(1)}, bf16[48,128]{1,0:T(8,128)(2,1)S(1)}, u32[]{:S(2)}, u32[]{:S(2)}) collective-permute-start(bf16[48,128]{1,0:T(8,128)(2,1)S(1)} %get-tuple-element.169), channel_id=1, source_target_pairs={{0,1},{1,0},{2,3},{3,2},{4,5},{5,4},{6,7},{7,6},{8,9},{9,8},{10,11... | collective-permute-start | bytes 36872 | tf_op jit(solution)/shard_map/ppermute | solution.py:634
  52.8 1.6 %collective-permute-start.22 = (bf16[4,288,128]{2,1,0:T(8,128)(2,1)S(1)}, bf16[4,288,128]{2,1,0:T(8,128)(2,1)S(1)}, u32[]{:S(2)}, u32[]{:S(2)}) collective-permute-start(bf16[4,288,128]{2,1,0:T(8,128)(2,1)S(1)} %stack.1.mine), channel_id=1, source_target_pairs={{0,1},{1,0},{2,3},{3,2},{4,5},{5,4},{6,7},{7,6},{8,9},{9,8},{10,11... | collective-permute-start | bytes 884744 | tf_op jit(solution)/shard_map/ppermute | solution.py:585

commit v9 on v8

--- a/solution.py
+++ b/solution.py
@@ -560,14 +560,14 @@
         grad[2 * i + 1] = pairs[i, :, c:].astype(bf16)
 
 
-def call(kernel, name, ins, outs, scratch, cost=0, room=16 << 20):
+def call(kernel, name, ins, outs, scratch, cost=0, room=16 << 20, out_spec=None):
     whole = pl.BlockSpec(memory_space=pltpu.VMEM)
     return pl.pallas_call(
         kernel,
         name=name,
         grid=(1,),
         in_specs=[spec or whole for _, spec in ins],
-        out_specs=[whole] * len(outs),
+        out_specs=[out_spec or whole] * len(outs),
         out_shape=outs,
         scratch_shapes=scratch,
         compiler_params=pltpu.CompilerParams(vmem_limit_bytes=room),
@@ -684,14 +684,21 @@
         refs[4][k] = refs[k][0:rows]
 
 
-def both_grads(mine, others, first, second):
+def both_grads(mine, others, first, second, one, two, sent):
     rows = mine.shape[1]
     core, seat = lax.axis_index("tile") & 1, seat_of()
+    copies = []
     for k in range(4):
+        here, there = mine[k].astype(f32), others[k].astype(f32)
+        one[k] = jnp.where(core == 0, here, there)
+        two[k] = jnp.where(core == 0, there, here)
         place = pl.ds(pl.multiple_of((seat ^ k) * rows, rows), rows)
-        one, two = mine[k].astype(f32), others[k].astype(f32)
-        first[place, :] = jnp.where(core == 0, one, two)
-        second[place, :] = jnp.where(core == 0, two, one)
+        for which, (room, out) in enumerate(((one, first), (two, second))):
+            copy = pltpu.make_async_copy(room.at[k], out.at[place], sent.at[which, k])
+            copy.start()
+            copies.append(copy)
+    for copy in copies:
+        copy.wait()
 
 
 def local(fields, weight_first, weight_second, neighbours, cotangent):
@@ -842,7 +849,8 @@
         "both_grads",
         whole([stacked, others]),
         [S((9 * c, c), f32)] * 2,
-        [],
+        [pltpu.VMEM(stacked.shape, f32)] * 2 + [pltpu.SemaphoreType.DMA((2, 4))],
+        out_spec=far,
     )
     grad_first, grad_second = (grad.reshape(shape) for grad in grads)
     return (out_field[None, None], grad_block[None, None], grad_first, grad_second)

time: 55.7 us -> 55.7 us (level)
  no operation moved by 1% of the time
where the time goes in v9:
time: 55.7 us; the launch traced here: 55.5 us
  starting transfers between devices  24.5 us (44%)
  waiting for transfers between devices  15.2 us (27%)
  Pallas kernels  15.1 us (27%)
  between operations  0.76 us (1%)
    pallas_call x15, Pallas kernels, call(): pl.pallas_call(kernel, name=name, grid=(1,), in_specs=[spec or whole for...  15.1 us
    ppermute x11, starting transfers between devices, flip_swap(): return lax.ppermute(block, ('ens', 'tile'), route)  11.7 us
    ppermute x8, starting transfers between devices, swap_all(): lax.ppermute(block, 'tile', list(enumerate(way)))  10.2 us
    ppermute x11, waiting for transfers between devices, flip_swap(): return lax.ppermute(block, ('ens', 'tile'), route)  7.01 us
    ppermute x4, waiting for transfers between devices, swap_line(): lax.ppermute(rider, 'tile', list(enumerate(way)))  4.58 us
    ppermute x8, waiting for transfers between devices, swap_all(): lax.ppermute(block, 'tile', list(enumerate(way)))  3.57 us
    ppermute x4, starting transfers between devices, swap_line(): lax.ppermute(rider, 'tile', list(enumerate(way)))  2.54 us
  transfers between devices with their start and end apart: 23, of which 10 were waited for; matrix products, arithmetic and copies ran while one was open for 0% of the time, Pallas kernels for 12%

profile of v9, /device:TPU:0, one launch (start us, length us, event | category | flops | bytes accessed | tf_op | source)
XLA Modules:
  0.0 55.5 jit_solution(3199795972025211859)
XLA Ops:
  0.6 1.4 %first_strips.1 = (bf16[96,128]{1,0:T(8,128)(2,1)S(1)}, bf16[96,128]{1,0:T(8,128)(2,1)S(1)}, bf16[96,128]{1,0:T(8,128)(2,1)S(1)}, bf16[96,128]{1,0:T(8,128)(2,1)...) custom-call(s32[4,16]{1,0:T(4,128)} %bitcast.24, ...), custom_call_target="tpu_custom_call" | custom-call | bytes 2097152 | tf_op jit(solution)/shard_map/first_strips/pallas_call | solution.py:565
  2.1 5.1 %collective-permute-start = (bf16[96,128]{1,0:T(8,128)(2,1)S(1)}, bf16[96,128]{1,0:T(8,128)(2,1)S(1)}, u32[]{:S(2)}, u32[]{:S(2)}) collective-permute-start(bf16[96,128]{1,0:T(8,128)(2,1)S(1)} %get-tuple-element.97), channel_id=1, source_target_pairs={{0,12},{1,13},{2,14},{3,15},{4,8},{5,9},{6,10},{7,11},{8,4},{9,5},... | collective-permute-start | bytes 73736 | tf_op jit(solution)/shard_map/ppermute | solution.py:94
  7.2 0.5 collective-permute-start.1
  7.7 1.7 %collective-permute-start.2 = (bf16[96,128]{1,0:T(8,128)(2,1)S(1)}, bf16[96,128]{1,0:T(8,128)(2,1)S(1)}, u32[]{:S(2)}, u32[]{:S(2)}) collective-permute-start(bf16[96,128]{1,0:T(8,128)(2,1)S(1)} %get-tuple-element.99), channel_id=1, source_target_pairs={{0,4},{1,5},{2,6},{3,7},{4,0},{5,1},{6,2},{7,3},{8,12},{9,13},{10,... | collective-permute-start | bytes 73736 | tf_op jit(solution)/shard_map/ppermute | solution.py:94
  9.3 0.0 collective-permute-start.3
  9.3 1.7 %first_bulk.1 = (bf16[1200,768]{1,0:T(8,128)(2,1)S(1)}, f32[24,48,256]{2,1,0:T(8,128)S(1)}, bf16[24,48,256]{2,1,0:T(8,128)(2,1)S(1)}, bf16[24,48,256]{2,1,0:T(8,128)(2,1)S(1)}) custom-call(bf16[48,48,128]{2,1,0:T(8,128)(2,1)S(1)} %get-tuple-element.94.block, bf16[9,128,128]{2,1,0:T(8,128)(2,1)S(1)} %get-tuple-element.95.weight.refs_4_), custom_call_target="tpu_custom_call" | custom-call | flops 679477248 | bytes 2097152 | tf_op jit(solution)/shard_map/first_bulk/pallas_call | solution.py:565
  11.0 2.1 %collective-permute-done.1.refs_1_.refs_14_ = bf16[96,128]{1,0:T(8,128)(2,1)S(1)} collective-permute-done((bf16[96,128]{1,0:T(8,128)(2,1)S(1)}, bf16[96,128]{1,0:T(8,128)(2,1)S(1)}, u32[]{:S(2)}, u32[]{:S(2)}) %collective-permute-start.1) | collective-permute-done | bytes 24608 | tf_op jit(solution)/shard_map/ppermute | solution.py:94
  13.1 0.0 copy-start.1
  13.2 0.7 %first_edges.1 = (bf16[112,128]{1,0:T(8,128)(2,1)S(1)}, bf16[112,128]{1,0:T(8,128)(2,1)S(1)}, bf16[112,128]{1,0:T(8,128)(2,1)S(1)}, bf16[112,128]{1,0:T(8,128)(2...) custom-call(s32[12,8,128]{2,1,0:T(8,128)S(1)} %get-tuple-element.93., ...), custom_call_target="tpu_custom_call" | custom-call | bytes 2097152 | tf_op jit(solution)/shard_map/first_edges/pallas_call | solution.py:565
  13.8 0.1 collective-permute-start.4
  13.9 1.8 %collective-permute-start.5 = (bf16[112,128]{1,0:T(8,128)(2,1)S(1)}, bf16[112,128]{1,0:T(8,128)(2,1)S(1)}, u32[]{:S(2)}, u32[]{:S(2)}) collective-permute-start(bf16[112,128]{1,0:T(8,128)(2,1)S(1)} %get-tuple-element.108), channel_id=1, source_target_pairs={{0,15},{1,2},{2,1},{3,4},{4,3},{5,6},{6,5},{7,8},{8,7},{9,10},{10,... | collective-permute-start | bytes 86024 | tf_op jit(solution)/shard_map/ppermute | solution.py:94
  15.8 1.0 %collective-permute-start.6 = (bf16[112,128]{1,0:T(8,128)(2,1)S(1)}, bf16[112,128]{1,0:T(8,128)(2,1)S(1)}, u32[]{:S(2)}, u32[]{:S(2)}) collective-permute-start(bf16[112,128]{1,0:T(8,128)(2,1)S(1)} %get-tuple-element.109), channel_id=1, source_target_pairs={{0,4},{1,5},{2,6},{3,7},{4,0},{5,1},{6,2},{7,3},{8,12},{9,13},{10,... | collective-permute-start | bytes 86024 | tf_op jit(solution)/shard_map/ppermute | solution.py:94
  16.8 0.0 collective-permute-start.7
  16.8 1.7 %second_bulk.1 = (bf16[1200,768]{1,0:T(8,128)(2,1)S(1)}, f32[24,48,256]{2,1,0:T(8,128)S(1)}, bf16[24,48,256]{2,1,0:T(8,128)(2,1)S(1)}, bf16[24,48,256]{2,1,0:T(8,128)(2,1)S(1)}) custom-call(bf16[24,48,256]{2,1,0:T(8,128)(2,1)S(1)} %get-tuple-element.96.hidden, f32[24,8,256]{2,1,0:T(8,128)S(1)} %get-tuple-element.102.left, ...), custom_call_target="tpu_custom_call" | custom-call | flops 679477248 | bytes 2097152 | tf_op jit(solution)/shard_map/second_bulk/pallas_call | solution.py:565
  18.5 1.1 %collective-permute-done.4.refs_0_.refs_17_ = bf16[112,128]{1,0:T(8,128)(2,1)S(1)} collective-permute-done((bf16[112,128]{1,0:T(8,128)(2,1)S(1)}, bf16[112,128]{1,0:T(8,128)(2,1)S(1)}, u32[]{:S(2)}, u32[]{:S(2)}) %collective-permute-start.4) | collective-permute-done | bytes 28704 | tf_op jit(solution)/shard_map/ppermute | solution.py:94
  19.6 0.4 collective-permute-done.5.refs_1_.refs_18_
  20.0 0.9 %second_edges.1 = (bf16[48,128]{1,0:T(8,128)(2,1)S(1)}, bf16[48,128]{1,0:T(8,128)(2,1)S(1)}, bf16[48,128]{1,0:T(8,128)(2,1)S(1)}, bf16[48,128]{1,0:T(8,128)(2,1)...) custom-call(s32[12,8,128]{2,1,0:T(8,128)S(1)} %get-tuple-element.93., ...), custom_call_target="tpu_custom_call" | custom-call | bytes 2097152 | tf_op jit(solution)/shard_map/second_edges/pallas_call | solution.py:565
  20.9 2.4 %second_back.1 = (f32[9,128,128]{2,1,0:T(8,128)S(1)}, f32[24,48,256]{2,1,0:T(8,128)S(1)}, bf16[24,48,256]{2,1,0:T(8,128)(2,1)S(1)}) custom-call(bf16[24,48,256]{2,1,0:T(8,128)(2,1)S(1)} %get-tuple-element.106.refs_0_, f32[24,8,256]{2,1,0:T(8,128)S(1)} %get-tuple-element.112.refs_1_, f32[24,8,256]{2,1,0:T(8,128)S(1)} %get-tuple-element.113.refs_2_, ...), custom_call_target="tpu_custom_call" | custom-call | flops 1358954496 | bytes 2097152 | tf_op jit(solution)/shard_map/second_back/pallas_call | solution.py:565
  23.3 1.6 %first_grads.1 = (bf16[24,48,256]{2,1,0:T(8,128)(2,1)S(1)}, f32[9,128,128]{2,1,0:T(8,128)S(1)}, bf16[9,128,128]{2,1,0:T(8,128)(2,1)S(1)}) custom-call(s32[12,8,128]{2,1,0:T(8,128)S(1)} %get-tuple-element.93.found, f32[24,48,256]{2,1,0:T(8,128)S(1)} %get-tuple-element.119.refs_0_.refs_1_.refs_2_.refs_3_.refs_5_.refs_6_.refs_7_.refs_8_, ...), custom_call_target="tpu_custom_call" | custom-call | flops 679477248 | bytes 2097152 | tf_op jit(solution)/shard_map/first_grads/pallas_call | solution.py:565
  24.9 0.1 collective-permute-start.8
  25.0 1.6 %collective-permute-done.8.given = bf16[1152,128]{1,0:T(8,128)(2,1)S(1)} collective-permute-done((bf16[1152,128]{1,0:T(8,128)(2,1)S(1)}, bf16[1152,128]{1,0:T(8,128)(2,1)S(1)}, u32[]{:S(2)}, u32[]{:S(2)}) %collective-permute-start.8) | collective-permute-done | bytes 294944 | tf_op jit(solution)/shard_map/ppermute | solution.py:585
  26.5 0.1 share_out.1
  26.6 2.0 %collective-permute-start.9 = (bf16[336,128]{1,0:T(8,128)(2,1)S(1)}, bf16[336,128]{1,0:T(8,128)(2,1)S(1)}, u32[]{:S(2)}, u32[]{:S(2)}) collective-permute-start(bf16[336,128]{1,0:T(8,128)(2,1)S(1)} %get-tuple-element.141), channel_id=1, source_target_pairs={{0,12},{1,13},{2,14},{3,15},{4,8},{5,9},{6,10},{7,11},{8,4},{9,5},... | collective-permute-start | bytes 258056 | tf_op jit(solution)/shard_map/ppermute | solution.py:585
  28.6 0.0 collective-permute-start.11
  28.6 2.4 %collective-permute-start.13 = (bf16[288,128]{1,0:T(8,128)(2,1)S(1)}, bf16[288,128]{1,0:T(8,128)(2,1)S(1)}, u32[]{:S(2)}, u32[]{:S(2)}) collective-permute-start(bf16[288,128]{1,0:T(8,128)(2,1)S(1)} %get-tuple-element.155), channel_id=1, source_target_pairs={{0,8},{1,9},{2,10},{3,11},{4,12},{5,13},{6,14},{7,15},{8,0},{9,1},... | collective-permute-start | bytes 221192 | tf_op jit(solution)/shard_map/ppermute | solution.py:585
  31.1 1.2 %collective-permute-start.10 = (bf16[48,128]{1,0:T(8,128)(2,1)S(1)}, bf16[48,128]{1,0:T(8,128)(2,1)S(1)}, u32[]{:S(2)}, u32[]{:S(2)}) collective-permute-start(bf16[48,128]{1,0:T(8,128)(2,1)S(1)} %get-tuple-element.142), channel_id=1, source_target_pairs={{0,15},{1,2},{2,1},{3,4},{4,3},{5,6},{6,5},{7,8},{8,7},{9,10},{10,... | collective-permute-start | bytes 36872 | tf_op jit(solution)/shard_map/ppermute | solution.py:634
  32.3 0.0 collective-permute-start.12
  32.3 3.2 %collective-permute-done.13.refs_1_ = bf16[288,128]{1,0:T(8,128)(2,1)S(1)} collective-permute-done((bf16[288,128]{1,0:T(8,128)(2,1)S(1)}, bf16[288,128]{1,0:T(8,128)(2,1)S(1)}, u32[]{:S(2)}, u32[]{:S(2)}) %collective-permute-start.13) | collective-permute-done | bytes 73760 | tf_op jit(solution)/shard_map/ppermute | solution.py:585
  35.5 0.0 collective-permute-done.9.refs_0_.refs_2_
  35.5 0.9 %collective-permute-done.11.refs_2_.refs_0_ = bf16[336,128]{1,0:T(8,128)(2,1)S(1)} collective-permute-done((bf16[336,128]{1,0:T(8,128)(2,1)S(1)}, bf16[336,128]{1,0:T(8,128)(2,1)S(1)}, u32[]{:S(2)}, u32[]{:S(2)}) %collective-permute-start.11) | collective-permute-done | bytes 86048 | tf_op jit(solution)/shard_map/ppermute | solution.py:585
  36.4 1.6 %collective-permute-start.16 = (bf16[288,128]{1,0:T(8,128)(2,1)S(1)}, bf16[288,128]{1,0:T(8,128)(2,1)S(1)}, u32[]{:S(2)}, u32[]{:S(2)}) collective-permute-start(bf16[288,128]{1,0:T(8,128)(2,1)S(1)} %add_up.2.base), channel_id=1, source_target_pairs={{0,18},{1,19},{2,16},{3,17},{4,22},{5,23},{6,20},{7,21},{8,26},{9,... | collective-permute-start | bytes 221192 | tf_op jit(solution)/shard_map/ppermute | solution.py:585
  38.0 0.5 collective-permute-start.15
  38.6 1.4 %collective-permute-start.14 = (bf16[288,128]{1,0:T(8,128)(2,1)S(1)}, bf16[288,128]{1,0:T(8,128)(2,1)S(1)}, u32[]{:S(2)}, u32[]{:S(2)}) collective-permute-start(bf16[288,128]{1,0:T(8,128)(2,1)S(1)} %add_up.2.base), channel_id=1, source_target_pairs={{0,2},{1,3},{2,0},{3,1},{4,6},{5,7},{6,4},{7,5},{8,10},{9,11},{10,... | collective-permute-start | bytes 221192 | tf_op jit(solution)/shard_map/ppermute | solution.py:585
  40.0 0.5 first_back.1
  40.4 2.0 %last_bulk.1 = (f32[24,48,256]{2,1,0:T(8,128)S(1)}, bf16[48,48,128]{2,1,0:T(8,128)(2,1)}) custom-call(bf16[24,48,256]{2,1,0:T(8,128)(2,1)S(1)} %get-tuple-element.130.delta, bf16[9,128,128]{2,1,0:T(8,128)(2,1)S(1)} %get-tuple-element.95.weight.refs_4_, bf16[24,48,256]{2,1,0:T(8,128)(2,1)S(1)} %get-tuple-element.131.bulk_out, ...), custom_call_target="tpu_custom_call" | custom-call | flops 679477248 | bytes 2097152 | tf_op jit(solution)/shard_map/last_bulk/pallas_call | solution.py:565
  42.5 0.0 collective-permute-done.15.refs_1_
  42.5 0.6 %collective-permute-done.14.refs_0_ = bf16[288,128]{1,0:T(8,128)(2,1)S(1)} collective-permute-done((bf16[288,128]{1,0:T(8,128)(2,1)S(1)}, bf16[288,128]{1,0:T(8,128)(2,1)S(1)}, u32[]{:S(2)}, u32[]{:S(2)}) %collective-permute-start.14) | collective-permute-done | bytes 73760 | tf_op jit(solution)/shard_map/ppermute | solution.py:585
  43.1 0.5 collective-permute-start.17
  43.7 2.5 %collective-permute-start.19 = (bf16[336,128]{1,0:T(8,128)(2,1)S(1)}, bf16[336,128]{1,0:T(8,128)(2,1)S(1)}, u32[]{:S(2)}, u32[]{:S(2)}) collective-permute-start(bf16[336,128]{1,0:T(8,128)(2,1)S(1)} %get-tuple-element.167), channel_id=1, source_target_pairs={{0,12},{1,13},{2,14},{3,15},{4,8},{5,9},{6,10},{7,11},{8,4},{9,5},... | collective-permute-start | bytes 258056 | tf_op jit(solution)/shard_map/ppermute | solution.py:585
  46.1 0.5 collective-permute-start.18
  46.7 0.2 collective-permute-start.20
  46.9 1.1 %collective-permute-start.21 = (bf16[48,128]{1,0:T(8,128)(2,1)S(1)}, bf16[48,128]{1,0:T(8,128)(2,1)S(1)}, u32[]{:S(2)}, u32[]{:S(2)}) collective-permute-start(bf16[48,128]{1,0:T(8,128)(2,1)S(1)} %get-tuple-element.169), channel_id=1, source_target_pairs={{0,1},{1,0},{2,3},{3,2},{4,5},{5,4},{6,7},{7,6},{8,9},{9,8},{10,11... | collective-permute-start | bytes 36872 | tf_op jit(solution)/shard_map/ppermute | solution.py:634
  48.0 4.6 %collective-permute-done.20.refs_1_ = bf16[48,128]{1,0:T(8,128)(2,1)S(1)} collective-permute-done((bf16[48,128]{1,0:T(8,128)(2,1)S(1)}, bf16[48,128]{1,0:T(8,128)(2,1)S(1)}, u32[]{:S(2)}, u32[]{:S(2)}) %collective-permute-start.20) | collective-permute-done | bytes 12320 | tf_op jit(solution)/shard_map/ppermute | solution.py:634
  52.6 0.1 collective-permute-done.18.refs_2_
  52.8 0.1 collective-permute-start.22
  52.9 1.0 %last_edges.1 = bf16[48,48,128]{2,1,0:T(8,128)(2,1)} custom-call(s32[12,8,128]{2,1,0:T(8,128)S(1)} %get-tuple-element.93.found, bf16[336,128]{1,0:T(8,128)(2,1)S(1)} %collective-permute-done.19.refs_3_.refs_0_, bf16[48,128]{1,0:T(8,128)(2,1)S(1)} %collective-permute-done.20.refs_1_, bf16[336,128]{1,0:T(8,128)(2,1)S(1)} %collective-permute-done.17.refs_1_.refs_2_, ...), custom_call_target="tpu_custom_call" | custom-call | bytes 2097152 | tf_op jit(solution)/shard_map/last_edges/pallas_call | solution.py:565
  53.8 0.6 %collective-permute-done.22.others = bf16[4,288,128]{2,1,0:T(8,128)(2,1)S(1)} collective-permute-done((bf16[4,288,128]{2,1,0:T(8,128)(2,1)S(1)}, bf16[4,288,128]{2,1,0:T(8,128)(2,1)S(1)}, u32[]{:S(2)}, u32[]{:S(2)}) %collective-permute-start.22) | collective-permute-done | bytes 294944 | tf_op jit(solution)/shard_map/ppermute | solution.py:585
  54.4 1.1 %both_grads.1 = (f32[1152,128]{1,0:T(8,128)}, f32[1152,128]{1,0:T(8,128)}) custom-call(bf16[4,288,128]{2,1,0:T(8,128)(2,1)S(1)} %stack.1.mine, bf16[4,288,128]{2,1,0:T(8,128)(2,1)S(1)} %collective-permute-done.22.others), custom_call_target="tpu_custom_call" | custom-call | bytes 2097152 | tf_op jit(solution)/shard_map/both_grads/pallas_call | solution.py:565
  (17 shorter events, 0.1 us)
Async XLA Ops:
  2.1 8.9 %collective-permute-start = (bf16[96,128]{1,0:T(8,128)(2,1)S(1)}, bf16[96,128]{1,0:T(8,128)(2,1)S(1)}, u32[]{:S(2)}, u32[]{:S(2)}) collective-permute-start(bf16[96,128]{1,0:T(8,128)(2,1)S(1)} %get-tuple-element.97), channel_id=1, source_target_pairs={{0,12},{1,13},{2,14},{3,15},{4,8},{5,9},{6,10},{7,11},{8,4},{9,5},... | collective-permute-start | bytes 73736 | tf_op jit(solution)/shard_map/ppermute | solution.py:94
  7.2 5.9 %collective-permute-start.1 = (bf16[96,128]{1,0:T(8,128)(2,1)S(1)}, bf16[96,128]{1,0:T(8,128)(2,1)S(1)}, u32[]{:S(2)}, u32[]{:S(2)}) collective-permute-start(bf16[96,128]{1,0:T(8,128)(2,1)S(1)} %get-tuple-element.98), channel_id=1, source_target_pairs={{0,15},{1,2},{2,1},{3,4},{4,3},{5,6},{6,5},{7,8},{8,7},{9,10},{10,... | collective-permute-start | bytes 73736 | tf_op jit(solution)/shard_map/ppermute | solution.py:94
  7.7 5.5 %collective-permute-start.2 = (bf16[96,128]{1,0:T(8,128)(2,1)S(1)}, bf16[96,128]{1,0:T(8,128)(2,1)S(1)}, u32[]{:S(2)}, u32[]{:S(2)}) collective-permute-start(bf16[96,128]{1,0:T(8,128)(2,1)S(1)} %get-tuple-element.99), channel_id=1, source_target_pairs={{0,4},{1,5},{2,6},{3,7},{4,0},{5,1},{6,2},{7,3},{8,12},{9,13},{10,... | collective-permute-start | bytes 73736 | tf_op jit(solution)/shard_map/ppermute | solution.py:94
  9.3 3.8 %collective-permute-start.3 = (bf16[96,128]{1,0:T(8,128)(2,1)S(1)}, bf16[96,128]{1,0:T(8,128)(2,1)S(1)}, u32[]{:S(2)}, u32[]{:S(2)}) collective-permute-start(bf16[96,128]{1,0:T(8,128)(2,1)S(1)} %get-tuple-element.100), channel_id=1, source_target_pairs={{0,1},{1,0},{2,3},{3,2},{4,5},{5,4},{6,7},{7,6},{8,9},{9,8},{10,11... | collective-permute-start | bytes 73736 | tf_op jit(solution)/shard_map/ppermute | solution.py:94
  13.1 3.7 %copy-start = (bf16[1,1,48,48,128]{4,3,2,1,0:T(8,128)(2,1)S(1)}, bf16[1,1,48,48,128]{4,3,2,1,0:T(8,128)(2,1)}, u32[]{:S(2)}) copy-start(bf16[1,1,48,48,128]{4,3,2,1,0:T(8,128)(2,1)} %param.9) | copy-start | bytes 1769476
  13.1 3.7 %copy-start.1 = (bf16[3,3,128,128]{3,2,1,0:T(8,128)(2,1)S(1)}, bf16[3,3,128,128]{3,2,1,0:T(8,128)(2,1)}, u32[]{:S(2)}) copy-start(bf16[3,3,128,128]{3,2,1,0:T(8,128)(2,1)} %param.7) | copy-start | bytes 884740
  13.8 5.8 %collective-permute-start.4 = (bf16[112,128]{1,0:T(8,128)(2,1)S(1)}, bf16[112,128]{1,0:T(8,128)(2,1)S(1)}, u32[]{:S(2)}, u32[]{:S(2)}) collective-permute-start(bf16[112,128]{1,0:T(8,128)(2,1)S(1)} %get-tuple-element.107), channel_id=1, source_target_pairs={{0,12},{1,13},{2,14},{3,15},{4,8},{5,9},{6,10},{7,11},{8,4},{9,5},... | collective-permute-start | bytes 86024 | tf_op jit(solution)/shard_map/ppermute | solution.py:94
  13.9 6.1 %collective-permute-start.5 = (bf16[112,128]{1,0:T(8,128)(2,1)S(1)}, bf16[112,128]{1,0:T(8,128)(2,1)S(1)}, u32[]{:S(2)}, u32[]{:S(2)}) collective-permute-start(bf16[112,128]{1,0:T(8,128)(2,1)S(1)} %get-tuple-element.108), channel_id=1, source_target_pairs={{0,15},{1,2},{2,1},{3,4},{4,3},{5,6},{6,5},{7,8},{8,7},{9,10},{10,... | collective-permute-start | bytes 86024 | tf_op jit(solution)/shard_map/ppermute | solution.py:94
  15.8 4.2 %collective-permute-start.6 = (bf16[112,128]{1,0:T(8,128)(2,1)S(1)}, bf16[112,128]{1,0:T(8,128)(2,1)S(1)}, u32[]{:S(2)}, u32[]{:S(2)}) collective-permute-start(bf16[112,128]{1,0:T(8,128)(2,1)S(1)} %get-tuple-element.109), channel_id=1, source_target_pairs={{0,4},{1,5},{2,6},{3,7},{4,0},{5,1},{6,2},{7,3},{8,12},{9,13},{10,... | collective-permute-start | bytes 86024 | tf_op jit(solution)/shard_map/ppermute | solution.py:94
  16.8 3.2 %collective-permute-start.7 = (bf16[112,128]{1,0:T(8,128)(2,1)S(1)}, bf16[112,128]{1,0:T(8,128)(2,1)S(1)}, u32[]{:S(2)}, u32[]{:S(2)}) collective-permute-start(bf16[112,128]{1,0:T(8,128)(2,1)S(1)} %get-tuple-element.110), channel_id=1, source_target_pairs={{0,1},{1,0},{2,3},{3,2},{4,5},{5,4},{6,7},{7,6},{8,9},{9,8},{10,11... | collective-permute-start | bytes 86024 | tf_op jit(solution)/shard_map/ppermute | solution.py:94
  24.9 1.6 %collective-permute-start.8 = (bf16[1152,128]{1,0:T(8,128)(2,1)S(1)}, bf16[1152,128]{1,0:T(8,128)(2,1)S(1)}, u32[]{:S(2)}, u32[]{:S(2)}) collective-permute-start(bf16[1152,128]{1,0:T(8,128)(2,1)S(1)} %bitcast.20), channel_id=1, source_target_pairs={{0,1},{1,0},{2,3},{3,2},{4,5},{5,4},{6,7},{7,6},{8,9},{9,8},{10,11... | collective-permute-start | bytes 884744 | tf_op jit(solution)/shard_map/ppermute | solution.py:585
  26.6 8.9 %collective-permute-start.9 = (bf16[336,128]{1,0:T(8,128)(2,1)S(1)}, bf16[336,128]{1,0:T(8,128)(2,1)S(1)}, u32[]{:S(2)}, u32[]{:S(2)}) collective-permute-start(bf16[336,128]{1,0:T(8,128)(2,1)S(1)} %get-tuple-element.141), channel_id=1, source_target_pairs={{0,12},{1,13},{2,14},{3,15},{4,8},{5,9},{6,10},{7,11},{8,4},{9,5},... | collective-permute-start | bytes 258056 | tf_op jit(solution)/shard_map/ppermute | solution.py:585
  28.6 7.7 %collective-permute-start.11 = (bf16[336,128]{1,0:T(8,128)(2,1)S(1)}, bf16[336,128]{1,0:T(8,128)(2,1)S(1)}, u32[]{:S(2)}, u32[]{:S(2)}) collective-permute-start(bf16[336,128]{1,0:T(8,128)(2,1)S(1)} %get-tuple-element.143), channel_id=1, source_target_pairs={{0,4},{1,5},{2,6},{3,7},{4,0},{5,1},{6,2},{7,3},{8,12},{9,13},{10,... | collective-permute-start | bytes 258056 | tf_op jit(solution)/shard_map/ppermute | solution.py:585
  28.6 6.8 %collective-permute-start.13 = (bf16[288,128]{1,0:T(8,128)(2,1)S(1)}, bf16[288,128]{1,0:T(8,128)(2,1)S(1)}, u32[]{:S(2)}, u32[]{:S(2)}) collective-permute-start(bf16[288,128]{1,0:T(8,128)(2,1)S(1)} %get-tuple-element.155), channel_id=1, source_target_pairs={{0,8},{1,9},{2,10},{3,11},{4,12},{5,13},{6,14},{7,15},{8,0},{9,1},... | collective-permute-start | bytes 221192 | tf_op jit(solution)/shard_map/ppermute | solution.py:585
  31.1 8.9 %collective-permute-start.10 = (bf16[48,128]{1,0:T(8,128)(2,1)S(1)}, bf16[48,128]{1,0:T(8,128)(2,1)S(1)}, u32[]{:S(2)}, u32[]{:S(2)}) collective-permute-start(bf16[48,128]{1,0:T(8,128)(2,1)S(1)} %get-tuple-element.142), channel_id=1, source_target_pairs={{0,15},{1,2},{2,1},{3,4},{4,3},{5,6},{6,5},{7,8},{8,7},{9,10},{10,... | collective-permute-start | bytes 36872 | tf_op jit(solution)/shard_map/ppermute | solution.py:634
  32.3 7.7 %collective-permute-start.12 = (bf16[48,128]{1,0:T(8,128)(2,1)S(1)}, bf16[48,128]{1,0:T(8,128)(2,1)S(1)}, u32[]{:S(2)}, u32[]{:S(2)}) collective-permute-start(bf16[48,128]{1,0:T(8,128)(2,1)S(1)} %get-tuple-element.144), channel_id=1, source_target_pairs={{0,1},{1,0},{2,3},{3,2},{4,5},{5,4},{6,7},{7,6},{8,9},{9,8},{10,11... | collective-permute-start | bytes 36872 | tf_op jit(solution)/shard_map/ppermute | solution.py:634
  36.4 6.1 %collective-permute-start.16 = (bf16[288,128]{1,0:T(8,128)(2,1)S(1)}, bf16[288,128]{1,0:T(8,128)(2,1)S(1)}, u32[]{:S(2)}, u32[]{:S(2)}) collective-permute-start(bf16[288,128]{1,0:T(8,128)(2,1)S(1)} %add_up.2.base), channel_id=1, source_target_pairs={{0,18},{1,19},{2,16},{3,17},{4,22},{5,23},{6,20},{7,21},{8,26},{9,... | collective-permute-start | bytes 221192 | tf_op jit(solution)/shard_map/ppermute | solution.py:585
  38.0 4.5 %collective-permute-start.15 = (bf16[288,128]{1,0:T(8,128)(2,1)S(1)}, bf16[288,128]{1,0:T(8,128)(2,1)S(1)}, u32[]{:S(2)}, u32[]{:S(2)}) collective-permute-start(bf16[288,128]{1,0:T(8,128)(2,1)S(1)} %add_up.2.base), channel_id=1, source_target_pairs={{0,16},{1,17},{2,18},{3,19},{4,20},{5,21},{6,22},{7,23},{8,24},{9,... | collective-permute-start | bytes 221192 | tf_op jit(solution)/shard_map/ppermute | solution.py:585
  38.6 4.5 %collective-permute-start.14 = (bf16[288,128]{1,0:T(8,128)(2,1)S(1)}, bf16[288,128]{1,0:T(8,128)(2,1)S(1)}, u32[]{:S(2)}, u32[]{:S(2)}) collective-permute-start(bf16[288,128]{1,0:T(8,128)(2,1)S(1)} %add_up.2.base), channel_id=1, source_target_pairs={{0,2},{1,3},{2,0},{3,1},{4,6},{5,7},{6,4},{7,5},{8,10},{9,11},{10,... | collective-permute-start | bytes 221192 | tf_op jit(solution)/shard_map/ppermute | solution.py:585
  43.1 9.6 %collective-permute-start.17 = (bf16[336,128]{1,0:T(8,128)(2,1)S(1)}, bf16[336,128]{1,0:T(8,128)(2,1)S(1)}, u32[]{:S(2)}, u32[]{:S(2)}) collective-permute-start(bf16[336,128]{1,0:T(8,128)(2,1)S(1)} %get-tuple-element.165), channel_id=1, source_target_pairs={{0,4},{1,5},{2,6},{3,7},{4,0},{5,1},{6,2},{7,3},{8,12},{9,13},{10,... | collective-permute-start | bytes 258056 | tf_op jit(solution)/shard_map/ppermute | solution.py:585
  43.7 9.1 %collective-permute-start.19 = (bf16[336,128]{1,0:T(8,128)(2,1)S(1)}, bf16[336,128]{1,0:T(8,128)(2,1)S(1)}, u32[]{:S(2)}, u32[]{:S(2)}) collective-permute-start(bf16[336,128]{1,0:T(8,128)(2,1)S(1)} %get-tuple-element.167), channel_id=1, source_target_pairs={{0,12},{1,13},{2,14},{3,15},{4,8},{5,9},{6,10},{7,11},{8,4},{9,5},... | collective-permute-start | bytes 258056 | tf_op jit(solution)/shard_map/ppermute | solution.py:585
  46.1 6.6 %collective-permute-start.18 = (bf16[288,128]{1,0:T(8,128)(2,1)S(1)}, bf16[288,128]{1,0:T(8,128)(2,1)S(1)}, u32[]{:S(2)}, u32[]{:S(2)}) collective-permute-start(bf16[288,128]{1,0:T(8,128)(2,1)S(1)} %get-tuple-element.166.refs_0_), channel_id=1, source_target_pairs={{0,8},{1,9},{2,10},{3,11},{4,12},{5,13},{6,14},{7,15},{8,0},{9,1},... | collective-permute-start | bytes 221192 | tf_op jit(solution)/shard_map/ppermute | solution.py:585
  46.7 5.9 %collective-permute-start.20 = (bf16[48,128]{1,0:T(8,128)(2,1)S(1)}, bf16[48,128]{1,0:T(8,128)(2,1)S(1)}, u32[]{:S(2)}, u32[]{:S(2)}) collective-permute-start(bf16[48,128]{1,0:T(8,128)(2,1)S(1)} %get-tuple-element.168), channel_id=1, source_target_pairs={{0,15},{1,2},{2,1},{3,4},{4,3},{5,6},{6,5},{7,8},{8,7},{9,10},{10,... | collective-permute-start | bytes 36872 | tf_op jit(solution)/shard_map/ppermute | solution.py:634
  46.9 5.7 %collective-permute-start.21 = (bf16[48,128]{1,0:T(8,128)(2,1)S(1)}, bf16[48,128]{1,0:T(8,128)(2,1)S(1)}, u32[]{:S(2)}, u32[]{:S(2)}) collective-permute-start(bf16[48,128]{1,0:T(8,128)(2,1)S(1)} %get-tuple-element.169), channel_id=1, source_target_pairs={{0,1},{1,0},{2,3},{3,2},{4,5},{5,4},{6,7},{7,6},{8,9},{9,8},{10,11... | collective-permute-start | bytes 36872 | tf_op jit(solution)/shard_map/ppermute | solution.py:634
  52.8 1.6 %collective-permute-start.22 = (bf16[4,288,128]{2,1,0:T(8,128)(2,1)S(1)}, bf16[4,288,128]{2,1,0:T(8,128)(2,1)S(1)}, u32[]{:S(2)}, u32[]{:S(2)}) collective-permute-start(bf16[4,288,128]{2,1,0:T(8,128)(2,1)S(1)} %stack.1.mine), channel_id=1, source_target_pairs={{0,1},{1,0},{2,3},{3,2},{4,5},{5,4},{6,7},{7,6},{8,9},{9,8},{10,11... | collective-permute-start | bytes 884744 | tf_op jit(solution)/shard_map/ppermute | solution.py:585
